TPU v7x, 32 devices: a whole 2x2x4 slice. The times are simulated.
32 devices in a mesh: expert: 8 (over z, x), tensor: 4 (over y, core).
Axes of the slice: x: 2, y: 2, z: 4, core: 2. Of those that a mesh axis runs over, the one named last changes fastest.
Arguments:
- inputs: bfloat16 [8192, 2048], P('expert'), may hold values from -6 to 6
- attn_gain: float32 [2048], replicated, may hold values from 0.25 to 1.75
- w_query: bfloat16 [2048, 2048], P(None, 'tensor'), may hold values from -1.5 to 1.5
- w_key: bfloat16 [2048, 2048], P(None, 'tensor'), may hold values from -1.5 to 1.5
- w_value: bfloat16 [2048, 2048], P(None, 'tensor'), may hold values from -0.125 to 0.125
- w_output: bfloat16 [2048, 2048], P('tensor'), may hold values from -2 to 2
- query_gain: float32 [2048], P('tensor'), may hold values from 0.25 to 1.75
- key_gain: float32 [2048], P('tensor'), may hold values from 0.25 to 1.75
- moe_gain: float32 [2048], replicated, may hold values from 0.25 to 1.75
- w_router: bfloat16 [2048, 64], replicated, may hold values from -0.0625 to 0.0625
- w_gate: bfloat16 [64, 2048, 1024], P('expert', None, 'tensor'), may hold values from -0.125 to 0.125
- w_up: bfloat16 [64, 2048, 1024], P('expert', None, 'tensor'), may hold values from -0.125 to 0.125
- w_down: bfloat16 [64, 1024, 2048], P('expert', 'tensor'), may hold values from -4 to 4
- routes: int32 [8192, 8], P('expert'), may hold values from 0 to 63, all different within a row; in each aligned block of 1024 rows (0 to 1023, 1024 to 2047, ...) at most 160 rows name the same one
- piece_start: int32 [8, 2], P('expert'), may hold values from 0 to 768, as said below
- piece_length: int32 [8, 2], P('expert'), may hold values from 128 to 256, as said below
- clip_threshold: float32 [16], P('tensor'), may hold values from 1.1313709 to 11.313708
- cotangent: float32 [8192, 2048], P('expert', 'tensor'), may hold values from -6 to 6
Outputs:
- out: float32 [8192, 2048], P('expert', 'tensor')
- grad_input: float32 [8192, 2048], P('expert', 'tensor')
- grad_attn_gain: float32 [2048], replicated
- grad_query: float32 [2048, 2048], P(None, 'tensor')
- grad_key: float32 [2048, 2048], P(None, 'tensor')
- grad_value: float32 [2048, 2048], P(None, 'tensor')
- grad_output: float32 [2048, 2048], P('tensor')
- grad_query_gain: float32 [2048], P('tensor')
- grad_key_gain: float32 [2048], P('tensor')
- grad_moe_gain: float32 [2048], P('tensor')
- grad_router: float32 [2048, 64], replicated
- grad_gate: float32 [64, 2048, 1024], P('expert', None, 'tensor')
- grad_up: float32 [64, 2048, 1024], P('expert', None, 'tensor')
- grad_down: float32 [64, 1024, 2048], P('expert', 'tensor')
- head_max: float32 [16], P('tensor')
- query_clipped: bfloat16 [2048, 2048], P(None, 'tensor')
- key_clipped: bfloat16 [2048, 2048], P(None, 'tensor')
Inputs may be any that keep to these rules, and one draw needn't show every extreme that they name: `routes`: each row names 8 different experts; in each aligned block of 1024 rows (the rows of one device) no expert is named by more than 160 rows. `piece_start`: piece 0 of a sequence lies in its first half, piece 1 starts in its second half. `piece_length`: in each sequence one of the two pieces holds exactly 256 tokens.
All inputs are finite; a program needn't handle non-finite values.
Results may differ from a plain program's by a relative error of at most 0.03.
Values may be sent and summed in bfloat16 or wider, within the bound.
No kernel may reach another device: no remote copies, remote signals or barrier semaphores. Data moves between devices by JAX's collectives and lax.ppermute only.
A program may use at most 576 MiB of HBM per device.

v0:
```python
from functools import partial
import math

import jax
import jax.numpy as jnp
from jax import lax
from jax.sharding import PartitionSpec as P

HD = 128
E = 64
TOP = 8
LENGTH = 1024
CAP = 160


def matmul(left, right):
    return jnp.dot(left, right, preferred_element_type=jnp.float32)


def inside_pieces(start, length, positions):
    return (positions[None, :] >= start[:, None]) & (positions[None, :] < (start + length)[:, None])


def allowed_block(start, length, first, rows):
    query_pos = first + jnp.arange(rows, dtype=jnp.int32)
    key_pos = jnp.arange(LENGTH, dtype=jnp.int32)
    query_in = inside_pieces(start, length, query_pos)
    key_in = inside_pieces(start, length, key_pos)
    return (key_pos[None, :] <= query_pos[:, None]) | jnp.any(
        query_in[:, :, None] & key_in[:, None, :], axis=0
    )


def head_stats(raw, heads):
    parts = raw.reshape(raw.shape[0], heads, HD)
    inverse = lax.rsqrt(jnp.mean(parts * parts, axis=-1, keepdims=True) + 1e-06)
    return (parts * inverse, inverse)


def head_backward(grad_heads, hat, inverse, gain):
    upstream = grad_heads * gain.reshape(hat.shape[1], HD)
    raw = inverse * (upstream - hat * jnp.mean(upstream * hat, axis=-1, keepdims=True))
    return (
        raw.reshape(hat.shape[0], -1).astype(jnp.bfloat16),
        jnp.sum(grad_heads * hat, axis=0).reshape(-1),
    )


def expert_apply(rows, gate_weights, up_weights, down_weights):
    gate_pre = jnp.einsum("slrd,ldf->slrf", rows, gate_weights, preferred_element_type=jnp.float32)
    up_pre = jnp.einsum("slrd,ldf->slrf", rows, up_weights, preferred_element_type=jnp.float32)
    hidden = (jax.nn.silu(gate_pre) * up_pre).astype(jnp.bfloat16)
    partial_out = jnp.einsum(
        "slrf,lfd->slrd", hidden, down_weights, preferred_element_type=jnp.float32
    )
    return (partial_out, gate_pre, up_pre)


def attend_forward(args, block, scale):
    queries, keys, values, start, length = args

    def one_block(index):
        first = index * block
        rows = lax.dynamic_slice_in_dim(queries, first, block, 0)
        scores = jnp.einsum("qhd,khd->hqk", rows, keys, preferred_element_type=jnp.float32) * scale
        masked = jnp.where(allowed_block(start, length, first, block)[None], scores, -1e30)
        top = jnp.max(masked, axis=-1, keepdims=True)
        weights = jnp.exp(masked - top)
        total = jnp.sum(weights, axis=-1, keepdims=True)
        probs = (weights / total).astype(jnp.bfloat16)
        result = jnp.einsum("hqk,khd->qhd", probs, values, preferred_element_type=jnp.float32)
        return (result, (top + jnp.log(total))[..., 0], jnp.max(masked, axis=(1, 2)))

    results, log_sums, tops = lax.map(one_block, jnp.arange(LENGTH // block, dtype=jnp.int32))
    return (results.reshape(LENGTH, queries.shape[1], HD), log_sums, jnp.max(tops, axis=0))


def attend_backward(args, block, scale):
    queries, keys, values, grads_o, log_sums, start, length = args

    def one_block(carry, index):
        key_acc, value_acc = carry
        first = index * block
        rows = lax.dynamic_slice_in_dim(queries, first, block, 0)
        grad_rows = lax.dynamic_slice_in_dim(grads_o, first, block, 0)
        scores = jnp.einsum("qhd,khd->hqk", rows, keys, preferred_element_type=jnp.float32) * scale
        masked = jnp.where(allowed_block(start, length, first, block)[None], scores, -1e30)
        probs = jnp.exp(masked - log_sums[index][:, :, None])
        grad_p = jnp.einsum("qhd,khd->hqk", grad_rows, values, preferred_element_type=jnp.float32)
        delta = jnp.sum(probs * grad_p, axis=-1, keepdims=True)
        grad_s = (probs * (grad_p - delta)).astype(jnp.bfloat16)
        query_part = (
            jnp.einsum("hqk,khd->qhd", grad_s, keys, preferred_element_type=jnp.float32) * scale
        )
        key_acc = (
            key_acc
            + jnp.einsum("hqk,qhd->khd", grad_s, rows, preferred_element_type=jnp.float32) * scale
        )
        value_acc = value_acc + jnp.einsum(
            "hqk,qhd->khd",
            probs.astype(jnp.bfloat16),
            grad_rows,
            preferred_element_type=jnp.float32,
        )
        return ((key_acc, value_acc), query_part)

    zeros = jnp.zeros(keys.shape, jnp.float32)
    (key_grad, value_grad), query_parts = lax.scan(
        one_block, (zeros, zeros), jnp.arange(LENGTH // block, dtype=jnp.int32)
    )
    return (query_parts.reshape(keys.shape), key_grad, value_grad)


def per_device(
    inputs,
    attn_gain,
    w_query,
    w_key,
    w_value,
    w_output,
    query_gain,
    key_gain,
    moe_gain,
    w_router,
    w_gate,
    w_up,
    w_down,
    routes,
    piece_start,
    piece_length,
    clip_threshold,
    cotangent,
):
    tokens_here, width = inputs.shape
    slice_width = cotangent.shape[1]
    column = lax.axis_index("tensor") * slice_width
    heads_here = query_gain.shape[0] // HD
    experts_here = w_gate.shape[0]
    owners = lax.axis_size("expert")
    sequences = tokens_here // LENGTH
    block = min(512, LENGTH)
    scale = 1.0 / math.sqrt(HD)
    inputs_f = inputs.astype(jnp.float32)
    attn_inv = lax.rsqrt(jnp.mean(inputs_f * inputs_f, axis=-1, keepdims=True) + 1e-05)
    attn_hat = inputs_f * attn_inv
    normed_a = (attn_hat * attn_gain).astype(jnp.bfloat16)
    query_hat, query_inv = head_stats(matmul(normed_a, w_query), heads_here)
    key_hat, key_inv = head_stats(matmul(normed_a, w_key), heads_here)
    values = matmul(normed_a, w_value).astype(jnp.bfloat16)
    queries = (query_hat * query_gain.reshape(heads_here, HD)).astype(jnp.bfloat16)
    keys = (key_hat * key_gain.reshape(heads_here, HD)).astype(jnp.bfloat16)
    shape4 = (sequences, LENGTH, heads_here, HD)
    seq_query = queries.reshape(shape4)
    seq_key = keys.reshape(shape4)
    seq_value = values.reshape(shape4)
    results, log_sums, tops = lax.map(
        partial(attend_forward, block=block, scale=scale),
        (seq_query, seq_key, seq_value, piece_start, piece_length),
    )
    attended = results.reshape(tokens_here, heads_here * HD).astype(jnp.bfloat16)
    head_top = lax.pmax(jnp.max(tops, axis=0), "expert")
    branch = lax.psum(matmul(attended, w_output).astype(jnp.bfloat16), "tensor").astype(jnp.float32)
    residual = inputs_f + branch
    moe_inv = lax.rsqrt(jnp.mean(residual * residual, axis=-1, keepdims=True) + 1e-05)
    moe_hat = residual * moe_inv
    normed_m = (moe_hat * moe_gain).astype(jnp.bfloat16)
    router = jax.nn.softmax(matmul(normed_m, w_router), axis=-1)
    picks = routes[:, :, None] == jnp.arange(E, dtype=jnp.int32)
    picks_f = picks.astype(jnp.float32)
    gates = jnp.einsum("nke,ne->nk", picks_f, router)
    chosen = jnp.any(picks, axis=1).astype(jnp.int32)
    earlier = jnp.cumsum(chosen, axis=0) - chosen
    slots = jnp.sum(jnp.where(picks, earlier[:, None, :], 0), axis=2)
    target = routes * CAP + slots
    holder = (
        jnp.full((E * CAP,), -1, jnp.int32)
        .at[target.reshape(-1)]
        .set(jnp.arange(tokens_here * TOP, dtype=jnp.int32))
    )
    filled = holder >= 0
    source = jnp.maximum(holder, 0)
    blank = jnp.zeros((), jnp.bfloat16)
    send_rows = jnp.where(filled[:, None], normed_m[source // TOP], blank).reshape(
        owners, experts_here, CAP, width
    )
    gate_weights, up_weights, down_weights = (w_gate, w_up, w_down)
    rows = lax.all_to_all(send_rows, "expert", split_axis=0, concat_axis=0, tiled=True)
    partial_out, gate_pre, up_pre = expert_apply(rows, w_gate, w_up, w_down)
    summed = lax.psum_scatter(
        partial_out.astype(jnp.bfloat16), "tensor", scatter_dimension=3, tiled=True
    )
    received = (summed, rows, gate_pre, up_pre)
    returned = lax.all_to_all(
        received[0], "expert", split_axis=0, concat_axis=0, tiled=True
    ).reshape(E * CAP, slice_width)
    expert_values = returned[target].astype(jnp.float32)
    mixture = jnp.einsum("nk,nkd->nd", gates, expert_values)
    out = lax.dynamic_slice_in_dim(residual, column, slice_width, 1) + mixture
    gate_grad_part = jnp.einsum("nkd,nd->nk", expert_values, cotangent)
    scaled = (
        (gates[:, :, None] * cotangent[:, None, :])
        .astype(jnp.bfloat16)
        .reshape(tokens_here * TOP, slice_width)
    )
    rows_back = jnp.where(filled[:, None], scaled[source], blank).reshape(
        owners, experts_here, CAP, slice_width
    )
    arrived = lax.all_to_all(rows_back, "expert", split_axis=0, concat_axis=0, tiled=True)
    grad_rows = lax.all_gather(arrived, "tensor", axis=3, tiled=True)
    kept_rows = received[1]
    gate_pre = received[2]
    up_pre = received[3]
    sigma = jax.nn.sigmoid(gate_pre)
    swish = gate_pre * sigma
    hidden = (swish * up_pre).astype(jnp.bfloat16)
    grad_hidden = jnp.einsum(
        "slrd,lfd->slrf", grad_rows, down_weights, preferred_element_type=jnp.float32
    )
    grad_down = jnp.einsum("slrf,slrd->lfd", hidden, grad_rows, preferred_element_type=jnp.float32)
    grad_gate_pre = (grad_hidden * up_pre * sigma * (1.0 + gate_pre * (1.0 - sigma))).astype(
        jnp.bfloat16
    )
    grad_up_pre = (grad_hidden * swish).astype(jnp.bfloat16)
    grad_gate = jnp.einsum(
        "slrd,slrf->ldf", kept_rows, grad_gate_pre, preferred_element_type=jnp.float32
    )
    grad_up = jnp.einsum(
        "slrd,slrf->ldf", kept_rows, grad_up_pre, preferred_element_type=jnp.float32
    )
    grad_in_rows = jnp.einsum(
        "slrf,ldf->slrd", grad_gate_pre, gate_weights, preferred_element_type=jnp.float32
    )
    grad_in_rows = grad_in_rows + jnp.einsum(
        "slrf,ldf->slrd", grad_up_pre, up_weights, preferred_element_type=jnp.float32
    )
    grad_in_sum = lax.psum_scatter(
        grad_in_rows.astype(jnp.bfloat16), "tensor", scatter_dimension=3, tiled=True
    ).astype(jnp.float32)
    grad_back = (
        lax.all_to_all(
            grad_in_sum.astype(jnp.bfloat16), "expert", split_axis=0, concat_axis=0, tiled=True
        )
        .astype(grad_in_sum.dtype)
        .reshape(E * CAP, slice_width)
    )
    expert_path = jnp.sum(grad_back[target], axis=1)
    moe_hat_slice = lax.dynamic_slice_in_dim(moe_hat, column, slice_width, 1)
    gain_slice = lax.dynamic_slice_in_dim(moe_gain, column, slice_width, 0)
    part_dot = jnp.sum(expert_path * gain_slice * moe_hat_slice, axis=-1)
    gate_grad, expert_dot = (
        lax.psum(gate_grad_part.astype(jnp.bfloat16), "tensor").astype(jnp.float32),
        lax.psum(part_dot.astype(jnp.bfloat16), "tensor").astype(jnp.float32),
    )
    grad_probs = jnp.einsum("nk,nke->ne", gate_grad, picks_f)
    grad_logits = (
        router * (grad_probs - jnp.sum(router * grad_probs, axis=-1, keepdims=True))
    ).astype(jnp.bfloat16)
    grad_router = jnp.einsum("nd,ne->de", normed_m, grad_logits, preferred_element_type=jnp.float32)
    router_path = jnp.einsum("ne,de->nd", grad_logits, w_router, preferred_element_type=jnp.float32)
    router_dot = jnp.sum(router_path * moe_gain * moe_hat, axis=-1)
    mean_dot = (expert_dot + router_dot) / width
    grad_normed_slice = expert_path + lax.dynamic_slice_in_dim(router_path, column, slice_width, 1)
    grad_moe_gain = jnp.sum(grad_normed_slice * moe_hat_slice, axis=0)
    grad_residual = cotangent + moe_inv * (
        grad_normed_slice * gain_slice - moe_hat_slice * mean_dot[:, None]
    )
    grad_branch = lax.all_gather(grad_residual.astype(jnp.bfloat16), "tensor", axis=1, tiled=True)
    grad_output = jnp.einsum("nc,nd->cd", attended, grad_branch, preferred_element_type=jnp.float32)
    grad_attended = jnp.einsum(
        "nd,cd->nc", grad_branch, w_output, preferred_element_type=jnp.float32
    ).astype(jnp.bfloat16)
    grad_q, grad_k, grad_v = lax.map(
        partial(attend_backward, block=block, scale=scale),
        (
            seq_query,
            seq_key,
            seq_value,
            grad_attended.reshape(shape4),
            log_sums,
            piece_start,
            piece_length,
        ),
    )
    heads_shape = (tokens_here, heads_here, HD)
    grad_query_raw, grad_query_gain = head_backward(
        grad_q.reshape(heads_shape), query_hat, query_inv, query_gain
    )
    grad_key_raw, grad_key_gain = head_backward(
        grad_k.reshape(heads_shape), key_hat, key_inv, key_gain
    )
    grad_value_raw = grad_v.reshape(tokens_here, heads_here * HD).astype(jnp.bfloat16)
    grad_query = jnp.einsum(
        "nd,nc->dc", normed_a, grad_query_raw, preferred_element_type=jnp.float32
    )
    grad_key = jnp.einsum("nd,nc->dc", normed_a, grad_key_raw, preferred_element_type=jnp.float32)
    grad_value = jnp.einsum(
        "nd,nc->dc", normed_a, grad_value_raw, preferred_element_type=jnp.float32
    )
    grad_normed_a = jnp.einsum(
        "nc,dc->nd", grad_query_raw, w_query, preferred_element_type=jnp.float32
    )
    grad_normed_a = grad_normed_a + jnp.einsum(
        "nc,dc->nd", grad_key_raw, w_key, preferred_element_type=jnp.float32
    )
    grad_normed_a = grad_normed_a + jnp.einsum(
        "nc,dc->nd", grad_value_raw, w_value, preferred_element_type=jnp.float32
    )
    grad_normed_a = lax.psum(grad_normed_a.astype(jnp.bfloat16), "tensor").astype(jnp.float32)
    upstream = grad_normed_a * attn_gain
    grad_attn_gain = jnp.sum(grad_normed_a * attn_hat, axis=0)
    grad_input_full = attn_inv * (
        upstream - attn_hat * jnp.mean(upstream * attn_hat, axis=-1, keepdims=True)
    )
    grad_input = grad_residual + lax.dynamic_slice_in_dim(grad_input_full, column, slice_width, 1)
    totals = (
        lax.psum(grad_query.astype(jnp.bfloat16), "expert").astype(jnp.float32),
        lax.psum(grad_key.astype(jnp.bfloat16), "expert").astype(jnp.float32),
        lax.psum(grad_value.astype(jnp.bfloat16), "expert").astype(jnp.float32),
        lax.psum(grad_output.astype(jnp.bfloat16), "expert").astype(jnp.float32),
        lax.psum(grad_query_gain.astype(jnp.bfloat16), "expert").astype(jnp.float32),
        lax.psum(grad_key_gain.astype(jnp.bfloat16), "expert").astype(jnp.float32),
        lax.psum(grad_attn_gain.astype(jnp.bfloat16), "expert").astype(jnp.float32),
        lax.psum(grad_moe_gain.astype(jnp.bfloat16), "expert").astype(jnp.float32),
        lax.psum(grad_router.astype(jnp.bfloat16), "expert").astype(jnp.float32),
    )
    factor = clip_threshold / jnp.maximum(head_top, clip_threshold)
    spread = jnp.repeat(jnp.sqrt(factor), HD)
    query_clipped = (w_query.astype(jnp.float32) * spread[None, :]).astype(jnp.bfloat16)
    key_clipped = (w_key.astype(jnp.float32) * spread[None, :]).astype(jnp.bfloat16)
    return (
        out,
        grad_input,
        totals[6],
        totals[0],
        totals[1],
        totals[2],
        totals[3],
        totals[4],
        totals[5],
        totals[7],
        totals[8],
        grad_gate,
        grad_up,
        grad_down,
        head_top,
        query_clipped,
        key_clipped,
    )


def solution(mesh):
    return jax.shard_map(
        per_device,
        mesh=mesh,
        in_specs=(
            P("expert", None),
            P(),
            P(None, "tensor"),
            P(None, "tensor"),
            P(None, "tensor"),
            P("tensor", None),
            P("tensor"),
            P("tensor"),
            P(),
            P(),
            P("expert", None, "tensor"),
            P("expert", None, "tensor"),
            P("expert", "tensor", None),
            P("expert", None),
            P("expert", None),
            P("expert", None),
            P("tensor"),
            P("expert", "tensor"),
        ),
        out_specs=(
            P("expert", "tensor"),
            P("expert", "tensor"),
            P(),
            P(None, "tensor"),
            P(None, "tensor"),
            P(None, "tensor"),
            P("tensor", None),
            P("tensor"),
            P("tensor"),
            P("tensor"),
            P(),
            P("expert", None, "tensor"),
            P("expert", None, "tensor"),
            P("expert", "tensor", None),
            P("tensor"),
            P(None, "tensor"),
            P(None, "tensor"),
        ),
        check_vma=False,
    )
```

profile of v0, /device:TPU:10, one launch (start us, length us, event | category | flops | bytes accessed | tf_op | source)
XLA Modules:
  0.0 3637.4 jit_solution(6125788330365120606)
XLA Ops:
  40.3 25.3 while.57
  73.9 18.0 reduce-window.6
  94.1 30.5 scatter_custom_fusion
  125.3 35.1 all-reduce.6.cloned.1.call-done
  174.7 79.1 %gather_fusion = bf16[10240,2048]{1,0:T(8,128)(2,1)} fusion(bf16[1024,2048]{1,0:T(8,128)(2,1)} %get-tuple-element.539, s32[10240]{0:T(1024)S(1)} %get-tuple-element.552), kind=kCustom, calls=%fused_computation | custom fusion | bytes 83927040 | tf_op jit(solution)/shard_map/gather | solution.py:183
  253.8 28.2 broadcast_select_fusion
  282.1 913.9 %all_to_all.20 = bf16[8,8,160,2048]{3,2,1,0:T(8,128)(2,1)} all-to-all(bf16[8,8,160,2048]{3,2,1,0:T(8,128)(2,1)} %broadcast_select_fusion), channel_id=1, replica_groups=mesh['expert'=8,'tensor'=4] {'expert'}, dimensions={0} | all-to-all | bytes 83886080 | tf_op jit(solution)/shard_map/all_to_all | solution.py:187
  1196.0 22.7 fusion.39
  1218.7 26.8 fusion.46
  1245.5 21.1 convert_bitcast_fusion
  1266.6 288.9 %reduce-scatter.3.cloned.1.call-done = bf16[8,8,160,512]{3,2,0,1:T(8,128)(2,1)} async-done(((bf16[8,8,160,2048]{3,2,0,1:T(8,128)(2,1)}), bf16[8,8,160,512]{3,2,0,1:T(8,128)(2,1)}) %reduce-scatter.3.cloned.1.call-update) | async-done | bytes 10485776 | tf_op jit(solution)/shard_map/reduce_scatter | solution.py:189
  1575.4 220.4 %all-to-all-done.1 = bf16[8,8,160,512]{3,2,1,0:T(8,128)(2,1)} async-done(((bf16[8,8,160,512]{3,2,1,0:T(8,128)(2,1)}), bf16[8,8,160,512]{3,2,1,0:T(8,128)(2,1)}, u32[]{:S(2)}, u32[]{:S(2)}) %all-to-all-start.1) | async-done | bytes 10485792 | tf_op jit(solution)/shard_map/all_to_all | solution.py:193
  1795.7 39.2 %gather_fusion.1 = bf16[8192,512]{1,0:T(8,128)(2,1)} fusion(bf16[10240,512]{1,0:T(8,128)(2,1)} %bitcast.30, s32[8192]{0:T(1024)S(1)} %broadcast_clamp_fusion), kind=kCustom, calls=%fused_computation.1 | custom fusion | bytes 16809984 | tf_op jit(solution)/shard_map/gather | solution.py:196
  1842.6 13.9 psum.92
  1864.7 46.6 %gather_fusion.2 = bf16[10240,512]{1,0:T(8,128)(2,1)} fusion(bf16[8192,512]{1,0:T(8,128)(2,1)} %fusion.41, s32[10240]{0:T(1024)S(1)} %copy-done.53), kind=kCustom, calls=%fused_computation.2 | custom fusion | bytes 21012480 | tf_op jit(solution)/shard_map/gather | solution.py:205
  1917.3 233.0 %all_to_all.21 = bf16[8,8,160,512]{3,2,1,0:T(8,128)(2,1)} all-to-all(bf16[8,8,160,512]{3,2,1,0:T(8,128)(2,1)S(1)} %broadcast_select_fusion.1), channel_id=1, replica_groups=mesh['expert'=8,'tensor'=4] {'expert'}, dimensions={0} | all-to-all | bytes 20971520 | tf_op jit(solution)/shard_map/all_to_all | solution.py:208
  2159.9 250.1 %all-gather.3.cloned.1.call-done = bf16[8,8,160,2048]{3,2,0,1:T(8,128)(2,1)} async-done(((bf16[8,8,160,512]{3,2,0,1:T(8,128)(2,1)}), bf16[8,8,160,2048]{3,2,0,1:T(8,128)(2,1)}) %all-gather.3.cloned.1.call-update) | async-done | bytes 41943056 | tf_op jit(solution)/shard_map/all_gather | solution.py:209
  2410.0 28.9 fusion.45
  2438.9 33.5 fusion.55
  2472.4 45.5 %fusion.36 = bf16[8,8,160,2048]{3,2,0,1:T(8,128)(2,1)} fusion(f32[8,8,160,2048]{3,2,1,0:T(8,128)} %fusion.55, bf16[8,8,160,256]{3,2,0,1:T(8,128)(2,1)} %get-tuple-element.545, bf16[8,2048,256]{2,1,0:T(8,128)(2,1)} %param.33), kind=kOutput, calls=%fused_computation.60 | convolution fusion | flops 10779361280 | bytes 139460608 | tf_op jit(solution)/shard_map/slrf,ldf->slrd/dot_general | solution.py:233
  2517.9 288.9 %reduce-scatter.5.cloned.1.call-done = bf16[8,8,160,512]{3,2,0,1:T(8,128)(2,1)} async-done(((bf16[8,8,160,2048]{3,2,0,1:T(8,128)(2,1)}), bf16[8,8,160,512]{3,2,0,1:T(8,128)(2,1)}) %reduce-scatter.5.cloned.1.call-update) | async-done | bytes 10485776 | tf_op jit(solution)/shard_map/reduce_scatter | solution.py:236
  2830.8 216.3 %all-to-all-done.3 = bf16[8,8,160,512]{3,2,1,0:T(8,128)(2,1)} async-done(((bf16[8,8,160,512]{3,2,1,0:T(8,128)(2,1)}), bf16[8,8,160,512]{3,2,1,0:T(8,128)(2,1)}, u32[]{:S(2)}, u32[]{:S(2)}) %all-to-all-start.3) | async-done | bytes 10485792 | tf_op jit(solution)/shard_map/all_to_all | solution.py:240
  3047.0 12.2 bitcast_convert_fusion
  3059.3 41.7 %gather_fusion.3 = f32[8192,512]{1,0:T(8,128)} fusion(f32[10240,512]{1,0:T(8,128)} %bitcast_convert_fusion, s32[8192]{0:T(1024)S(1)} %copy-done.13), kind=kCustom, calls=%fused_computation.3 | custom fusion | bytes 33587200 | tf_op jit(solution)/shard_map/gather | solution.py:246
  3126.2 18.3 pmax.7
  3174.4 43.8 %while.58 = (s32[]{:T(128)}, f32[1024,4,128]{0,2,1:T(8,128)}, f32[1024,4,128]{0,2,1:T(8,128)}, f32[2,512,4,128]{3,1,2,0:T(8,128)}, s32[2]{0:T(128)S(1)}, /*index...) while((s32[]{:T(128)}, f32[1024,4,128]{0,2,1:T(8,128)}, ...), condition=%wide.region_29.30_spmd.clone.clone, body=%wide.region_26.29_spmd.clone.sunk.clone | while | flops 2721324544 | bytes 126947808 | solution.py:108
  3263.9 23.8 convolution_bitcast_fusion
  3287.7 24.6 convolution_bitcast_fusion.1
  3312.4 24.5 convolution_bitcast_fusion.2
  3336.9 9.8 fusion.51
  3346.7 22.0 all-reduce
  3375.6 240.7 %all-reduce.10.cloned.1.call-done = (bf16[2048,512]{1,0:T(8,128)(2,1)}, bf16[2048,512]{1,0:T(8,128)(2,1)}, bf16[2048,512]{1,0:T(8,128)(2,1)}, bf16[512,2048]{1,0:T(8,128)(2,1)}, bf16[2048,64]{0,1:T(8,128)(2,1)}) async-done(((bf16[2048,512]{1,0:T(8,128)(2,1)}, bf16[2048,512]{1,0:T(8,128)(2,1)}, bf16[2048,512]{1,0:T(8,128)(2,1)}, bf16[512,2048]{1,0:T(8,128)(2,1)}, bf16[2048,64]{0,1:T(8,128)(2,1)}), ...) | async-done | bytes 8650768 | tf_op jit(solution)/shard_map/psum | solution.py:316
  (350 shorter events, 316.8 us)
Async XLA Ops:
  7.2 61.9 %copy-start = (bf16[512,2048]{1,0:T(8,128)(2,1)S(1)}, bf16[512,2048]{1,0:T(8,128)(2,1)}, u32[]{:S(2)}) copy-start(bf16[512,2048]{1,0:T(8,128)(2,1)} %param.27) | copy-start | bytes 6291460
  7.2 153.2 %all-reduce.6.cloned.1.call-start = ((), (), s32[]{:S(2)}) async-start(), calls=%async_computation.6 | async-start | bytes 8388608 | tf_op jit(solution)/shard_map/psum | solution.py:162
  11.5 16.4 copy-start.61
  27.9 9.6 copy-start.49
  27.9 9.6 copy-start.75
  27.9 9.6 copy-start.67
  65.6 7.8 copy-start.5
  65.6 7.8 copy-start.73
  73.5 1482.0 %reduce-scatter.3.cloned.1.call-start = ((), (), s32[]{:S(2)}) async-start(), calls=%async_computation.7 | async-start | bytes 52428800 | tf_op jit(solution)/shard_map/reduce_scatter | solution.py:189
  124.7 129.2 %copy-start.54 = (pred[8,8,160]{2,1,0:T(8,128)(4,1)}, pred[8,8,160]{2,1,0:T(8,128)(4,1)S(1)}, u32[]{:S(2)}) copy-start(pred[8,8,160]{2,1,0:T(8,128)(4,1)S(1)} %broadcast_in_dim.176) | copy-start | bytes 30724
  125.3 43.4 %copy-start.59 = (f32[2048]{0:T(1024)S(1)}, f32[2048]{0:T(1024)}, u32[]{:S(2)}) copy-start(f32[2048]{0:T(1024)} %param.30) | copy-start | bytes 24580
  160.4 8.3 copy-start.8
  160.4 8.3 copy-start.18
  1564.8 230.9 %all-to-all-start.1 = ((bf16[8,8,160,512]{3,2,1,0:T(8,128)(2,1)}), bf16[8,8,160,512]{3,2,1,0:T(8,128)(2,1)}, u32[]{:S(2)}, u32[]{:S(2)}) async-start(bf16[8,8,160,512]{3,2,1,0:T(8,128)(2,1)} %copy.108), calls=%async_computation.2 | async-start | bytes 20971520 | tf_op jit(solution)/shard_map/all_to_all | solution.py:193
  1571.0 838.9 %all-gather.3.cloned.1.call-start = ((), (), s32[]{:S(2)}) async-start(), calls=%async_computation.8 | async-start | bytes 52428800 | tf_op jit(solution)/shard_map/all_gather | solution.py:209
  1571.7 263.2 %copy-start.12 = (s32[8192]{0:T(1024)}, s32[8192]{0:T(1024)S(1)}, u32[]{:S(2)}) copy-start(s32[8192]{0:T(1024)S(1)} %broadcast_clamp_fusion) | copy-start | bytes 98308
  1834.9 21.6 copy-start.44
  1864.7 46.6 %copy-start.55 = (pred[8,8,160]{2,1,0:T(8,128)(4,1)S(1)}, pred[8,8,160]{2,1,0:T(8,128)(4,1)}, u32[]{:S(2)}) copy-start(pred[8,8,160]{2,1,0:T(8,128)(4,1)} %copy-done.54) | copy-start | bytes 30724
  2159.6 647.1 %reduce-scatter.5.cloned.1.call-start = ((), (), s32[]{:S(2)}) async-start(), calls=%async_computation.9 | async-start | bytes 52428800 | tf_op jit(solution)/shard_map/reduce_scatter | solution.py:236
  2816.1 230.9 %all-to-all-start.3 = ((bf16[8,8,160,512]{3,2,1,0:T(8,128)(2,1)}), bf16[8,8,160,512]{3,2,1,0:T(8,128)(2,1)}, u32[]{:S(2)}, u32[]{:S(2)}) async-start(bf16[8,8,160,512]{3,2,1,0:T(8,128)(2,1)} %copy.111), calls=%async_computation.5 | async-start | bytes 20971520 | tf_op jit(solution)/shard_map/all_to_all | solution.py:240
  2822.3 346.4 %all-gather.5.cloned.1.call-start = ((), (), s32[]{:S(2)}) async-start(), calls=%async_computation.10 | async-start | bytes 5242880 | tf_op jit(solution)/shard_map/all_gather | solution.py:267
  2830.8 228.5 %copy-start.13 = (s32[8192]{0:T(1024)S(1)}, s32[8192]{0:T(1024)}, u32[]{:S(2)}) copy-start(s32[8192]{0:T(1024)} %copy-done.12) | copy-start | bytes 98308
  3109.8 10.6 copy-start.64
  3126.1 26.5 copy-start.76
  3126.1 210.8 %all-reduce.8.cloned.1.call-start = ((), (), s32[]{:S(2)}) async-start(), calls=%async_computation.11 | async-start | bytes 8388608 | tf_op jit(solution)/shard_map/psum | solution.py:308
  3144.5 13.4 copy-start.77
  3218.1 9.1 copy-start.48
  3218.1 9.1 copy-start.68
  3244.4 6.9 copy-start.39
  3244.5 371.9 %all-reduce.10.cloned.1.call-start = ((), (), s32[]{:S(2)}) async-start(), calls=%async_computation.12 | async-start | bytes 17301504 | tf_op jit(solution)/shard_map/psum | solution.py:316
  3336.9 9.8 copy-start.72
  3618.3 7.0 copy-start.34
  (65 other events, 253.1 us)
Sparse Core Ops, SparseCore 0:
  73.6 86.7 all-reduce.5
  1266.7 288.7 reduce-scatter.2
  2159.8 250.1 all-gather.2
  2518.0 288.7 reduce-scatter.4
  3126.2 36.3 all-gather.4
  3244.6 87.2 all-reduce.7
  3337.8 278.4 all-reduce.9
where the time goes:
time: 3650 us; the launch traced here: 3640 us
  waiting for transfers between devices  1540 us (42%)
  blocking collectives  1210 us (33%)
  matrix products  375 us (10%)
  local copies, waits for them, and re-layouts  303 us (8%)
  other arithmetic  176 us (5%)
    all_to_all x1, blocking collectives, per_device(): lax.all_to_all(send_rows, 'expert', split_axis=0, concat_axis=0, tiled=True)  914 us
    reduce_scatter x1, waiting for transfers between devices, per_device(): lax.psum_scatter(partial_out.astype(jnp.bfloat16), 'tensor', scatter_dime...  289 us
    reduce_scatter x1, waiting for transfers between devices, per_device(): lax.psum_scatter(grad_in_rows.astype(jnp.bfloat16), 'tensor', scatter_dim...  289 us
    all_gather x1, waiting for transfers between devices, per_device(): grad_rows = lax.all_gather(arrived, 'tensor', axis=3, tiled=True)  250 us
    psum x1, waiting for transfers between devices, per_device(): lax.psum(grad_query.astype(jnp.bfloat16), 'expert').astype(jnp.float32)  241 us
    all_to_all x1, blocking collectives, per_device(): lax.all_to_all(rows_back, 'expert', split_axis=0, concat_axis=0, tiled=True)  233 us
    all_to_all x1, waiting for transfers between devices, per_device(): lax.all_to_all(received[0], 'expert', split_axis=0, concat_axis=0, tiled=...  220 us
    all_to_all x1, waiting for transfers between devices, per_device(): lax.all_to_all(grad_in_sum.astype(jnp.bfloat16), 'expert', split_axis=0,...  216 us
  transfers between devices with their start and end apart: 9, of which 7 were waited for; matrix products, arithmetic and copies ran while one was open for 5% of the time, Pallas kernels for 0%

commit v1 on v0

v1 whole, which is shorter than its diff:
```python
from functools import partial
import math

import jax
import jax.numpy as jnp
from jax import lax
from jax.experimental import pallas as pl
from jax.experimental.pallas import tpu as pltpu
from jax.sharding import PartitionSpec as P

HD = 128
E = 64
TOP = 8
LENGTH = 1024
CAP = 160
NB = 2
BOTH = ("expert", "tensor")
F32 = jnp.float32
BF16 = jnp.bfloat16
VMEM = 60 * 1024 * 1024


def matmul(left, right):
    return jnp.dot(left, right, preferred_element_type=F32)


def matmul_nt(left, right):
    return lax.dot_general(left, right, (((1,), (1,)), ((), ())), preferred_element_type=F32)


def matmul_tn(left, right):
    return lax.dot_general(left, right, (((0,), (0,)), ((), ())), preferred_element_type=F32)


def flip(dz, dx, dy, dc):
    pairs = []
    for z in range(4):
        for x in range(2):
            for y in range(2):
                for c in range(2):
                    pairs.append(
                        (
                            ((z * 2 + x) * 2 + y) * 2 + c,
                            (((z ^ dz) * 2 + (x ^ dx)) * 2 + (y ^ dy)) * 2 + (c ^ dc),
                        )
                    )
    return pairs


def send(value, dz=0, dx=0, dy=0, dc=0):
    return lax.ppermute(value, BOTH, flip(dz, dx, dy, dc))


def is_cube():
    return lax.axis_size("expert") == 8 and lax.axis_size("tensor") == 4


def core_swap(value):
    if is_cube():
        return send(value, dc=1)
    count = lax.axis_size("tensor")
    return lax.ppermute(value, "tensor", [(i, i ^ 1) for i in range(count)])


def slot_blocks():
    owner, part = lax.axis_index("expert"), lax.axis_index("tensor")
    core = part % 2
    if is_cube():
        blocks = [[owner ^ (k * 2 + b) for b in range(NB)] for k in range(4)]
        mine = [part ^ (y * 2) for y in range(2)]
    else:
        blocks = [[k * NB + b for b in range(NB)] for k in range(lax.axis_size("expert") // NB)]
        mine = [y * 2 + core for y in range(lax.axis_size("tensor") // 2)]
    theirs = [m ^ 1 for m in mine]
    return [jnp.stack([jnp.asarray(v, jnp.int32) for v in b + mine + theirs]) for b in blocks]


def same_core():
    count = lax.axis_size("tensor")
    return [[y * 2 + c for y in range(count // 2)] for c in range(2)]


def gather_slots(own):
    if not is_cube():
        blocks = lax.all_gather(own, "expert")
        full = lax.all_gather(blocks, "tensor", axis_index_groups=same_core())
        return [
            [[full[y, k * NB + b] for y in range(full.shape[0])] for b in range(NB)]
            for k in range(full.shape[1] // NB)
        ]
    half = own.shape[0] // 2
    starts = [own] + [send(own, dz=k) for k in (1, 2, 3)]
    slots = []
    for block in starts:
        over_x = send(block, dx=1)
        over_y = send(block, dy=1)
        low = send(over_x[:half], dy=1)
        high = send(over_y[half:], dx=1)
        slots.append([[block, over_y], [over_x, jnp.concatenate([low, high], axis=0)]])
    return slots


def scatter_slot(parts):
    half = parts[0][0].shape[0] // 2
    low = send(parts[1][1][:half], dy=1)
    high = send(parts[1][1][half:], dx=1)

    def joined(first, second):
        return (first.astype(F32) + second.astype(F32)).astype(BF16)

    to_x = jnp.concatenate([joined(parts[1][0][:half], low), parts[1][0][half:]], axis=0)
    to_y = jnp.concatenate([parts[0][1][:half], joined(parts[0][1][half:], high)], axis=0)
    from_x = send(to_x, dx=1)
    from_y = send(to_y, dy=1)
    return parts[0][0].astype(F32) + from_x.astype(F32) + from_y.astype(F32)


def scatter_slots(slots):
    if not is_cube():
        full = jnp.stack(
            [jnp.stack([s[b][y] for s in slots for b in range(NB)]) for y in range(len(slots[0][0]))]
        )
        mine = lax.psum_scatter(full, "tensor", axis_index_groups=same_core(), scatter_dimension=0)
        return lax.psum_scatter(mine, "expert", scatter_dimension=0).astype(F32)
    total = None
    for k, parts in enumerate(slots):
        term = scatter_slot(parts)
        if k:
            term = send(term.astype(BF16), dz=k).astype(F32)
        total = term if total is None else total + term
    return total


def tensor_gather(own, over_y=None):
    if not is_cube():
        full = lax.all_gather(own, "tensor")
        return [full[i] for i in range(full.shape[0])]
    if over_y is None:
        over_y = send(own, dy=1)
    return [own, send(own, dc=1), over_y, send(over_y, dc=1)]


def tensor_order():
    part = lax.axis_index("tensor")
    count = lax.axis_size("tensor")
    if is_cube():
        return [part ^ i for i in range(count)]
    return [jnp.int32(i) for i in range(count)]


def one_hot(pos_row):
    rows = lax.broadcasted_iota(jnp.int32, (CAP, pos_row.shape[1]), 0)
    return rows == pos_row


def as_bf16(mask):
    return jnp.where(mask, 1.0, 0.0).astype(BF16)


def pick_kernel(group, slices, where_ref, *refs):
    pos_refs, x_refs = refs[:NB], refs[NB : NB + NB * slices]
    out_ref, hot_ref = refs[-2:]
    step = pl.program_id(0)
    for b in range(NB):
        for i in range(group):
            hot_ref[b, i * CAP : (i + 1) * CAP, :] = as_bf16(
                one_hot(pos_refs[b][0, pl.ds(step * group + i, 1), :])
            )
        for y in range(slices):
            out_ref[b, y] = matmul(hot_ref[b], x_refs[b * slices + y][...]).astype(BF16)


def pick_rows(where, pos, blocks):
    slices = len(blocks[0])
    tokens, width = blocks[0][0].shape
    held = pos.shape[1]
    group = 2
    flat = [a for b in blocks for a in b]

    def block_spec(b):
        return pl.BlockSpec((1, held, tokens), lambda i, where: (where[b], 0, 0))

    return pl.pallas_call(
        partial(pick_kernel, group, slices),
        grid_spec=pltpu.PrefetchScalarGridSpec(
            num_scalar_prefetch=1,
            grid=(held // group,),
            in_specs=[block_spec(b) for b in range(NB)]
            + [pl.BlockSpec((tokens, width), lambda i, where: (0, 0)) for _ in flat],
            out_specs=pl.BlockSpec(
                (NB, slices, group * CAP, width), lambda i, where: (0, 0, i, 0)
            ),
            scratch_shapes=[pltpu.VMEM((NB, group * CAP, tokens), BF16)],
        ),
        out_shape=jax.ShapeDtypeStruct((NB, slices, held * CAP, width), BF16),
        compiler_params=pltpu.CompilerParams(vmem_limit_bytes=VMEM),
        cost_estimate=pl.CostEstimate(
            flops=2 * NB * slices * held * CAP * tokens * width,
            bytes_accessed=2 * NB * slices * (held * CAP + tokens) * width,
            transcendentals=0,
        ),
        name="pick_rows",
    )(where, *([pos] * NB), *flat)


def expert_kernel(slices, where_ref, *refs):
    pos_refs, gate_refs = refs[:NB], refs[NB : 2 * NB]
    rows_mine, rows_theirs, cot_mine, cot_theirs, wg_ref, wu_ref, wd_ref = refs[2 * NB : 2 * NB + 7]
    scaled_ref, gate_grad_ref, up_grad_ref, prob_ref, keep_ref, give_ref = refs[2 * NB + 7 :]
    e = pl.program_id(0)
    width = rows_mine.shape[3]
    ff = wg_ref.shape[2]
    gate_pre = jnp.zeros((NB * CAP, ff), F32)
    up_pre = jnp.zeros((NB * CAP, ff), F32)
    grad_hidden = jnp.zeros((NB * CAP, ff), F32)

    def columns(j):
        return pl.ds(pl.multiple_of(where_ref[NB + j] * width, width), width)

    for j in range(2 * slices):
        x_ref, c_ref = (rows_mine, cot_mine) if j < slices else (rows_theirs, cot_theirs)
        x = x_ref[:, j % slices].reshape(NB * CAP, width)
        c = c_ref[:, j % slices].reshape(NB * CAP, width)
        gate_pre = gate_pre + matmul(x, wg_ref[0, columns(j), :])
        up_pre = up_pre + matmul(x, wu_ref[0, columns(j), :])
        grad_hidden = grad_hidden + matmul_nt(c, wd_ref[0, :, columns(j)])
    masks = [one_hot(pos_refs[b][0, pl.ds(e, 1), :]) for b in range(NB)]
    gates = jnp.concatenate(
        [
            jnp.sum(jnp.where(masks[b], gate_refs[b][0, pl.ds(e, 1), :], 0.0), axis=1, keepdims=True)
            for b in range(NB)
        ],
        axis=0,
    )
    sigma = jax.nn.sigmoid(gate_pre)
    swish = gate_pre * sigma
    hidden = (swish * up_pre).astype(BF16).astype(F32)
    prob = jnp.sum(hidden * grad_hidden, axis=1, keepdims=True)
    for b in range(NB):
        prob_ref[0, b : b + 1, :] = jnp.sum(
            jnp.where(masks[b], prob[b * CAP : (b + 1) * CAP], 0.0), axis=0, keepdims=True
        )
    grad_hidden = grad_hidden * gates
    scaled_ref[0] = (hidden * gates).astype(BF16)
    gate_grad = (grad_hidden * up_pre * (sigma * (1.0 + gate_pre * (1.0 - sigma)))).astype(BF16)
    up_grad = (grad_hidden * swish).astype(BF16)
    gate_grad_ref[0] = gate_grad
    up_grad_ref[0] = up_grad
    for j in range(2 * slices):
        to = keep_ref if j < slices else give_ref
        back = matmul_nt(gate_grad, wg_ref[0, columns(j), :]) + matmul_nt(
            up_grad, wu_ref[0, columns(j), :]
        )
        to[:, j % slices] = back.astype(BF16).reshape(NB, CAP, width)


def expert_slot(where, pos, gate, rows, cots, w_gate, w_up, w_down):
    held, depth, ff = w_gate.shape
    tokens = pos.shape[2]
    slices, width = rows[0].shape[1], rows[0].shape[3]

    def block_spec(b):
        return pl.BlockSpec((1, held, tokens), lambda e, where: (where[b], 0, 0))

    rows_spec = pl.BlockSpec((NB, slices, CAP, width), lambda e, where: (0, 0, e, 0))
    rows_shape = jax.ShapeDtypeStruct((NB, slices, held * CAP, width), BF16)
    in_spec = pl.BlockSpec((1, depth, ff), lambda e, where: (e, 0, 0))
    hidden_spec = pl.BlockSpec((1, NB * CAP, ff), lambda e, where: (e, 0, 0))
    hidden_shape = jax.ShapeDtypeStruct((held, NB * CAP, ff), BF16)
    return pl.pallas_call(
        partial(expert_kernel, slices),
        grid_spec=pltpu.PrefetchScalarGridSpec(
            num_scalar_prefetch=1,
            grid=(held,),
            in_specs=[block_spec(b) for b in range(NB)] * 2
            + [rows_spec] * 4
            + [in_spec, in_spec, pl.BlockSpec((1, ff, depth), lambda e, where: (e, 0, 0))],
            out_specs=[hidden_spec] * 3
            + [pl.BlockSpec((1, NB, tokens), lambda e, where: (e, 0, 0)), rows_spec, rows_spec],
        ),
        out_shape=[hidden_shape] * 3
        + [jax.ShapeDtypeStruct((held, NB, tokens), F32), rows_shape, rows_shape],
        compiler_params=pltpu.CompilerParams(vmem_limit_bytes=VMEM),
        cost_estimate=pl.CostEstimate(
            flops=10 * NB * held * CAP * depth * ff,
            bytes_accessed=6 * held * depth * ff + 6 * NB * held * CAP * depth,
            transcendentals=NB * held * CAP * ff,
        ),
        name="expert_slot",
    )(where, *([pos] * NB), *([gate] * NB), *rows, *cots, w_gate, w_up, w_down)


def down_kernel(slices, where_ref, scaled_ref, wd_ref, keep_ref, give_ref):
    width = keep_ref.shape[3]
    for j in range(2 * slices):
        to = keep_ref if j < slices else give_ref
        columns = pl.ds(pl.multiple_of(where_ref[NB + j] * width, width), width)
        rows = matmul(scaled_ref[0], wd_ref[0, :, columns])
        to[:, j % slices] = rows.astype(BF16).reshape(NB, CAP, width)


def down_slot(where, scaled, w_down, slices):
    held, ff, depth = w_down.shape
    width = depth // (2 * slices)
    rows_spec = pl.BlockSpec((NB, slices, CAP, width), lambda e, where: (0, 0, e, 0))
    rows_shape = jax.ShapeDtypeStruct((NB, slices, held * CAP, width), BF16)
    return pl.pallas_call(
        partial(down_kernel, slices),
        grid_spec=pltpu.PrefetchScalarGridSpec(
            num_scalar_prefetch=1,
            grid=(held,),
            in_specs=[
                pl.BlockSpec((1, NB * CAP, ff), lambda e, where: (e, 0, 0)),
                pl.BlockSpec((1, ff, depth), lambda e, where: (e, 0, 0)),
            ],
            out_specs=[rows_spec, rows_spec],
        ),
        out_shape=[rows_shape, rows_shape],
        compiler_params=pltpu.CompilerParams(vmem_limit_bytes=VMEM),
        cost_estimate=pl.CostEstimate(
            flops=2 * NB * held * CAP * depth * ff,
            bytes_accessed=2 * held * depth * ff + 2 * NB * held * CAP * depth,
            transcendentals=0,
        ),
        name="down_slot",
    )(where, scaled, w_down)


def place_kernel(slices, held, where_ref, *refs):
    at_refs, mine_ref, theirs_ref = refs[:NB], refs[NB], refs[NB + 1]
    out_refs, hot_ref = refs[NB + 2 : -1], refs[-1]
    b, y = pl.program_id(0), pl.program_id(1)
    tokens = hot_ref.shape[0]
    for block in range(NB):

        @pl.when((b == block) & (y == 0))
        def _():
            at = at_refs[block][0]
            for tile in range(held * CAP // 128):
                lanes = lax.broadcasted_iota(jnp.int32, (tokens, 128), 1) + tile * 128
                mask = None
                for e in range(tile * 128 // CAP, (tile * 128 + 127) // CAP + 1):
                    hit = at[:, e : e + 1] == lanes
                    mask = hit if mask is None else mask | hit
                hot_ref[:, tile * 128 : (tile + 1) * 128] = as_bf16(mask)

    rows = (mine_ref[0, 0].astype(F32) + theirs_ref[0, 0].astype(F32)).astype(BF16)
    placed = matmul(hot_ref[...], rows).astype(BF16)
    for block in range(NB):
        for part in range(slices):

            @pl.when((b == block) & (y == part))
            def _():
                out_refs[block * slices + part][...] = placed


def place_rows(where, at, mine, theirs):
    _, slices, count, width = mine.shape
    _, tokens, held = at.shape

    def block_spec(b):
        return pl.BlockSpec((1, tokens, held), lambda i, y, where: (where[b], 0, 0))

    rows_spec = pl.BlockSpec((1, 1, count, width), lambda i, y, where: (i, y, 0, 0))
    out = pl.pallas_call(
        partial(place_kernel, slices, held),
        grid_spec=pltpu.PrefetchScalarGridSpec(
            num_scalar_prefetch=1,
            grid=(NB, slices),
            in_specs=[block_spec(b) for b in range(NB)] + [rows_spec, rows_spec],
            out_specs=[pl.BlockSpec((tokens, width), lambda i, y, where: (0, 0))] * (NB * slices),
            scratch_shapes=[pltpu.VMEM((tokens, count), BF16)],
        ),
        out_shape=[jax.ShapeDtypeStruct((tokens, width), BF16)] * (NB * slices),
        compiler_params=pltpu.CompilerParams(vmem_limit_bytes=VMEM),
        cost_estimate=pl.CostEstimate(
            flops=2 * NB * slices * count * tokens * width,
            bytes_accessed=2 * NB * slices * (2 * count + tokens) * width,
            transcendentals=0,
        ),
        name="place_rows",
    )(where, *([at] * NB), mine, theirs)
    return [out[b * slices : (b + 1) * slices] for b in range(NB)]


def weight_kernel(slots, slices, where_ref, *refs):
    rows, cots, scaled, gate_grads, up_grads = (
        refs[: 2 * slots],
        refs[2 * slots : 4 * slots],
        refs[4 * slots : 5 * slots],
        refs[5 * slots : 6 * slots],
        refs[6 * slots : 7 * slots],
    )
    gate_ref, up_ref, down_ref = refs[7 * slots :]
    width = rows[0].shape[3]
    for j in range(2 * slices):
        columns = pl.ds(pl.multiple_of(where_ref[NB + j] * width, width), width)
        side = j // slices
        gate = up = down = None
        for k in range(slots):
            x = rows[2 * k + side][:, j % slices].reshape(NB * CAP, width)
            c = cots[2 * k + side][:, j % slices].reshape(NB * CAP, width)
            terms = (
                matmul_tn(x, gate_grads[k][0]),
                matmul_tn(x, up_grads[k][0]),
                matmul_tn(scaled[k][0], c),
            )
            if gate is None:
                gate, up, down = terms
            else:
                gate, up, down = gate + terms[0], up + terms[1], down + terms[2]
        gate_ref[0, columns, :] = gate
        up_ref[0, columns, :] = up
        down_ref[0, :, columns] = down


def weight_grads(where, rows, cots, scaled, gate_grads, up_grads, depth):
    slots = len(rows)
    held, _, ff = scaled[0].shape
    slices, width = rows[0][0].shape[1], rows[0][0].shape[3]
    rows_spec = pl.BlockSpec((NB, slices, CAP, width), lambda e, where: (0, 0, e, 0))
    hidden_spec = pl.BlockSpec((1, NB * CAP, ff), lambda e, where: (e, 0, 0))
    in_spec = pl.BlockSpec((1, depth, ff), lambda e, where: (e, 0, 0))
    return pl.pallas_call(
        partial(weight_kernel, slots, slices),
        grid_spec=pltpu.PrefetchScalarGridSpec(
            num_scalar_prefetch=1,
            grid=(held,),
            in_specs=[rows_spec] * (4 * slots) + [hidden_spec] * (3 * slots),
            out_specs=[in_spec, in_spec, pl.BlockSpec((1, ff, depth), lambda e, where: (e, 0, 0))],
        ),
        out_shape=[jax.ShapeDtypeStruct((held, depth, ff), F32)] * 2
        + [jax.ShapeDtypeStruct((held, ff, depth), F32)],
        compiler_params=pltpu.CompilerParams(vmem_limit_bytes=VMEM),
        cost_estimate=pl.CostEstimate(
            flops=6 * slots * NB * held * CAP * depth * ff,
            bytes_accessed=12 * held * depth * ff + 4 * slots * NB * held * CAP * depth,
            transcendentals=0,
        ),
        name="weight_grads",
    )(
        where,
        *[a for pair in rows for a in pair],
        *[a for pair in cots for a in pair],
        *scaled,
        *gate_grads,
        *up_grads,
    )


def inside_pieces(start, length, positions):
    return (positions[None, :] >= start[:, None]) & (positions[None, :] < (start + length)[:, None])


def allowed_block(start, length, first, rows):
    query_pos = first + jnp.arange(rows, dtype=jnp.int32)
    key_pos = jnp.arange(LENGTH, dtype=jnp.int32)
    query_in = inside_pieces(start, length, query_pos)
    key_in = inside_pieces(start, length, key_pos)
    return (key_pos[None, :] <= query_pos[:, None]) | jnp.any(
        query_in[:, :, None] & key_in[:, None, :], axis=0
    )


def head_stats(raw, heads):
    parts = raw.reshape(raw.shape[0], heads, HD)
    inverse = lax.rsqrt(jnp.mean(parts * parts, axis=-1, keepdims=True) + 1e-06)
    return (parts * inverse, inverse)


def head_backward(grad_heads, hat, inverse, gain):
    upstream = grad_heads * gain.reshape(hat.shape[1], HD)
    raw = inverse * (upstream - hat * jnp.mean(upstream * hat, axis=-1, keepdims=True))
    return (
        raw.reshape(hat.shape[0], -1).astype(jnp.bfloat16),
        jnp.sum(grad_heads * hat, axis=0).reshape(-1),
    )


def attend_forward(args, block, scale):
    queries, keys, values, start, length = args

    def one_block(index):
        first = index * block
        rows = lax.dynamic_slice_in_dim(queries, first, block, 0)
        scores = jnp.einsum("qhd,khd->hqk", rows, keys, preferred_element_type=jnp.float32) * scale
        masked = jnp.where(allowed_block(start, length, first, block)[None], scores, -1e30)
        top = jnp.max(masked, axis=-1, keepdims=True)
        weights = jnp.exp(masked - top)
        total = jnp.sum(weights, axis=-1, keepdims=True)
        probs = (weights / total).astype(jnp.bfloat16)
        result = jnp.einsum("hqk,khd->qhd", probs, values, preferred_element_type=jnp.float32)
        return (result, (top + jnp.log(total))[..., 0], jnp.max(masked, axis=(1, 2)))

    results, log_sums, tops = lax.map(one_block, jnp.arange(LENGTH // block, dtype=jnp.int32))
    return (results.reshape(LENGTH, queries.shape[1], HD), log_sums, jnp.max(tops, axis=0))


def attend_backward(args, block, scale):
    queries, keys, values, grads_o, log_sums, start, length = args

    def one_block(carry, index):
        key_acc, value_acc = carry
        first = index * block
        rows = lax.dynamic_slice_in_dim(queries, first, block, 0)
        grad_rows = lax.dynamic_slice_in_dim(grads_o, first, block, 0)
        scores = jnp.einsum("qhd,khd->hqk", rows, keys, preferred_element_type=jnp.float32) * scale
        masked = jnp.where(allowed_block(start, length, first, block)[None], scores, -1e30)
        probs = jnp.exp(masked - log_sums[index][:, :, None])
        grad_p = jnp.einsum("qhd,khd->hqk", grad_rows, values, preferred_element_type=jnp.float32)
        delta = jnp.sum(probs * grad_p, axis=-1, keepdims=True)
        grad_s = (probs * (grad_p - delta)).astype(jnp.bfloat16)
        query_part = (
            jnp.einsum("hqk,khd->qhd", grad_s, keys, preferred_element_type=jnp.float32) * scale
        )
        key_acc = (
            key_acc
            + jnp.einsum("hqk,qhd->khd", grad_s, rows, preferred_element_type=jnp.float32) * scale
        )
        value_acc = value_acc + jnp.einsum(
            "hqk,qhd->khd",
            probs.astype(jnp.bfloat16),
            grad_rows,
            preferred_element_type=jnp.float32,
        )
        return ((key_acc, value_acc), query_part)

    zeros = jnp.zeros(keys.shape, jnp.float32)
    (key_grad, value_grad), query_parts = lax.scan(
        one_block, (zeros, zeros), jnp.arange(LENGTH // block, dtype=jnp.int32)
    )
    return (query_parts.reshape(keys.shape), key_grad, value_grad)


def per_device(
    inputs,
    attn_gain,
    w_query,
    w_key,
    w_value,
    w_output,
    query_gain,
    key_gain,
    moe_gain,
    w_router,
    w_gate,
    w_up,
    w_down,
    routes,
    piece_start,
    piece_length,
    clip_threshold,
    cotangent,
):
    tokens_here, width = inputs.shape
    slice_width = cotangent.shape[1]
    part = lax.axis_index("tensor")
    owner = lax.axis_index("expert")
    column = part * slice_width
    heads_here = query_gain.shape[0] // HD
    experts_here = w_gate.shape[0]
    owners = lax.axis_size("expert")
    sequences = tokens_here // LENGTH
    block = min(512, LENGTH)
    scale = 1.0 / math.sqrt(HD)

    cot_own = cotangent.astype(BF16)
    cot_slots = gather_slots(cot_own)
    cot_pieces = tensor_gather(cot_own, cot_slots[0][0][1])
    output_pieces = jnp.concatenate(tensor_gather(w_output), axis=0)

    all_routes = lax.all_gather(routes, "expert")
    held_ids = owner * experts_here + jnp.arange(experts_here, dtype=jnp.int32)
    chosen = jnp.any(all_routes[:, None, :, :] == held_ids[None, :, None, None], axis=3)
    places = jnp.arange(tokens_here, dtype=jnp.int32)
    before = (places[:, None] < places[None, :]).astype(BF16)
    earlier = jnp.einsum(
        "set,tu->seu", chosen.astype(BF16), before, preferred_element_type=F32
    ).astype(jnp.int32)
    pos = jnp.where(chosen, earlier, -1)
    at = jnp.where(
        chosen, earlier + jnp.arange(experts_here, dtype=jnp.int32)[None, :, None] * CAP, -1
    ).transpose(0, 2, 1)
    where = slot_blocks()

    inputs_f = inputs.astype(F32)
    attn_inv = lax.rsqrt(jnp.mean(inputs_f * inputs_f, axis=-1, keepdims=True) + 1e-05)
    attn_hat = inputs_f * attn_inv
    normed_a = (attn_hat * attn_gain).astype(BF16)
    query_hat, query_inv = head_stats(matmul(normed_a, w_query), heads_here)
    key_hat, key_inv = head_stats(matmul(normed_a, w_key), heads_here)
    values = matmul(normed_a, w_value).astype(BF16)
    queries = (query_hat * query_gain.reshape(heads_here, HD)).astype(BF16)
    keys = (key_hat * key_gain.reshape(heads_here, HD)).astype(BF16)
    shape4 = (sequences, LENGTH, heads_here, HD)
    seq_query = queries.reshape(shape4)
    seq_key = keys.reshape(shape4)
    seq_value = values.reshape(shape4)
    results, log_sums, tops = lax.map(
        partial(attend_forward, block=block, scale=scale),
        (seq_query, seq_key, seq_value, piece_start, piece_length),
    )
    attended = results.reshape(tokens_here, heads_here * HD).astype(BF16)
    head_top = lax.pmax(jnp.max(tops, axis=0), "expert")
    attended_pieces = jnp.concatenate(tensor_gather(attended), axis=1)
    residual = inputs_f + matmul(attended_pieces, output_pieces)
    moe_inv = lax.rsqrt(jnp.mean(residual * residual, axis=-1, keepdims=True) + 1e-05)
    moe_hat = residual * moe_inv
    normed_m = (moe_hat * moe_gain).astype(BF16)

    normed_slots = gather_slots(lax.dynamic_slice_in_dim(normed_m, column, slice_width, 1))
    router = jax.nn.softmax(
        lax.dot_general(w_router, normed_m, (((0,), (1,)), ((), ())), preferred_element_type=F32),
        axis=0,
    )
    gate = lax.all_to_all(
        router.reshape(owners, experts_here, tokens_here),
        "expert",
        split_axis=0,
        concat_axis=0,
        tiled=True,
    )

    slots = len(where)
    slices = len(cot_slots[0][0])
    cots, rows, scaled, gate_grads, up_grads, probs, back = [], [], [], [], [], [], []
    for k in range(slots):
        mine = pick_rows(where[k], pos, cot_slots[k])
        cots.append((mine, core_swap(mine)))
    for k in range(slots):
        mine = pick_rows(where[k], pos, normed_slots[k])
        rows.append((mine, core_swap(mine)))
        kept, gate_grad, up_grad, prob, keep, give = expert_slot(
            where[k], pos, gate, rows[k], cots[k], w_gate, w_up, w_down
        )
        scaled.append(kept)
        gate_grads.append(gate_grad)
        up_grads.append(up_grad)
        probs.append(prob)
        back.append(place_rows(where[k], at, keep, core_swap(give)))
    expert_path = scatter_slots(back)

    prob_grads = jnp.stack([probs[k][:, b] for k in range(slots) for b in range(NB)])
    if is_cube():
        prob_grads = prob_grads[jnp.arange(owners, dtype=jnp.int32) ^ owner]
    prob_grads = lax.all_to_all(prob_grads, "expert", split_axis=0, concat_axis=0, tiled=True)
    prob_grads = lax.psum(prob_grads, "tensor").reshape(E, tokens_here)
    grad_logits = (
        router * (prob_grads - jnp.sum(router * prob_grads, axis=0, keepdims=True))
    ).astype(BF16)
    grad_router = lax.dot_general(
        normed_m, grad_logits, (((0,), (1,)), ((), ())), preferred_element_type=F32
    )
    router_slice = lax.dynamic_slice_in_dim(w_router, column, slice_width, 0)
    grad_normed = expert_path + lax.dot_general(
        grad_logits, router_slice, (((0,), (1,)), ((), ())), preferred_element_type=F32
    )
    moe_hat_slice = lax.dynamic_slice_in_dim(moe_hat, column, slice_width, 1)
    gain_slice = lax.dynamic_slice_in_dim(moe_gain, column, slice_width, 0)
    grad_moe_gain = jnp.sum(grad_normed * moe_hat_slice, axis=0)

    order = tensor_order()
    normed_pieces = tensor_gather(grad_normed.astype(BF16))
    hats = [lax.dynamic_slice_in_dim(moe_hat, o * slice_width, slice_width, 1) for o in order]
    gains = [lax.dynamic_slice_in_dim(moe_gain, o * slice_width, slice_width, 0) for o in order]
    ups = [p.astype(F32) * g for p, g in zip(normed_pieces, gains)]
    mean_dot = (
        sum(jnp.sum(u * h, axis=-1, keepdims=True) for u, h in zip(ups, hats)) / width
    )
    grad_residual = cotangent + moe_inv * (grad_normed * gain_slice - moe_hat_slice * mean_dot)
    grad_branch = jnp.zeros((tokens_here, width), BF16)
    for o, c, u, h in zip(order, cot_pieces, ups, hats):
        piece = (c.astype(F32) + moe_inv * (u - h * mean_dot)).astype(BF16)
        grad_branch = lax.dynamic_update_slice_in_dim(grad_branch, piece, o * slice_width, 1)

    placed = []
    for k in range(slots):
        keep, give = down_slot(where[k], scaled[k], w_down, slices)
        placed.append(place_rows(where[k], at, keep, core_swap(give)))
    mixture = scatter_slots(placed)
    out = lax.dynamic_slice_in_dim(residual, column, slice_width, 1) + mixture
    grad_gate, grad_up, grad_down = weight_grads(
        where[0], rows, cots, scaled, gate_grads, up_grads, width
    )

    grad_output = matmul_tn(attended, grad_branch)
    grad_attended = matmul_nt(grad_branch, w_output).astype(BF16)
    grad_q, grad_k, grad_v = lax.map(
        partial(attend_backward, block=block, scale=scale),
        (
            seq_query,
            seq_key,
            seq_value,
            grad_attended.reshape(shape4),
            log_sums,
            piece_start,
            piece_length,
        ),
    )
    heads_shape = (tokens_here, heads_here, HD)
    grad_query_raw, grad_query_gain = head_backward(
        grad_q.reshape(heads_shape), query_hat, query_inv, query_gain
    )
    grad_key_raw, grad_key_gain = head_backward(
        grad_k.reshape(heads_shape), key_hat, key_inv, key_gain
    )
    grad_value_raw = grad_v.reshape(tokens_here, heads_here * HD).astype(BF16)
    grad_query = matmul_tn(normed_a, grad_query_raw)
    grad_key = matmul_tn(normed_a, grad_key_raw)
    grad_value = matmul_tn(normed_a, grad_value_raw)
    grad_normed_a = matmul_nt(grad_query_raw, w_query)
    grad_normed_a = grad_normed_a + matmul_nt(grad_key_raw, w_key)
    grad_normed_a = grad_normed_a + matmul_nt(grad_value_raw, w_value)
    grad_normed_a = lax.psum(grad_normed_a.astype(BF16), "tensor").astype(F32)
    upstream = grad_normed_a * attn_gain
    grad_attn_gain = jnp.sum(grad_normed_a * attn_hat, axis=0)
    grad_input_full = attn_inv * (
        upstream - attn_hat * jnp.mean(upstream * attn_hat, axis=-1, keepdims=True)
    )
    grad_input = grad_residual + lax.dynamic_slice_in_dim(grad_input_full, column, slice_width, 1)
    totals = [
        lax.psum(g.astype(BF16), "expert").astype(F32)
        for g in (
            grad_query,
            grad_key,
            grad_value,
            grad_output,
            grad_query_gain,
            grad_key_gain,
            grad_attn_gain,
            grad_moe_gain,
            grad_router,
        )
    ]
    factor = clip_threshold / jnp.maximum(head_top, clip_threshold)
    spread = jnp.repeat(jnp.sqrt(factor), HD)
    query_clipped = (w_query.astype(F32) * spread[None, :]).astype(BF16)
    key_clipped = (w_key.astype(F32) * spread[None, :]).astype(BF16)
    return (
        out,
        grad_input,
        totals[6],
        totals[0],
        totals[1],
        totals[2],
        totals[3],
        totals[4],
        totals[5],
        totals[7],
        totals[8],
        grad_gate,
        grad_up,
        grad_down,
        head_top,
        query_clipped,
        key_clipped,
    )


def solution(mesh):
    return jax.shard_map(
        per_device,
        mesh=mesh,
        in_specs=(
            P("expert", None),
            P(),
            P(None, "tensor"),
            P(None, "tensor"),
            P(None, "tensor"),
            P("tensor", None),
            P("tensor"),
            P("tensor"),
            P(),
            P(),
            P("expert", None, "tensor"),
            P("expert", None, "tensor"),
            P("expert", "tensor", None),
            P("expert", None),
            P("expert", None),
            P("expert", None),
            P("tensor"),
            P("expert", "tensor"),
        ),
        out_specs=(
            P("expert", "tensor"),
            P("expert", "tensor"),
            P(),
            P(None, "tensor"),
            P(None, "tensor"),
            P(None, "tensor"),
            P("tensor", None),
            P("tensor"),
            P("tensor"),
            P("tensor"),
            P(),
            P("expert", None, "tensor"),
            P("expert", None, "tensor"),
            P("expert", "tensor", None),
            P("tensor"),
            P(None, "tensor"),
            P(None, "tensor"),
        ),
        check_vma=False,
    )
```

time: 3650 us -> 1750 us (0.48)
  blocking collectives: 1210 us -> 85.6 us
  waiting for transfers between devices: 1540 us -> 695 us
  Pallas kernels: 0 us -> 418 us
  matrix products: 375 us -> 140 us
  local copies, waits for them, and re-layouts: 303 us -> 124 us
  starting transfers between devices: 13.6 us -> 101 us
    all_to_all x2 -> x0, blocking collectives: 1150 us -> none  [the longest x1 914 us: per_device(): lax.all_to_all(send_rows, 'expert', split_axis=0, concat_axis=0, tiled=True)]
    reduce_scatter x2 -> x0, waiting for transfers between devices: 578 us -> none  [the longest x1 289 us: per_device(): lax.psum_scatter(partial_out.astype(jnp.bfloat16), 'tensor', scatter_dime...]
    ppermute x0 -> x103, waiting for transfers between devices: none -> 545 us  [send(): return lax.ppermute(value, BOTH, flip(dz, dx, dy, dc))]
    all_to_all x2, waiting for transfers between devices: 437 us -> 0.01 us  [the longest x1 0.01 us: per_device(): lax.all_to_all(prob_grads, 'expert', split_axis=0, concat_axis=0, tiled=T...]
    pallas_call x0 -> x25, Pallas kernels: none -> 418 us  [the longest x8 112 us: place_rows(): pl.pallas_call(partial(place_kernel, slices, held), grid_spec=pltpu.Prefe...]
    dot_general x26 -> x16, matrix products: 335 us -> 79.8 us  [the longest x4 31.8 us: matmul(): return jnp.dot(left, right, preferred_element_type=F32)]
    all_gather x2 -> x0, waiting for transfers between devices: 250 us -> none  [the longest x1 250 us: per_device(): grad_rows = lax.all_gather(arrived, 'tensor', axis=3, tiled=True)]
    gather x4 -> x1, local copies, waits for them, and re-layouts: 207 us -> 1.27 us  [per_device(): prob_grads = prob_grads[jnp.arange(owners, dtype=jnp.int32) ^ owner]]
  transfers between devices with their start and end apart: 9 -> 108, of which waited for: 7 -> 36; matrix products, arithmetic and copies ran while one was open for 5% -> 19% of each run, Pallas kernels for 0% -> 24%
where the time goes in v1:
time: 1750 us; the launch traced here: 1730 us
  waiting for transfers between devices  695 us (40%)
  Pallas kernels  418 us (24%)
  other arithmetic  147 us (8%)
  matrix products  140 us (8%)
  local copies, waits for them, and re-layouts  124 us (7%)
  starting transfers between devices  101 us (6%)
  blocking collectives  85.6 us (5%)
    ppermute x103, waiting for transfers between devices, send(): return lax.ppermute(value, BOTH, flip(dz, dx, dy, dc))  545 us
    psum x1, waiting for transfers between devices, per_device(): lax.psum(g.astype(BF16), 'expert').astype(F32)  137 us
    pallas_call x8, Pallas kernels, place_rows(): pl.pallas_call(partial(place_kernel, slices, held), grid_spec=pltpu.Prefe...  112 us
    pallas_call x4, Pallas kernels, expert_slot(): pl.pallas_call(partial(expert_kernel, slices), grid_spec=pltpu.PrefetchSc...  111 us
    ppermute x103, starting transfers between devices, send(): return lax.ppermute(value, BOTH, flip(dz, dx, dy, dc))  84.6 us
    pallas_call x8, Pallas kernels, pick_rows(): pl.pallas_call(partial(pick_kernel, group, slices), grid_spec=pltpu.Prefe...  81.5 us
    pallas_call x1, Pallas kernels, weight_grads(): pl.pallas_call(partial(weight_kernel, slots, slices), grid_spec=pltpu.Pre...  63 us
    pallas_call x4, Pallas kernels, down_slot(): pl.pallas_call(partial(down_kernel, slices), grid_spec=pltpu.PrefetchScal...  50.1 us
  transfers between devices with their start and end apart: 108, of which 36 were waited for; matrix products, arithmetic and copies ran while one was open for 19% of the time, Pallas kernels for 24%

profile of v1, /device:TPU:10, one launch (start us, length us, event | category | flops | bytes accessed | tf_op | source)
XLA Modules:
  0.0 1734.1 jit_solution(15775973308371753073)
XLA Ops:
  40.7 27.4 %while.57 = (s32[]{:T(128)}, bf16[2,512,4,128]{3,1,2,0:T(8,128)(2,1)}, f32[2,4,512]{2,1,0:T(4,128)S(1)}, f32[2,4]{1,0:T(2,128)S(1)}, s32[2]{0:T(128)S(1)}, /*ind...) while((s32[]{:T(128)}, ...), condition=%wide.region_8.9_spmd.clone, body=%wide.region_3.8_spmd.sunk.clone | while | flops 1103633920 | bytes 46739844 | solution.py:495
  79.5 18.9 %collective-permute-done.1 = bf16[1024,512]{1,0:T(8,128)(2,1)} collective-permute-done((bf16[1024,512]{1,0:T(8,128)(2,1)}, bf16[1024,512]{1,0:T(8,128)(2,1)}, u32[]{:S(2)}, u32[]{:S(2)}) %collective-permute-start.1) | collective-permute-done | bytes 1048608 | tf_op jit(solution)/shard_map/ppermute | solution.py:51
  98.9 46.8 %collective-permute-done.63.refs_2_ = bf16[1024,512]{1,0:T(8,128)(2,1)S(1)} collective-permute-done((bf16[1024,512]{1,0:T(8,128)(2,1)}, bf16[1024,512]{1,0:T(8,128)(2,1)S(1)}, u32[]{:S(2)}, u32[]{:S(2)}) %collective-permute-start.63) | collective-permute-done | bytes 1048608 | tf_op jit(solution)/shard_map/ppermute | solution.py:51
  147.2 19.1 %collective-permute-done.45.refs_2_ = bf16[1024,512]{1,0:T(8,128)(2,1)S(1)} collective-permute-done((bf16[1024,512]{1,0:T(8,128)(2,1)}, bf16[1024,512]{1,0:T(8,128)(2,1)S(1)}, u32[]{:S(2)}, u32[]{:S(2)}) %collective-permute-start.45) | collective-permute-done | bytes 1048608 | tf_op jit(solution)/shard_map/ppermute | solution.py:51
  169.9 18.3 %collective-permute-done.64.refs_3_ = bf16[1024,512]{1,0:T(8,128)(2,1)} collective-permute-done((bf16[1024,512]{1,0:T(8,128)(2,1)S(1)}, bf16[1024,512]{1,0:T(8,128)(2,1)}, u32[]{:S(2)}, u32[]{:S(2)}) %collective-permute-start.64) | collective-permute-done | bytes 1048608 | tf_op jit(solution)/shard_map/ppermute | solution.py:51
  192.5 17.0 collective-permute-done.46.refs_3_
  238.0 15.2 multiply_reduce_fusion.2
  283.1 50.0 %all-gather = s32[8192,8]{0,1:T(8,128)S(1)} all-gather(s32[1024,8]{0,1:T(8,128)S(1)} %copy-done.120), channel_id=2, replica_groups=mesh['expert'=8,'tensor'=4] {'expert'}, dimensions={0}, use_global_device_ids=true | all-gather | bytes 294912 | tf_op jit(solution)/shard_map/all_gather | solution.py:572
  429.2 14.0 collective-permute-done.41.refs_4_
  452.9 16.6 collective-permute-done.23.refs_4_
  560.4 16.5 pmax.7
  580.5 27.8 %expert_slot.4 = (bf16[8,320,256]{2,1,0:T(8,128)(2,1)}, bf16[8,320,256]{2,1,0:T(8,128)(2,1)}, bf16[8,320,256]{2,1,0:T(8,128)(2,1)}, f32[8,2,1024]{2,1,0:T(2,128)...) custom-call(s32[6]{0:T(128)} %stack.69.where_ref, s32[8,8,1024]{2,1,0:T(8,128)} %copy.211.refs_0_.refs_1_, ...), custom_call_target="tpu_custom_call" | custom-call | flops 13421772800 | bytes 56623104 | tf_op jit(solution)/shard_map/expert_slot/pallas_call | solution.py:270
  620.7 27.8 %expert_slot.7 = (bf16[8,320,256]{2,1,0:T(8,128)(2,1)}, bf16[8,320,256]{2,1,0:T(8,128)(2,1)}, bf16[8,320,256]{2,1,0:T(8,128)(2,1)}, f32[8,2,1024]{2,1,0:T(2,128)...) custom-call(s32[6]{0:T(128)} %stack.78.where_ref, s32[8,8,1024]{2,1,0:T(8,128)} %copy.211.refs_0_.refs_1_, ...), custom_call_target="tpu_custom_call" | custom-call | flops 13421772800 | bytes 56623104 | tf_op jit(solution)/shard_map/expert_slot/pallas_call | solution.py:270
  649.2 27.8 %expert_slot.6 = (bf16[8,320,256]{2,1,0:T(8,128)(2,1)}, bf16[8,320,256]{2,1,0:T(8,128)(2,1)}, bf16[8,320,256]{2,1,0:T(8,128)(2,1)}, f32[8,2,1024]{2,1,0:T(2,128)...) custom-call(s32[6]{0:T(128)} %stack.75.where_ref, s32[8,8,1024]{2,1,0:T(8,128)} %copy.211.refs_0_.refs_1_, ...), custom_call_target="tpu_custom_call" | custom-call | flops 13421772800 | bytes 56623104 | tf_op jit(solution)/shard_map/expert_slot/pallas_call | solution.py:270
  677.6 27.8 %expert_slot.5 = (bf16[8,320,256]{2,1,0:T(8,128)(2,1)}, bf16[8,320,256]{2,1,0:T(8,128)(2,1)}, bf16[8,320,256]{2,1,0:T(8,128)(2,1)}, f32[8,2,1024]{2,1,0:T(2,128)...) custom-call(s32[6]{0:T(128)} %stack.72.where_ref, s32[8,8,1024]{2,1,0:T(8,128)} %copy.211.refs_0_.refs_1_, ...), custom_call_target="tpu_custom_call" | custom-call | flops 13421772800 | bytes 56623104 | tf_op jit(solution)/shard_map/expert_slot/pallas_call | solution.py:270
  818.9 14.2 place_rows.13
  866.5 20.6 %collective-permute-done.96 = bf16[1024,512]{1,0:T(8,128)(2,1)S(1)} collective-permute-done((bf16[1024,512]{1,0:T(8,128)(2,1)S(1)}, bf16[1024,512]{1,0:T(8,128)(2,1)S(1)}, u32[]{:S(2)}, u32[]{:S(2)}) %collective-permute-start.96) | collective-permute-done | bytes 1048608 | tf_op jit(solution)/shard_map/ppermute | solution.py:51
  889.9 19.6 %collective-permute-done.90 = bf16[1024,512]{1,0:T(8,128)(2,1)S(1)} collective-permute-done((bf16[1024,512]{1,0:T(8,128)(2,1)S(1)}, bf16[1024,512]{1,0:T(8,128)(2,1)S(1)}, u32[]{:S(2)}, u32[]{:S(2)}) %collective-permute-start.90) | collective-permute-done | bytes 1048608 | tf_op jit(solution)/shard_map/ppermute | solution.py:51
  964.0 35.4 %collective-permute-done.97 = bf16[1024,512]{1,0:T(8,128)(2,1)} collective-permute-done((bf16[1024,512]{1,0:T(8,128)(2,1)}, bf16[1024,512]{1,0:T(8,128)(2,1)}, u32[]{:S(2)}, u32[]{:S(2)}) %collective-permute-start.97) | collective-permute-done | bytes 1048608 | tf_op jit(solution)/shard_map/ppermute | solution.py:51
  1004.5 15.3 collective-permute-done.91
  1019.7 22.1 %collective-permute-done.85 = bf16[1024,512]{1,0:T(8,128)(2,1)S(1)} collective-permute-done((bf16[1024,512]{1,0:T(8,128)(2,1)S(1)}, bf16[1024,512]{1,0:T(8,128)(2,1)S(1)}, u32[]{:S(2)}, u32[]{:S(2)}) %collective-permute-start.85) | collective-permute-done | bytes 1048608 | tf_op jit(solution)/shard_map/ppermute | solution.py:51
  1066.8 14.1 place_rows.10
  1085.1 14.1 place_rows.9
  1133.9 66.9 %while.58 = (s32[]{:T(128)}, f32[1024,4,128]{0,2,1:T(8,128)}, f32[1024,4,128]{0,2,1:T(8,128)}, f32[2,512,4,128]{3,1,2,0:T(8,128)}, s32[2]{0:T(128)S(1)}, /*index...) while((s32[]{:T(128)}, f32[1024,4,128]{0,2,1:T(8,128)}, ...), condition=%wide.region_22.23_spmd.clone.clone, body=%wide.region_19.22_spmd.clone.sunk.clone | while | flops 2721324544 | bytes 168890992 | solution.py:529
  1276.3 32.1 %collective-permute-done.73 = bf16[1024,512]{1,0:T(8,128)(2,1)S(1)} collective-permute-done((bf16[1024,512]{1,0:T(8,128)(2,1)S(1)}, bf16[1024,512]{1,0:T(8,128)(2,1)S(1)}, u32[]{:S(2)}, u32[]{:S(2)}) %collective-permute-start.73) | collective-permute-done | bytes 1048608 | tf_op jit(solution)/shard_map/ppermute | solution.py:51
  1313.2 40.2 %collective-permute-done.55 = bf16[1024,512]{1,0:T(8,128)(2,1)S(1)} collective-permute-done((bf16[1024,512]{1,0:T(8,128)(2,1)S(1)}, bf16[1024,512]{1,0:T(8,128)(2,1)S(1)}, u32[]{:S(2)}, u32[]{:S(2)}) %collective-permute-start.55) | collective-permute-done | bytes 1048608 | tf_op jit(solution)/shard_map/ppermute | solution.py:51
  1356.9 23.0 %collective-permute-done.37 = bf16[1024,512]{1,0:T(8,128)(2,1)S(1)} collective-permute-done((bf16[1024,512]{1,0:T(8,128)(2,1)S(1)}, bf16[1024,512]{1,0:T(8,128)(2,1)S(1)}, u32[]{:S(2)}, u32[]{:S(2)}) %collective-permute-start.37) | collective-permute-done | bytes 1048608 | tf_op jit(solution)/shard_map/ppermute | solution.py:51
  1384.3 63.0 %weight_grads.1 = (f32[8,2048,256]{2,1,0:T(8,128)}, f32[8,2048,256]{2,1,0:T(8,128)}, f32[8,256,2048]{2,1,0:T(8,128)}) custom-call(s32[6]{0:T(128)} %stack.69.where_ref, bf16[2,2,1280,512]{3,2,1,0:T(8,128)(2,1)} %pick_rows.8.refs_4_.refs_0_, bf16[2,2,1280,512]{3,2,1,0:T(8,128)(2,1)} %collective-permute-done.10.refs_5_.refs_1_, ...), custom_call_target="tpu_custom_call" | custom-call | flops 32212254720 | bytes 134217728 | tf_op jit(solution)/shard_map/weight_grads/pallas_call | solution.py:424
  1447.3 20.8 %collective-permute-done.74 = bf16[1024,512]{1,0:T(8,128)(2,1)} collective-permute-done((bf16[1024,512]{1,0:T(8,128)(2,1)}, bf16[1024,512]{1,0:T(8,128)(2,1)}, u32[]{:S(2)}, u32[]{:S(2)}) %collective-permute-start.74) | collective-permute-done | bytes 1048608 | tf_op jit(solution)/shard_map/ppermute | solution.py:51
  1468.2 66.6 %collective-permute-done.56 = bf16[1024,512]{1,0:T(8,128)(2,1)} collective-permute-done((bf16[1024,512]{1,0:T(8,128)(2,1)}, bf16[1024,512]{1,0:T(8,128)(2,1)}, u32[]{:S(2)}, u32[]{:S(2)}) %collective-permute-start.56) | collective-permute-done | bytes 1048608 | tf_op jit(solution)/shard_map/ppermute | solution.py:51
  1550.0 19.1 %all-reduce = (bf16[2048]{0:T(1024)(128)(2,1)S(1)}, bf16[512]{0:T(512)(128)(2,1)S(1)}, bf16[512]{0:T(512)(128)(2,1)S(1)}, bf16[512]{0:T(512)(128)(2,1)S(1)}) all-reduce(bf16[2048]{0:T(1024)(128)(2,1)S(1)} %get-tuple-element.628, bf16[512]{0:T(512)(128)(2,1)S(1)} %bitcast.256, ...), channel_id=1, replica_groups=mesh['expert'=8,'tensor'=4] {'expert'}, use_global_device_ids=true, to_apply=%region_28.29 | all-reduce | flops 3584 | bytes 14336 | tf_op jit(solution)/shard_map/psum | solution.py:722
  1577.4 136.8 %all-reduce.10.cloned.1.call-done = (bf16[2048,512]{1,0:T(8,128)(2,1)}, bf16[2048,512]{1,0:T(8,128)(2,1)}, bf16[2048,512]{1,0:T(8,128)(2,1)}, bf16[512,2048]{1,0:T(8,128)(2,1)}, bf16[2048,64]{0,1:T(8,128)(2,1)}) async-done(((bf16[2048,512]{1,0:T(8,128)(2,1)}, bf16[2048,512]{1,0:T(8,128)(2,1)}, bf16[2048,512]{1,0:T(8,128)(2,1)}, bf16[512,2048]{1,0:T(8,128)(2,1)}, bf16[2048,64]{0,1:T(8,128)(2,1)}), ...) | async-done | bytes 8650768 | tf_op jit(solution)/shard_map/psum | solution.py:722
  (764 shorter events, 809.6 us)
Async XLA Ops:
  73.5 94.9 %collective-permute-start.4 = (bf16[512,2048]{1,0:T(8,128)(2,1)}, bf16[512,2048]{1,0:T(8,128)(2,1)}, u32[]{:S(2)}, u32[]{:S(2)}) collective-permute-start(bf16[512,2048]{1,0:T(8,128)(2,1)} %param.27), channel_id=1, source_target_pairs={{0,2},{1,3},{2,0},{3,1},{4,6},{5,7},{6,4},{7,5},{8,10},{9,11},{10,... | collective-permute-start | bytes 6291464 | tf_op jit(solution)/shard_map/ppermute | solution.py:51
  383.5 140.0 %collective-permute-start.15 = (bf16[2,2,1280,512]{3,2,1,0:T(8,128)(2,1)}, bf16[2,2,1280,512]{3,2,1,0:T(8,128)(2,1)}, u32[]{:S(2)}, u32[]{:S(2)}) collective-permute-start(bf16[2,2,1280,512]{3,2,1,0:T(8,128)(2,1)} %pick_rows.9.refs_6_.refs_8_), channel_id=1, source_target_pairs={{0,1},{1,0},{2,3},{3,2},{4,5},{5,4},{6,7},{7,6},{8,9},{9,8},{10,11... | collective-permute-start | bytes 15728648 | tf_op jit(solution)/shard_map/ppermute | solution.py:51
  411.7 126.8 %collective-permute-start.68 = (bf16[2,2,1280,512]{3,2,1,0:T(8,128)(2,1)}, bf16[2,2,1280,512]{3,2,1,0:T(8,128)(2,1)}, u32[]{:S(2)}, u32[]{:S(2)}) collective-permute-start(bf16[2,2,1280,512]{3,2,1,0:T(8,128)(2,1)} %pick_rows.15.refs_6_.refs_14_), channel_id=1, source_target_pairs={{0,1},{1,0},{2,3},{3,2},{4,5},{5,4},{6,7},{7,6},{8,9},{9,8},{10,11... | collective-permute-start | bytes 15728648 | tf_op jit(solution)/shard_map/ppermute | solution.py:51
  421.9 127.0 %collective-permute-start.10 = (bf16[2,2,1280,512]{3,2,1,0:T(8,128)(2,1)}, bf16[2,2,1280,512]{3,2,1,0:T(8,128)(2,1)}, u32[]{:S(2)}, u32[]{:S(2)}) collective-permute-start(bf16[2,2,1280,512]{3,2,1,0:T(8,128)(2,1)} %pick_rows.8.refs_4_.refs_0_), channel_id=1, source_target_pairs={{0,1},{1,0},{2,3},{3,2},{4,5},{5,4},{6,7},{7,6},{8,9},{9,8},{10,11... | collective-permute-start | bytes 15728648 | tf_op jit(solution)/shard_map/ppermute | solution.py:51
  495.6 125.2 %collective-permute-start.62 = (bf16[2,2,1280,512]{3,2,1,0:T(8,128)(2,1)}, bf16[2,2,1280,512]{3,2,1,0:T(8,128)(2,1)}, u32[]{:S(2)}, u32[]{:S(2)}) collective-permute-start(bf16[2,2,1280,512]{3,2,1,0:T(8,128)(2,1)} %pick_rows.14.refs_4_.refs_6_), channel_id=1, source_target_pairs={{0,1},{1,0},{2,3},{3,2},{4,5},{5,4},{6,7},{7,6},{8,9},{9,8},{10,11... | collective-permute-start | bytes 15728648 | tf_op jit(solution)/shard_map/ppermute | solution.py:51
  523.5 125.0 %collective-permute-start.50 = (bf16[2,2,1280,512]{3,2,1,0:T(8,128)(2,1)}, bf16[2,2,1280,512]{3,2,1,0:T(8,128)(2,1)}, u32[]{:S(2)}, u32[]{:S(2)}) collective-permute-start(bf16[2,2,1280,512]{3,2,1,0:T(8,128)(2,1)} %pick_rows.13.refs_6_.refs_12_), channel_id=1, source_target_pairs={{0,1},{1,0},{2,3},{3,2},{4,5},{5,4},{6,7},{7,6},{8,9},{9,8},{10,11... | collective-permute-start | bytes 15728648 | tf_op jit(solution)/shard_map/ppermute | solution.py:51
  523.5 125.6 %collective-permute-start.44 = (bf16[2,2,1280,512]{3,2,1,0:T(8,128)(2,1)}, bf16[2,2,1280,512]{3,2,1,0:T(8,128)(2,1)}, u32[]{:S(2)}, u32[]{:S(2)}) collective-permute-start(bf16[2,2,1280,512]{3,2,1,0:T(8,128)(2,1)} %pick_rows.12.refs_4_), channel_id=1, source_target_pairs={{0,1},{1,0},{2,3},{3,2},{4,5},{5,4},{6,7},{7,6},{8,9},{9,8},{10,11... | collective-permute-start | bytes 15728648 | tf_op jit(solution)/shard_map/ppermute | solution.py:51
  538.5 138.5 %collective-permute-start.32 = (bf16[2,2,1280,512]{3,2,1,0:T(8,128)(2,1)}, bf16[2,2,1280,512]{3,2,1,0:T(8,128)(2,1)}, u32[]{:S(2)}, u32[]{:S(2)}) collective-permute-start(bf16[2,2,1280,512]{3,2,1,0:T(8,128)(2,1)} %pick_rows.11.refs_6_.refs_10_), channel_id=1, source_target_pairs={{0,1},{1,0},{2,3},{3,2},{4,5},{5,4},{6,7},{7,6},{8,9},{9,8},{10,11... | collective-permute-start | bytes 15728648 | tf_op jit(solution)/shard_map/ppermute | solution.py:51
  548.8 128.7 %collective-permute-start.26 = (bf16[2,2,1280,512]{3,2,1,0:T(8,128)(2,1)}, bf16[2,2,1280,512]{3,2,1,0:T(8,128)(2,1)}, u32[]{:S(2)}, u32[]{:S(2)}) collective-permute-start(bf16[2,2,1280,512]{3,2,1,0:T(8,128)(2,1)} %pick_rows.10.refs_4_.refs_2_), channel_id=1, source_target_pairs={{0,1},{1,0},{2,3},{3,2},{4,5},{5,4},{6,7},{7,6},{8,9},{9,8},{10,11... | collective-permute-start | bytes 15728648 | tf_op jit(solution)/shard_map/ppermute | solution.py:51
  620.7 124.5 %collective-permute-start.75 = (bf16[2,2,1280,512]{3,2,1,0:T(8,128)(2,1)}, bf16[2,2,1280,512]{3,2,1,0:T(8,128)(2,1)}, u32[]{:S(2)}, u32[]{:S(2)}) collective-permute-start(bf16[2,2,1280,512]{3,2,1,0:T(8,128)(2,1)} %get-tuple-element.434), channel_id=1, source_target_pairs={{0,1},{1,0},{2,3},{3,2},{4,5},{5,4},{6,7},{7,6},{8,9},{9,8},{10,11... | collective-permute-start | bytes 15728648 | tf_op jit(solution)/shard_map/ppermute | solution.py:51
  648.6 113.2 %collective-permute-start.16 = (bf16[2,2,1280,512]{3,2,1,0:T(8,128)(2,1)}, bf16[2,2,1280,512]{3,2,1,0:T(8,128)(2,1)}, u32[]{:S(2)}, u32[]{:S(2)}) collective-permute-start(bf16[2,2,1280,512]{3,2,1,0:T(8,128)(2,1)} %get-tuple-element.407), channel_id=1, source_target_pairs={{0,1},{1,0},{2,3},{3,2},{4,5},{5,4},{6,7},{7,6},{8,9},{9,8},{10,11... | collective-permute-start | bytes 15728648 | tf_op jit(solution)/shard_map/ppermute | solution.py:51
  649.1 133.0 %collective-permute-start.92 = (bf16[2,2,1280,512]{3,2,1,0:T(8,128)(2,1)}, bf16[2,2,1280,512]{3,2,1,0:T(8,128)(2,1)}, u32[]{:S(2)}, u32[]{:S(2)}) collective-permute-start(bf16[2,2,1280,512]{3,2,1,0:T(8,128)(2,1)} %get-tuple-element.452), channel_id=1, source_target_pairs={{0,1},{1,0},{2,3},{3,2},{4,5},{5,4},{6,7},{7,6},{8,9},{9,8},{10,11... | collective-permute-start | bytes 15728648 | tf_op jit(solution)/shard_map/ppermute | solution.py:51
  677.1 123.8 %collective-permute-start.86 = (bf16[2,2,1280,512]{3,2,1,0:T(8,128)(2,1)}, bf16[2,2,1280,512]{3,2,1,0:T(8,128)(2,1)}, u32[]{:S(2)}, u32[]{:S(2)}) collective-permute-start(bf16[2,2,1280,512]{3,2,1,0:T(8,128)(2,1)} %get-tuple-element.446), channel_id=1, source_target_pairs={{0,1},{1,0},{2,3},{3,2},{4,5},{5,4},{6,7},{7,6},{8,9},{9,8},{10,11... | collective-permute-start | bytes 15728648 | tf_op jit(solution)/shard_map/ppermute | solution.py:51
  705.4 112.0 %collective-permute-start.80 = (bf16[2,2,1280,512]{3,2,1,0:T(8,128)(2,1)}, bf16[2,2,1280,512]{3,2,1,0:T(8,128)(2,1)}, u32[]{:S(2)}, u32[]{:S(2)}) collective-permute-start(bf16[2,2,1280,512]{3,2,1,0:T(8,128)(2,1)} %get-tuple-element.440), channel_id=1, source_target_pairs={{0,1},{1,0},{2,3},{3,2},{4,5},{5,4},{6,7},{7,6},{8,9},{9,8},{10,11... | collective-permute-start | bytes 15728648 | tf_op jit(solution)/shard_map/ppermute | solution.py:51
  710.5 212.7 %all-to-all-start.1 = ((f32[8,8,1024]{2,1,0:T(8,128)}), f32[8,8,1024]{2,1,0:T(8,128)}, u32[]{:S(2)}, u32[]{:S(2)}) async-start(f32[8,8,1024]{2,1,0:T(8,128)} %gather_fusion), calls=%async_computation.1 | async-start | bytes 524288 | tf_op jit(solution)/shard_map/all_to_all | solution.py:646
  720.2 235.7 %all-reduce.6.cloned.1.call-start = ((), (), s32[]{:S(2)}) async-start(), calls=%async_computation.2 | async-start | bytes 524288 | tf_op jit(solution)/shard_map/psum | solution.py:647
  864.7 183.1 %collective-permute-start.69 = (bf16[2,2,1280,512]{3,2,1,0:T(8,128)(2,1)}, bf16[2,2,1280,512]{3,2,1,0:T(8,128)(2,1)}, u32[]{:S(2)}, u32[]{:S(2)}) collective-permute-start(bf16[2,2,1280,512]{3,2,1,0:T(8,128)(2,1)} %get-tuple-element.428), channel_id=1, source_target_pairs={{0,1},{1,0},{2,3},{3,2},{4,5},{5,4},{6,7},{7,6},{8,9},{9,8},{10,11... | collective-permute-start | bytes 15728648 | tf_op jit(solution)/shard_map/ppermute | solution.py:51
  887.1 178.3 %collective-permute-start.51 = (bf16[2,2,1280,512]{3,2,1,0:T(8,128)(2,1)}, bf16[2,2,1280,512]{3,2,1,0:T(8,128)(2,1)}, u32[]{:S(2)}, u32[]{:S(2)}) collective-permute-start(bf16[2,2,1280,512]{3,2,1,0:T(8,128)(2,1)} %get-tuple-element.421), channel_id=1, source_target_pairs={{0,1},{1,0},{2,3},{3,2},{4,5},{5,4},{6,7},{7,6},{8,9},{9,8},{10,11... | collective-permute-start | bytes 15728648 | tf_op jit(solution)/shard_map/ppermute | solution.py:51
  923.1 161.5 %collective-permute-start.33 = (bf16[2,2,1280,512]{3,2,1,0:T(8,128)(2,1)}, bf16[2,2,1280,512]{3,2,1,0:T(8,128)(2,1)}, u32[]{:S(2)}, u32[]{:S(2)}) collective-permute-start(bf16[2,2,1280,512]{3,2,1,0:T(8,128)(2,1)} %get-tuple-element.414), channel_id=1, source_target_pairs={{0,1},{1,0},{2,3},{3,2},{4,5},{5,4},{6,7},{7,6},{8,9},{9,8},{10,11... | collective-permute-start | bytes 15728648 | tf_op jit(solution)/shard_map/ppermute | solution.py:51
  923.2 617.4 %all-reduce.8.cloned.1.call-start = ((), (), s32[]{:S(2)}) async-start(), calls=%async_computation.3 | async-start | bytes 8388608 | tf_op jit(solution)/shard_map/psum | solution.py:714
  1019.7 98.5 %collective-permute-start.101 = (bf16[1024,512]{1,0:T(8,128)(2,1)}, bf16[1024,512]{1,0:T(8,128)(2,1)}, u32[]{:S(2)}, u32[]{:S(2)}) collective-permute-start(bf16[1024,512]{1,0:T(8,128)(2,1)} %convert_element_type.448.refs_2_), channel_id=1, source_target_pairs={{0,1},{1,0},{2,3},{3,2},{4,5},{5,4},{6,7},{7,6},{8,9},{9,8},{10,11... | collective-permute-start | bytes 3145736 | tf_op jit(solution)/shard_map/ppermute | solution.py:51
  1065.4 210.2 %collective-permute-start.17 = (bf16[512,512]{1,0:T(8,128)(2,1)}, bf16[512,512]{1,0:T(8,128)(2,1)}, u32[]{:S(2)}, u32[]{:S(2)}) collective-permute-start(bf16[512,512]{1,0:T(8,128)(2,1)} %get-tuple-element.710), channel_id=1, source_target_pairs={{0,2},{1,3},{2,0},{3,1},{4,6},{5,7},{6,4},{7,5},{8,10},{9,11},{10,... | collective-permute-start | bytes 1572872 | tf_op jit(solution)/shard_map/ppermute | solution.py:51
  1108.0 137.3 %collective-permute-start.72 = (bf16[512,512]{1,0:T(8,128)(2,1)}, bf16[512,512]{1,0:T(8,128)(2,1)}, u32[]{:S(2)}, u32[]{:S(2)}) collective-permute-start(bf16[512,512]{1,0:T(8,128)(2,1)} %get-tuple-element.717), channel_id=1, source_target_pairs={{0,4},{1,5},{2,6},{3,7},{4,0},{5,1},{6,2},{7,3},{8,12},{9,13},{10,... | collective-permute-start | bytes 1572872 | tf_op jit(solution)/shard_map/ppermute | solution.py:51
  1109.0 138.7 %collective-permute-start.70 = (bf16[512,512]{1,0:T(8,128)(2,1)}, bf16[512,512]{1,0:T(8,128)(2,1)}, u32[]{:S(2)}, u32[]{:S(2)}) collective-permute-start(bf16[512,512]{1,0:T(8,128)(2,1)} %get-tuple-element.716), channel_id=1, source_target_pairs={{0,2},{1,3},{2,0},{3,1},{4,6},{5,7},{6,4},{7,5},{8,10},{9,11},{10,... | collective-permute-start | bytes 1572872 | tf_op jit(solution)/shard_map/ppermute | solution.py:51
  1118.2 131.5 %collective-permute-start.54 = (bf16[512,512]{1,0:T(8,128)(2,1)}, bf16[512,512]{1,0:T(8,128)(2,1)}, u32[]{:S(2)}, u32[]{:S(2)}) collective-permute-start(bf16[512,512]{1,0:T(8,128)(2,1)} %get-tuple-element.715), channel_id=1, source_target_pairs={{0,4},{1,5},{2,6},{3,7},{4,0},{5,1},{6,2},{7,3},{8,12},{9,13},{10,... | collective-permute-start | bytes 1572872 | tf_op jit(solution)/shard_map/ppermute | solution.py:51
  1123.6 128.9 %collective-permute-start.52 = (bf16[512,512]{1,0:T(8,128)(2,1)}, bf16[512,512]{1,0:T(8,128)(2,1)}, u32[]{:S(2)}, u32[]{:S(2)}) collective-permute-start(bf16[512,512]{1,0:T(8,128)(2,1)} %get-tuple-element.714), channel_id=1, source_target_pairs={{0,2},{1,3},{2,0},{3,1},{4,6},{5,7},{6,4},{7,5},{8,10},{9,11},{10,... | collective-permute-start | bytes 1572872 | tf_op jit(solution)/shard_map/ppermute | solution.py:51
  1225.4 488.8 %all-reduce.10.cloned.1.call-start = ((), (), s32[]{:S(2)}) async-start(), calls=%async_computation.4 | async-start | bytes 17301504 | tf_op jit(solution)/shard_map/psum | solution.py:722
  1275.6 104.3 %collective-permute-start.37 = (bf16[1024,512]{1,0:T(8,128)(2,1)S(1)}, bf16[1024,512]{1,0:T(8,128)(2,1)S(1)}, u32[]{:S(2)}, u32[]{:S(2)}) collective-permute-start(bf16[1024,512]{1,0:T(8,128)(2,1)S(1)} %pad_maximum_fusion.7), channel_id=1, source_target_pairs={{0,2},{1,3},{2,0},{3,1},{4,6},{5,7},{6,4},{7,5},{8,10},{9,11},{10,... | collective-permute-start | bytes 3145736 | tf_op jit(solution)/shard_map/ppermute | solution.py:51
  1311.3 136.1 %collective-permute-start.20 = (bf16[1024,512]{1,0:T(8,128)(2,1)S(1)}, bf16[1024,512]{1,0:T(8,128)(2,1)}, u32[]{:S(2)}, u32[]{:S(2)}) collective-permute-start(bf16[1024,512]{1,0:T(8,128)(2,1)S(1)} %copy-done.71), channel_id=1, source_target_pairs={{0,2},{1,3},{2,0},{3,1},{4,6},{5,7},{6,4},{7,5},{8,10},{9,11},{10,... | collective-permute-start | bytes 3145736 | tf_op jit(solution)/shard_map/ppermute | solution.py:51
  1353.9 114.2 %collective-permute-start.74 = (bf16[1024,512]{1,0:T(8,128)(2,1)}, bf16[1024,512]{1,0:T(8,128)(2,1)}, u32[]{:S(2)}, u32[]{:S(2)}) collective-permute-start(bf16[1024,512]{1,0:T(8,128)(2,1)} %add_convert_fusion.8), channel_id=1, source_target_pairs={{0,24},{1,25},{2,26},{3,27},{4,28},{5,29},{6,30},{7,31},{8,16},{9,... | collective-permute-start | bytes 3145736 | tf_op jit(solution)/shard_map/ppermute | solution.py:51
  1379.8 154.9 %collective-permute-start.56 = (bf16[1024,512]{1,0:T(8,128)(2,1)}, bf16[1024,512]{1,0:T(8,128)(2,1)}, u32[]{:S(2)}, u32[]{:S(2)}) collective-permute-start(bf16[1024,512]{1,0:T(8,128)(2,1)} %add_convert_fusion.9), channel_id=1, source_target_pairs={{0,16},{1,17},{2,18},{3,19},{4,20},{5,21},{6,22},{7,23},{8,24},{9,... | collective-permute-start | bytes 3145736 | tf_op jit(solution)/shard_map/ppermute | solution.py:51
  1383.7 151.1 %collective-permute-start.38 = (bf16[1024,512]{1,0:T(8,128)(2,1)}, bf16[1024,512]{1,0:T(8,128)(2,1)}, u32[]{:S(2)}, u32[]{:S(2)}) collective-permute-start(bf16[1024,512]{1,0:T(8,128)(2,1)} %add_convert_fusion.10), channel_id=1, source_target_pairs={{0,8},{1,9},{2,10},{3,11},{4,12},{5,13},{6,14},{7,15},{8,0},{9,1},... | collective-permute-start | bytes 3145736 | tf_op jit(solution)/shard_map/ppermute | solution.py:51
  (230 other events, 4991.9 us)
Sparse Core Ops, SparseCore 0:
  923.4 32.5 all-reduce.5
  1225.5 136.1 all-reduce.7
  1367.2 347.0 all-reduce.9

commit v2 on v1

v2 whole, which is shorter than its diff:
```python
from functools import partial
import math

import jax
import jax.numpy as jnp
from jax import lax
from jax.experimental import pallas as pl
from jax.experimental.pallas import tpu as pltpu
from jax.sharding import PartitionSpec as P

HD = 128
E = 64
TOP = 8
LENGTH = 1024
CAP = 160
NB = 2
BOTH = ("expert", "tensor")
F32 = jnp.float32
BF16 = jnp.bfloat16
VMEM = 60 * 1024 * 1024
DUE = {
    ("attended", 0): "cx0 cy0 cz1",
    ("branch", 0): "cz2 cx1",
    ("normed", 0): "cy1",
    ("cot", 1): "cx2 cz3 nx0 ny0 nz1",
    ("row", 0): "cy2 nz2",
    ("expert", 0): "nx1 ny1 cd2",
    ("row", 1): "nx2",
    ("place", 0): "cx3 nz3",
    ("expert", 1): "ny2",
    ("row", 2): "e00 nx3 cy3",
    ("place", 1): "e10",
    ("expert", 2): "ny3",
    ("row", 3): "e01",
    ("place", 2): "e11",
    ("expert", 3): "e02",
    ("place", 3): "e12",
}


def matmul(left, right):
    return jnp.dot(left, right, preferred_element_type=F32)


def matmul_nt(left, right):
    return lax.dot_general(left, right, (((1,), (1,)), ((), ())), preferred_element_type=F32)


def matmul_tn(left, right):
    return lax.dot_general(left, right, (((0,), (0,)), ((), ())), preferred_element_type=F32)


def after(value, *others):
    return lax.optimization_barrier((value, *others))[0]


def flip(dz, dx, dy, dc):
    pairs = []
    for z in range(4):
        for x in range(2):
            for y in range(2):
                for c in range(2):
                    pairs.append(
                        (
                            ((z * 2 + x) * 2 + y) * 2 + c,
                            (((z ^ dz) * 2 + (x ^ dx)) * 2 + (y ^ dy)) * 2 + (c ^ dc),
                        )
                    )
    return pairs


def send(value, dz=0, dx=0, dy=0, dc=0):
    return lax.ppermute(value, BOTH, flip(dz, dx, dy, dc))


def is_cube():
    return lax.axis_size("expert") == 8 and lax.axis_size("tensor") == 4


def core_swap(value):
    if is_cube():
        return send(value, dc=1)
    count = lax.axis_size("tensor")
    return lax.ppermute(value, "tensor", [(i, i ^ 1) for i in range(count)])


def slot_blocks():
    owner, part = lax.axis_index("expert"), lax.axis_index("tensor")
    core = part % 2
    if is_cube():
        blocks = [[owner ^ (k * 2 + b) for b in range(NB)] for k in range(4)]
        mine = [part ^ (y * 2) for y in range(2)]
    else:
        blocks = [[k * NB + b for b in range(NB)] for k in range(lax.axis_size("expert") // NB)]
        mine = [y * 2 + core for y in range(lax.axis_size("tensor") // 2)]
    theirs = [m ^ 1 for m in mine]
    return [jnp.stack([jnp.asarray(v, jnp.int32) for v in b + mine + theirs]) for b in blocks]


def same_core():
    count = lax.axis_size("tensor")
    return [[y * 2 + c for y in range(count // 2)] for c in range(2)]


def gather_slots(own):
    if not is_cube():
        blocks = lax.all_gather(own, "expert")
        full = lax.all_gather(blocks, "tensor", axis_index_groups=same_core())
        return [
            [[full[y, k * NB + b] for y in range(full.shape[0])] for b in range(NB)]
            for k in range(full.shape[1] // NB)
        ]
    slots = []
    for k in range(4):
        block = send(own, dz=k) if k else own
        over_x = send(block, dx=1)
        over_y = send(block, dy=1)
        far = send(over_x, dy=1) if k % 2 else send(over_y, dx=1)
        slots.append([[block, over_y], [over_x, far]])
    return slots


def added(*terms):
    return sum(t.astype(F32) for t in terms)


def scatter_plane(parts, odd):
    near, over_y, over_x, far = parts[0][0], parts[0][1], parts[1][0], parts[1][1]
    if odd:
        far = send(far, dy=1)
        from_y = send(over_y, dy=1)
        from_x = send(added(over_x, far).astype(BF16), dx=1)
        return added(near, from_x, from_y), (far, from_y), (from_x,)
    far = send(far, dx=1)
    from_x = send(over_x, dx=1)
    from_y = send(added(over_y, far).astype(BF16), dy=1)
    return added(near, from_x, from_y), (far, from_x), (from_y,)


def scatter_all(slots):
    full = jnp.stack(
        [jnp.stack([s[b][y] for s in slots for b in range(NB)]) for y in range(len(slots[0][0]))]
    )
    mine = lax.psum_scatter(full, "tensor", axis_index_groups=same_core(), scatter_dimension=0)
    return lax.psum_scatter(mine, "expert", scatter_dimension=0).astype(F32)


def scatter_pairs(pairs):
    if not is_cube():
        return scatter_all(
            [[[a[i] for a in b] for b in pair] for pair in pairs for i in range(pair[0][0].shape[0])]
        )
    low, high = (scatter_plane(p, k)[0] for k, p in enumerate(pairs))
    total = low + send(high.astype(BF16), dz=2).astype(F32)
    return total[0] + send(total[1].astype(BF16), dz=1).astype(F32)


def tensor_order():
    part = lax.axis_index("tensor")
    if is_cube():
        return [part ^ i for i in (0, 2, 1, 3)]
    return [jnp.int32(i) for i in range(lax.axis_size("tensor"))]


def tensor_gather(own):
    if not is_cube():
        full = lax.all_gather(own, "tensor")
        return [full[i] for i in range(full.shape[0])]
    over_y = send(own, dy=1)
    return [own, over_y, core_swap(own), core_swap(over_y)]


def tensor_scatter(product, pieces):
    if not is_cube():
        full = jnp.concatenate([product(p).astype(BF16) for p in pieces], axis=1)
        return lax.psum_scatter(full, "tensor", scatter_dimension=1, tiled=True).astype(F32)
    away_y = product(pieces[3]).astype(BF16)
    away = product(pieces[2]).astype(BF16)
    from_y, near = core_swap(away_y), core_swap(away)
    over_y = send(added(product(pieces[1]), from_y).astype(BF16), dy=1)
    return added(product(pieces[0]), near, over_y)


def tensor_sum(value):
    if not is_cube():
        return lax.psum(value, "tensor")
    value = value + core_swap(value)
    return value + send(value, dy=1)


def one_hot(pos_row):
    rows = lax.broadcasted_iota(jnp.int32, (CAP, pos_row.shape[1]), 0)
    return rows == pos_row


def as_bf16(mask):
    return jnp.where(mask, 1.0, 0.0).astype(BF16)


def pick_kernel(group, slices, where_ref, *refs):
    pos_refs, x_refs = refs[:NB], refs[NB : NB + NB * slices]
    out_ref, hot_ref = refs[-2:]
    step = pl.program_id(0)
    for b in range(NB):
        for i in range(group):
            hot_ref[b, i * CAP : (i + 1) * CAP, :] = as_bf16(
                one_hot(pos_refs[b][0, pl.ds(step * group + i, 1), :])
            )
        for y in range(slices):
            out_ref[b, y] = matmul(hot_ref[b], x_refs[b * slices + y][...]).astype(BF16)


def pick_rows(where, pos, blocks):
    slices = len(blocks[0])
    tokens, width = blocks[0][0].shape
    held = pos.shape[1]
    group = 2
    flat = [a for b in blocks for a in b]

    def block_spec(b):
        return pl.BlockSpec((1, held, tokens), lambda i, where: (where[b], 0, 0))

    return pl.pallas_call(
        partial(pick_kernel, group, slices),
        grid_spec=pltpu.PrefetchScalarGridSpec(
            num_scalar_prefetch=1,
            grid=(held // group,),
            in_specs=[block_spec(b) for b in range(NB)]
            + [pl.BlockSpec((tokens, width), lambda i, where: (0, 0)) for _ in flat],
            out_specs=pl.BlockSpec(
                (NB, slices, group * CAP, width), lambda i, where: (0, 0, i, 0)
            ),
            scratch_shapes=[pltpu.VMEM((NB, group * CAP, tokens), BF16)],
        ),
        out_shape=jax.ShapeDtypeStruct((NB, slices, held * CAP, width), BF16),
        compiler_params=pltpu.CompilerParams(vmem_limit_bytes=VMEM),
        cost_estimate=pl.CostEstimate(
            flops=2 * NB * slices * held * CAP * tokens * width,
            bytes_accessed=2 * NB * slices * (held * CAP + tokens) * width,
            transcendentals=0,
        ),
        name="pick_rows",
    )(where, *([pos] * NB), *flat)


def expert_kernel(slices, where_ref, *refs):
    pos_refs, gate_refs = refs[:NB], refs[NB : 2 * NB]
    rows_mine, rows_theirs, cot_mine, cot_theirs, wg_ref, wu_ref, wd_ref = refs[2 * NB : 2 * NB + 7]
    scaled_ref, gate_grad_ref, up_grad_ref, prob_ref, keep_ref, give_ref = refs[2 * NB + 7 :]
    e = pl.program_id(0)
    width = rows_mine.shape[3]
    ff = wg_ref.shape[2]
    gate_pre = jnp.zeros((NB * CAP, ff), F32)
    up_pre = jnp.zeros((NB * CAP, ff), F32)
    grad_hidden = jnp.zeros((NB * CAP, ff), F32)

    def columns(j):
        return pl.ds(pl.multiple_of(where_ref[NB + j] * width, width), width)

    for j in range(2 * slices):
        x_ref, c_ref = (rows_mine, cot_mine) if j < slices else (rows_theirs, cot_theirs)
        x = x_ref[:, j % slices].reshape(NB * CAP, width)
        c = c_ref[:, j % slices].reshape(NB * CAP, width)
        gate_pre = gate_pre + matmul(x, wg_ref[0, columns(j), :])
        up_pre = up_pre + matmul(x, wu_ref[0, columns(j), :])
        grad_hidden = grad_hidden + matmul_nt(c, wd_ref[0, :, columns(j)])
    masks = [one_hot(pos_refs[b][0, pl.ds(e, 1), :]) for b in range(NB)]
    gates = jnp.concatenate(
        [
            jnp.sum(jnp.where(masks[b], gate_refs[b][0, pl.ds(e, 1), :], 0.0), axis=1, keepdims=True)
            for b in range(NB)
        ],
        axis=0,
    )
    sigma = jax.nn.sigmoid(gate_pre)
    swish = gate_pre * sigma
    hidden = (swish * up_pre).astype(BF16).astype(F32)
    prob = jnp.sum(hidden * grad_hidden, axis=1, keepdims=True)
    for b in range(NB):
        prob_ref[0, b : b + 1, :] = jnp.sum(
            jnp.where(masks[b], prob[b * CAP : (b + 1) * CAP], 0.0), axis=0, keepdims=True
        )
    grad_hidden = grad_hidden * gates
    scaled_ref[0] = (hidden * gates).astype(BF16)
    gate_grad = (grad_hidden * up_pre * (sigma * (1.0 + gate_pre * (1.0 - sigma)))).astype(BF16)
    up_grad = (grad_hidden * swish).astype(BF16)
    gate_grad_ref[0] = gate_grad
    up_grad_ref[0] = up_grad
    for j in range(2 * slices):
        to = keep_ref if j < slices else give_ref
        back = matmul_nt(gate_grad, wg_ref[0, columns(j), :]) + matmul_nt(
            up_grad, wu_ref[0, columns(j), :]
        )
        to[:, j % slices] = back.astype(BF16).reshape(NB, CAP, width)


def expert_slot(where, pos, gate, rows, cots, w_gate, w_up, w_down):
    held, depth, ff = w_gate.shape
    tokens = pos.shape[2]
    slices, width = rows[0].shape[1], rows[0].shape[3]

    def block_spec(b):
        return pl.BlockSpec((1, held, tokens), lambda e, where: (where[b], 0, 0))

    rows_spec = pl.BlockSpec((NB, slices, CAP, width), lambda e, where: (0, 0, e, 0))
    rows_shape = jax.ShapeDtypeStruct((NB, slices, held * CAP, width), BF16)
    in_spec = pl.BlockSpec((1, depth, ff), lambda e, where: (e, 0, 0))
    hidden_spec = pl.BlockSpec((1, NB * CAP, ff), lambda e, where: (e, 0, 0))
    hidden_shape = jax.ShapeDtypeStruct((held, NB * CAP, ff), BF16)
    return pl.pallas_call(
        partial(expert_kernel, slices),
        grid_spec=pltpu.PrefetchScalarGridSpec(
            num_scalar_prefetch=1,
            grid=(held,),
            in_specs=[block_spec(b) for b in range(NB)] * 2
            + [rows_spec] * 4
            + [in_spec, in_spec, pl.BlockSpec((1, ff, depth), lambda e, where: (e, 0, 0))],
            out_specs=[hidden_spec] * 3
            + [pl.BlockSpec((1, NB, tokens), lambda e, where: (e, 0, 0)), rows_spec, rows_spec],
        ),
        out_shape=[hidden_shape] * 3
        + [jax.ShapeDtypeStruct((held, NB, tokens), F32), rows_shape, rows_shape],
        compiler_params=pltpu.CompilerParams(vmem_limit_bytes=VMEM),
        cost_estimate=pl.CostEstimate(
            flops=10 * NB * held * CAP * depth * ff,
            bytes_accessed=6 * held * depth * ff + 6 * NB * held * CAP * depth,
            transcendentals=NB * held * CAP * ff,
        ),
        name="expert_slot",
    )(where, *([pos] * NB), *([gate] * NB), *rows, *cots, w_gate, w_up, w_down)


def down_kernel(slices, slots, where_ref, *refs):
    scaled_refs, wd_ref, keep_ref, give_ref = refs[:slots], refs[slots], refs[-2], refs[-1]
    width = keep_ref.shape[3]
    for j in range(2 * slices):
        to = keep_ref if j < slices else give_ref
        columns = pl.ds(pl.multiple_of(where_ref[NB + j] * width, width), width)
        for k in range(slots):
            rows = matmul(scaled_refs[k][0], wd_ref[0, :, columns])
            to[k * NB : (k + 1) * NB, j % slices] = rows.astype(BF16).reshape(NB, CAP, width)


def down_slots(where, scaled, w_down, slices):
    held, ff, depth = w_down.shape
    width = depth // (2 * slices)
    slots = len(scaled)
    rows_spec = pl.BlockSpec((slots * NB, slices, CAP, width), lambda e, where: (0, 0, e, 0))
    rows_shape = jax.ShapeDtypeStruct((slots * NB, slices, held * CAP, width), BF16)
    return pl.pallas_call(
        partial(down_kernel, slices, slots),
        grid_spec=pltpu.PrefetchScalarGridSpec(
            num_scalar_prefetch=1,
            grid=(held,),
            in_specs=[pl.BlockSpec((1, NB * CAP, ff), lambda e, where: (e, 0, 0))] * slots
            + [pl.BlockSpec((1, ff, depth), lambda e, where: (e, 0, 0))],
            out_specs=[rows_spec, rows_spec],
        ),
        out_shape=[rows_shape, rows_shape],
        compiler_params=pltpu.CompilerParams(vmem_limit_bytes=VMEM),
        cost_estimate=pl.CostEstimate(
            flops=2 * slots * NB * held * CAP * depth * ff,
            bytes_accessed=2 * held * depth * ff + 2 * slots * NB * held * CAP * depth,
            transcendentals=0,
        ),
        name="down_slots",
    )(where, *scaled, w_down)


def place_kernel(slices, held, slots, where_ref, *refs):
    count = NB * slots
    at_refs, mine_ref, theirs_ref = refs[:count], refs[count], refs[count + 1]
    out_refs, hot_ref = refs[count + 2 : -1], refs[-1]
    b, y = pl.program_id(0), pl.program_id(1)
    tokens = hot_ref.shape[0]
    for block in range(count):

        @pl.when((b == block) & (y == 0))
        def _():
            at = at_refs[block][0]
            for tile in range(held * CAP // 128):
                lanes = lax.broadcasted_iota(jnp.int32, (tokens, 128), 1) + tile * 128
                mask = None
                for e in range(tile * 128 // CAP, (tile * 128 + 127) // CAP + 1):
                    hit = at[:, e : e + 1] == lanes
                    mask = hit if mask is None else mask | hit
                hot_ref[:, tile * 128 : (tile + 1) * 128] = as_bf16(mask)

    rows = (mine_ref[0, 0].astype(F32) + theirs_ref[0, 0].astype(F32)).astype(BF16)
    placed = matmul(hot_ref[...], rows).astype(BF16)
    for block in range(count):
        for part in range(slices):

            @pl.when((b == block) & (y == part))
            def _():
                out_refs[block % NB * slices + part][block // NB] = placed


def place_rows(wheres, at, mine, theirs):
    _, slices, count, width = mine.shape
    _, tokens, held = at.shape
    slots = len(wheres)
    blocks = jnp.concatenate([w[:NB] for w in wheres])

    def block_spec(b):
        return pl.BlockSpec((1, tokens, held), lambda i, y, where: (where[b], 0, 0))

    rows_spec = pl.BlockSpec((1, 1, count, width), lambda i, y, where: (i, y, 0, 0))
    out = pl.pallas_call(
        partial(place_kernel, slices, held, slots),
        grid_spec=pltpu.PrefetchScalarGridSpec(
            num_scalar_prefetch=1,
            grid=(NB * slots, slices),
            in_specs=[block_spec(b) for b in range(NB * slots)] + [rows_spec, rows_spec],
            out_specs=[pl.BlockSpec((slots, tokens, width), lambda i, y, where: (0, 0, 0))]
            * (NB * slices),
            scratch_shapes=[pltpu.VMEM((tokens, count), BF16)],
        ),
        out_shape=[jax.ShapeDtypeStruct((slots, tokens, width), BF16)] * (NB * slices),
        compiler_params=pltpu.CompilerParams(vmem_limit_bytes=VMEM),
        cost_estimate=pl.CostEstimate(
            flops=2 * NB * slots * slices * count * tokens * width,
            bytes_accessed=2 * NB * slots * slices * (2 * count + tokens) * width,
            transcendentals=0,
        ),
        name="place_rows",
    )(blocks, *([at] * (NB * slots)), mine, theirs)
    return [out[b * slices : (b + 1) * slices] for b in range(NB)]


def weight_kernel(slots, slices, where_ref, *refs):
    rows, gate_grads, up_grads = refs[: 2 * slots], refs[2 * slots : 3 * slots], refs[3 * slots : 4 * slots]
    gate_ref, up_ref = refs[4 * slots :]
    width = rows[0].shape[3]
    for j in range(2 * slices):
        columns = pl.ds(pl.multiple_of(where_ref[NB + j] * width, width), width)
        gate = up = None
        for k in range(slots):
            x = rows[2 * k + j // slices][:, j % slices].reshape(NB * CAP, width)
            terms = matmul_tn(x, gate_grads[k][0]), matmul_tn(x, up_grads[k][0])
            gate, up = terms if gate is None else (gate + terms[0], up + terms[1])
        gate_ref[0, columns, :] = gate
        up_ref[0, columns, :] = up


def weight_down_kernel(slots, slices, where_ref, *refs):
    cots, scaled, down_ref = refs[: 2 * slots], refs[2 * slots : 3 * slots], refs[3 * slots]
    width = cots[0].shape[3]
    for j in range(2 * slices):
        columns = pl.ds(pl.multiple_of(where_ref[NB + j] * width, width), width)
        down = None
        for k in range(slots):
            c = cots[2 * k + j // slices][:, j % slices].reshape(NB * CAP, width)
            term = matmul_tn(scaled[k][0], c)
            down = term if down is None else down + term
        down_ref[0, :, columns] = down


def weight_grads(kernel, where, rows, hiddens, outs, name):
    slots = len(rows)
    held, _, ff = hiddens[0].shape
    slices, width = rows[0][0].shape[1], rows[0][0].shape[3]
    depth = 2 * slices * width
    rows_spec = pl.BlockSpec((NB, slices, CAP, width), lambda e, where: (0, 0, e, 0))
    hidden_spec = pl.BlockSpec((1, NB * CAP, ff), lambda e, where: (e, 0, 0))
    return pl.pallas_call(
        partial(kernel, slots, slices),
        grid_spec=pltpu.PrefetchScalarGridSpec(
            num_scalar_prefetch=1,
            grid=(held,),
            in_specs=[rows_spec] * (2 * slots) + [hidden_spec] * len(hiddens),
            out_specs=[pl.BlockSpec((1, *o), lambda e, where: (e, 0, 0)) for o in outs],
        ),
        out_shape=[jax.ShapeDtypeStruct((held, *o), F32) for o in outs],
        compiler_params=pltpu.CompilerParams(vmem_limit_bytes=VMEM),
        cost_estimate=pl.CostEstimate(
            flops=2 * len(outs) * slots * NB * held * CAP * depth * ff,
            bytes_accessed=4 * len(outs) * held * depth * ff + 2 * slots * NB * held * CAP * depth,
            transcendentals=0,
        ),
        name=name,
    )(where, *[a for pair in rows for a in pair], *hiddens)


def project_kernel(x_ref, wq_ref, wk_ref, wv_ref, qg_ref, kg_ref, qr_ref, kr_ref, q_ref, k_ref, v_ref):
    x = x_ref[...]
    for w_ref, gain_ref, raw_ref, to_ref in ((wq_ref, qg_ref, qr_ref, q_ref), (wk_ref, kg_ref, kr_ref, k_ref)):
        raw = matmul(x, w_ref[...])
        raw_ref[...] = raw
        for h in range(raw.shape[1] // HD):
            part = raw[:, h * HD : (h + 1) * HD]
            inverse = lax.rsqrt(jnp.mean(part * part, axis=1, keepdims=True) + 1e-06)
            gain = gain_ref[:, h * HD : (h + 1) * HD]
            to_ref[:, h * HD : (h + 1) * HD] = (part * inverse * gain).astype(BF16)
    v_ref[...] = matmul(x, wv_ref[...]).astype(BF16)


def project(x, w_query, w_key, w_value, query_gain, key_gain):
    tokens, depth = x.shape
    columns = w_query.shape[1]
    step = min(256, columns)
    weight = pl.BlockSpec((depth, step), lambda i: (0, i))
    gain = pl.BlockSpec((1, step), lambda i: (0, i))
    out = pl.BlockSpec((tokens, step), lambda i: (0, i))
    return pl.pallas_call(
        project_kernel,
        grid=(columns // step,),
        in_specs=[pl.BlockSpec((tokens, depth), lambda i: (0, 0)), weight, weight, weight, gain, gain],
        out_specs=[out] * 5,
        out_shape=[jax.ShapeDtypeStruct((tokens, columns), t) for t in (F32, F32, BF16, BF16, BF16)],
        compiler_params=pltpu.CompilerParams(vmem_limit_bytes=VMEM),
        cost_estimate=pl.CostEstimate(
            flops=6 * tokens * depth * columns,
            bytes_accessed=2 * tokens * depth + 6 * depth * columns + 14 * tokens * columns,
            transcendentals=0,
        ),
        name="project",
    )(x, w_query, w_key, w_value, query_gain.reshape(1, -1), key_gain.reshape(1, -1))


def allowed_pairs(pieces_ref, base, first, rows, keys):
    query = first + lax.broadcasted_iota(jnp.int32, (rows, 1), 0)
    key = lax.broadcasted_iota(jnp.int32, (1, keys), 1)

    def piece_of(at, other):
        found = jnp.full(at.shape, other, jnp.int32)
        for j in range(2):
            start, length = pieces_ref[base + j], pieces_ref[base + 2 + j]
            found = jnp.where((at >= start) & (at < start + length), j, found)
        return found

    return (key <= query) | (piece_of(query, -1) == piece_of(key, -2))


def query_blocks():
    half = LENGTH // 2
    return ((0, half, half), (half, half, LENGTH))


def attend_kernel(scale, pieces_ref, q_ref, k_ref, v_ref, o_ref, log_ref, top_ref):
    base = pl.program_id(0) * 4
    best = None
    for first, rows, keys in query_blocks():
        allowed = allowed_pairs(pieces_ref, base, first, rows, keys)
        scores = matmul_nt(q_ref[first : first + rows, :], k_ref[:keys, :]) * scale
        masked = jnp.where(allowed, scores, -1e30)
        top = jnp.max(masked, axis=1, keepdims=True)
        weights = jnp.exp(masked - top)
        total = jnp.sum(weights, axis=1, keepdims=True)
        probs = (weights * (1.0 / total)).astype(BF16)
        o_ref[first : first + rows, :] = matmul(probs, v_ref[:keys, :]).astype(BF16)
        log_ref[0, first : first + rows, :] = top + jnp.log(total)
        most = jnp.max(top, axis=0, keepdims=True)
        best = most if best is None else jnp.maximum(best, most)
    top_ref[0] = jnp.broadcast_to(best, (8, HD))


def attend(pieces, queries, keys, values, scale):
    tokens, columns = queries.shape
    sequences, heads = tokens // LENGTH, columns // HD
    block = pl.BlockSpec((LENGTH, HD), lambda s, h, pieces: (s, h))
    return pl.pallas_call(
        partial(attend_kernel, scale),
        grid_spec=pltpu.PrefetchScalarGridSpec(
            num_scalar_prefetch=1,
            grid=(sequences, heads),
            in_specs=[block] * 3,
            out_specs=[
                block,
                pl.BlockSpec((1, LENGTH, 1), lambda s, h, pieces: (h, s, 0)),
                pl.BlockSpec((1, 8, HD), lambda s, h, pieces: (s * heads + h, 0, 0)),
            ],
        ),
        out_shape=[
            jax.ShapeDtypeStruct((tokens, columns), BF16),
            jax.ShapeDtypeStruct((heads, tokens, 1), F32),
            jax.ShapeDtypeStruct((sequences * heads, 8, HD), F32),
        ],
        compiler_params=pltpu.CompilerParams(vmem_limit_bytes=VMEM),
        cost_estimate=pl.CostEstimate(
            flops=4 * tokens * LENGTH * columns,
            bytes_accessed=8 * tokens * columns,
            transcendentals=tokens * heads * LENGTH,
        ),
        name="attend",
    )(pieces, queries, keys, values)


def attend_back_kernel(
    scale, pieces_ref, q_ref, k_ref, v_ref, g_ref, log_ref, qr_ref, kr_ref, qg_ref, kg_ref,
    gq_ref, gk_ref, gv_ref, gqg_ref, gkg_ref, dq_ref, dk_ref, dv_ref,
):
    base = pl.program_id(0) * 4
    blocks = query_blocks()
    for first, rows, keys in blocks[::-1]:
        allowed = allowed_pairs(pieces_ref, base, first, rows, keys)
        q, g = q_ref[first : first + rows, :], g_ref[first : first + rows, :]
        k, v = k_ref[:keys, :], v_ref[:keys, :]
        scores = matmul_nt(q, k) * scale
        probs = jnp.exp(jnp.where(allowed, scores, -1e30) - log_ref[0, first : first + rows, :])
        grad_p = matmul_nt(g, v)
        delta = jnp.sum(probs * grad_p, axis=1, keepdims=True)
        grad_s = (probs * (grad_p - delta)).astype(BF16)
        dq_ref[first : first + rows, :] = matmul(grad_s, k) * scale
        dk = matmul_tn(grad_s, q) * scale
        dv = matmul_tn(probs.astype(BF16), g)
        if keys == LENGTH:
            dk_ref[...] = dk
            dv_ref[...] = dv
        else:
            dk_ref[:keys, :] += dk
            dv_ref[:keys, :] += dv
    gv_ref[...] = dv_ref[...].astype(BF16)
    for raw_ref, gain_ref, grad_ref, to_ref, sum_ref in (
        (qr_ref, qg_ref, dq_ref, gq_ref, gqg_ref),
        (kr_ref, kg_ref, dk_ref, gk_ref, gkg_ref),
    ):
        raw, grad = raw_ref[...], grad_ref[...]
        inverse = lax.rsqrt(jnp.mean(raw * raw, axis=1, keepdims=True) + 1e-06)
        hat = raw * inverse
        up = grad * gain_ref[...]
        mean = jnp.mean(up * hat, axis=1, keepdims=True)
        to_ref[...] = (inverse * (up - hat * mean)).astype(BF16)
        sum_ref[0] = jnp.sum(grad * hat, axis=0, keepdims=True)


def attend_back(pieces, queries, keys, values, grads, logs, query_raw, key_raw, query_gain, key_gain, scale):
    tokens, columns = queries.shape
    sequences, heads = tokens // LENGTH, columns // HD
    block = pl.BlockSpec((LENGTH, HD), lambda s, h, pieces: (s, h))
    gain = pl.BlockSpec((1, HD), lambda s, h, pieces: (0, h))
    sums = pl.BlockSpec((1, 1, HD), lambda s, h, pieces: (s, 0, h))
    return pl.pallas_call(
        partial(attend_back_kernel, scale),
        grid_spec=pltpu.PrefetchScalarGridSpec(
            num_scalar_prefetch=1,
            grid=(sequences, heads),
            in_specs=[block] * 4
            + [pl.BlockSpec((1, LENGTH, 1), lambda s, h, pieces: (h, s, 0)), block, block, gain, gain],
            out_specs=[block, block, block, sums, sums],
            scratch_shapes=[pltpu.VMEM((LENGTH, HD), F32)] * 3,
        ),
        out_shape=[jax.ShapeDtypeStruct((tokens, columns), BF16)] * 3
        + [jax.ShapeDtypeStruct((sequences, 1, columns), F32)] * 2,
        compiler_params=pltpu.CompilerParams(vmem_limit_bytes=VMEM),
        cost_estimate=pl.CostEstimate(
            flops=10 * tokens * LENGTH * columns,
            bytes_accessed=22 * tokens * columns,
            transcendentals=tokens * heads * LENGTH,
        ),
        name="attend_back",
    )(
        pieces, queries, keys, values, grads, logs, query_raw, key_raw,
        query_gain.reshape(1, -1), key_gain.reshape(1, -1),
    )


def expert_steps(slots):
    steps = [("cot", 0), ("cot", 1), ("row", 0)]
    for k in range(slots):
        steps.append(("expert", k))
        if k + 2 < slots:
            steps.append(("cot", k + 2))
        if k + 1 < slots:
            steps.append(("row", k + 1))
        steps.append(("place", k))
    return steps


def transfers_due(kind, k, cots, rows, terms):
    if not is_cube():
        return []
    at = {"z": (0, 0), "y": (0, 1), "x": (1, 0), "d": (1, 1)}
    due = DUE.get((kind, k), "").split()
    found = []
    for name in due:
        if name[0] == "e":
            found.extend(terms[int(name[2])][int(name[1])])
        else:
            b, y = at[name[1]]
            found.append((cots if name[0] == "c" else rows)[int(name[2])][b][y])
    return found


def per_device(
    inputs,
    attn_gain,
    w_query,
    w_key,
    w_value,
    w_output,
    query_gain,
    key_gain,
    moe_gain,
    w_router,
    w_gate,
    w_up,
    w_down,
    routes,
    piece_start,
    piece_length,
    clip_threshold,
    cotangent,
):
    tokens_here, width = inputs.shape
    slice_width = cotangent.shape[1]
    owner = lax.axis_index("expert")
    column = lax.axis_index("tensor") * slice_width
    heads_here = query_gain.shape[0] // HD
    experts_here = w_gate.shape[0]
    owners = lax.axis_size("expert")
    sequences = tokens_here // LENGTH
    scale = 1.0 / math.sqrt(HD)
    where = slot_blocks()
    slots = len(where)
    slices = lax.axis_size("tensor") // 2

    def own_columns(value):
        return lax.dynamic_slice_in_dim(value, column, slice_width, value.ndim - 1)

    all_routes = lax.all_to_all(
        jnp.broadcast_to(routes.T[None], (owners, TOP, tokens_here)),
        "expert",
        split_axis=0,
        concat_axis=0,
        tiled=True,
    )
    cot_slots = gather_slots(cotangent.astype(BF16))

    held_ids = owner * experts_here + jnp.arange(experts_here, dtype=jnp.int32)
    chosen = jnp.any(all_routes[:, None] == held_ids[None, :, None, None], axis=2)
    places = jnp.arange(tokens_here, dtype=jnp.int32)
    before = (places[:, None] < places[None, :]).astype(BF16)
    earlier = jnp.einsum(
        "set,tu->seu", chosen.astype(BF16), before, preferred_element_type=F32
    ).astype(jnp.int32)
    pos = jnp.where(chosen, earlier, -1)
    at = jnp.where(
        chosen, earlier + jnp.arange(experts_here, dtype=jnp.int32)[None, :, None] * CAP, -1
    ).transpose(0, 2, 1)

    order = tensor_order()
    output_pieces = [lax.dynamic_slice_in_dim(w_output, o * slice_width, slice_width, 1) for o in order]
    inputs_f = inputs.astype(F32)
    attn_inv = lax.rsqrt(jnp.mean(inputs_f * inputs_f, axis=-1, keepdims=True) + 1e-05)
    normed_a = (inputs_f * attn_inv * attn_gain).astype(BF16)
    query_raw, key_raw, queries, keys, values = project(
        normed_a, w_query, w_key, w_value, query_gain, key_gain
    )
    pieces = jnp.concatenate([piece_start, piece_length], axis=1).reshape(-1)
    attended, logs, tops = attend(pieces, queries, keys, values, scale)
    head_top = lax.pmax(
        jnp.max(tops[:, 0, 0].reshape(sequences, heads_here), axis=0), "expert"
    )
    attended = after(attended, *transfers_due("attended", 0, cot_slots, None, None))
    branch = tensor_scatter(partial(matmul, attended), output_pieces)
    first_cot = pick_rows(after(where[0], attended), pos, cot_slots[0])
    branch = after(branch, first_cot, *transfers_due("branch", 0, cot_slots, None, None))
    residual = own_columns(inputs).astype(F32) + branch
    gain_slice = own_columns(moe_gain)
    router_slice = lax.dynamic_slice_in_dim(w_router, column, slice_width, 0)
    lifted = residual * gain_slice
    row_sums = tensor_sum(
        jnp.concatenate(
            [
                lax.dot_general(
                    router_slice,
                    lifted.astype(BF16),
                    (((0,), (1,)), ((), ())),
                    preferred_element_type=F32,
                ),
                jnp.sum(residual * residual, axis=1)[None],
            ],
            axis=0,
        )
    )
    moe_inv_row = lax.rsqrt(row_sums[E] / width + 1e-05)
    moe_inv = moe_inv_row[:, None]
    normed_m = (lifted * moe_inv).astype(BF16)
    normed_m = after(normed_m, *transfers_due("normed", 0, cot_slots, None, None))

    normed_slots = gather_slots(normed_m)
    router = jax.nn.softmax(row_sums[:E] * moe_inv_row[None], axis=0)
    gate = lax.all_to_all(
        router.reshape(owners, experts_here, tokens_here),
        "expert",
        split_axis=0,
        concat_axis=0,
        tiled=True,
    )

    cots, rows, scaled, gate_grads, up_grads, probs, back = [], [], [], [], [], [], []
    terms = []
    last = first_cot
    for kind, k in expert_steps(slots):
        due = [last] + transfers_due(kind, k, cot_slots, normed_slots, terms)
        now = after(where[k], *due)
        if kind == "cot":
            last = pick_rows(now, pos, cot_slots[k]) if k else first_cot
            cots.append((last, core_swap(last)))
        elif kind == "row":
            last = pick_rows(now, pos, normed_slots[k])
            rows.append((last, core_swap(last)))
        elif kind == "expert":
            kept, gate_grad, up_grad, prob, keep, give = expert_slot(
                now, pos, gate, rows[k], cots[k], w_gate, w_up, w_down
            )
            last = kept
            scaled.append(kept)
            gate_grads.append(gate_grad)
            up_grads.append(up_grad)
            probs.append(prob)
            back.append((keep, core_swap(give)))
        else:
            placed = place_rows([now], at, *back[k])
            last = placed[0][0]
            back[k] = [[a[0] for a in b] for b in placed]
            if is_cube():
                term, first, second = scatter_plane(back[k], k % 2)
                if k:
                    term = send(term.astype(BF16), dz=k).astype(F32)
                terms.append((term, first, second))
    expert_path = sum(t[0] for t in terms) if is_cube() else scatter_all(back)

    prob_grads = jnp.stack([probs[k][:, b] for k in range(slots) for b in range(NB)])
    if is_cube():
        prob_grads = prob_grads[jnp.arange(owners, dtype=jnp.int32) ^ owner]
    prob_grads = lax.all_to_all(prob_grads, "expert", split_axis=0, concat_axis=0, tiled=True)
    prob_grads = tensor_sum(prob_grads.reshape(E, tokens_here))
    grad_logits = (
        router * (prob_grads - jnp.sum(router * prob_grads, axis=0, keepdims=True))
    ).astype(BF16)
    grad_router = lax.dot_general(
        normed_m, grad_logits, (((0,), (1,)), ((), ())), preferred_element_type=F32
    )
    router_path = lax.dot_general(
        grad_logits, router_slice, (((0,), (1,)), ((), ())), preferred_element_type=F32
    )
    grad_normed = expert_path + router_path
    moe_hat = residual * moe_inv
    grad_moe_gain = jnp.sum(grad_normed * moe_hat, axis=0)
    upstream = grad_normed * gain_slice
    mean_dot = tensor_sum(jnp.sum(upstream * moe_hat, axis=-1).reshape(8, -1)).reshape(-1, 1) / width
    grad_residual = cotangent + moe_inv * (upstream - moe_hat * mean_dot)
    branch_pieces = tensor_gather(grad_residual.astype(BF16))
    grad_branch = jnp.concatenate(branch_pieces, axis=1)

    pairs = []
    for k in range(0, slots, 2):
        now = after(where[0], last)
        keep, give = down_slots(now, scaled[k : k + 2], w_down, slices)
        last = keep
        pairs.append((keep, core_swap(give)))
    for i, pair in enumerate(pairs):
        now = after(where[2 * i], branch_pieces[0]) if i else after(where[0], last)
        placed = place_rows([now, where[2 * i + 1]], at, *pair)
        last = placed[0][0]
        if is_cube():
            placed = [[after(a, branch_pieces[1]) for a in b] for b in placed]
        pairs[i] = placed
    mixture = scatter_pairs(pairs)
    out = residual + mixture
    grad_output = matmul_tn(attended, grad_branch)
    grad_attended = matmul_nt(grad_branch, jnp.concatenate(output_pieces, axis=1)).astype(BF16)
    grad_query_raw, grad_key_raw, grad_v, grad_query_gain, grad_key_gain = attend_back(
        pieces, queries, keys, values, grad_attended, logs, query_raw, key_raw, query_gain, key_gain, scale
    )
    grad_query = matmul_tn(normed_a, grad_query_raw)
    grad_key = matmul_tn(normed_a, grad_key_raw)
    grad_value = matmul_tn(normed_a, grad_v)
    grad_gate, grad_up = weight_grads(
        weight_kernel, after(where[0], grad_value), rows, gate_grads + up_grads, [w_gate.shape[1:]] * 2, "weight_grads"
    )
    (grad_down,) = weight_grads(
        weight_down_kernel, after(where[0], grad_gate), cots, scaled, [w_down.shape[1:]], "weight_down_grads"
    )
    grad_raw = jnp.concatenate([grad_query_raw, grad_key_raw, grad_v], axis=1)
    weights = jnp.concatenate([w_query, w_key, w_value], axis=1)
    weight_pieces = [lax.dynamic_slice_in_dim(weights, o * slice_width, slice_width, 0) for o in order]
    grad_normed_a = tensor_scatter(partial(matmul_nt, grad_raw), weight_pieces)
    attn_hat = own_columns(inputs).astype(F32) * attn_inv
    upstream = grad_normed_a * own_columns(attn_gain)
    grad_attn_gain = jnp.sum(grad_normed_a * attn_hat, axis=0)
    mean_dot = tensor_sum(jnp.sum(upstream * attn_hat, axis=-1).reshape(8, -1)).reshape(-1, 1) / width
    grad_input = grad_residual + attn_inv * (upstream - attn_hat * mean_dot)

    def total(*values):
        return [lax.psum(v.astype(BF16), "expert").astype(F32) for v in values]

    sum_output, sum_moe_gain, sum_router = total(grad_output, grad_moe_gain, grad_router)
    grad_query = after(grad_query, sum_output)
    sum_query, sum_key, sum_value, sum_query_gain, sum_key_gain, sum_attn_gain = total(
        grad_query,
        grad_key,
        grad_value,
        jnp.sum(grad_query_gain, axis=(0, 1)),
        jnp.sum(grad_key_gain, axis=(0, 1)),
        grad_attn_gain,
    )
    sum_attn_gain = lax.all_gather(sum_attn_gain, "tensor", tiled=True)
    sum_router = lax.all_gather(sum_router, "tensor", tiled=True)
    ordered = jnp.zeros_like(sum_output)
    for i, o in enumerate(order):
        ordered = lax.dynamic_update_slice_in_dim(
            ordered, sum_output[:, i * slice_width : (i + 1) * slice_width], o * slice_width, 1
        )
    factor = clip_threshold / jnp.maximum(head_top, clip_threshold)
    spread = jnp.repeat(jnp.sqrt(factor), HD)
    query_clipped = (w_query.astype(F32) * spread[None, :]).astype(BF16)
    key_clipped = (w_key.astype(F32) * spread[None, :]).astype(BF16)
    return (
        out,
        grad_input,
        sum_attn_gain,
        sum_query,
        sum_key,
        sum_value,
        ordered,
        sum_query_gain,
        sum_key_gain,
        sum_moe_gain,
        sum_router,
        grad_gate,
        grad_up,
        grad_down,
        head_top,
        query_clipped,
        key_clipped,
    )


def solution(mesh):
    return jax.shard_map(
        per_device,
        mesh=mesh,
        in_specs=(
            P("expert", None),
            P(),
            P(None, "tensor"),
            P(None, "tensor"),
            P(None, "tensor"),
            P("tensor", None),
            P("tensor"),
            P("tensor"),
            P(),
            P(),
            P("expert", None, "tensor"),
            P("expert", None, "tensor"),
            P("expert", "tensor", None),
            P("expert", None),
            P("expert", None),
            P("expert", None),
            P("tensor"),
            P("expert", "tensor"),
        ),
        out_specs=(
            P("expert", "tensor"),
            P("expert", "tensor"),
            P(),
            P(None, "tensor"),
            P(None, "tensor"),
            P(None, "tensor"),
            P("tensor", None),
            P("tensor"),
            P("tensor"),
            P("tensor"),
            P(),
            P("expert", None, "tensor"),
            P("expert", None, "tensor"),
            P("expert", "tensor", None),
            P("tensor"),
            P(None, "tensor"),
            P(None, "tensor"),
        ),
        check_vma=False,
    )
```

time: 1750 us -> 1500 us (0.86)
  local copies, waits for them, and re-layouts: 124 us -> 37.1 us
  matrix products: 140 us -> 66.9 us
  other arithmetic: 147 us -> 84.2 us
  waiting for transfers between devices: 695 us -> 650 us
  Pallas kernels: 418 us -> 443 us
    psum x3 -> x2, waiting for transfers between devices: 150 us -> 5.14 us  [total(): return [lax.psum(v.astype(BF16), 'expert').astype(F32) for v in values]]
    ppermute x103 -> x84, waiting for transfers between devices: 545 us -> 620 us  [send(): return lax.ppermute(value, BOTH, flip(dz, dx, dy, dc))]
    dot_general x15 -> x1, matrix products: 63.6 us -> 0.45 us  [per_device(): lax.dot_general(router_slice, lifted.astype(BF16), (((0,), (1,)), ((), ()...]
    psum x1, blocking collectives: 19.1 us -> 73.7 us  [total(): return [lax.psum(v.astype(BF16), 'expert').astype(F32) for v in values]]
    slice x40 -> x1, local copies, waits for them, and re-layouts: 53.7 us -> 0.83 us  [per_device(): tops[:, 0, 0].reshape(sequences, heads_here)]
    all_gather x1 -> x2, blocking collectives: 50 us -> 12.4 us  [the longest x1 7.2 us: per_device(): sum_router = lax.all_gather(sum_router, 'tensor', tiled=True)]
    all_to_all x0 -> x1, waiting for transfers between devices: none -> 25 us  [per_device(): lax.all_to_all(jnp.broadcast_to(routes.T[None], (owners, TOP, tokens_here...]
    pallas_call x13, Pallas kernels: 225 us -> 250 us  [the longest x6 106 us: place_rows(): pl.pallas_call(partial(place_kernel, slices, held, slots), grid_spec=pltp...]
  transfers between devices with their start and end apart: 108 -> 89, of which waited for: 36 -> 36; matrix products, arithmetic and copies ran while one was open for 19% -> 11% of each run, Pallas kernels for 24% -> 27%
where the time goes in v2:
time: 1500 us; the launch traced here: 1490 us
  waiting for transfers between devices  650 us (43%)
  Pallas kernels  443 us (30%)
  blocking collectives  101 us (7%)
  starting transfers between devices  88.7 us (6%)
  other arithmetic  84.2 us (6%)
  matrix products  66.9 us (4%)
  local copies, waits for them, and re-layouts  37.1 us (2%)
  between operations  15.3 us (1%)
    ppermute x84, waiting for transfers between devices, send(): return lax.ppermute(value, BOTH, flip(dz, dx, dy, dc))  620 us
    pallas_call x4, Pallas kernels, expert_slot(): pl.pallas_call(partial(expert_kernel, slices), grid_spec=pltpu.PrefetchSc...  112 us
    pallas_call x6, Pallas kernels, place_rows(): pl.pallas_call(partial(place_kernel, slices, held, slots), grid_spec=pltp...  106 us
    pallas_call x8, Pallas kernels, pick_rows(): pl.pallas_call(partial(pick_kernel, group, slices), grid_spec=pltpu.Prefe...  81.8 us
    psum x1, blocking collectives, total(): return [lax.psum(v.astype(BF16), 'expert').astype(F32) for v in values]  73.7 us
    pallas_call x2, Pallas kernels, weight_grads(): pl.pallas_call(partial(kernel, slots, slices), grid_spec=pltpu.PrefetchSc...  71.2 us
    ppermute x84, starting transfers between devices, send(): return lax.ppermute(value, BOTH, flip(dz, dx, dy, dc))  69.1 us
    pallas_call x2, Pallas kernels, down_slots(): pl.pallas_call(partial(down_kernel, slices, slots), grid_spec=pltpu.Prefe...  31.6 us
  transfers between devices with their start and end apart: 89, of which 36 were waited for; matrix products, arithmetic and copies ran while one was open for 11% of the time, Pallas kernels for 27%

profile of v2, /device:TPU:10, one launch (start us, length us, event | category | flops | bytes accessed | tf_op | source)
XLA Modules:
  0.0 1487.0 jit_solution(8844757527913253907)
XLA Ops:
  62.2 25.0 %all-to-all-done = s32[8,8,1024]{2,1,0:T(8,128)S(1)} async-done(((s32[8,8,1024]{2,1,0:T(8,128)}), s32[8,8,1024]{2,1,0:T(8,128)S(1)}, u32[]{:S(2)}, u32[]{:S(2)}) %all-to-all-start) | async-done | bytes 262176 | tf_op jit(solution)/shard_map/all_to_all | solution.py:721
  148.4 28.1 %collective-permute-done.12 = f32[65,1024]{1,0:T(8,128)S(1)} collective-permute-done((f32[65,1024]{1,0:T(8,128)S(1)}, f32[65,1024]{1,0:T(8,128)S(1)}, u32[]{:S(2)}, u32[]{:S(2)}) %collective-permute-start.12) | collective-permute-done | bytes 266272 | tf_op jit(solution)/shard_map/ppermute | solution.py:73
  206.9 21.6 %collective-permute-done.17.refs_5_ = bf16[1024,512]{1,0:T(8,128)(2,1)} collective-permute-done((bf16[1024,512]{1,0:T(8,128)(2,1)}, bf16[1024,512]{1,0:T(8,128)(2,1)}, u32[]{:S(2)}, u32[]{:S(2)}) %collective-permute-start.17) | collective-permute-done | bytes 1048608 | tf_op jit(solution)/shard_map/ppermute | solution.py:73
  270.6 17.4 %collective-permute-done.23.refs_5_ = bf16[1024,512]{1,0:T(8,128)(2,1)} collective-permute-done((bf16[1024,512]{1,0:T(8,128)(2,1)}, bf16[1024,512]{1,0:T(8,128)(2,1)}, u32[]{:S(2)}, u32[]{:S(2)}) %collective-permute-start.23) | collective-permute-done | bytes 1048608 | tf_op jit(solution)/shard_map/ppermute | solution.py:73
  288.0 22.4 %collective-permute-done.21.refs_4_ = bf16[1024,512]{1,0:T(8,128)(2,1)} collective-permute-done((bf16[1024,512]{1,0:T(8,128)(2,1)}, bf16[1024,512]{1,0:T(8,128)(2,1)}, u32[]{:S(2)}, u32[]{:S(2)}) %collective-permute-start.21) | collective-permute-done | bytes 1048608 | tf_op jit(solution)/shard_map/ppermute | solution.py:73
  311.9 27.8 %expert_slot.4 = (bf16[8,320,256]{2,1,0:T(8,128)(2,1)}, bf16[8,320,256]{2,1,0:T(8,128)(2,1)}, bf16[8,320,256]{2,1,0:T(8,128)(2,1)}, f32[8,2,1024]{2,1,0:T(2,128)...) custom-call(s32[6]{0:T(128)} %stack.69.where_ref, s32[8,8,1024]{2,1,0:T(8,128)} %copy.152.refs_0_.refs_1_, ...), custom_call_target="tpu_custom_call" | custom-call | flops 13421772800 | bytes 56623104 | tf_op jit(solution)/shard_map/expert_slot/pallas_call | solution.py:310
  363.2 22.9 %collective-permute-done.28.refs_4_ = bf16[1024,512]{1,0:T(8,128)(2,1)} collective-permute-done((bf16[1024,512]{1,0:T(8,128)(2,1)}, bf16[1024,512]{1,0:T(8,128)(2,1)}, u32[]{:S(2)}, u32[]{:S(2)}) %collective-permute-start.28) | collective-permute-done | bytes 1048608 | tf_op jit(solution)/shard_map/ppermute | solution.py:73
  393.8 16.2 %collective-permute-done.29.refs_2_ = bf16[1024,512]{1,0:T(8,128)(2,1)} collective-permute-done((bf16[1024,512]{1,0:T(8,128)(2,1)}, bf16[1024,512]{1,0:T(8,128)(2,1)}, u32[]{:S(2)}, u32[]{:S(2)}) %collective-permute-start.29) | collective-permute-done | bytes 1048608 | tf_op jit(solution)/shard_map/ppermute | solution.py:73
  427.9 28.0 %expert_slot.5 = (bf16[8,320,256]{2,1,0:T(8,128)(2,1)}, bf16[8,320,256]{2,1,0:T(8,128)(2,1)}, bf16[8,320,256]{2,1,0:T(8,128)(2,1)}, f32[8,2,1024]{2,1,0:T(2,128)...) custom-call(s32[6]{0:T(128)} %stack.78.where_ref, s32[8,8,1024]{2,1,0:T(8,128)} %copy.152.refs_0_.refs_1_, ...), custom_call_target="tpu_custom_call" | custom-call | flops 13421772800 | bytes 56623104 | tf_op jit(solution)/shard_map/expert_slot/pallas_call | solution.py:310
  484.2 24.2 %collective-permute-done.38 = bf16[1024,512]{1,0:T(8,128)(2,1)} collective-permute-done((bf16[1024,512]{1,0:T(8,128)(2,1)}, bf16[1024,512]{1,0:T(8,128)(2,1)}, u32[]{:S(2)}, u32[]{:S(2)}) %collective-permute-start.38) | collective-permute-done | bytes 1048608 | tf_op jit(solution)/shard_map/ppermute | solution.py:73
  510.0 20.6 %collective-permute-done.39 = bf16[1024,512]{1,0:T(8,128)(2,1)} collective-permute-done((bf16[1024,512]{1,0:T(8,128)(2,1)}, bf16[1024,512]{1,0:T(8,128)(2,1)}, u32[]{:S(2)}, u32[]{:S(2)}) %collective-permute-start.39) | collective-permute-done | bytes 1048608 | tf_op jit(solution)/shard_map/ppermute | solution.py:73
  545.9 27.8 %expert_slot.6 = (bf16[8,320,256]{2,1,0:T(8,128)(2,1)}, bf16[8,320,256]{2,1,0:T(8,128)(2,1)}, bf16[8,320,256]{2,1,0:T(8,128)(2,1)}, f32[8,2,1024]{2,1,0:T(2,128)...) custom-call(s32[6]{0:T(128)} %stack.75.where_ref, s32[8,8,1024]{2,1,0:T(8,128)} %copy.152.refs_0_.refs_1_, ...), custom_call_target="tpu_custom_call" | custom-call | flops 13421772800 | bytes 56623104 | tf_op jit(solution)/shard_map/expert_slot/pallas_call | solution.py:310
  586.9 24.3 %collective-permute-done.45 = bf16[1024,512]{1,0:T(8,128)(2,1)} collective-permute-done((bf16[1024,512]{1,0:T(8,128)(2,1)}, bf16[1024,512]{1,0:T(8,128)(2,1)}, u32[]{:S(2)}, u32[]{:S(2)}) %collective-permute-start.45) | collective-permute-done | bytes 1048608 | tf_op jit(solution)/shard_map/ppermute | solution.py:73
  611.2 22.0 %collective-permute-done.46 = bf16[1024,512]{1,0:T(8,128)(2,1)} collective-permute-done((bf16[1024,512]{1,0:T(8,128)(2,1)}, bf16[1024,512]{1,0:T(8,128)(2,1)}, u32[]{:S(2)}, u32[]{:S(2)}) %collective-permute-start.46) | collective-permute-done | bytes 1048608 | tf_op jit(solution)/shard_map/ppermute | solution.py:73
  647.1 27.9 %expert_slot.7 = (bf16[8,320,256]{2,1,0:T(8,128)(2,1)}, bf16[8,320,256]{2,1,0:T(8,128)(2,1)}, bf16[8,320,256]{2,1,0:T(8,128)(2,1)}, f32[8,2,1024]{2,1,0:T(2,128)...) custom-call(s32[6]{0:T(128)} %stack.72.where_ref, s32[8,8,1024]{2,1,0:T(8,128)} %copy.152.refs_0_.refs_1_, ...), custom_call_target="tpu_custom_call" | custom-call | flops 13421772800 | bytes 56623104 | tf_op jit(solution)/shard_map/expert_slot/pallas_call | solution.py:310
  677.3 24.1 %collective-permute-done.50 = bf16[1024,512]{1,0:T(8,128)(2,1)} collective-permute-done((bf16[1024,512]{1,0:T(8,128)(2,1)}, bf16[1024,512]{1,0:T(8,128)(2,1)}, u32[]{:S(2)}, u32[]{:S(2)}) %collective-permute-start.50) | collective-permute-done | bytes 1048608 | tf_op jit(solution)/shard_map/ppermute | solution.py:73
  701.4 22.0 %collective-permute-done.51 = bf16[1024,512]{1,0:T(8,128)(2,1)} collective-permute-done((bf16[1024,512]{1,0:T(8,128)(2,1)}, bf16[1024,512]{1,0:T(8,128)(2,1)}, u32[]{:S(2)}, u32[]{:S(2)}) %collective-permute-start.51) | collective-permute-done | bytes 1048608 | tf_op jit(solution)/shard_map/ppermute | solution.py:73
  753.7 15.9 %down_slots.3 = (bf16[4,2,1280,512]{3,2,1,0:T(8,128)(2,1)}, bf16[4,2,1280,512]{3,2,1,0:T(8,128)(2,1)}) custom-call(s32[6]{0:T(128)} %stack.69.where_ref, bf16[8,320,256]{2,1,0:T(8,128)(2,1)} %get-tuple-element.147.refs_0_.refs_10_, bf16[8,320,256]{2,1,0:T(8,128)(2,1)} %get-tuple-element.156.refs_1_.refs_11_, bf16[8,256,2048]{2,1,0:T(8,128)(2,1)} %refs_2_.3), custom_call_target="tpu_custom_call" | custom-call | flops 5368709120 | bytes 29360128 | tf_op jit(solution)/shard_map/down_slots/pallas_call | solution.py:350
  812.0 19.9 %collective-permute-done.61 = bf16[1024,512]{1,0:T(8,128)(2,1)} collective-permute-done((bf16[1024,512]{1,0:T(8,128)(2,1)}, bf16[1024,512]{1,0:T(8,128)(2,1)}, u32[]{:S(2)}, u32[]{:S(2)}) %collective-permute-start.61) | collective-permute-done | bytes 1048608 | tf_op jit(solution)/shard_map/ppermute | solution.py:73
  837.8 20.8 %collective-permute-done.64 = f32[64,1024]{1,0:T(8,128)S(1)} collective-permute-done((f32[64,1024]{1,0:T(8,128)S(1)}, f32[64,1024]{1,0:T(8,128)S(1)}, u32[]{:S(2)}, u32[]{:S(2)}) %collective-permute-start.64) | collective-permute-done | bytes 262176 | tf_op jit(solution)/shard_map/ppermute | solution.py:73
  860.3 40.2 %collective-permute-done.58 = bf16[1024,512]{1,0:T(8,128)(2,1)S(1)} collective-permute-done((bf16[1024,512]{1,0:T(8,128)(2,1)S(1)}, bf16[1024,512]{1,0:T(8,128)(2,1)S(1)}, u32[]{:S(2)}, u32[]{:S(2)}) %collective-permute-start.58) | collective-permute-done | bytes 1048608 | tf_op jit(solution)/shard_map/ppermute | solution.py:73
  900.5 22.6 %collective-permute-done.62 = bf16[1024,512]{1,0:T(8,128)(2,1)S(1)} collective-permute-done((bf16[1024,512]{1,0:T(8,128)(2,1)S(1)}, bf16[1024,512]{1,0:T(8,128)(2,1)S(1)}, u32[]{:S(2)}, u32[]{:S(2)}) %collective-permute-start.62) | collective-permute-done | bytes 1048608 | tf_op jit(solution)/shard_map/ppermute | solution.py:73
  955.2 16.8 %collective-permute-done.67 = bf16[1024,512]{1,0:T(8,128)(2,1)S(1)} collective-permute-done((bf16[1024,512]{1,0:T(8,128)(2,1)S(1)}, bf16[1024,512]{1,0:T(8,128)(2,1)S(1)}, u32[]{:S(2)}, u32[]{:S(2)}) %collective-permute-start.67) | collective-permute-done | bytes 1048608 | tf_op jit(solution)/shard_map/ppermute | solution.py:73
  981.9 16.0 %attend_back.1 = (bf16[1024,512]{1,0:T(8,128)(2,1)}, bf16[1024,512]{1,0:T(8,128)(2,1)}, bf16[1024,512]{1,0:T(8,128)(2,1)}, f32[1,1,512]{2,1,0:T(1,128)}, f32[1,1,512]{2,1,0:T(1,128)}) custom-call(s32[4]{0:T(128)} %add_bitcast_fusion.pieces_ref, bf16[1024,512]{1,0:T(8,128)(2,1)} %get-tuple-element.118.q_ref, bf16[1024,512]{1,0:T(8,128)(2,1)} %get-tuple-element.119.k_ref, ...), custom_call_target="tpu_custom_call" | custom-call | flops 5368709120 | bytes 11534336 | tf_op jit(solution)/shard_map/attend_back/pallas_call | solution.py:633
  1009.2 25.2 %place_rows.11 = (bf16[2,1024,512]{2,1,0:T(8,128)(2,1)}, bf16[2,1024,512]{2,1,0:T(8,128)(2,1)}, bf16[2,1024,512]{2,1,0:T(8,128)(2,1)}, bf16[2,1024,512]{2,1,0:T(8,128)(2,1)}) custom-call(s32[4]{0:T(128)} %pad_add_fusion.1.where_ref, s32[8,1024,8]{2,1,0:T(8,128)} %bitcast.142, s32[8,1024,8]{2,1,0:T(8,128)} %bitcast.143, s32[8,1024,8]{2,1,0:T(8,128)} %bitcast.144, ...), custom_call_target="tpu_custom_call" | custom-call | flops 10737418240 | bytes 29360128 | tf_op jit(solution)/shard_map/place_rows/pallas_call | solution.py:409
  1035.0 42.7 %weight_grads.1 = (f32[8,2048,256]{2,1,0:T(8,128)}, f32[8,2048,256]{2,1,0:T(8,128)}) custom-call(s32[6]{0:T(128)} %stack.69.where_ref, bf16[2,2,1280,512]{3,2,1,0:T(8,128)(2,1)} %pick_rows.10.refs_4_.refs_0_, bf16[2,2,1280,512]{3,2,1,0:T(8,128)(2,1)} %collective-permute-done.24.refs_5_.refs_1_, bf16[2,2,1280,512]{3,2,1,0:T(8,128)(2,1)} %pick_rows.12.refs_4_.refs_2_, ...), custom_call_target="tpu_custom_call" | custom-call | flops 21474836480 | bytes 75497472 | tf_op jit(solution)/shard_map/weight_grads/pallas_call | solution.py:466
  1087.9 25.3 %place_rows.10 = (bf16[2,1024,512]{2,1,0:T(8,128)(2,1)}, bf16[2,1024,512]{2,1,0:T(8,128)(2,1)}, bf16[2,1024,512]{2,1,0:T(8,128)(2,1)}, bf16[2,1024,512]{2,1,0:T(8,128)(2,1)}) custom-call(s32[4]{0:T(128)} %pad_add_fusion.where_ref, s32[8,1024,8]{2,1,0:T(8,128)} %bitcast.146, s32[8,1024,8]{2,1,0:T(8,128)} %bitcast.147, s32[8,1024,8]{2,1,0:T(8,128)} %bitcast.148, ...), custom_call_target="tpu_custom_call" | custom-call | flops 10737418240 | bytes 29360128 | tf_op jit(solution)/shard_map/place_rows/pallas_call | solution.py:409
  1146.2 27.4 %collective-permute-done.69 = bf16[2,1024,512]{2,1,0:T(8,128)(2,1)} collective-permute-done((bf16[2,1024,512]{2,1,0:T(8,128)(2,1)}, bf16[2,1024,512]{2,1,0:T(8,128)(2,1)}, u32[]{:S(2)}, u32[]{:S(2)}) %collective-permute-start.69) | collective-permute-done | bytes 2097184 | tf_op jit(solution)/shard_map/ppermute | solution.py:73
  1180.5 54.5 %collective-permute-done.73 = bf16[2,1024,512]{2,1,0:T(8,128)(2,1)} collective-permute-done((bf16[2,1024,512]{2,1,0:T(8,128)(2,1)}, bf16[2,1024,512]{2,1,0:T(8,128)(2,1)}, u32[]{:S(2)}, u32[]{:S(2)}) %collective-permute-start.73) | collective-permute-done | bytes 2097184 | tf_op jit(solution)/shard_map/ppermute | solution.py:73
  1241.8 28.5 %weight_down_grads.1 = f32[8,256,2048]{2,1,0:T(8,128)} custom-call(s32[6]{0:T(128)} %stack.69.where_ref, bf16[2,2,1280,512]{3,2,1,0:T(8,128)(2,1)} %pick_rows.8.refs_6_.refs_0_, bf16[2,2,1280,512]{3,2,1,0:T(8,128)(2,1)} %collective-permute-done.25.refs_7_.refs_1_, bf16[2,2,1280,512]{3,2,1,0:T(8,128)(2,1)} %pick_rows.9.refs_6_.refs_2_, ...), custom_call_target="tpu_custom_call" | custom-call | flops 10737418240 | bytes 58720256 | tf_op jit(solution)/shard_map/weight_down_grads/pallas_call | solution.py:466
  1285.8 70.0 %collective-permute-done.75 = bf16[2,1024,512]{2,1,0:T(8,128)(2,1)} collective-permute-done((bf16[2,1024,512]{2,1,0:T(8,128)(2,1)}, bf16[2,1024,512]{2,1,0:T(8,128)(2,1)}, u32[]{:S(2)}, u32[]{:S(2)}) %collective-permute-start.75) | collective-permute-done | bytes 2097184 | tf_op jit(solution)/shard_map/ppermute | solution.py:73
  1367.7 73.7 %all-reduce = (bf16[512]{0:T(512)(128)(2,1)S(1)}, bf16[512]{0:T(512)(128)(2,1)S(1)}, bf16[512]{0:T(512)(128)(2,1)S(1)}, bf16[512]{0:T(512)(128)(2,1)S(1)}) all-reduce(bf16[512]{0:T(512)(128)(2,1)S(1)} %get-tuple-element.219, bf16[512]{0:T(512)(128)(2,1)S(1)} %get-tuple-element.256, ...), channel_id=1, replica_groups=mesh['expert'=8,'tensor'=4] {'expert'}, use_global_device_ids=true, to_apply=%region_9.10 | all-reduce | flops 2048 | bytes 8192 | tf_op jit(solution)/shard_map/psum | solution.py:888
  (407 shorter events, 569.9 us)
Async XLA Ops:
  58.5 73.7 %collective-permute-start.7 = (bf16[1024,512]{1,0:T(8,128)(2,1)}, bf16[1024,512]{1,0:T(8,128)(2,1)}, u32[]{:S(2)}, u32[]{:S(2)}) collective-permute-start(bf16[1024,512]{1,0:T(8,128)(2,1)} %convert_element_type.309.refs_2_), channel_id=1, source_target_pairs={{0,16},{1,17},{2,18},{3,19},{4,20},{5,21},{6,22},{7,23},{8,24},{9,... | collective-permute-start | bytes 3145736 | tf_op jit(solution)/shard_map/ppermute | solution.py:73
  195.9 53.6 %collective-permute-start.18 = (bf16[1024,512]{1,0:T(8,128)(2,1)}, bf16[1024,512]{1,0:T(8,128)(2,1)}, u32[]{:S(2)}, u32[]{:S(2)}) collective-permute-start(bf16[1024,512]{1,0:T(8,128)(2,1)} %collective-permute-done.7.refs_2_), channel_id=1, source_target_pairs={{0,2},{1,3},{2,0},{3,1},{4,6},{5,7},{6,4},{7,5},{8,10},{9,11},{10,... | collective-permute-start | bytes 3145736 | tf_op jit(solution)/shard_map/ppermute | solution.py:73
  206.9 104.3 %collective-permute-start.25 = (bf16[2,2,1280,512]{3,2,1,0:T(8,128)(2,1)}, bf16[2,2,1280,512]{3,2,1,0:T(8,128)(2,1)}, u32[]{:S(2)}, u32[]{:S(2)}) collective-permute-start(bf16[2,2,1280,512]{3,2,1,0:T(8,128)(2,1)} %pick_rows.8.refs_6_.refs_0_), channel_id=1, source_target_pairs={{0,1},{1,0},{2,3},{3,2},{4,5},{5,4},{6,7},{7,6},{8,9},{9,8},{10,11... | collective-permute-start | bytes 15728648 | tf_op jit(solution)/shard_map/ppermute | solution.py:73
  259.6 51.6 %collective-permute-start.24 = (bf16[2,2,1280,512]{3,2,1,0:T(8,128)(2,1)}, bf16[2,2,1280,512]{3,2,1,0:T(8,128)(2,1)}, u32[]{:S(2)}, u32[]{:S(2)}) collective-permute-start(bf16[2,2,1280,512]{3,2,1,0:T(8,128)(2,1)} %pick_rows.10.refs_4_.refs_0_), channel_id=1, source_target_pairs={{0,1},{1,0},{2,3},{3,2},{4,5},{5,4},{6,7},{7,6},{8,9},{9,8},{10,11... | collective-permute-start | bytes 15728648 | tf_op jit(solution)/shard_map/ppermute | solution.py:73
  288.0 138.2 %collective-permute-start.33 = (bf16[2,2,1280,512]{3,2,1,0:T(8,128)(2,1)}, bf16[2,2,1280,512]{3,2,1,0:T(8,128)(2,1)}, u32[]{:S(2)}, u32[]{:S(2)}) collective-permute-start(bf16[2,2,1280,512]{3,2,1,0:T(8,128)(2,1)} %pick_rows.9.refs_6_.refs_2_), channel_id=1, source_target_pairs={{0,1},{1,0},{2,3},{3,2},{4,5},{5,4},{6,7},{7,6},{8,9},{9,8},{10,11... | collective-permute-start | bytes 15728648 | tf_op jit(solution)/shard_map/ppermute | solution.py:73
  339.7 71.8 %collective-permute-start.30 = (bf16[2,2,1280,512]{3,2,1,0:T(8,128)(2,1)}, bf16[2,2,1280,512]{3,2,1,0:T(8,128)(2,1)}, u32[]{:S(2)}, u32[]{:S(2)}) collective-permute-start(bf16[2,2,1280,512]{3,2,1,0:T(8,128)(2,1)} %get-tuple-element.134), channel_id=1, source_target_pairs={{0,1},{1,0},{2,3},{3,2},{4,5},{5,4},{6,7},{7,6},{8,9},{9,8},{10,11... | collective-permute-start | bytes 15728648 | tf_op jit(solution)/shard_map/ppermute | solution.py:73
  360.2 67.7 %collective-permute-start.32 = (bf16[2,2,1280,512]{3,2,1,0:T(8,128)(2,1)}, bf16[2,2,1280,512]{3,2,1,0:T(8,128)(2,1)}, u32[]{:S(2)}, u32[]{:S(2)}) collective-permute-start(bf16[2,2,1280,512]{3,2,1,0:T(8,128)(2,1)} %pick_rows.12.refs_4_.refs_2_), channel_id=1, source_target_pairs={{0,1},{1,0},{2,3},{3,2},{4,5},{5,4},{6,7},{7,6},{8,9},{9,8},{10,11... | collective-permute-start | bytes 15728648 | tf_op jit(solution)/shard_map/ppermute | solution.py:73
  427.9 118.0 %collective-permute-start.43 = (bf16[2,2,1280,512]{3,2,1,0:T(8,128)(2,1)}, bf16[2,2,1280,512]{3,2,1,0:T(8,128)(2,1)}, u32[]{:S(2)}, u32[]{:S(2)}) collective-permute-start(bf16[2,2,1280,512]{3,2,1,0:T(8,128)(2,1)} %pick_rows.11.refs_6_.refs_4_), channel_id=1, source_target_pairs={{0,1},{1,0},{2,3},{3,2},{4,5},{5,4},{6,7},{7,6},{8,9},{9,8},{10,11... | collective-permute-start | bytes 15728648 | tf_op jit(solution)/shard_map/ppermute | solution.py:73
  455.9 76.1 %collective-permute-start.40 = (bf16[2,2,1280,512]{3,2,1,0:T(8,128)(2,1)}, bf16[2,2,1280,512]{3,2,1,0:T(8,128)(2,1)}, u32[]{:S(2)}, u32[]{:S(2)}) collective-permute-start(bf16[2,2,1280,512]{3,2,1,0:T(8,128)(2,1)} %get-tuple-element.144), channel_id=1, source_target_pairs={{0,1},{1,0},{2,3},{3,2},{4,5},{5,4},{6,7},{7,6},{8,9},{9,8},{10,11... | collective-permute-start | bytes 15728648 | tf_op jit(solution)/shard_map/ppermute | solution.py:73
  482.2 63.7 %collective-permute-start.42 = (bf16[2,2,1280,512]{3,2,1,0:T(8,128)(2,1)}, bf16[2,2,1280,512]{3,2,1,0:T(8,128)(2,1)}, u32[]{:S(2)}, u32[]{:S(2)}) collective-permute-start(bf16[2,2,1280,512]{3,2,1,0:T(8,128)(2,1)} %pick_rows.14.refs_4_), channel_id=1, source_target_pairs={{0,1},{1,0},{2,3},{3,2},{4,5},{5,4},{6,7},{7,6},{8,9},{9,8},{10,11... | collective-permute-start | bytes 15728648 | tf_op jit(solution)/shard_map/ppermute | solution.py:73
  573.7 59.5 %collective-permute-start.47 = (bf16[2,2,1280,512]{3,2,1,0:T(8,128)(2,1)}, bf16[2,2,1280,512]{3,2,1,0:T(8,128)(2,1)}, u32[]{:S(2)}, u32[]{:S(2)}) collective-permute-start(bf16[2,2,1280,512]{3,2,1,0:T(8,128)(2,1)} %get-tuple-element.153), channel_id=1, source_target_pairs={{0,1},{1,0},{2,3},{3,2},{4,5},{5,4},{6,7},{7,6},{8,9},{9,8},{10,11... | collective-permute-start | bytes 15728648 | tf_op jit(solution)/shard_map/ppermute | solution.py:73
  573.8 73.2 %collective-permute-start.49 = (bf16[2,2,1280,512]{3,2,1,0:T(8,128)(2,1)}, bf16[2,2,1280,512]{3,2,1,0:T(8,128)(2,1)}, u32[]{:S(2)}, u32[]{:S(2)}) collective-permute-start(bf16[2,2,1280,512]{3,2,1,0:T(8,128)(2,1)} %pick_rows.13.refs_6_), channel_id=1, source_target_pairs={{0,1},{1,0},{2,3},{3,2},{4,5},{5,4},{6,7},{7,6},{8,9},{9,8},{10,11... | collective-permute-start | bytes 15728648 | tf_op jit(solution)/shard_map/ppermute | solution.py:73
  584.8 62.2 %collective-permute-start.48 = (bf16[2,2,1280,512]{3,2,1,0:T(8,128)(2,1)}, bf16[2,2,1280,512]{3,2,1,0:T(8,128)(2,1)}, u32[]{:S(2)}, u32[]{:S(2)}) collective-permute-start(bf16[2,2,1280,512]{3,2,1,0:T(8,128)(2,1)} %pick_rows.15.refs_4_.refs_6_), channel_id=1, source_target_pairs={{0,1},{1,0},{2,3},{3,2},{4,5},{5,4},{6,7},{7,6},{8,9},{9,8},{10,11... | collective-permute-start | bytes 15728648 | tf_op jit(solution)/shard_map/ppermute | solution.py:73
  769.6 239.6 %collective-permute-start.71 = (bf16[4,2,1280,512]{3,2,1,0:T(8,128)(2,1)}, bf16[4,2,1280,512]{3,2,1,0:T(8,128)(2,1)}, u32[]{:S(2)}, u32[]{:S(2)}) collective-permute-start(bf16[4,2,1280,512]{3,2,1,0:T(8,128)(2,1)} %get-tuple-element.188), channel_id=1, source_target_pairs={{0,1},{1,0},{2,3},{3,2},{4,5},{5,4},{6,7},{7,6},{8,9},{9,8},{10,11... | collective-permute-start | bytes 31457288 | tf_op jit(solution)/shard_map/ppermute | solution.py:73
  780.1 349.8 %all-reduce.5.cloned.1.call-start = ((), (), s32[]{:S(2)}) async-start(), calls=%async_computation.3 | async-start | bytes 4194304 | tf_op jit(solution)/shard_map/psum | solution.py:888
  803.9 56.3 %collective-permute-start.54 = (bf16[1024,512]{1,0:T(8,128)(2,1)S(1)}, bf16[1024,512]{1,0:T(8,128)(2,1)S(1)}, u32[]{:S(2)}, u32[]{:S(2)}) collective-permute-start(bf16[1024,512]{1,0:T(8,128)(2,1)S(1)} %copy-done.22), channel_id=1, source_target_pairs={{0,2},{1,3},{2,0},{3,1},{4,6},{5,7},{6,4},{7,5},{8,10},{9,11},{10,... | collective-permute-start | bytes 3145736 | tf_op jit(solution)/shard_map/ppermute | solution.py:73
  833.4 67.1 %collective-permute-start.58 = (bf16[1024,512]{1,0:T(8,128)(2,1)S(1)}, bf16[1024,512]{1,0:T(8,128)(2,1)S(1)}, u32[]{:S(2)}, u32[]{:S(2)}) collective-permute-start(bf16[1024,512]{1,0:T(8,128)(2,1)S(1)} %fusion.32), channel_id=1, source_target_pairs={{0,16},{1,17},{2,18},{3,19},{4,20},{5,21},{6,22},{7,23},{8,24},{9,... | collective-permute-start | bytes 3145736 | tf_op jit(solution)/shard_map/ppermute | solution.py:73
  858.5 64.6 %collective-permute-start.62 = (bf16[1024,512]{1,0:T(8,128)(2,1)S(1)}, bf16[1024,512]{1,0:T(8,128)(2,1)S(1)}, u32[]{:S(2)}, u32[]{:S(2)}) collective-permute-start(bf16[1024,512]{1,0:T(8,128)(2,1)S(1)} %fusion.29), channel_id=1, source_target_pairs={{0,24},{1,25},{2,26},{3,27},{4,28},{5,29},{6,30},{7,31},{8,16},{9,... | collective-permute-start | bytes 3145736 | tf_op jit(solution)/shard_map/ppermute | solution.py:73
  860.2 227.7 %collective-permute-start.53 = (bf16[4,2,1280,512]{3,2,1,0:T(8,128)(2,1)}, bf16[4,2,1280,512]{3,2,1,0:T(8,128)(2,1)}, u32[]{:S(2)}, u32[]{:S(2)}) collective-permute-start(bf16[4,2,1280,512]{3,2,1,0:T(8,128)(2,1)} %get-tuple-element.168), channel_id=1, source_target_pairs={{0,1},{1,0},{2,3},{3,2},{4,5},{5,4},{6,7},{7,6},{8,9},{9,8},{10,11... | collective-permute-start | bytes 31457288 | tf_op jit(solution)/shard_map/ppermute | solution.py:73
  1008.7 449.6 %all-reduce.7.cloned.1.call-start = ((), (), s32[]{:S(2)}) async-start(), calls=%async_computation.4 | async-start | bytes 12713984 | tf_op jit(solution)/shard_map/psum | solution.py:888
  1034.4 82.2 %collective-permute-start.72 = (bf16[2,1024,512]{2,1,0:T(8,128)(2,1)}, bf16[2,1024,512]{2,1,0:T(8,128)(2,1)}, u32[]{:S(2)}, u32[]{:S(2)}) collective-permute-start(bf16[2,1024,512]{2,1,0:T(8,128)(2,1)} %get-tuple-element.194), channel_id=1, source_target_pairs={{0,2},{1,3},{2,0},{3,1},{4,6},{5,7},{6,4},{7,5},{8,10},{9,11},{10,... | collective-permute-start | bytes 6291464 | tf_op jit(solution)/shard_map/ppermute | solution.py:73
  1113.1 60.5 %collective-permute-start.69 = (bf16[2,1024,512]{2,1,0:T(8,128)(2,1)}, bf16[2,1024,512]{2,1,0:T(8,128)(2,1)}, u32[]{:S(2)}, u32[]{:S(2)}) collective-permute-start(bf16[2,1024,512]{2,1,0:T(8,128)(2,1)} %get-tuple-element.186), channel_id=1, source_target_pairs={{0,4},{1,5},{2,6},{3,7},{4,0},{5,1},{6,2},{7,3},{8,12},{9,13},{10,... | collective-permute-start | bytes 6291464 | tf_op jit(solution)/shard_map/ppermute | solution.py:73
  1115.0 64.0 %collective-permute-start.74 = (bf16[2,1024,512]{2,1,0:T(8,128)(2,1)}, bf16[2,1024,512]{2,1,0:T(8,128)(2,1)}, u32[]{:S(2)}, u32[]{:S(2)}) collective-permute-start(bf16[2,1024,512]{2,1,0:T(8,128)(2,1)} %get-tuple-element.196), channel_id=1, source_target_pairs={{0,2},{1,3},{2,0},{3,1},{4,6},{5,7},{6,4},{7,5},{8,10},{9,11},{10,... | collective-permute-start | bytes 6291464 | tf_op jit(solution)/shard_map/ppermute | solution.py:73
  1120.7 114.4 %collective-permute-start.73 = (bf16[2,1024,512]{2,1,0:T(8,128)(2,1)}, bf16[2,1024,512]{2,1,0:T(8,128)(2,1)}, u32[]{:S(2)}, u32[]{:S(2)}) collective-permute-start(bf16[2,1024,512]{2,1,0:T(8,128)(2,1)} %add_convert_fusion.1), channel_id=1, source_target_pairs={{0,4},{1,5},{2,6},{3,7},{4,0},{5,1},{6,2},{7,3},{8,12},{9,13},{10,... | collective-permute-start | bytes 6291464 | tf_op jit(solution)/shard_map/ppermute | solution.py:73
  1139.2 131.2 %collective-permute-start.79 = (bf16[1024,512]{1,0:T(8,128)(2,1)}, bf16[1024,512]{1,0:T(8,128)(2,1)S(1)}, u32[]{:S(2)}, u32[]{:S(2)}) collective-permute-start(bf16[1024,512]{1,0:T(8,128)(2,1)} %fusion.53), channel_id=1, source_target_pairs={{0,1},{1,0},{2,3},{3,2},{4,5},{5,4},{6,7},{7,6},{8,9},{9,8},{10,11... | collective-permute-start | bytes 3145736 | tf_op jit(solution)/shard_map/ppermute | solution.py:73
  1146.0 124.3 %collective-permute-start.81 = (bf16[1024,512]{1,0:T(8,128)(2,1)}, bf16[1024,512]{1,0:T(8,128)(2,1)}, u32[]{:S(2)}, u32[]{:S(2)}) collective-permute-start(bf16[1024,512]{1,0:T(8,128)(2,1)} %add_convert_fusion.3), channel_id=1, source_target_pairs={{0,2},{1,3},{2,0},{3,1},{4,6},{5,7},{6,4},{7,5},{8,10},{9,11},{10,... | collective-permute-start | bytes 3145736 | tf_op jit(solution)/shard_map/ppermute | solution.py:73
  1173.6 112.2 %collective-permute-start.68 = (bf16[2,1024,512]{2,1,0:T(8,128)(2,1)}, bf16[2,1024,512]{2,1,0:T(8,128)(2,1)}, u32[]{:S(2)}, u32[]{:S(2)}) collective-permute-start(bf16[2,1024,512]{2,1,0:T(8,128)(2,1)} %get-tuple-element.182), channel_id=1, source_target_pairs={{0,4},{1,5},{2,6},{3,7},{4,0},{5,1},{6,2},{7,3},{8,12},{9,13},{10,... | collective-permute-start | bytes 6291464 | tf_op jit(solution)/shard_map/ppermute | solution.py:73
  1179.0 106.8 %collective-permute-start.70 = (bf16[2,1024,512]{2,1,0:T(8,128)(2,1)}, bf16[2,1024,512]{2,1,0:T(8,128)(2,1)}, u32[]{:S(2)}, u32[]{:S(2)}) collective-permute-start(bf16[2,1024,512]{2,1,0:T(8,128)(2,1)} %add_convert_fusion.2), channel_id=1, source_target_pairs={{0,2},{1,3},{2,0},{3,1},{4,6},{5,7},{6,4},{7,5},{8,10},{9,11},{10,... | collective-permute-start | bytes 6291464 | tf_op jit(solution)/shard_map/ppermute | solution.py:73
  1239.5 116.3 %collective-permute-start.75 = (bf16[2,1024,512]{2,1,0:T(8,128)(2,1)}, bf16[2,1024,512]{2,1,0:T(8,128)(2,1)}, u32[]{:S(2)}, u32[]{:S(2)}) collective-permute-start(bf16[2,1024,512]{2,1,0:T(8,128)(2,1)} %add_convert_fusion), channel_id=1, source_target_pairs={{0,16},{1,17},{2,18},{3,19},{4,20},{5,21},{6,22},{7,23},{8,24},{9,... | collective-permute-start | bytes 6291464 | tf_op jit(solution)/shard_map/ppermute | solution.py:73
  1276.9 89.3 %collective-permute-start.82 = (f32[8,128]{1,0:T(8,128)S(1)}, f32[8,128]{1,0:T(8,128)S(1)}, u32[]{:S(2)}, u32[]{:S(2)}) collective-permute-start(f32[8,128]{1,0:T(8,128)S(1)} %bitcast.164), channel_id=1, source_target_pairs={{0,1},{1,0},{2,3},{3,2},{4,5},{5,4},{6,7},{7,6},{8,9},{9,8},{10,11... | collective-permute-start | bytes 12296 | tf_op jit(solution)/shard_map/ppermute | solution.py:73
  1362.9 112.3 %collective-permute-start.76 = (bf16[1024,512]{1,0:T(8,128)(2,1)}, bf16[1024,512]{1,0:T(8,128)(2,1)}, u32[]{:S(2)}, u32[]{:S(2)}) collective-permute-start(bf16[1024,512]{1,0:T(8,128)(2,1)} %fusion.62), channel_id=1, source_target_pairs={{0,8},{1,9},{2,10},{3,11},{4,12},{5,13},{6,14},{7,15},{8,0},{9,1},... | collective-permute-start | bytes 3145736 | tf_op jit(solution)/shard_map/ppermute | solution.py:73
  1366.2 82.0 %collective-permute-start.83 = (f32[8,128]{1,0:T(8,128)S(1)}, f32[8,128]{1,0:T(8,128)S(1)}, u32[]{:S(2)}, u32[]{:S(2)}) collective-permute-start(f32[8,128]{1,0:T(8,128)S(1)} %bitcast_add_fusion), channel_id=1, source_target_pairs={{0,2},{1,3},{2,0},{3,1},{4,6},{5,7},{6,4},{7,5},{8,10},{9,11},{10,... | collective-permute-start | bytes 12296 | tf_op jit(solution)/shard_map/ppermute | solution.py:73
  (118 other events, 3211.8 us)
Sparse Core Ops, SparseCore 0:
  1008.8 102.6 all-reduce.4
  1134.2 324.1 all-reduce.6

commit v3 on v2

--- a/solution.py
+++ b/solution.py
@@ -18,23 +18,35 @@
 F32 = jnp.float32
 BF16 = jnp.bfloat16
 VMEM = 60 * 1024 * 1024
+ORDER = (0, 2, 3, 1)
+ODD = (1, 2)
 DUE = {
-    ("attended", 0): "cx0 cy0 cz1",
-    ("branch", 0): "cz2 cx1",
-    ("normed", 0): "cy1",
-    ("cot", 1): "cx2 cz3 nx0 ny0 nz1",
-    ("row", 0): "cy2 nz2",
-    ("expert", 0): "nx1 ny1 cd2",
-    ("row", 1): "nx2",
-    ("place", 0): "cx3 nz3",
-    ("expert", 1): "ny2",
-    ("row", 2): "e00 nx3 cy3",
-    ("place", 1): "e10",
-    ("expert", 2): "ny3",
-    ("row", 3): "e01",
-    ("place", 2): "e11",
-    ("expert", 3): "e02",
-    ("place", 3): "e12",
+    "attend": ("cx0", "cy0"),
+    "mmB": ("cz2",),
+    "addB": ("cd0", "b0"),
+    "cot0": ("b1",),
+    "sums": ("by", "cz3"),
+    "normed": ("cz1", "sc0"),
+    "row0": ("cx1", "cy1", "nx0", "cx2", "ny0", "cy2", "nd0"),
+    "cot2": ("cy3", "nz3", "cd2"),
+    "exp0": ("nz2", "cx3", "sr0"),
+    "row2": ("cd3", "sc2", "ny3", "nx2", "ny2", "sg0", "nd2"),
+    "place0": ("nz1",),
+    "cot3": ("cd1", "sr2", "nd3"),
+    "exp2": ("nx3",),
+    "row3": ("ny1", "sc3"),
+    "place2": ("nx1", "sg2"),
+    "cot1": ("sr3", "ed0", "ex0"),
+    "row1": ("sc1", "nd1"),
+    "place3": ("sg3",),
+    "exp1": ("sr1",),
+    "down0": ("ey2", "ed2", "ey0"),
+    "place1": ("sg1",),
+    "down1": ("ed3", "ex3"),
+    "pd0": ("sd0", "ex2"),
+    "pd1": ("sd1",),
+    "weight": ("hs", "gd0", "gx0", "gd1"),
+    "weight_down": ("gy0", "gy1", "gx1"),
 }
 
 
@@ -87,14 +99,26 @@
 def slot_blocks():
     owner, part = lax.axis_index("expert"), lax.axis_index("tensor")
     core = part % 2
-    if is_cube():
-        blocks = [[owner ^ (k * 2 + b) for b in range(NB)] for k in range(4)]
-        mine = [part ^ (y * 2) for y in range(2)]
-    else:
-        blocks = [[k * NB + b for b in range(NB)] for k in range(lax.axis_size("expert") // NB)]
-        mine = [y * 2 + core for y in range(lax.axis_size("tensor") // 2)]
-    theirs = [m ^ 1 for m in mine]
-    return [jnp.stack([jnp.asarray(v, jnp.int32) for v in b + mine + theirs]) for b in blocks]
+    found = []
+    for k in range(lax.axis_size("expert") // NB):
+        places = [k * NB + b for b in range(NB)]
+        if is_cube():
+            owners = [owner ^ p for p in places]
+            mine = [part ^ (y * 2) for y in range(2)]
+        else:
+            owners = places
+            mine = [y * 2 + core for y in range(lax.axis_size("tensor") // 2)]
+        theirs = [m ^ 1 for m in mine]
+        found.append(jnp.stack([jnp.asarray(v, jnp.int32) for v in places + owners + mine + theirs]))
+    return found
+
+
+def gather_routes(routes):
+    if not is_cube():
+        return lax.all_gather(routes, "expert")
+    both = jnp.stack([routes, send(routes, dx=1)])
+    both = jnp.concatenate([both, send(both, dz=1)])
+    return jnp.concatenate([both, send(both, dz=2)])
 
 
 def same_core():
@@ -102,7 +126,7 @@
     return [[y * 2 + c for y in range(count // 2)] for c in range(2)]
 
 
-def gather_slots(own):
+def gather_slots(own, tag, seen):
     if not is_cube():
         blocks = lax.all_gather(own, "expert")
         full = lax.all_gather(blocks, "tensor", axis_index_groups=same_core())
@@ -115,7 +139,9 @@
         block = send(own, dz=k) if k else own
         over_x = send(block, dx=1)
         over_y = send(block, dy=1)
-        far = send(over_x, dy=1) if k % 2 else send(over_y, dx=1)
+        far = send(over_x, dy=1) if k in ODD else send(over_y, dx=1)
+        for link, value in zip("zxyd", (block, over_x, over_y, far)):
+            seen[tag + link + str(k)] = value
         slots.append([[block, over_y], [over_x, far]])
     return slots
 
@@ -124,17 +150,17 @@
     return sum(t.astype(F32) for t in terms)
 
 
-def scatter_plane(parts, odd):
+def scatter_plane(parts, odd, hold=()):
     near, over_y, over_x, far = parts[0][0], parts[0][1], parts[1][0], parts[1][1]
     if odd:
         far = send(far, dy=1)
         from_y = send(over_y, dy=1)
-        from_x = send(added(over_x, far).astype(BF16), dx=1)
-        return added(near, from_x, from_y), (far, from_y), (from_x,)
-    far = send(far, dx=1)
-    from_x = send(over_x, dx=1)
-    from_y = send(added(over_y, far).astype(BF16), dy=1)
-    return added(near, from_x, from_y), (far, from_x), (from_y,)
+        from_x = send(after(added(over_x, far).astype(BF16), *hold), dx=1)
+    else:
+        far = send(far, dx=1)
+        from_x = send(over_x, dx=1)
+        from_y = send(after(added(over_y, far).astype(BF16), *hold), dy=1)
+    return added(near, from_x, from_y), {"d": far, "x": from_x, "y": from_y}
 
 
 def scatter_all(slots):
@@ -145,12 +171,14 @@
     return lax.psum_scatter(mine, "expert", scatter_dimension=0).astype(F32)
 
 
-def scatter_pairs(pairs):
+def scatter_pairs(pairs, hold, seen):
     if not is_cube():
         return scatter_all(
             [[[a[i] for a in b] for b in pair] for pair in pairs for i in range(pair[0][0].shape[0])]
         )
-    low, high = (scatter_plane(p, k)[0] for k, p in enumerate(pairs))
+    (low, low_sent), (high, high_sent) = (scatter_plane(p, k, hold) for k, p in enumerate(pairs))
+    seen.update({"g" + link + "0": value for link, value in low_sent.items()})
+    seen.update({"g" + link + "1": value for link, value in high_sent.items()})
     total = low + send(high.astype(BF16), dz=2).astype(F32)
     return total[0] + send(total[1].astype(BF16), dz=1).astype(F32)
 
@@ -170,14 +198,16 @@
     return [own, over_y, core_swap(own), core_swap(over_y)]
 
 
-def tensor_scatter(product, pieces):
+def tensor_scatter(product, pieces, tag, seen):
     if not is_cube():
         full = jnp.concatenate([product(p).astype(BF16) for p in pieces], axis=1)
         return lax.psum_scatter(full, "tensor", scatter_dimension=1, tiled=True).astype(F32)
     away_y = product(pieces[3]).astype(BF16)
     away = product(pieces[2]).astype(BF16)
     from_y, near = core_swap(away_y), core_swap(away)
-    over_y = send(added(product(pieces[1]), from_y).astype(BF16), dy=1)
+    away = added(product(pieces[1]), from_y).astype(BF16)
+    over_y = send(away, dy=1)
+    seen.update({tag + "0": from_y, tag + "1": near, tag + "y": over_y, tag + "s": away})
     return added(product(pieces[0]), near, over_y)
 
 
@@ -186,6 +216,17 @@
         return lax.psum(value, "tensor")
     value = value + core_swap(value)
     return value + send(value, dy=1)
+
+
+def expert_total(sums, tops):
+    if not is_cube():
+        return lax.psum(sums, "expert"), lax.pmax(tops, "expert")
+    count = sums.shape[0]
+    both = jnp.concatenate([sums, tops], axis=0)
+    for step in ({"dx": 1}, {"dz": 1}, {"dz": 2}):
+        other = send(both, **step)
+        both = jnp.concatenate([both[:count] + other[:count], jnp.maximum(both[count:], other[count:])])
+    return both[:count], both[count:]
 
 
 def one_hot(pos_row):
@@ -255,7 +296,7 @@
     grad_hidden = jnp.zeros((NB * CAP, ff), F32)
 
     def columns(j):
-        return pl.ds(pl.multiple_of(where_ref[NB + j] * width, width), width)
+        return pl.ds(pl.multiple_of(where_ref[2 * NB + j] * width, width), width)
 
     for j in range(2 * slices):
         x_ref, c_ref = (rows_mine, cot_mine) if j < slices else (rows_theirs, cot_theirs)
@@ -312,7 +353,7 @@
         grid_spec=pltpu.PrefetchScalarGridSpec(
             num_scalar_prefetch=1,
             grid=(held,),
-            in_specs=[block_spec(b) for b in range(NB)] * 2
+            in_specs=[block_spec(b) for b in range(2 * NB)]
             + [rows_spec] * 4
             + [in_spec, in_spec, pl.BlockSpec((1, ff, depth), lambda e, where: (e, 0, 0))],
             out_specs=[hidden_spec] * 3
@@ -335,7 +376,7 @@
     width = keep_ref.shape[3]
     for j in range(2 * slices):
         to = keep_ref if j < slices else give_ref
-        columns = pl.ds(pl.multiple_of(where_ref[NB + j] * width, width), width)
+        columns = pl.ds(pl.multiple_of(where_ref[2 * NB + j] * width, width), width)
         for k in range(slots):
             rows = matmul(scaled_refs[k][0], wd_ref[0, :, columns])
             to[k * NB : (k + 1) * NB, j % slices] = rows.astype(BF16).reshape(NB, CAP, width)
@@ -433,7 +474,7 @@
     gate_ref, up_ref = refs[4 * slots :]
     width = rows[0].shape[3]
     for j in range(2 * slices):
-        columns = pl.ds(pl.multiple_of(where_ref[NB + j] * width, width), width)
+        columns = pl.ds(pl.multiple_of(where_ref[2 * NB + j] * width, width), width)
         gate = up = None
         for k in range(slots):
             x = rows[2 * k + j // slices][:, j % slices].reshape(NB * CAP, width)
@@ -447,7 +488,7 @@
     cots, scaled, down_ref = refs[: 2 * slots], refs[2 * slots : 3 * slots], refs[3 * slots]
     width = cots[0].shape[3]
     for j in range(2 * slices):
-        columns = pl.ds(pl.multiple_of(where_ref[NB + j] * width, width), width)
+        columns = pl.ds(pl.multiple_of(where_ref[2 * NB + j] * width, width), width)
         down = None
         for k in range(slots):
             c = cots[2 * k + j // slices][:, j % slices].reshape(NB * CAP, width)
@@ -473,16 +514,23 @@
         ),
         out_shape=[jax.ShapeDtypeStruct((held, *o), F32) for o in outs],
         compiler_params=pltpu.CompilerParams(vmem_limit_bytes=VMEM),
-        cost_estimate=pl.CostEstimate(
-            flops=2 * len(outs) * slots * NB * held * CAP * depth * ff,
-            bytes_accessed=4 * len(outs) * held * depth * ff + 2 * slots * NB * held * CAP * depth,
-            transcendentals=0,
-        ),
+        cost_estimate=pl.CostEstimate(flops=10**6, bytes_accessed=10**6, transcendentals=0),
         name=name,
     )(where, *[a for pair in rows for a in pair], *hiddens)
 
 
-def project_kernel(x_ref, wq_ref, wk_ref, wv_ref, qg_ref, kg_ref, qr_ref, kr_ref, q_ref, k_ref, v_ref):
+def project_kernel(
+    in_ref, ag_ref, wq_ref, wk_ref, wv_ref, qg_ref, kg_ref,
+    x_ref, inv_ref, qr_ref, kr_ref, q_ref, k_ref, v_ref,
+):
+    @pl.when(pl.program_id(0) == 0)
+    def _():
+        for first in range(0, in_ref.shape[0], 256):
+            rows = in_ref[first : first + 256, :].astype(F32)
+            inverse = lax.rsqrt(jnp.mean(rows * rows, axis=1, keepdims=True) + 1e-05)
+            inv_ref[first : first + 256, :] = inverse
+            x_ref[first : first + 256, :] = (rows * inverse * ag_ref[...]).astype(BF16)
+
     x = x_ref[...]
     for w_ref, gain_ref, raw_ref, to_ref in ((wq_ref, qg_ref, qr_ref, q_ref), (wk_ref, kg_ref, kr_ref, k_ref)):
         raw = matmul(x, w_ref[...])
@@ -495,27 +543,35 @@
     v_ref[...] = matmul(x, wv_ref[...]).astype(BF16)
 
 
-def project(x, w_query, w_key, w_value, query_gain, key_gain):
-    tokens, depth = x.shape
+def project(inputs, attn_gain, w_query, w_key, w_value, query_gain, key_gain):
+    tokens, depth = inputs.shape
     columns = w_query.shape[1]
     step = min(256, columns)
+    whole = pl.BlockSpec((tokens, depth), lambda i: (0, 0))
     weight = pl.BlockSpec((depth, step), lambda i: (0, i))
     gain = pl.BlockSpec((1, step), lambda i: (0, i))
     out = pl.BlockSpec((tokens, step), lambda i: (0, i))
     return pl.pallas_call(
         project_kernel,
         grid=(columns // step,),
-        in_specs=[pl.BlockSpec((tokens, depth), lambda i: (0, 0)), weight, weight, weight, gain, gain],
-        out_specs=[out] * 5,
-        out_shape=[jax.ShapeDtypeStruct((tokens, columns), t) for t in (F32, F32, BF16, BF16, BF16)],
+        in_specs=[whole, pl.BlockSpec((1, depth), lambda i: (0, 0)), weight, weight, weight, gain, gain],
+        out_specs=[whole, pl.BlockSpec((tokens, 1), lambda i: (0, 0))] + [out] * 5,
+        out_shape=[
+            jax.ShapeDtypeStruct((tokens, depth), BF16),
+            jax.ShapeDtypeStruct((tokens, 1), F32),
+        ]
+        + [jax.ShapeDtypeStruct((tokens, columns), t) for t in (F32, F32, BF16, BF16, BF16)],
         compiler_params=pltpu.CompilerParams(vmem_limit_bytes=VMEM),
         cost_estimate=pl.CostEstimate(
             flops=6 * tokens * depth * columns,
-            bytes_accessed=2 * tokens * depth + 6 * depth * columns + 14 * tokens * columns,
+            bytes_accessed=4 * tokens * depth + 6 * depth * columns + 14 * tokens * columns,
             transcendentals=0,
         ),
         name="project",
-    )(x, w_query, w_key, w_value, query_gain.reshape(1, -1), key_gain.reshape(1, -1))
+    )(
+        inputs, attn_gain.reshape(1, -1), w_query, w_key, w_value,
+        query_gain.reshape(1, -1), key_gain.reshape(1, -1),
+    )
 
 
 def allowed_pairs(pieces_ref, base, first, rows, keys):
@@ -656,30 +712,22 @@
 
 
 def expert_steps(slots):
-    steps = [("cot", 0), ("cot", 1), ("row", 0)]
-    for k in range(slots):
-        steps.append(("expert", k))
-        if k + 2 < slots:
-            steps.append(("cot", k + 2))
-        if k + 1 < slots:
-            steps.append(("row", k + 1))
+    order = ORDER if is_cube() else range(slots)
+    steps = [("row", order[0]), ("cot", order[1])]
+    for i, k in enumerate(order):
+        steps.append(("exp", k))
+        if i + 1 < slots:
+            steps.append(("row", order[i + 1]))
+        else:
+            steps.append(("down", 0))
         steps.append(("place", k))
+        if i + 2 < slots:
+            steps.append(("cot", order[i + 2]))
     return steps
 
 
-def transfers_due(kind, k, cots, rows, terms):
-    if not is_cube():
-        return []
-    at = {"z": (0, 0), "y": (0, 1), "x": (1, 0), "d": (1, 1)}
-    due = DUE.get((kind, k), "").split()
-    found = []
-    for name in due:
-        if name[0] == "e":
-            found.extend(terms[int(name[2])][int(name[1])])
-        else:
-            b, y = at[name[1]]
-            found.append((cots if name[0] == "c" else rows)[int(name[2])][b][y])
-    return found
+def due(step, seen):
+    return [seen[name] for name in DUE.get(step, ()) if name in seen]
 
 
 def per_device(
@@ -718,14 +766,11 @@
     def own_columns(value):
         return lax.dynamic_slice_in_dim(value, column, slice_width, value.ndim - 1)
 
-    all_routes = lax.all_to_all(
-        jnp.broadcast_to(routes.T[None], (owners, TOP, tokens_here)),
-        "expert",
-        split_axis=0,
-        concat_axis=0,
-        tiled=True,
-    )
-    cot_slots = gather_slots(cotangent.astype(BF16))
+    seen = {}
+    all_routes = gather_routes(routes.T)
+    cot_slots = gather_slots(cotangent.astype(BF16), "c", seen)
+    order = tensor_order()
+    first_slot = ORDER[0] if is_cube() else 0
 
     held_ids = owner * experts_here + jnp.arange(experts_here, dtype=jnp.int32)
     chosen = jnp.any(all_routes[:, None] == held_ids[None, :, None, None], axis=2)
@@ -739,23 +784,23 @@
         chosen, earlier + jnp.arange(experts_here, dtype=jnp.int32)[None, :, None] * CAP, -1
     ).transpose(0, 2, 1)
 
-    order = tensor_order()
     output_pieces = [lax.dynamic_slice_in_dim(w_output, o * slice_width, slice_width, 1) for o in order]
-    inputs_f = inputs.astype(F32)
-    attn_inv = lax.rsqrt(jnp.mean(inputs_f * inputs_f, axis=-1, keepdims=True) + 1e-05)
-    normed_a = (inputs_f * attn_inv * attn_gain).astype(BF16)
-    query_raw, key_raw, queries, keys, values = project(
-        normed_a, w_query, w_key, w_value, query_gain, key_gain
+    normed_a, attn_inv, query_raw, key_raw, queries, keys, values = project(
+        inputs, attn_gain, w_query, w_key, w_value, query_gain, key_gain
     )
     pieces = jnp.concatenate([piece_start, piece_length], axis=1).reshape(-1)
-    attended, logs, tops = attend(pieces, queries, keys, values, scale)
-    head_top = lax.pmax(
-        jnp.max(tops[:, 0, 0].reshape(sequences, heads_here), axis=0), "expert"
-    )
-    attended = after(attended, *transfers_due("attended", 0, cot_slots, None, None))
-    branch = tensor_scatter(partial(matmul, attended), output_pieces)
-    first_cot = pick_rows(after(where[0], attended), pos, cot_slots[0])
-    branch = after(branch, first_cot, *transfers_due("branch", 0, cot_slots, None, None))
+    attended, logs, tops = attend(
+        after(pieces, values, *due("attend", seen)), queries, keys, values, scale
+    )
+    head_top = jnp.max(tops[:, 0, 0].reshape(sequences, heads_here), axis=0)
+    attended = after(attended, *due("mmB", seen))
+    branch = tensor_scatter(partial(matmul, attended), output_pieces, "b", seen)
+    first_cot = pick_rows(
+        after(where[first_slot], attended, *due("addB", seen), *due("cot" + str(first_slot), seen)),
+        pos,
+        cot_slots[first_slot],
+    )
+    branch = after(branch, first_cot, *due("sums", seen))
     residual = own_columns(inputs).astype(F32) + branch
     gain_slice = own_columns(moe_gain)
     router_slice = lax.dynamic_slice_in_dim(w_router, column, slice_width, 0)
@@ -777,9 +822,9 @@
     moe_inv_row = lax.rsqrt(row_sums[E] / width + 1e-05)
     moe_inv = moe_inv_row[:, None]
     normed_m = (lifted * moe_inv).astype(BF16)
-    normed_m = after(normed_m, *transfers_due("normed", 0, cot_slots, None, None))
-
-    normed_slots = gather_slots(normed_m)
+    normed_m = after(normed_m, *due("normed", seen))
+
+    normed_slots = gather_slots(normed_m, "n", seen)
     router = jax.nn.softmax(row_sums[:E] * moe_inv_row[None], axis=0)
     gate = lax.all_to_all(
         router.reshape(owners, experts_here, tokens_here),
@@ -789,38 +834,63 @@
         tiled=True,
     )
 
-    cots, rows, scaled, gate_grads, up_grads, probs, back = [], [], [], [], [], [], []
-    terms = []
+    rows, cots, back, sums = [None] * slots, [None] * slots, [None] * slots, [None] * slots
+    scaled, gate_grads, up_grads, probs = [None] * slots, [None] * slots, [None] * slots, [None] * slots
     last = first_cot
+    cots[first_slot] = (first_cot, core_swap(first_cot))
+    seen["sc" + str(first_slot)] = cots[first_slot][1]
+    downs = {}
+
+    def turn(name, k):
+        return after(where[k], last, *due(name, seen))
+
+    def lower(k):
+        keep, give = down_slots(turn("down" + str(k), 0), scaled[2 * k : 2 * k + 2], w_down, slices)
+        downs[k] = (keep, core_swap(give))
+        seen["sd" + str(k)] = downs[k][1]
+        return keep
+
     for kind, k in expert_steps(slots):
-        due = [last] + transfers_due(kind, k, cot_slots, normed_slots, terms)
-        now = after(where[k], *due)
+        now = turn(kind + str(k), k)
         if kind == "cot":
-            last = pick_rows(now, pos, cot_slots[k]) if k else first_cot
-            cots.append((last, core_swap(last)))
+            last = pick_rows(now, pos, cot_slots[k])
+            cots[k] = (last, core_swap(last))
+            seen["sc" + str(k)] = cots[k][1]
         elif kind == "row":
             last = pick_rows(now, pos, normed_slots[k])
-            rows.append((last, core_swap(last)))
-        elif kind == "expert":
-            kept, gate_grad, up_grad, prob, keep, give = expert_slot(
+            rows[k] = (last, core_swap(last))
+            seen["sr" + str(k)] = rows[k][1]
+        elif kind == "exp":
+            scaled[k], gate_grads[k], up_grads[k], probs[k], keep, give = expert_slot(
                 now, pos, gate, rows[k], cots[k], w_gate, w_up, w_down
             )
-            last = kept
-            scaled.append(kept)
-            gate_grads.append(gate_grad)
-            up_grads.append(up_grad)
-            probs.append(prob)
-            back.append((keep, core_swap(give)))
+            last = scaled[k]
+            back[k] = (keep, core_swap(give))
+            seen["sg" + str(k)] = back[k][1]
+        elif kind == "down":
+            last = lower(k)
         else:
             placed = place_rows([now], at, *back[k])
             last = placed[0][0]
             back[k] = [[a[0] for a in b] for b in placed]
             if is_cube():
-                term, first, second = scatter_plane(back[k], k % 2)
+                sums[k], sent = scatter_plane(back[k], k in ODD)
                 if k:
-                    term = send(term.astype(BF16), dz=k).astype(F32)
-                terms.append((term, first, second))
-    expert_path = sum(t[0] for t in terms) if is_cube() else scatter_all(back)
+                    sent["z"] = send(sums[k].astype(BF16), dz=k)
+                    sums[k] = sent["z"].astype(F32)
+                seen.update({"e" + link + str(k): value for link, value in sent.items()})
+    for k in range(1, slots // 2):
+        last = lower(k)
+    pairs = []
+    for k in range(slots // 2):
+        now = turn("pd" + str(k), 2 * k)
+        placed = place_rows([now, where[2 * k + 1]], at, *downs[k])
+        last = placed[0][0]
+        pairs.append(placed)
+    if is_cube():
+        expert_path = sum(after(s, last) for s in sums)
+    else:
+        expert_path = scatter_all(back)
 
     prob_grads = jnp.stack([probs[k][:, b] for k in range(slots) for b in range(NB)])
     if is_cube():
@@ -845,60 +915,64 @@
     branch_pieces = tensor_gather(grad_residual.astype(BF16))
     grad_branch = jnp.concatenate(branch_pieces, axis=1)
 
-    pairs = []
-    for k in range(0, slots, 2):
-        now = after(where[0], last)
-        keep, give = down_slots(now, scaled[k : k + 2], w_down, slices)
-        last = keep
-        pairs.append((keep, core_swap(give)))
-    for i, pair in enumerate(pairs):
-        now = after(where[2 * i], branch_pieces[0]) if i else after(where[0], last)
-        placed = place_rows([now, where[2 * i + 1]], at, *pair)
-        last = placed[0][0]
-        if is_cube():
-            placed = [[after(a, branch_pieces[1]) for a in b] for b in placed]
-        pairs[i] = placed
-    mixture = scatter_pairs(pairs)
+    if is_cube():
+        ends = [seen["e" + link + str(ORDER[i])] for i in (-2, -1) for link in "xyd"]
+        pairs[0] = [[after(a, *ends) for a in b] for b in pairs[0]]
+        pairs[1] = [[after(a, branch_pieces[1]) for a in b] for b in pairs[1]]
+    mixture = scatter_pairs(pairs, branch_pieces[1:2], seen)
     out = residual + mixture
-    grad_output = matmul_tn(attended, grad_branch)
+
+    grad_output = matmul_tn(attended, grad_branch).astype(BF16)
     grad_attended = matmul_nt(grad_branch, jnp.concatenate(output_pieces, axis=1)).astype(BF16)
+    grad_attended = after(grad_attended, grad_output)
     grad_query_raw, grad_key_raw, grad_v, grad_query_gain, grad_key_gain = attend_back(
         pieces, queries, keys, values, grad_attended, logs, query_raw, key_raw, query_gain, key_gain, scale
     )
-    grad_query = matmul_tn(normed_a, grad_query_raw)
-    grad_key = matmul_tn(normed_a, grad_key_raw)
-    grad_value = matmul_tn(normed_a, grad_v)
-    grad_gate, grad_up = weight_grads(
-        weight_kernel, after(where[0], grad_value), rows, gate_grads + up_grads, [w_gate.shape[1:]] * 2, "weight_grads"
-    )
-    (grad_down,) = weight_grads(
-        weight_down_kernel, after(where[0], grad_gate), cots, scaled, [w_down.shape[1:]], "weight_down_grads"
-    )
     grad_raw = jnp.concatenate([grad_query_raw, grad_key_raw, grad_v], axis=1)
+    grad_three = matmul_tn(normed_a, grad_raw).astype(BF16)
+    sum_output = lax.psum(grad_output, "expert").astype(F32)
+    sum_three = lax.psum_scatter(grad_three, "expert", scatter_dimension=0, tiled=True)
+    grad_raw = after(grad_raw, grad_three)
     weights = jnp.concatenate([w_query, w_key, w_value], axis=1)
     weight_pieces = [lax.dynamic_slice_in_dim(weights, o * slice_width, slice_width, 0) for o in order]
-    grad_normed_a = tensor_scatter(partial(matmul_nt, grad_raw), weight_pieces)
+    grad_normed_a = tensor_scatter(partial(matmul_nt, grad_raw), weight_pieces, "h", seen)
+    now = after(where[0], sum_output, *due("weight", seen))
+    grad_gate, grad_up = weight_grads(
+        weight_kernel, now, rows, gate_grads + up_grads, [w_gate.shape[1:]] * 2, "weight_grads"
+    )
+    (grad_down,) = weight_grads(
+        weight_down_kernel, after(now, grad_gate, sum_three, *due("weight_down", seen)), cots, scaled, [w_down.shape[1:]], "weight_down_grads"
+    )
+    sum_three = lax.all_gather(sum_three, "expert", tiled=True)
+    sum_query, sum_key, sum_value = jnp.split(sum_three.astype(F32), 3, axis=1)
+    grad_normed_a = after(grad_normed_a, grad_gate)
     attn_hat = own_columns(inputs).astype(F32) * attn_inv
     upstream = grad_normed_a * own_columns(attn_gain)
     grad_attn_gain = jnp.sum(grad_normed_a * attn_hat, axis=0)
     mean_dot = tensor_sum(jnp.sum(upstream * attn_hat, axis=-1).reshape(8, -1)).reshape(-1, 1) / width
     grad_input = grad_residual + attn_inv * (upstream - attn_hat * mean_dot)
 
-    def total(*values):
-        return [lax.psum(v.astype(BF16), "expert").astype(F32) for v in values]
-
-    sum_output, sum_moe_gain, sum_router = total(grad_output, grad_moe_gain, grad_router)
-    grad_query = after(grad_query, sum_output)
-    sum_query, sum_key, sum_value, sum_query_gain, sum_key_gain, sum_attn_gain = total(
-        grad_query,
-        grad_key,
-        grad_value,
-        jnp.sum(grad_query_gain, axis=(0, 1)),
-        jnp.sum(grad_key_gain, axis=(0, 1)),
-        grad_attn_gain,
-    )
-    sum_attn_gain = lax.all_gather(sum_attn_gain, "tensor", tiled=True)
-    sum_router = lax.all_gather(sum_router, "tensor", tiled=True)
+    small = jnp.concatenate(
+        [
+            grad_router.T,
+            jnp.stack(
+                [
+                    grad_attn_gain,
+                    grad_moe_gain,
+                    jnp.sum(grad_query_gain, axis=(0, 1)),
+                    jnp.sum(grad_key_gain, axis=(0, 1)),
+                ]
+            ),
+        ],
+        axis=0,
+    )
+    top_row = jnp.pad(head_top, (0, slice_width - heads_here), constant_values=-3e38)
+    small, top_row = expert_total(small, top_row[None])
+    head_top = top_row[0, :heads_here]
+    sum_moe_gain, sum_query_gain, sum_key_gain = small[E + 1], small[E + 2], small[E + 3]
+    every = lax.all_gather(small[: E + 1], "tensor")
+    sum_router = every[:, :E].transpose(0, 2, 1).reshape(width, E)
+    sum_attn_gain = every[:, E].reshape(width)
     ordered = jnp.zeros_like(sum_output)
     for i, o in enumerate(order):
         ordered = lax.dynamic_update_slice_in_dim(

time: 1500 us -> 1700 us (1.13)
  waiting for transfers between devices: 650 us -> 921 us
  blocking collectives: 101 us -> 7.52 us
  local copies, waits for them, and re-layouts: 37.1 us -> 59.5 us
    reduce_scatter x0 -> x1, waiting for transfers between devices: none -> 122 us  [per_device(): lax.psum_scatter(grad_three, 'expert', scatter_dimension=0, tiled=True)]
    ppermute x84 -> x90, waiting for transfers between devices: 620 us -> 697 us  [send(): return lax.ppermute(value, BOTH, flip(dz, dx, dy, dc))]
    psum x1 -> x0, blocking collectives: 73.7 us -> none  [total(): return [lax.psum(v.astype(BF16), 'expert').astype(F32) for v in values]]
    all_to_all x1, waiting for transfers between devices: 0.6 us -> 51.2 us  [per_device(): lax.all_to_all(prob_grads, 'expert', split_axis=0, concat_axis=0, tiled=T...]
    psum x2 -> x1, waiting for transfers between devices: 5.14 us -> 47.3 us  [per_device(): sum_output = lax.psum(grad_output, 'expert').astype(F32)]
    all_to_all x1 -> x0, waiting for transfers between devices: 25 us -> none  [per_device(): lax.all_to_all(jnp.broadcast_to(routes.T[None], (owners, TOP, tokens_here...]
    ppermute x84 -> x90, starting transfers between devices: 69.1 us -> 88.1 us  [send(): return lax.ppermute(value, BOTH, flip(dz, dx, dy, dc))]
    convert_element_type x21 -> x14, other arithmetic: 48.5 us -> 34.3 us  [the longest x3 8.29 us: per_device(): sent['z'] = send(sums[k].astype(BF16), dz=k)]
  transfers between devices with their start and end apart: 89 -> 95, of which waited for: 36 -> 49; matrix products, arithmetic and copies ran while one was open for 11% -> 8% of each run, Pallas kernels for 27% -> 21%
where the time goes in v3:
time: 1700 us; the launch traced here: 1690 us
  waiting for transfers between devices  921 us (54%)
  Pallas kernels  458 us (27%)
  starting transfers between devices  98 us (6%)
  other arithmetic  70.5 us (4%)
  local copies, waits for them, and re-layouts  59.5 us (4%)
  matrix products  55.8 us (3%)
    ppermute x90, waiting for transfers between devices, send(): return lax.ppermute(value, BOTH, flip(dz, dx, dy, dc))  697 us
    reduce_scatter x1, waiting for transfers between devices, per_device(): lax.psum_scatter(grad_three, 'expert', scatter_dimension=0, tiled=True)  122 us
    pallas_call x4, Pallas kernels, expert_slot(): pl.pallas_call(partial(expert_kernel, slices), grid_spec=pltpu.PrefetchSc...  112 us
    pallas_call x6, Pallas kernels, place_rows(): pl.pallas_call(partial(place_kernel, slices, held, slots), grid_spec=pltp...  107 us
    pallas_call x8, Pallas kernels, pick_rows(): pl.pallas_call(partial(pick_kernel, group, slices), grid_spec=pltpu.Prefe...  93.7 us
    ppermute x90, starting transfers between devices, send(): return lax.ppermute(value, BOTH, flip(dz, dx, dy, dc))  88.1 us
    pallas_call x2, Pallas kernels, weight_grads(): pl.pallas_call(partial(kernel, slots, slices), grid_spec=pltpu.PrefetchSc...  70.3 us
    all_to_all x1, waiting for transfers between devices, per_device(): lax.all_to_all(prob_grads, 'expert', split_axis=0, concat_axis=0, tiled=T...  51.2 us
  transfers between devices with their start and end apart: 95, of which 49 were waited for; matrix products, arithmetic and copies ran while one was open for 8% of the time, Pallas kernels for 21%

profile of v3, /device:TPU:10, one launch (start us, length us, event | category | flops | bytes accessed | tf_op | source)
XLA Modules:
  0.0 1685.4 jit_solution(15202676559007211389)
XLA Ops:
  76.9 23.2 %collective-permute-done.9 = s32[4,8,1024]{2,1,0:T(8,128)S(1)} collective-permute-done((s32[4,8,1024]{2,1,0:T(8,128)S(1)}, s32[4,8,1024]{2,1,0:T(8,128)S(1)}, u32[]{:S(2)}, u32[]{:S(2)}) %collective-permute-start.9) | collective-permute-done | bytes 131104 | tf_op jit(solution)/shard_map/ppermute | solution.py:85
  128.5 22.0 %pick_rows.8.refs_6_.refs_0_ = bf16[2,2,1280,512]{3,2,1,0:T(8,128)(2,1)} custom-call(s32[8]{0:T(128)} %stack.90.where_ref, s32[8,8,1024]{2,1,0:T(8,128)} %copy.155.refs_0_.refs_1_, s32[8,8,1024]{2,1,0:T(8,128)} %copy.155.refs_0_.refs_1_, bf16[1024,512]{1,0:T(8,128)(2,1)} %convert_element_type.253.refs_2_, bf16[1024,512]{1,0:T(8,128)(2,1)} %collective-permute-done.1.refs_3_, ...), custom_call_target="tpu_custom_call" | custom-call | flops 5368709120 | bytes 9437184 | tf_op jit(solution)/shard_map/pick_rows/pallas_call | solution.py:264
  214.7 20.9 %collective-permute-done.19.refs_3_ = bf16[1024,512]{1,0:T(8,128)(2,1)S(1)} collective-permute-done((bf16[1024,512]{1,0:T(8,128)(2,1)}, bf16[1024,512]{1,0:T(8,128)(2,1)S(1)}, u32[]{:S(2)}, u32[]{:S(2)}) %collective-permute-start.19) | collective-permute-done | bytes 1048608 | tf_op jit(solution)/shard_map/ppermute | solution.py:85
  263.6 23.1 %collective-permute-done.21.refs_3_ = bf16[1024,512]{1,0:T(8,128)(2,1)S(1)} collective-permute-done((bf16[1024,512]{1,0:T(8,128)(2,1)}, bf16[1024,512]{1,0:T(8,128)(2,1)S(1)}, u32[]{:S(2)}, u32[]{:S(2)}) %collective-permute-start.21) | collective-permute-done | bytes 1048608 | tf_op jit(solution)/shard_map/ppermute | solution.py:85
  288.2 20.2 %collective-permute-done.23.refs_5_ = bf16[1024,512]{1,0:T(8,128)(2,1)} collective-permute-done((bf16[1024,512]{1,0:T(8,128)(2,1)}, bf16[1024,512]{1,0:T(8,128)(2,1)}, u32[]{:S(2)}, u32[]{:S(2)}) %collective-permute-start.23) | collective-permute-done | bytes 1048608 | tf_op jit(solution)/shard_map/ppermute | solution.py:85
  328.3 30.3 %collective-permute-done.24.refs_2_ = bf16[1024,512]{1,0:T(8,128)(2,1)} collective-permute-done((bf16[1024,512]{1,0:T(8,128)(2,1)}, bf16[1024,512]{1,0:T(8,128)(2,1)}, u32[]{:S(2)}, u32[]{:S(2)}) %collective-permute-start.24) | collective-permute-done | bytes 1048608 | tf_op jit(solution)/shard_map/ppermute | solution.py:85
  362.3 27.8 %expert_slot.4 = (bf16[8,320,256]{2,1,0:T(8,128)(2,1)}, bf16[8,320,256]{2,1,0:T(8,128)(2,1)}, bf16[8,320,256]{2,1,0:T(8,128)(2,1)}, f32[8,2,1024]{2,1,0:T(2,128)...) custom-call(s32[8]{0:T(128)} %stack.90.where_ref, s32[8,8,1024]{2,1,0:T(8,128)} %copy.155.refs_0_.refs_1_, ...), custom_call_target="tpu_custom_call" | custom-call | flops 13421772800 | bytes 56623104 | tf_op jit(solution)/shard_map/expert_slot/pallas_call | solution.py:351
  393.8 22.4 %collective-permute-done.28.refs_5_ = bf16[1024,512]{1,0:T(8,128)(2,1)S(1)} collective-permute-done((bf16[1024,512]{1,0:T(8,128)(2,1)S(1)}, bf16[1024,512]{1,0:T(8,128)(2,1)S(1)}, u32[]{:S(2)}, u32[]{:S(2)}) %collective-permute-start.28) | collective-permute-done | bytes 1048608 | tf_op jit(solution)/shard_map/ppermute | solution.py:85
  417.8 20.6 %collective-permute-done.31.refs_4_ = bf16[1024,512]{1,0:T(8,128)(2,1)S(1)} collective-permute-done((bf16[1024,512]{1,0:T(8,128)(2,1)}, bf16[1024,512]{1,0:T(8,128)(2,1)S(1)}, u32[]{:S(2)}, u32[]{:S(2)}) %collective-permute-start.31) | collective-permute-done | bytes 1048608 | tf_op jit(solution)/shard_map/ppermute | solution.py:85
  441.4 22.2 %collective-permute-done.34.refs_5_ = bf16[1024,512]{1,0:T(8,128)(2,1)S(1)} collective-permute-done((bf16[1024,512]{1,0:T(8,128)(2,1)S(1)}, bf16[1024,512]{1,0:T(8,128)(2,1)S(1)}, u32[]{:S(2)}, u32[]{:S(2)}) %collective-permute-start.34) | collective-permute-done | bytes 1048608 | tf_op jit(solution)/shard_map/ppermute | solution.py:85
  530.7 22.9 %collective-permute-done.39.refs_4_ = bf16[1024,512]{1,0:T(8,128)(2,1)} collective-permute-done((bf16[1024,512]{1,0:T(8,128)(2,1)S(1)}, bf16[1024,512]{1,0:T(8,128)(2,1)}, u32[]{:S(2)}, u32[]{:S(2)}) %collective-permute-start.39) | collective-permute-done | bytes 1048608 | tf_op jit(solution)/shard_map/ppermute | solution.py:85
  553.6 28.2 %expert_slot.5 = (bf16[8,320,256]{2,1,0:T(8,128)(2,1)}, bf16[8,320,256]{2,1,0:T(8,128)(2,1)}, bf16[8,320,256]{2,1,0:T(8,128)(2,1)}, f32[8,2,1024]{2,1,0:T(2,128)...) custom-call(s32[8]{0:T(128)} %stack.102.where_ref, s32[8,8,1024]{2,1,0:T(8,128)} %copy.155.refs_0_.refs_1_, ...), custom_call_target="tpu_custom_call" | custom-call | flops 13421772800 | bytes 56623104 | tf_op jit(solution)/shard_map/expert_slot/pallas_call | solution.py:351
  596.5 22.5 %collective-permute-done.42.refs_4_ = bf16[1024,512]{1,0:T(8,128)(2,1)} collective-permute-done((bf16[1024,512]{1,0:T(8,128)(2,1)}, bf16[1024,512]{1,0:T(8,128)(2,1)}, u32[]{:S(2)}, u32[]{:S(2)}) %collective-permute-start.42) | collective-permute-done | bytes 1048608 | tf_op jit(solution)/shard_map/ppermute | solution.py:85
  641.3 21.6 %collective-permute-done.46 = bf16[1024,512]{1,0:T(8,128)(2,1)S(1)} collective-permute-done((bf16[1024,512]{1,0:T(8,128)(2,1)}, bf16[1024,512]{1,0:T(8,128)(2,1)S(1)}, u32[]{:S(2)}, u32[]{:S(2)}) %collective-permute-start.46) | collective-permute-done | bytes 1048608 | tf_op jit(solution)/shard_map/ppermute | solution.py:85
  674.6 27.8 %expert_slot.6 = (bf16[8,320,256]{2,1,0:T(8,128)(2,1)}, bf16[8,320,256]{2,1,0:T(8,128)(2,1)}, bf16[8,320,256]{2,1,0:T(8,128)(2,1)}, f32[8,2,1024]{2,1,0:T(2,128)...) custom-call(s32[8]{0:T(128)} %stack.99.where_ref, s32[8,8,1024]{2,1,0:T(8,128)} %copy.155.refs_0_.refs_1_, ...), custom_call_target="tpu_custom_call" | custom-call | flops 13421772800 | bytes 56623104 | tf_op jit(solution)/shard_map/expert_slot/pallas_call | solution.py:351
  728.2 27.9 %expert_slot.7 = (bf16[8,320,256]{2,1,0:T(8,128)(2,1)}, bf16[8,320,256]{2,1,0:T(8,128)(2,1)}, bf16[8,320,256]{2,1,0:T(8,128)(2,1)}, f32[8,2,1024]{2,1,0:T(2,128)...) custom-call(s32[8]{0:T(128)} %stack.96.where_ref, s32[8,8,1024]{2,1,0:T(8,128)} %copy.155.refs_0_.refs_1_, ...), custom_call_target="tpu_custom_call" | custom-call | flops 13421772800 | bytes 56623104 | tf_op jit(solution)/shard_map/expert_slot/pallas_call | solution.py:351
  761.9 22.2 %collective-permute-done.53 = bf16[1024,512]{1,0:T(8,128)(2,1)S(1)} collective-permute-done((bf16[1024,512]{1,0:T(8,128)(2,1)S(1)}, bf16[1024,512]{1,0:T(8,128)(2,1)S(1)}, u32[]{:S(2)}, u32[]{:S(2)}) %collective-permute-start.53) | collective-permute-done | bytes 1048608 | tf_op jit(solution)/shard_map/ppermute | solution.py:85
  785.3 21.4 %collective-permute-done.51 = bf16[1024,512]{1,0:T(8,128)(2,1)} collective-permute-done((bf16[1024,512]{1,0:T(8,128)(2,1)S(1)}, bf16[1024,512]{1,0:T(8,128)(2,1)}, u32[]{:S(2)}, u32[]{:S(2)}) %collective-permute-start.51) | collective-permute-done | bytes 1048608 | tf_op jit(solution)/shard_map/ppermute | solution.py:85
  806.7 21.9 %collective-permute-done.52 = bf16[1024,512]{1,0:T(8,128)(2,1)} collective-permute-done((bf16[1024,512]{1,0:T(8,128)(2,1)S(1)}, bf16[1024,512]{1,0:T(8,128)(2,1)}, u32[]{:S(2)}, u32[]{:S(2)}) %collective-permute-start.52) | collective-permute-done | bytes 1048608 | tf_op jit(solution)/shard_map/ppermute | solution.py:85
  881.7 19.4 %collective-permute-done.60 = bf16[1024,512]{1,0:T(8,128)(2,1)S(1)} collective-permute-done((bf16[1024,512]{1,0:T(8,128)(2,1)}, bf16[1024,512]{1,0:T(8,128)(2,1)S(1)}, u32[]{:S(2)}, u32[]{:S(2)}) %collective-permute-start.60) | collective-permute-done | bytes 1048608 | tf_op jit(solution)/shard_map/ppermute | solution.py:85
  906.9 16.7 collective-permute-done.59
  946.3 51.2 %all-to-all-done.1 = f32[8,8,1024]{2,1,0:T(8,128)S(1)} async-done(((f32[8,8,1024]{2,1,0:T(8,128)}), f32[8,8,1024]{2,1,0:T(8,128)S(1)}, u32[]{:S(2)}, u32[]{:S(2)}) %all-to-all-start.1) | async-done | bytes 262176 | tf_op jit(solution)/shard_map/all_to_all | solution.py:898
  1028.6 25.5 %place_rows.10 = (bf16[2,1024,512]{2,1,0:T(8,128)(2,1)}, bf16[2,1024,512]{2,1,0:T(8,128)(2,1)}, bf16[2,1024,512]{2,1,0:T(8,128)(2,1)}, bf16[2,1024,512]{2,1,0:T(8,128)(2,1)}) custom-call(s32[4]{0:T(128)} %pad_add_fusion.3.where_ref, s32[8,1024,8]{2,1,0:T(8,128)} %bitcast.156, s32[8,1024,8]{2,1,0:T(8,128)} %bitcast.157, s32[8,1024,8]{2,1,0:T(8,128)} %bitcast.158, ...), custom_call_target="tpu_custom_call" | custom-call | flops 10737418240 | bytes 29360128 | tf_op jit(solution)/shard_map/place_rows/pallas_call | solution.py:450
  1054.7 25.4 %place_rows.11 = (bf16[2,1024,512]{2,1,0:T(8,128)(2,1)}, bf16[2,1024,512]{2,1,0:T(8,128)(2,1)}, bf16[2,1024,512]{2,1,0:T(8,128)(2,1)}, bf16[2,1024,512]{2,1,0:T(8,128)(2,1)}) custom-call(s32[4]{0:T(128)} %pad_add_fusion.4.where_ref, s32[8,1024,8]{2,1,0:T(8,128)} %bitcast.160, s32[8,1024,8]{2,1,0:T(8,128)} %bitcast.161, s32[8,1024,8]{2,1,0:T(8,128)} %bitcast.162, ...), custom_call_target="tpu_custom_call" | custom-call | flops 10737418240 | bytes 29360128 | tf_op jit(solution)/shard_map/place_rows/pallas_call | solution.py:450
  1092.2 23.5 %collective-permute-done.73 = bf16[1024,512]{1,0:T(8,128)(2,1)S(1)} collective-permute-done((bf16[1024,512]{1,0:T(8,128)(2,1)S(1)}, bf16[1024,512]{1,0:T(8,128)(2,1)S(1)}, u32[]{:S(2)}, u32[]{:S(2)}) %collective-permute-start.73) | collective-permute-done | bytes 1048608 | tf_op jit(solution)/shard_map/ppermute | solution.py:85
  1166.8 122.3 %reduce-scatter.2.cloned.1.call-done = bf16[256,1536]{1,0:T(8,128)(2,1)} async-done(((bf16[2048,1536]{1,0:T(8,128)(2,1)}), bf16[256,1536]{1,0:T(8,128)(2,1)}) %reduce-scatter.2.cloned.1.call-update) | async-done | bytes 786448 | tf_op jit(solution)/shard_map/reduce_scatter | solution.py:934
  1320.9 27.4 %collective-permute-done.75 = bf16[2,1024,512]{2,1,0:T(8,128)(2,1)S(1)} collective-permute-done((bf16[2,1024,512]{2,1,0:T(8,128)(2,1)}, bf16[2,1024,512]{2,1,0:T(8,128)(2,1)S(1)}, u32[]{:S(2)}, u32[]{:S(2)}) %collective-permute-start.75) | collective-permute-done | bytes 2097184 | tf_op jit(solution)/shard_map/ppermute | solution.py:85
  1351.6 47.3 %all-reduce.3.cloned.1.call-done = bf16[512,2048]{1,0:T(8,128)(2,1)} async-done(((bf16[512,2048]{1,0:T(8,128)(2,1)}), bf16[512,2048]{1,0:T(8,128)(2,1)}) %all-reduce.3.cloned.1.call-update) | async-done | bytes 2097168 | tf_op jit(solution)/shard_map/psum | solution.py:933
  1403.7 42.7 %weight_grads.1 = (f32[8,2048,256]{2,1,0:T(8,128)}, f32[8,2048,256]{2,1,0:T(8,128)}) custom-call(s32[8]{0:T(128)} %stack.90.where_ref, bf16[2,2,1280,512]{3,2,1,0:T(8,128)(2,1)} %pick_rows.9.refs_4_.refs_0_, bf16[2,2,1280,512]{3,2,1,0:T(8,128)(2,1)} %collective-permute-done.26.refs_5_.refs_1_, bf16[2,2,1280,512]{3,2,1,0:T(8,128)(2,1)} %pick_rows.15.refs_4_.refs_2_, ...), custom_call_target="tpu_custom_call" | custom-call | flops 1000000 | bytes 1000000 | tf_op jit(solution)/shard_map/weight_grads/pallas_call | solution.py:507
  1490.4 110.9 %collective-permute-done.89 = f32[69,512]{1,0:T(8,128)S(1)} collective-permute-done((f32[69,512]{1,0:T(8,128)S(1)}, f32[69,512]{1,0:T(8,128)S(1)}, u32[]{:S(2)}, u32[]{:S(2)}) %collective-permute-start.89) | collective-permute-done | bytes 141344 | tf_op jit(solution)/shard_map/ppermute | solution.py:85
  1620.9 20.1 %collective-permute-done.79 = bf16[1024,512]{1,0:T(8,128)(2,1)S(1)} collective-permute-done((bf16[1024,512]{1,0:T(8,128)(2,1)S(1)}, bf16[1024,512]{1,0:T(8,128)(2,1)S(1)}, u32[]{:S(2)}, u32[]{:S(2)}) %collective-permute-start.79) | collective-permute-done | bytes 1048608 | tf_op jit(solution)/shard_map/ppermute | solution.py:85
  1642.9 27.6 %weight_down_grads.1 = f32[8,256,2048]{2,1,0:T(8,128)} custom-call(s32[8]{0:T(128)} %stack.90.where_ref, bf16[2,2,1280,512]{3,2,1,0:T(8,128)(2,1)} %pick_rows.8.refs_6_.refs_0_, bf16[2,2,1280,512]{3,2,1,0:T(8,128)(2,1)} %collective-permute-done.27.refs_7_.refs_1_, bf16[2,2,1280,512]{3,2,1,0:T(8,128)(2,1)} %pick_rows.14.refs_6_.refs_2_, ...), custom_call_target="tpu_custom_call" | custom-call | flops 1000000 | bytes 1000000 | tf_op jit(solution)/shard_map/weight_down_grads/pallas_call | solution.py:507
  (464 shorter events, 661.2 us)
Async XLA Ops:
  74.0 78.8 %collective-permute-start.10 = (bf16[1024,512]{1,0:T(8,128)(2,1)}, bf16[1024,512]{1,0:T(8,128)(2,1)}, u32[]{:S(2)}, u32[]{:S(2)}) collective-permute-start(bf16[1024,512]{1,0:T(8,128)(2,1)} %convert_element_type.253.refs_2_), channel_id=1, source_target_pairs={{0,24},{1,25},{2,26},{3,27},{4,28},{5,29},{6,30},{7,31},{8,16},{9,... | collective-permute-start | bytes 3145736 | tf_op jit(solution)/shard_map/ppermute | solution.py:85
  74.0 83.2 %collective-permute-start.11 = (bf16[1024,512]{1,0:T(8,128)(2,1)}, bf16[1024,512]{1,0:T(8,128)(2,1)}, u32[]{:S(2)}, u32[]{:S(2)}) collective-permute-start(bf16[1024,512]{1,0:T(8,128)(2,1)} %convert_element_type.253.refs_2_), channel_id=1, source_target_pairs={{0,8},{1,9},{2,10},{3,11},{4,12},{5,13},{6,14},{7,15},{8,0},{9,1},... | collective-permute-start | bytes 3145736 | tf_op jit(solution)/shard_map/ppermute | solution.py:85
  169.7 65.9 %collective-permute-start.19 = (bf16[1024,512]{1,0:T(8,128)(2,1)}, bf16[1024,512]{1,0:T(8,128)(2,1)S(1)}, u32[]{:S(2)}, u32[]{:S(2)}) collective-permute-start(bf16[1024,512]{1,0:T(8,128)(2,1)} %collective-permute-done.2.refs_2_), channel_id=1, source_target_pairs={{0,2},{1,3},{2,0},{3,1},{4,6},{5,7},{6,4},{7,5},{8,10},{9,11},{10,... | collective-permute-start | bytes 3145736 | tf_op jit(solution)/shard_map/ppermute | solution.py:85
  192.2 57.6 %collective-permute-start.20 = (bf16[1024,512]{1,0:T(8,128)(2,1)S(1)}, bf16[1024,512]{1,0:T(8,128)(2,1)}, u32[]{:S(2)}, u32[]{:S(2)}) collective-permute-start(bf16[1024,512]{1,0:T(8,128)(2,1)S(1)} %collective-permute-done.18.refs_3_), channel_id=1, source_target_pairs={{0,4},{1,5},{2,6},{3,7},{4,0},{5,1},{6,2},{7,3},{8,12},{9,13},{10,... | collective-permute-start | bytes 3145736 | tf_op jit(solution)/shard_map/ppermute | solution.py:85
  260.0 98.7 %collective-permute-start.26 = (bf16[2,2,1280,512]{3,2,1,0:T(8,128)(2,1)}, bf16[2,2,1280,512]{3,2,1,0:T(8,128)(2,1)}, u32[]{:S(2)}, u32[]{:S(2)}) collective-permute-start(bf16[2,2,1280,512]{3,2,1,0:T(8,128)(2,1)} %pick_rows.9.refs_4_.refs_0_), channel_id=1, source_target_pairs={{0,1},{1,0},{2,3},{3,2},{4,5},{5,4},{6,7},{7,6},{8,9},{9,8},{10,11... | collective-permute-start | bytes 15728648 | tf_op jit(solution)/shard_map/ppermute | solution.py:85
  260.0 101.6 %collective-permute-start.27 = (bf16[2,2,1280,512]{3,2,1,0:T(8,128)(2,1)}, bf16[2,2,1280,512]{3,2,1,0:T(8,128)(2,1)}, u32[]{:S(2)}, u32[]{:S(2)}) collective-permute-start(bf16[2,2,1280,512]{3,2,1,0:T(8,128)(2,1)} %pick_rows.8.refs_6_.refs_0_), channel_id=1, source_target_pairs={{0,1},{1,0},{2,3},{3,2},{4,5},{5,4},{6,7},{7,6},{8,9},{9,8},{10,11... | collective-permute-start | bytes 15728648 | tf_op jit(solution)/shard_map/ppermute | solution.py:85
  328.3 135.3 %collective-permute-start.29 = (bf16[2,2,1280,512]{3,2,1,0:T(8,128)(2,1)}, bf16[2,2,1280,512]{3,2,1,0:T(8,128)(2,1)}, u32[]{:S(2)}, u32[]{:S(2)}) collective-permute-start(bf16[2,2,1280,512]{3,2,1,0:T(8,128)(2,1)} %pick_rows.10.refs_6_.refs_4_), channel_id=1, source_target_pairs={{0,1},{1,0},{2,3},{3,2},{4,5},{5,4},{6,7},{7,6},{8,9},{9,8},{10,11... | collective-permute-start | bytes 15728648 | tf_op jit(solution)/shard_map/ppermute | solution.py:85
  390.1 73.5 %collective-permute-start.33 = (bf16[2,2,1280,512]{3,2,1,0:T(8,128)(2,1)}, bf16[2,2,1280,512]{3,2,1,0:T(8,128)(2,1)S(1)}, u32[]{:S(2)}, u32[]{:S(2)}) collective-permute-start(bf16[2,2,1280,512]{3,2,1,0:T(8,128)(2,1)} %get-tuple-element.142), channel_id=1, source_target_pairs={{0,1},{1,0},{2,3},{3,2},{4,5},{5,4},{6,7},{7,6},{8,9},{9,8},{10,11... | collective-permute-start | bytes 15728648 | tf_op jit(solution)/shard_map/ppermute | solution.py:85
  592.2 70.8 %collective-permute-start.44 = (bf16[2,2,1280,512]{3,2,1,0:T(8,128)(2,1)}, bf16[2,2,1280,512]{3,2,1,0:T(8,128)(2,1)}, u32[]{:S(2)}, u32[]{:S(2)}) collective-permute-start(bf16[2,2,1280,512]{3,2,1,0:T(8,128)(2,1)} %pick_rows.13.refs_4_.refs_6_), channel_id=1, source_target_pairs={{0,1},{1,0},{2,3},{3,2},{4,5},{5,4},{6,7},{7,6},{8,9},{9,8},{10,11... | collective-permute-start | bytes 15728648 | tf_op jit(solution)/shard_map/ppermute | solution.py:85
  594.7 68.3 %collective-permute-start.46 = (bf16[1024,512]{1,0:T(8,128)(2,1)}, bf16[1024,512]{1,0:T(8,128)(2,1)S(1)}, u32[]{:S(2)}, u32[]{:S(2)}) collective-permute-start(bf16[1024,512]{1,0:T(8,128)(2,1)} %bitcast.210), channel_id=1, source_target_pairs={{0,4},{1,5},{2,6},{3,7},{4,0},{5,1},{6,2},{7,3},{8,12},{9,13},{10,... | collective-permute-start | bytes 3145736 | tf_op jit(solution)/shard_map/ppermute | solution.py:85
  756.2 88.2 %collective-permute-start.54 = (bf16[2,2,1280,512]{3,2,1,0:T(8,128)(2,1)}, bf16[2,2,1280,512]{3,2,1,0:T(8,128)(2,1)}, u32[]{:S(2)}, u32[]{:S(2)}) collective-permute-start(bf16[2,2,1280,512]{3,2,1,0:T(8,128)(2,1)} %get-tuple-element.172), channel_id=1, source_target_pairs={{0,1},{1,0},{2,3},{3,2},{4,5},{5,4},{6,7},{7,6},{8,9},{9,8},{10,11... | collective-permute-start | bytes 15728648 | tf_op jit(solution)/shard_map/ppermute | solution.py:85
  760.2 68.4 %collective-permute-start.52 = (bf16[1024,512]{1,0:T(8,128)(2,1)S(1)}, bf16[1024,512]{1,0:T(8,128)(2,1)}, u32[]{:S(2)}, u32[]{:S(2)}) collective-permute-start(bf16[1024,512]{1,0:T(8,128)(2,1)S(1)} %bitcast.208), channel_id=1, source_target_pairs={{0,2},{1,3},{2,0},{3,1},{4,6},{5,7},{6,4},{7,5},{8,10},{9,11},{10,... | collective-permute-start | bytes 3145736 | tf_op jit(solution)/shard_map/ppermute | solution.py:85
  760.7 97.7 %collective-permute-start.55 = (bf16[1024,512]{1,0:T(8,128)(2,1)}, bf16[1024,512]{1,0:T(8,128)(2,1)}, u32[]{:S(2)}, u32[]{:S(2)}) collective-permute-start(bf16[1024,512]{1,0:T(8,128)(2,1)} %bitcast.30), channel_id=1, source_target_pairs={{0,4},{1,5},{2,6},{3,7},{4,0},{5,1},{6,2},{7,3},{8,12},{9,13},{10,... | collective-permute-start | bytes 3145736 | tf_op jit(solution)/shard_map/ppermute | solution.py:85
  784.2 74.3 %collective-permute-start.56 = (bf16[1024,512]{1,0:T(8,128)(2,1)}, bf16[1024,512]{1,0:T(8,128)(2,1)}, u32[]{:S(2)}, u32[]{:S(2)}) collective-permute-start(bf16[1024,512]{1,0:T(8,128)(2,1)} %bitcast.31), channel_id=1, source_target_pairs={{0,4},{1,5},{2,6},{3,7},{4,0},{5,1},{6,2},{7,3},{8,12},{9,13},{10,... | collective-permute-start | bytes 3145736 | tf_op jit(solution)/shard_map/ppermute | solution.py:85
  844.4 183.6 %collective-permute-start.57 = (bf16[4,2,1280,512]{3,2,1,0:T(8,128)(2,1)}, bf16[4,2,1280,512]{3,2,1,0:T(8,128)(2,1)}, u32[]{:S(2)}, u32[]{:S(2)}) collective-permute-start(bf16[4,2,1280,512]{3,2,1,0:T(8,128)(2,1)} %get-tuple-element.180), channel_id=1, source_target_pairs={{0,1},{1,0},{2,3},{3,2},{4,5},{5,4},{6,7},{7,6},{8,9},{9,8},{10,11... | collective-permute-start | bytes 31457288 | tf_op jit(solution)/shard_map/ppermute | solution.py:85
  874.2 179.9 %collective-permute-start.65 = (bf16[4,2,1280,512]{3,2,1,0:T(8,128)(2,1)}, bf16[4,2,1280,512]{3,2,1,0:T(8,128)(2,1)}, u32[]{:S(2)}, u32[]{:S(2)}) collective-permute-start(bf16[4,2,1280,512]{3,2,1,0:T(8,128)(2,1)} %get-tuple-element.195), channel_id=1, source_target_pairs={{0,1},{1,0},{2,3},{3,2},{4,5},{5,4},{6,7},{7,6},{8,9},{9,8},{10,11... | collective-permute-start | bytes 31457288 | tf_op jit(solution)/shard_map/ppermute | solution.py:85
  903.0 94.5 %collective-permute-start.61 = (bf16[1024,512]{1,0:T(8,128)(2,1)}, bf16[1024,512]{1,0:T(8,128)(2,1)}, u32[]{:S(2)}, u32[]{:S(2)}) collective-permute-start(bf16[1024,512]{1,0:T(8,128)(2,1)} %fusion.31), channel_id=1, source_target_pairs={{0,4},{1,5},{2,6},{3,7},{4,0},{5,1},{6,2},{7,3},{8,12},{9,13},{10,... | collective-permute-start | bytes 3145736 | tf_op jit(solution)/shard_map/ppermute | solution.py:85
  923.6 79.1 %collective-permute-start.67 = (bf16[1024,512]{1,0:T(8,128)(2,1)}, bf16[1024,512]{1,0:T(8,128)(2,1)}, u32[]{:S(2)}, u32[]{:S(2)}) collective-permute-start(bf16[1024,512]{1,0:T(8,128)(2,1)} %fusion.27), channel_id=1, source_target_pairs={{0,16},{1,17},{2,18},{3,19},{4,20},{5,21},{6,22},{7,23},{8,24},{9,... | collective-permute-start | bytes 3145736 | tf_op jit(solution)/shard_map/ppermute | solution.py:85
  927.7 69.8 %all-to-all-start.1 = ((f32[8,8,1024]{2,1,0:T(8,128)}), f32[8,8,1024]{2,1,0:T(8,128)S(1)}, u32[]{:S(2)}, u32[]{:S(2)}) async-start(f32[8,8,1024]{2,1,0:T(8,128)} %gather_fusion), calls=%async_computation.1 | async-start | bytes 524288 | tf_op jit(solution)/shard_map/all_to_all | solution.py:898
  932.3 356.8 %reduce-scatter.2.cloned.1.call-start = ((), (), s32[]{:S(2)}) async-start(), calls=%async_computation.4 | async-start | bytes 7077888 | tf_op jit(solution)/shard_map/reduce_scatter | solution.py:934
  945.2 76.0 %collective-permute-start.68 = (bf16[1024,512]{1,0:T(8,128)(2,1)}, bf16[1024,512]{1,0:T(8,128)(2,1)}, u32[]{:S(2)}, u32[]{:S(2)}) collective-permute-start(bf16[1024,512]{1,0:T(8,128)(2,1)} %fusion.25), channel_id=1, source_target_pairs={{0,24},{1,25},{2,26},{3,27},{4,28},{5,29},{6,30},{7,31},{8,16},{9,... | collective-permute-start | bytes 3145736 | tf_op jit(solution)/shard_map/ppermute | solution.py:85
  1159.4 239.6 %all-reduce.3.cloned.1.call-start = ((), (), s32[]{:S(2)}) async-start(), calls=%async_computation.3 | async-start | bytes 4194304 | tf_op jit(solution)/shard_map/psum | solution.py:933
  1160.1 510.4 %all-gather.4.cloned.1.call-start = ((), (), s32[]{:S(2)}) async-start(), calls=%async_computation.5 | async-start | bytes 7077888 | tf_op jit(solution)/shard_map/all_gather | solution.py:946
  1165.6 147.1 %collective-permute-start.64 = (bf16[2,1024,512]{2,1,0:T(8,128)(2,1)}, bf16[2,1024,512]{2,1,0:T(8,128)(2,1)}, u32[]{:S(2)}, u32[]{:S(2)}) collective-permute-start(bf16[2,1024,512]{2,1,0:T(8,128)(2,1)} %get-tuple-element.194), channel_id=1, source_target_pairs={{0,4},{1,5},{2,6},{3,7},{4,0},{5,1},{6,2},{7,3},{8,12},{9,13},{10,... | collective-permute-start | bytes 6291464 | tf_op jit(solution)/shard_map/ppermute | solution.py:85
  1302.1 101.0 %collective-permute-start.63 = (bf16[2,1024,512]{2,1,0:T(8,128)(2,1)}, bf16[2,1024,512]{2,1,0:T(8,128)(2,1)}, u32[]{:S(2)}, u32[]{:S(2)}) collective-permute-start(bf16[2,1024,512]{2,1,0:T(8,128)(2,1)} %get-tuple-element.190), channel_id=1, source_target_pairs={{0,4},{1,5},{2,6},{3,7},{4,0},{5,1},{6,2},{7,3},{8,12},{9,13},{10,... | collective-permute-start | bytes 6291464 | tf_op jit(solution)/shard_map/ppermute | solution.py:85
  1308.0 138.4 %collective-permute-start.82 = (bf16[1024,512]{1,0:T(8,128)(2,1)}, bf16[1024,512]{1,0:T(8,128)(2,1)S(1)}, u32[]{:S(2)}, u32[]{:S(2)}) collective-permute-start(bf16[1024,512]{1,0:T(8,128)(2,1)} %fusion.46), channel_id=1, source_target_pairs={{0,1},{1,0},{2,3},{3,2},{4,5},{5,4},{6,7},{7,6},{8,9},{9,8},{10,11... | collective-permute-start | bytes 3145736 | tf_op jit(solution)/shard_map/ppermute | solution.py:85
  1312.2 134.2 %collective-permute-start.84 = (bf16[1024,512]{1,0:T(8,128)(2,1)}, bf16[1024,512]{1,0:T(8,128)(2,1)}, u32[]{:S(2)}, u32[]{:S(2)}) collective-permute-start(bf16[1024,512]{1,0:T(8,128)(2,1)} %add_convert_fusion.3), channel_id=1, source_target_pairs={{0,2},{1,3},{2,0},{3,1},{4,6},{5,7},{6,4},{7,5},{8,10},{9,11},{10,... | collective-permute-start | bytes 3145736 | tf_op jit(solution)/shard_map/ppermute | solution.py:85
  1316.3 294.6 %collective-permute-start.74 = (bf16[2,1024,512]{2,1,0:T(8,128)(2,1)}, bf16[2,1024,512]{2,1,0:T(8,128)(2,1)}, u32[]{:S(2)}, u32[]{:S(2)}) collective-permute-start(bf16[2,1024,512]{2,1,0:T(8,128)(2,1)} %add_convert_fusion.2), channel_id=1, source_target_pairs={{0,2},{1,3},{2,0},{3,1},{4,6},{5,7},{6,4},{7,5},{8,10},{9,11},{10,... | collective-permute-start | bytes 6291464 | tf_op jit(solution)/shard_map/ppermute | solution.py:85
  1348.3 129.9 %collective-permute-start.77 = (bf16[2,1024,512]{2,1,0:T(8,128)(2,1)}, bf16[2,1024,512]{2,1,0:T(8,128)(2,1)}, u32[]{:S(2)}, u32[]{:S(2)}) collective-permute-start(bf16[2,1024,512]{2,1,0:T(8,128)(2,1)} %get-tuple-element.214), channel_id=1, source_target_pairs={{0,2},{1,3},{2,0},{3,1},{4,6},{5,7},{6,4},{7,5},{8,10},{9,11},{10,... | collective-permute-start | bytes 6291464 | tf_op jit(solution)/shard_map/ppermute | solution.py:85
  1403.1 75.1 %collective-permute-start.76 = (bf16[2,1024,512]{2,1,0:T(8,128)(2,1)}, bf16[2,1024,512]{2,1,0:T(8,128)(2,1)}, u32[]{:S(2)}, u32[]{:S(2)}) collective-permute-start(bf16[2,1024,512]{2,1,0:T(8,128)(2,1)} %add_convert_fusion.1), channel_id=1, source_target_pairs={{0,4},{1,5},{2,6},{3,7},{4,0},{5,1},{6,2},{7,3},{8,12},{9,13},{10,... | collective-permute-start | bytes 6291464 | tf_op jit(solution)/shard_map/ppermute | solution.py:85
  1482.1 128.7 %collective-permute-start.78 = (bf16[2,1024,512]{2,1,0:T(8,128)(2,1)S(1)}, bf16[2,1024,512]{2,1,0:T(8,128)(2,1)S(1)}, u32[]{:S(2)}, u32[]{:S(2)}) collective-permute-start(bf16[2,1024,512]{2,1,0:T(8,128)(2,1)S(1)} %add_convert_fusion), channel_id=1, source_target_pairs={{0,16},{1,17},{2,18},{3,19},{4,20},{5,21},{6,22},{7,23},{8,24},{9,... | collective-permute-start | bytes 6291464 | tf_op jit(solution)/shard_map/ppermute | solution.py:85
  1487.0 114.3 %collective-permute-start.89 = (f32[69,512]{1,0:T(8,128)S(1)}, f32[69,512]{1,0:T(8,128)S(1)}, u32[]{:S(2)}, u32[]{:S(2)}) collective-permute-start(f32[69,512]{1,0:T(8,128)S(1)} %pad_maximum_fusion.5), channel_id=1, source_target_pairs={{0,16},{1,17},{2,18},{3,19},{4,20},{5,21},{6,22},{7,23},{8,24},{9,... | collective-permute-start | bytes 423944 | tf_op jit(solution)/shard_map/ppermute | solution.py:85
  (142 other events, 3710.0 us)
Sparse Core Ops, SparseCore 0:
  1159.5 129.6 reduce-scatter.1
  1292.8 106.1 all-reduce.2
  1401.2 164.3 all-gather.3

commit v4 on v3

--- a/solution.py
+++ b/solution.py
@@ -18,36 +18,34 @@
 F32 = jnp.float32
 BF16 = jnp.bfloat16
 VMEM = 60 * 1024 * 1024
+WEIGHT = 16
 ORDER = (0, 2, 3, 1)
 ODD = (1, 2)
 DUE = {
-    "attend": ("cx0", "cy0"),
-    "mmB": ("cz2",),
-    "addB": ("cd0", "b0"),
-    "cot0": ("b1",),
-    "sums": ("by", "cz3"),
-    "normed": ("cz1", "sc0"),
-    "row0": ("cx1", "cy1", "nx0", "cx2", "ny0", "cy2", "nd0"),
-    "cot2": ("cy3", "nz3", "cd2"),
-    "exp0": ("nz2", "cx3", "sr0"),
-    "row2": ("cd3", "sc2", "ny3", "nx2", "ny2", "sg0", "nd2"),
-    "place0": ("nz1",),
-    "cot3": ("cd1", "sr2", "nd3"),
-    "exp2": ("nx3",),
-    "row3": ("ny1", "sc3"),
-    "place2": ("nx1", "sg2"),
-    "cot1": ("sr3", "ed0", "ex0"),
-    "row1": ("sc1", "nd1"),
-    "place3": ("sg3",),
-    "exp1": ("sr1",),
-    "down0": ("ey2", "ed2", "ey0"),
-    "place1": ("sg1",),
-    "down1": ("ed3", "ex3"),
-    "pd0": ("sd0", "ex2"),
-    "pd1": ("sd1",),
-    "weight": ("hs", "gd0", "gx0", "gd1"),
-    "weight_down": ("gy0", "gy1", "gx1"),
+    "attended": ("cx0", "cy0"),
+    "normed": ("cz2", "cd0", "cx2"),
+    "row0": ("cz3", "cy2"),
+    "cot2": ("nz2",),
+    "exp0": ("cx3",),
+    "row2": ("sc2", "cy3"),
+    "cot3": ("sg0",),
+    "place0": ("sr2",),
+    "exp2": ("sc3",),
+    "cot1": ("sg2",),
+    "place2": ("sr3", "ed0"),
+    "exp3": ("sc1",),
+    "place3": ("ex0", "ey0", "ed2"),
+    "down1": ("ex2", "ey2", "ed3"),
+    "pd0": ("ed1", "sd0"),
+    "weight": ("ex3", "ey3", "ex1", "ey1"),
+    "weight_down": ("hs", "gd0", "gd1"),
 }
+
+
+def cost(flops, bytes_accessed, transcendentals):
+    return pl.CostEstimate(
+        flops=flops * WEIGHT, bytes_accessed=bytes_accessed * WEIGHT, transcendentals=transcendentals * WEIGHT
+    )
 
 
 def matmul(left, right):
@@ -109,7 +107,10 @@
             owners = places
             mine = [y * 2 + core for y in range(lax.axis_size("tensor") // 2)]
         theirs = [m ^ 1 for m in mine]
-        found.append(jnp.stack([jnp.asarray(v, jnp.int32) for v in places + owners + mine + theirs]))
+        rows = [m // 2 for m in mine]
+        found.append(
+            jnp.stack([jnp.asarray(v, jnp.int32) for v in places + owners + mine + theirs + rows])
+        )
     return found
 
 
@@ -126,14 +127,16 @@
     return [[y * 2 + c for y in range(count // 2)] for c in range(2)]
 
 
+def gather_all(own):
+    owners, parts = lax.axis_size("expert"), lax.axis_size("tensor")
+    groups = [[e * parts + t for e in range(owners) for t in range(c, parts, 2)] for c in range(2)]
+    full = lax.all_gather(own, BOTH, axis_index_groups=groups)
+    return full.reshape(owners, parts // 2, *own.shape)
+
+
 def gather_slots(own, tag, seen):
     if not is_cube():
-        blocks = lax.all_gather(own, "expert")
-        full = lax.all_gather(blocks, "tensor", axis_index_groups=same_core())
-        return [
-            [[full[y, k * NB + b] for y in range(full.shape[0])] for b in range(NB)]
-            for k in range(full.shape[1] // NB)
-        ]
+        return [gather_all(own)] * (lax.axis_size("expert") // NB)
     slots = []
     for k in range(4):
         block = send(own, dz=k) if k else own
@@ -150,16 +153,15 @@
     return sum(t.astype(F32) for t in terms)
 
 
-def scatter_plane(parts, odd, hold=()):
+def scatter_plane(parts, odd):
     near, over_y, over_x, far = parts[0][0], parts[0][1], parts[1][0], parts[1][1]
     if odd:
         far = send(far, dy=1)
-        from_y = send(over_y, dy=1)
-        from_x = send(after(added(over_x, far).astype(BF16), *hold), dx=1)
+        over_x, over_y = added(over_x, far).astype(BF16), after(over_y, far)
     else:
         far = send(far, dx=1)
-        from_x = send(over_x, dx=1)
-        from_y = send(after(added(over_y, far).astype(BF16), *hold), dy=1)
+        over_x, over_y = after(over_x, far), added(over_y, far).astype(BF16)
+    from_x, from_y = send(over_x, dx=1), send(over_y, dy=1)
     return added(near, from_x, from_y), {"d": far, "x": from_x, "y": from_y}
 
 
@@ -171,12 +173,12 @@
     return lax.psum_scatter(mine, "expert", scatter_dimension=0).astype(F32)
 
 
-def scatter_pairs(pairs, hold, seen):
+def scatter_pairs(pairs, seen):
     if not is_cube():
         return scatter_all(
             [[[a[i] for a in b] for b in pair] for pair in pairs for i in range(pair[0][0].shape[0])]
         )
-    (low, low_sent), (high, high_sent) = (scatter_plane(p, k, hold) for k, p in enumerate(pairs))
+    (low, low_sent), (high, high_sent) = (scatter_plane(p, True) for p in pairs)
     seen.update({"g" + link + "0": value for link, value in low_sent.items()})
     seen.update({"g" + link + "1": value for link, value in high_sent.items()})
     total = low + send(high.astype(BF16), dz=2).astype(F32)
@@ -252,11 +254,24 @@
 
 
 def pick_rows(where, pos, blocks):
-    slices = len(blocks[0])
-    tokens, width = blocks[0][0].shape
     held = pos.shape[1]
     group = 2
-    flat = [a for b in blocks for a in b]
+    if isinstance(blocks, list):
+        slices = len(blocks[0])
+        flat = [a for b in blocks for a in b]
+        tokens, width = flat[0].shape
+        specs = [pl.BlockSpec((tokens, width), lambda i, where: (0, 0)) for _ in flat]
+    else:
+        slices, tokens, width = blocks.shape[1:]
+        flat = [blocks] * (NB * slices)
+
+        def part_spec(b, y):
+            return pl.BlockSpec(
+                (None, None, tokens, width),
+                lambda i, where: (where[NB + b], where[2 * NB + 2 * slices + y], 0, 0),
+            )
+
+        specs = [part_spec(b, y) for b in range(NB) for y in range(slices)]
 
     def block_spec(b):
         return pl.BlockSpec((1, held, tokens), lambda i, where: (where[b], 0, 0))
@@ -267,7 +282,7 @@
             num_scalar_prefetch=1,
             grid=(held // group,),
             in_specs=[block_spec(b) for b in range(NB)]
-            + [pl.BlockSpec((tokens, width), lambda i, where: (0, 0)) for _ in flat],
+            + specs,
             out_specs=pl.BlockSpec(
                 (NB, slices, group * CAP, width), lambda i, where: (0, 0, i, 0)
             ),
@@ -275,7 +290,7 @@
         ),
         out_shape=jax.ShapeDtypeStruct((NB, slices, held * CAP, width), BF16),
         compiler_params=pltpu.CompilerParams(vmem_limit_bytes=VMEM),
-        cost_estimate=pl.CostEstimate(
+        cost_estimate=cost(
             flops=2 * NB * slices * held * CAP * tokens * width,
             bytes_accessed=2 * NB * slices * (held * CAP + tokens) * width,
             transcendentals=0,
@@ -362,7 +377,7 @@
         out_shape=[hidden_shape] * 3
         + [jax.ShapeDtypeStruct((held, NB, tokens), F32), rows_shape, rows_shape],
         compiler_params=pltpu.CompilerParams(vmem_limit_bytes=VMEM),
-        cost_estimate=pl.CostEstimate(
+        cost_estimate=cost(
             flops=10 * NB * held * CAP * depth * ff,
             bytes_accessed=6 * held * depth * ff + 6 * NB * held * CAP * depth,
             transcendentals=NB * held * CAP * ff,
@@ -399,7 +414,7 @@
         ),
         out_shape=[rows_shape, rows_shape],
         compiler_params=pltpu.CompilerParams(vmem_limit_bytes=VMEM),
-        cost_estimate=pl.CostEstimate(
+        cost_estimate=cost(
             flops=2 * slots * NB * held * CAP * depth * ff,
             bytes_accessed=2 * held * depth * ff + 2 * slots * NB * held * CAP * depth,
             transcendentals=0,
@@ -459,7 +474,7 @@
         ),
         out_shape=[jax.ShapeDtypeStruct((slots, tokens, width), BF16)] * (NB * slices),
         compiler_params=pltpu.CompilerParams(vmem_limit_bytes=VMEM),
-        cost_estimate=pl.CostEstimate(
+        cost_estimate=cost(
             flops=2 * NB * slots * slices * count * tokens * width,
             bytes_accessed=2 * NB * slots * slices * (2 * count + tokens) * width,
             transcendentals=0,
@@ -514,7 +529,7 @@
         ),
         out_shape=[jax.ShapeDtypeStruct((held, *o), F32) for o in outs],
         compiler_params=pltpu.CompilerParams(vmem_limit_bytes=VMEM),
-        cost_estimate=pl.CostEstimate(flops=10**6, bytes_accessed=10**6, transcendentals=0),
+        cost_estimate=cost(flops=10**10, bytes_accessed=10**6, transcendentals=0),
         name=name,
     )(where, *[a for pair in rows for a in pair], *hiddens)
 
@@ -562,7 +577,7 @@
         ]
         + [jax.ShapeDtypeStruct((tokens, columns), t) for t in (F32, F32, BF16, BF16, BF16)],
         compiler_params=pltpu.CompilerParams(vmem_limit_bytes=VMEM),
-        cost_estimate=pl.CostEstimate(
+        cost_estimate=cost(
             flops=6 * tokens * depth * columns,
             bytes_accessed=4 * tokens * depth + 6 * depth * columns + 14 * tokens * columns,
             transcendentals=0,
@@ -633,7 +648,7 @@
             jax.ShapeDtypeStruct((sequences * heads, 8, HD), F32),
         ],
         compiler_params=pltpu.CompilerParams(vmem_limit_bytes=VMEM),
-        cost_estimate=pl.CostEstimate(
+        cost_estimate=cost(
             flops=4 * tokens * LENGTH * columns,
             bytes_accessed=8 * tokens * columns,
             transcendentals=tokens * heads * LENGTH,
@@ -699,7 +714,7 @@
         out_shape=[jax.ShapeDtypeStruct((tokens, columns), BF16)] * 3
         + [jax.ShapeDtypeStruct((sequences, 1, columns), F32)] * 2,
         compiler_params=pltpu.CompilerParams(vmem_limit_bytes=VMEM),
-        cost_estimate=pl.CostEstimate(
+        cost_estimate=cost(
             flops=10 * tokens * LENGTH * columns,
             bytes_accessed=22 * tokens * columns,
             transcendentals=tokens * heads * LENGTH,
@@ -712,17 +727,18 @@
 
 
 def expert_steps(slots):
-    order = ORDER if is_cube() else range(slots)
-    steps = [("row", order[0]), ("cot", order[1])]
+    order = list(ORDER) if is_cube() else list(range(slots))
+    steps = [("cot", order[0]), ("row", order[0]), ("cot", order[1]), ("exp", order[0])]
     for i, k in enumerate(order):
-        steps.append(("exp", k))
         if i + 1 < slots:
             steps.append(("row", order[i + 1]))
         else:
             steps.append(("down", 0))
-        steps.append(("place", k))
         if i + 2 < slots:
             steps.append(("cot", order[i + 2]))
+        steps.append(("place", k))
+        if i + 1 < slots:
+            steps.append(("exp", order[i + 1]))
     return steps
 
 
@@ -770,7 +786,6 @@
     all_routes = gather_routes(routes.T)
     cot_slots = gather_slots(cotangent.astype(BF16), "c", seen)
     order = tensor_order()
-    first_slot = ORDER[0] if is_cube() else 0
 
     held_ids = owner * experts_here + jnp.arange(experts_here, dtype=jnp.int32)
     chosen = jnp.any(all_routes[:, None] == held_ids[None, :, None, None], axis=2)
@@ -790,17 +805,11 @@
     )
     pieces = jnp.concatenate([piece_start, piece_length], axis=1).reshape(-1)
     attended, logs, tops = attend(
-        after(pieces, values, *due("attend", seen)), queries, keys, values, scale
+        after(pieces, values, all_routes), queries, keys, values, scale
     )
     head_top = jnp.max(tops[:, 0, 0].reshape(sequences, heads_here), axis=0)
-    attended = after(attended, *due("mmB", seen))
+    attended = after(attended, *due("attended", seen))
     branch = tensor_scatter(partial(matmul, attended), output_pieces, "b", seen)
-    first_cot = pick_rows(
-        after(where[first_slot], attended, *due("addB", seen), *due("cot" + str(first_slot), seen)),
-        pos,
-        cot_slots[first_slot],
-    )
-    branch = after(branch, first_cot, *due("sums", seen))
     residual = own_columns(inputs).astype(F32) + branch
     gain_slice = own_columns(moe_gain)
     router_slice = lax.dynamic_slice_in_dim(w_router, column, slice_width, 0)
@@ -836,9 +845,7 @@
 
     rows, cots, back, sums = [None] * slots, [None] * slots, [None] * slots, [None] * slots
     scaled, gate_grads, up_grads, probs = [None] * slots, [None] * slots, [None] * slots, [None] * slots
-    last = first_cot
-    cots[first_slot] = (first_cot, core_swap(first_cot))
-    seen["sc" + str(first_slot)] = cots[first_slot][1]
+    last = normed_m
     downs = {}
 
     def turn(name, k):
@@ -876,19 +883,22 @@
             if is_cube():
                 sums[k], sent = scatter_plane(back[k], k in ODD)
                 if k:
-                    sent["z"] = send(sums[k].astype(BF16), dz=k)
-                    sums[k] = sent["z"].astype(F32)
+                    sums[k] = sent["z"] = send(sums[k].astype(BF16), dz=k)
                 seen.update({"e" + link + str(k): value for link, value in sent.items()})
     for k in range(1, slots // 2):
         last = lower(k)
-    pairs = []
-    for k in range(slots // 2):
-        now = turn("pd" + str(k), 2 * k)
-        placed = place_rows([now, where[2 * k + 1]], at, *downs[k])
-        last = placed[0][0]
-        pairs.append(placed)
+    pairs = [place_rows([turn("pd0", 0), where[1]], at, *downs[0])]
+    last = pairs[0][0][0]
+    grad_gate, grad_up = weight_grads(
+        weight_kernel,
+        turn("weight", 0),
+        rows,
+        gate_grads + up_grads,
+        [w_gate.shape[1:]] * 2,
+        "weight_grads",
+    )
     if is_cube():
-        expert_path = sum(after(s, last) for s in sums)
+        expert_path = added(*[after(s, grad_gate) for s in sums])
     else:
         expert_path = scatter_all(back)
 
@@ -915,16 +925,18 @@
     branch_pieces = tensor_gather(grad_residual.astype(BF16))
     grad_branch = jnp.concatenate(branch_pieces, axis=1)
 
+    for k in range(1, slots // 2):
+        now = after(where[2 * k], branch_pieces[0])
+        pairs.append(place_rows([now, where[2 * k + 1]], at, *downs[k]))
+    last = pairs[-1][0][0]
     if is_cube():
-        ends = [seen["e" + link + str(ORDER[i])] for i in (-2, -1) for link in "xyd"]
-        pairs[0] = [[after(a, *ends) for a in b] for b in pairs[0]]
-        pairs[1] = [[after(a, branch_pieces[1]) for a in b] for b in pairs[1]]
-    mixture = scatter_pairs(pairs, branch_pieces[1:2], seen)
+        pairs = [[[after(a, branch_pieces[1]) for a in b] for b in pair] for pair in pairs]
+    mixture = scatter_pairs(pairs, seen)
     out = residual + mixture
 
     grad_output = matmul_tn(attended, grad_branch).astype(BF16)
     grad_attended = matmul_nt(grad_branch, jnp.concatenate(output_pieces, axis=1)).astype(BF16)
-    grad_attended = after(grad_attended, grad_output)
+    grad_attended = after(grad_attended, grad_output, last)
     grad_query_raw, grad_key_raw, grad_v, grad_query_gain, grad_key_gain = attend_back(
         pieces, queries, keys, values, grad_attended, logs, query_raw, key_raw, query_gain, key_gain, scale
     )
@@ -936,16 +948,13 @@
     weights = jnp.concatenate([w_query, w_key, w_value], axis=1)
     weight_pieces = [lax.dynamic_slice_in_dim(weights, o * slice_width, slice_width, 0) for o in order]
     grad_normed_a = tensor_scatter(partial(matmul_nt, grad_raw), weight_pieces, "h", seen)
-    now = after(where[0], sum_output, *due("weight", seen))
-    grad_gate, grad_up = weight_grads(
-        weight_kernel, now, rows, gate_grads + up_grads, [w_gate.shape[1:]] * 2, "weight_grads"
-    )
+    now = after(where[0], *due("weight_down", seen))
     (grad_down,) = weight_grads(
-        weight_down_kernel, after(now, grad_gate, sum_three, *due("weight_down", seen)), cots, scaled, [w_down.shape[1:]], "weight_down_grads"
+        weight_down_kernel, now, cots, scaled, [w_down.shape[1:]], "weight_down_grads"
     )
     sum_three = lax.all_gather(sum_three, "expert", tiled=True)
     sum_query, sum_key, sum_value = jnp.split(sum_three.astype(F32), 3, axis=1)
-    grad_normed_a = after(grad_normed_a, grad_gate)
+    grad_normed_a = after(grad_normed_a, grad_down)
     attn_hat = own_columns(inputs).astype(F32) * attn_inv
     upstream = grad_normed_a * own_columns(attn_gain)
     grad_attn_gain = jnp.sum(grad_normed_a * attn_hat, axis=0)

time: 1700 us -> 1440 us (0.85)
  waiting for transfers between devices: 921 us -> 689 us
    reduce_scatter x1, waiting for transfers between devices: 122 us -> 0.01 us  [per_device(): lax.psum_scatter(grad_three, 'expert', scatter_dimension=0, tiled=True)]
    ppermute x90, waiting for transfers between devices: 697 us -> 623 us  [send(): return lax.ppermute(value, BOTH, flip(dz, dx, dy, dc))]
    all_to_all x1, waiting for transfers between devices: 51.2 us -> 0.01 us  [per_device(): lax.all_to_all(prob_grads, 'expert', split_axis=0, concat_axis=0, tiled=T...]
    psum x1, waiting for transfers between devices: 47.3 us -> 66.2 us  [per_device(): sum_output = lax.psum(grad_output, 'expert').astype(F32)]
  transfers between devices with their start and end apart: 95 -> 95, of which waited for: 49 -> 32; matrix products, arithmetic and copies ran while one was open for 8% -> 9% of each run, Pallas kernels for 21% -> 27%
where the time goes in v4:
time: 1440 us; the launch traced here: 1420 us
  waiting for transfers between devices  689 us (48%)
  Pallas kernels  446 us (31%)
  starting transfers between devices  98.9 us (7%)
  other arithmetic  65.3 us (5%)
  local copies, waits for them, and re-layouts  47.6 us (3%)
  matrix products  45.3 us (3%)
  between operations  15.2 us (1%)
    ppermute x90, waiting for transfers between devices, send(): return lax.ppermute(value, BOTH, flip(dz, dx, dy, dc))  623 us
    pallas_call x4, Pallas kernels, expert_slot(): pl.pallas_call(partial(expert_kernel, slices), grid_spec=pltpu.PrefetchSc...  112 us
    pallas_call x6, Pallas kernels, place_rows(): pl.pallas_call(partial(place_kernel, slices, held, slots), grid_spec=pltp...  106 us
    ppermute x90, starting transfers between devices, send(): return lax.ppermute(value, BOTH, flip(dz, dx, dy, dc))  84.6 us
    pallas_call x8, Pallas kernels, pick_rows(): pl.pallas_call(partial(pick_kernel, group, slices), grid_spec=pltpu.Prefe...  81.5 us
    pallas_call x2, Pallas kernels, weight_grads(): pl.pallas_call(partial(kernel, slots, slices), grid_spec=pltpu.PrefetchSc...  70.7 us
    psum x1, waiting for transfers between devices, per_device(): sum_output = lax.psum(grad_output, 'expert').astype(F32)  66.2 us
    pallas_call x2, Pallas kernels, down_slots(): pl.pallas_call(partial(down_kernel, slices, slots), grid_spec=pltpu.Prefe...  32 us
  transfers between devices with their start and end apart: 95, of which 32 were waited for; matrix products, arithmetic and copies ran while one was open for 9% of the time, Pallas kernels for 27%

profile of v4, /device:TPU:10, one launch (start us, length us, event | category | flops | bytes accessed | tf_op | source)
XLA Modules:
  0.0 1415.4 jit_solution(9474503948238704156)
XLA Ops:
  14.1 15.6 %project.1 = (bf16[1024,2048]{1,0:T(8,128)(2,1)}, f32[1024,1]{1,0:T(8,128)}, f32[1024,512]{1,0:T(8,128)}, f32[1024,512]{1,0:T(8,128)}, bf16[1024,512]{1,0:T(8,12...) custom-call(bf16[1024,2048]{1,0:T(8,128)(2,1)} %in_ref.1, f32[1,2048]{1,0:T(1,128)} %bitcast.205, ...), custom_call_target="tpu_custom_call" | custom-call | flops 103079215104 | bytes 352321536 | tf_op jit(solution)/shard_map/project/pallas_call | solution.py:569
  60.2 19.8 %collective-permute-done.7 = bf16[1024,512]{1,0:T(8,128)(2,1)S(1)} collective-permute-done((bf16[1024,512]{1,0:T(8,128)(2,1)S(1)}, bf16[1024,512]{1,0:T(8,128)(2,1)S(1)}, u32[]{:S(2)}, u32[]{:S(2)}) %collective-permute-start.7) | collective-permute-done | bytes 1048608 | tf_op jit(solution)/shard_map/ppermute | solution.py:83
  87.9 37.8 %collective-permute-done.10.refs_2_ = bf16[1024,512]{1,0:T(8,128)(2,1)} collective-permute-done((bf16[1024,512]{1,0:T(8,128)(2,1)}, bf16[1024,512]{1,0:T(8,128)(2,1)}, u32[]{:S(2)}, u32[]{:S(2)}) %collective-permute-start.10) | collective-permute-done | bytes 1048608 | tf_op jit(solution)/shard_map/ppermute | solution.py:83
  136.3 14.7 %collective-permute-done.12.refs_4_ = bf16[1024,512]{1,0:T(8,128)(2,1)} collective-permute-done((bf16[1024,512]{1,0:T(8,128)(2,1)}, bf16[1024,512]{1,0:T(8,128)(2,1)}, u32[]{:S(2)}, u32[]{:S(2)}) %collective-permute-start.12) | collective-permute-done | bytes 1048608 | tf_op jit(solution)/shard_map/ppermute | solution.py:83
  223.5 18.9 %collective-permute-done.17.refs_5_ = bf16[1024,512]{1,0:T(8,128)(2,1)} collective-permute-done((bf16[1024,512]{1,0:T(8,128)(2,1)}, bf16[1024,512]{1,0:T(8,128)(2,1)}, u32[]{:S(2)}, u32[]{:S(2)}) %collective-permute-start.17) | collective-permute-done | bytes 1048608 | tf_op jit(solution)/shard_map/ppermute | solution.py:83
  255.9 31.8 %collective-permute-done.18.refs_2_ = bf16[1024,512]{1,0:T(8,128)(2,1)} collective-permute-done((bf16[1024,512]{1,0:T(8,128)(2,1)}, bf16[1024,512]{1,0:T(8,128)(2,1)}, u32[]{:S(2)}, u32[]{:S(2)}) %collective-permute-start.18) | collective-permute-done | bytes 1048608 | tf_op jit(solution)/shard_map/ppermute | solution.py:83
  316.1 27.8 %expert_slot.4 = (bf16[8,320,256]{2,1,0:T(8,128)(2,1)}, bf16[8,320,256]{2,1,0:T(8,128)(2,1)}, bf16[8,320,256]{2,1,0:T(8,128)(2,1)}, f32[8,2,1024]{2,1,0:T(2,128)...) custom-call(s32[10]{0:T(128)} %stack.107.where_ref, s32[8,8,1024]{2,1,0:T(8,128)} %copy.160.refs_0_.refs_1_, ...), custom_call_target="tpu_custom_call" | custom-call | flops 214748364800 | bytes 905969664 | tf_op jit(solution)/shard_map/expert_slot/pallas_call | solution.py:366
  344.9 16.3 %collective-permute-done.27.refs_5_ = bf16[1024,512]{1,0:T(8,128)(2,1)} collective-permute-done((bf16[1024,512]{1,0:T(8,128)(2,1)}, bf16[1024,512]{1,0:T(8,128)(2,1)}, u32[]{:S(2)}, u32[]{:S(2)}) %collective-permute-start.27) | collective-permute-done | bytes 1048608 | tf_op jit(solution)/shard_map/ppermute | solution.py:83
  382.0 14.1 place_rows.6
  403.5 18.0 %collective-permute-done.42 = bf16[1024,512]{1,0:T(8,128)(2,1)S(1)} collective-permute-done((bf16[1024,512]{1,0:T(8,128)(2,1)}, bf16[1024,512]{1,0:T(8,128)(2,1)S(1)}, u32[]{:S(2)}, u32[]{:S(2)}) %collective-permute-start.42) | collective-permute-done | bytes 1048608 | tf_op jit(solution)/shard_map/ppermute | solution.py:83
  428.1 27.8 %expert_slot.5 = (bf16[8,320,256]{2,1,0:T(8,128)(2,1)}, bf16[8,320,256]{2,1,0:T(8,128)(2,1)}, bf16[8,320,256]{2,1,0:T(8,128)(2,1)}, f32[8,2,1024]{2,1,0:T(2,128)...) custom-call(s32[10]{0:T(128)} %stack.116.where_ref, s32[8,8,1024]{2,1,0:T(8,128)} %copy.160.refs_0_.refs_1_, ...), custom_call_target="tpu_custom_call" | custom-call | flops 214748364800 | bytes 905969664 | tf_op jit(solution)/shard_map/expert_slot/pallas_call | solution.py:366
  457.4 17.0 %collective-permute-done.46.refs_4_ = bf16[1024,512]{1,0:T(8,128)(2,1)} collective-permute-done((bf16[1024,512]{1,0:T(8,128)(2,1)}, bf16[1024,512]{1,0:T(8,128)(2,1)}, u32[]{:S(2)}, u32[]{:S(2)}) %collective-permute-start.46) | collective-permute-done | bytes 1048608 | tf_op jit(solution)/shard_map/ppermute | solution.py:83
  474.9 19.9 %collective-permute-done.35.refs_5_ = bf16[1024,512]{1,0:T(8,128)(2,1)} collective-permute-done((bf16[1024,512]{1,0:T(8,128)(2,1)}, bf16[1024,512]{1,0:T(8,128)(2,1)}, u32[]{:S(2)}, u32[]{:S(2)}) %collective-permute-start.35) | collective-permute-done | bytes 1048608 | tf_op jit(solution)/shard_map/ppermute | solution.py:83
  532.9 28.0 %expert_slot.6 = (bf16[8,320,256]{2,1,0:T(8,128)(2,1)}, bf16[8,320,256]{2,1,0:T(8,128)(2,1)}, bf16[8,320,256]{2,1,0:T(8,128)(2,1)}, f32[8,2,1024]{2,1,0:T(2,128)...) custom-call(s32[10]{0:T(128)} %stack.113.where_ref, s32[8,8,1024]{2,1,0:T(8,128)} %copy.160.refs_0_.refs_1_, ...), custom_call_target="tpu_custom_call" | custom-call | flops 214748364800 | bytes 905969664 | tf_op jit(solution)/shard_map/expert_slot/pallas_call | solution.py:366
  572.4 13.9 place_rows.8
  586.3 28.0 %expert_slot.7 = (bf16[8,320,256]{2,1,0:T(8,128)(2,1)}, bf16[8,320,256]{2,1,0:T(8,128)(2,1)}, bf16[8,320,256]{2,1,0:T(8,128)(2,1)}, f32[8,2,1024]{2,1,0:T(2,128)...) custom-call(s32[10]{0:T(128)} %stack.110.where_ref, s32[8,8,1024]{2,1,0:T(8,128)} %copy.160.refs_0_.refs_1_, ...), custom_call_target="tpu_custom_call" | custom-call | flops 214748364800 | bytes 905969664 | tf_op jit(solution)/shard_map/expert_slot/pallas_call | solution.py:366
  633.4 16.1 %down_slots.2 = (bf16[4,2,1280,512]{3,2,1,0:T(8,128)(2,1)}, bf16[4,2,1280,512]{3,2,1,0:T(8,128)(2,1)}) custom-call(s32[10]{0:T(128)} %stack.107.where_ref, bf16[8,320,256]{2,1,0:T(8,128)(2,1)} %get-tuple-element.143.refs_0_.refs_8_, bf16[8,320,256]{2,1,0:T(8,128)(2,1)} %get-tuple-element.171.refs_1_.refs_9_, bf16[8,256,2048]{2,1,0:T(8,128)(2,1)} %refs_2_.3), custom_call_target="tpu_custom_call" | custom-call | flops 85899345920 | bytes 469762048 | tf_op jit(solution)/shard_map/down_slots/pallas_call | solution.py:406
  649.7 28.1 %collective-permute-done.56 = bf16[1024,512]{1,0:T(8,128)(2,1)S(1)} collective-permute-done((bf16[1024,512]{1,0:T(8,128)(2,1)}, bf16[1024,512]{1,0:T(8,128)(2,1)S(1)}, u32[]{:S(2)}, u32[]{:S(2)}) %collective-permute-start.56) | collective-permute-done | bytes 1048608 | tf_op jit(solution)/shard_map/ppermute | solution.py:83
  679.3 13.9 place_rows.9
  716.2 14.0 collective-permute-done.57
  731.7 15.8 %down_slots.3 = (bf16[4,2,1280,512]{3,2,1,0:T(8,128)(2,1)}, bf16[4,2,1280,512]{3,2,1,0:T(8,128)(2,1)}) custom-call(s32[10]{0:T(128)} %stack.107.where_ref, bf16[8,320,256]{2,1,0:T(8,128)(2,1)} %get-tuple-element.151.refs_0_.refs_10_, bf16[8,320,256]{2,1,0:T(8,128)(2,1)} %get-tuple-element.160.refs_1_.refs_11_, bf16[8,256,2048]{2,1,0:T(8,128)(2,1)} %refs_2_.3), custom_call_target="tpu_custom_call" | custom-call | flops 85899345920 | bytes 469762048 | tf_op jit(solution)/shard_map/down_slots/pallas_call | solution.py:406
  759.6 25.2 %place_rows.10 = (bf16[2,1024,512]{2,1,0:T(8,128)(2,1)}, bf16[2,1024,512]{2,1,0:T(8,128)(2,1)}, bf16[2,1024,512]{2,1,0:T(8,128)(2,1)}, bf16[2,1024,512]{2,1,0:T(8,128)(2,1)}) custom-call(s32[4]{0:T(128)} %pad_add_fusion.3.where_ref, s32[8,1024,8]{2,1,0:T(8,128)} %bitcast.158, s32[8,1024,8]{2,1,0:T(8,128)} %bitcast.159, s32[8,1024,8]{2,1,0:T(8,128)} %bitcast.160, ...), custom_call_target="tpu_custom_call" | custom-call | flops 171798691840 | bytes 469762048 | tf_op jit(solution)/shard_map/place_rows/pallas_call | solution.py:465
  784.8 42.9 %weight_grads.1 = (f32[8,2048,256]{2,1,0:T(8,128)}, f32[8,2048,256]{2,1,0:T(8,128)}) custom-call(s32[10]{0:T(128)} %stack.107.where_ref, bf16[2,2,1280,512]{3,2,1,0:T(8,128)(2,1)} %pick_rows.9.refs_4_.refs_0_, bf16[2,2,1280,512]{3,2,1,0:T(8,128)(2,1)} %collective-permute-done.21.refs_5_.refs_1_, bf16[2,2,1280,512]{3,2,1,0:T(8,128)(2,1)} %pick_rows.15.refs_4_.refs_2_, ...), custom_call_target="tpu_custom_call" | custom-call | flops 160000000000 | bytes 16000000 | tf_op jit(solution)/shard_map/weight_grads/pallas_call | solution.py:522
  839.4 23.6 %collective-permute-done.70 = bf16[1024,512]{1,0:T(8,128)(2,1)S(1)} collective-permute-done((bf16[1024,512]{1,0:T(8,128)(2,1)S(1)}, bf16[1024,512]{1,0:T(8,128)(2,1)S(1)}, u32[]{:S(2)}, u32[]{:S(2)}) %collective-permute-start.70) | collective-permute-done | bytes 1048608 | tf_op jit(solution)/shard_map/ppermute | solution.py:83
  873.4 25.1 %place_rows.11 = (bf16[2,1024,512]{2,1,0:T(8,128)(2,1)}, bf16[2,1024,512]{2,1,0:T(8,128)(2,1)}, bf16[2,1024,512]{2,1,0:T(8,128)(2,1)}, bf16[2,1024,512]{2,1,0:T(8,128)(2,1)}) custom-call(s32[4]{0:T(128)} %pad_add_fusion.4.where_ref, s32[8,1024,8]{2,1,0:T(8,128)} %bitcast.162, s32[8,1024,8]{2,1,0:T(8,128)} %bitcast.163, s32[8,1024,8]{2,1,0:T(8,128)} %bitcast.164, ...), custom_call_target="tpu_custom_call" | custom-call | flops 171798691840 | bytes 469762048 | tf_op jit(solution)/shard_map/place_rows/pallas_call | solution.py:465
  898.4 16.3 %attend_back.1 = (bf16[1024,512]{1,0:T(8,128)(2,1)}, bf16[1024,512]{1,0:T(8,128)(2,1)}, bf16[1024,512]{1,0:T(8,128)(2,1)}, f32[1,1,512]{2,1,0:T(1,128)}, f32[1,1,512]{2,1,0:T(1,128)}) custom-call(s32[4]{0:T(128)} %add_bitcast_fusion.pieces_ref, bf16[1024,512]{1,0:T(8,128)(2,1)} %get-tuple-element.134.q_ref, bf16[1024,512]{1,0:T(8,128)(2,1)} %get-tuple-element.135.k_ref, ...), custom_call_target="tpu_custom_call" | custom-call | flops 85899345920 | bytes 184549376 | tf_op jit(solution)/shard_map/attend_back/pallas_call | solution.py:704
  939.1 37.5 %collective-permute-done.71 = bf16[2,1024,512]{2,1,0:T(8,128)(2,1)} collective-permute-done((bf16[2,1024,512]{2,1,0:T(8,128)(2,1)}, bf16[2,1024,512]{2,1,0:T(8,128)(2,1)}, u32[]{:S(2)}, u32[]{:S(2)}) %collective-permute-start.71) | collective-permute-done | bytes 2097184 | tf_op jit(solution)/shard_map/ppermute | solution.py:83
  996.9 73.6 %collective-permute-done.75 = bf16[2,1024,512]{2,1,0:T(8,128)(2,1)} collective-permute-done((bf16[2,1024,512]{2,1,0:T(8,128)(2,1)}, bf16[2,1024,512]{2,1,0:T(8,128)(2,1)}, u32[]{:S(2)}, u32[]{:S(2)}) %collective-permute-start.75) | collective-permute-done | bytes 2097184 | tf_op jit(solution)/shard_map/ppermute | solution.py:83
  1071.0 27.8 %weight_down_grads.1 = f32[8,256,2048]{2,1,0:T(8,128)} custom-call(s32[10]{0:T(128)} %stack.107.where_ref, bf16[2,2,1280,512]{3,2,1,0:T(8,128)(2,1)} %pick_rows.8.refs_6_.refs_0_, bf16[2,2,1280,512]{3,2,1,0:T(8,128)(2,1)} %collective-permute-done.22.refs_7_.refs_1_, bf16[2,2,1280,512]{3,2,1,0:T(8,128)(2,1)} %pick_rows.14.refs_6_.refs_2_, ...), custom_call_target="tpu_custom_call" | custom-call | flops 160000000000 | bytes 16000000 | tf_op jit(solution)/shard_map/weight_down_grads/pallas_call | solution.py:522
  1106.9 66.2 %all-reduce.3.cloned.1.call-done = bf16[512,2048]{1,0:T(8,128)(2,1)} async-done(((bf16[512,2048]{1,0:T(8,128)(2,1)}), bf16[512,2048]{1,0:T(8,128)(2,1)}) %all-reduce.3.cloned.1.call-update) | async-done | bytes 2097168 | tf_op jit(solution)/shard_map/psum | solution.py:945
  1206.2 151.5 %collective-permute-done.89 = f32[69,512]{1,0:T(8,128)S(1)} collective-permute-done((f32[69,512]{1,0:T(8,128)S(1)}, f32[69,512]{1,0:T(8,128)S(1)}, u32[]{:S(2)}, u32[]{:S(2)}) %collective-permute-start.89) | collective-permute-done | bytes 141344 | tf_op jit(solution)/shard_map/ppermute | solution.py:83
  1378.5 20.1 %collective-permute-done.79 = bf16[1024,512]{1,0:T(8,128)(2,1)S(1)} collective-permute-done((bf16[1024,512]{1,0:T(8,128)(2,1)S(1)}, bf16[1024,512]{1,0:T(8,128)(2,1)S(1)}, u32[]{:S(2)}, u32[]{:S(2)}) %collective-permute-start.79) | collective-permute-done | bytes 1048608 | tf_op jit(solution)/shard_map/ppermute | solution.py:83
  (464 shorter events, 453.3 us)
Async XLA Ops:
  55.3 70.4 %collective-permute-start.10 = (bf16[1024,512]{1,0:T(8,128)(2,1)}, bf16[1024,512]{1,0:T(8,128)(2,1)}, u32[]{:S(2)}, u32[]{:S(2)}) collective-permute-start(bf16[1024,512]{1,0:T(8,128)(2,1)} %convert_element_type.253.refs_2_), channel_id=1, source_target_pairs={{0,16},{1,17},{2,18},{3,19},{4,20},{5,21},{6,22},{7,23},{8,24},{9,... | collective-permute-start | bytes 3145736 | tf_op jit(solution)/shard_map/ppermute | solution.py:83
  82.5 88.6 %collective-permute-start.13 = (bf16[1024,512]{1,0:T(8,128)(2,1)}, bf16[1024,512]{1,0:T(8,128)(2,1)}, u32[]{:S(2)}, u32[]{:S(2)}) collective-permute-start(bf16[1024,512]{1,0:T(8,128)(2,1)} %convert_element_type.253.refs_2_), channel_id=1, source_target_pairs={{0,24},{1,25},{2,26},{3,27},{4,28},{5,29},{6,30},{7,31},{8,16},{9,... | collective-permute-start | bytes 3145736 | tf_op jit(solution)/shard_map/ppermute | solution.py:83
  84.2 203.6 %collective-permute-start.37 = (bf16[1024,512]{1,0:T(8,128)(2,1)}, bf16[1024,512]{1,0:T(8,128)(2,1)}, u32[]{:S(2)}, u32[]{:S(2)}) collective-permute-start(bf16[1024,512]{1,0:T(8,128)(2,1)} %convert_element_type.253.refs_2_), channel_id=1, source_target_pairs={{0,8},{1,9},{2,10},{3,11},{4,12},{5,13},{6,14},{7,15},{8,0},{9,1},... | collective-permute-start | bytes 3145736 | tf_op jit(solution)/shard_map/ppermute | solution.py:83
  171.1 128.3 %collective-permute-start.20 = (bf16[1024,512]{1,0:T(8,128)(2,1)}, bf16[1024,512]{1,0:T(8,128)(2,1)}, u32[]{:S(2)}, u32[]{:S(2)}) collective-permute-start(bf16[1024,512]{1,0:T(8,128)(2,1)} %collective-permute-done.13.refs_2_), channel_id=1, source_target_pairs={{0,4},{1,5},{2,6},{3,7},{4,0},{5,1},{6,2},{7,3},{8,12},{9,13},{10,... | collective-permute-start | bytes 3145736 | tf_op jit(solution)/shard_map/ppermute | solution.py:83
  197.8 103.1 %collective-permute-start.24 = (bf16[1024,512]{1,0:T(8,128)(2,1)}, bf16[1024,512]{1,0:T(8,128)(2,1)}, u32[]{:S(2)}, u32[]{:S(2)}) collective-permute-start(bf16[1024,512]{1,0:T(8,128)(2,1)} %collective-permute-done.13.refs_2_), channel_id=1, source_target_pairs={{0,2},{1,3},{2,0},{3,1},{4,6},{5,7},{6,4},{7,5},{8,10},{9,11},{10,... | collective-permute-start | bytes 3145736 | tf_op jit(solution)/shard_map/ppermute | solution.py:83
  201.3 114.8 %all-to-all-start = ((f32[8,8,1024]{2,1,0:T(8,128)}), f32[8,8,1024]{2,1,0:T(8,128)}, u32[]{:S(2)}, u32[]{:S(2)}) async-start(f32[8,8,1024]{2,1,0:T(8,128)} %fusion.79), calls=%async_computation | async-start | bytes 524288 | tf_op jit(solution)/shard_map/all_to_all | solution.py:838
  222.0 66.3 %collective-permute-start.19 = (bf16[1024,512]{1,0:T(8,128)(2,1)}, bf16[1024,512]{1,0:T(8,128)(2,1)S(1)}, u32[]{:S(2)}, u32[]{:S(2)}) collective-permute-start(bf16[1024,512]{1,0:T(8,128)(2,1)} %collective-permute-done.12.refs_4_), channel_id=1, source_target_pairs={{0,2},{1,3},{2,0},{3,1},{4,6},{5,7},{6,4},{7,5},{8,10},{9,11},{10,... | collective-permute-start | bytes 3145736 | tf_op jit(solution)/shard_map/ppermute | solution.py:83
  299.4 103.6 %collective-permute-start.39 = (bf16[1024,512]{1,0:T(8,128)(2,1)}, bf16[1024,512]{1,0:T(8,128)(2,1)}, u32[]{:S(2)}, u32[]{:S(2)}) collective-permute-start(bf16[1024,512]{1,0:T(8,128)(2,1)} %collective-permute-done.37.refs_2_), channel_id=1, source_target_pairs={{0,4},{1,5},{2,6},{3,7},{4,0},{5,1},{6,2},{7,3},{8,12},{9,13},{10,... | collective-permute-start | bytes 3145736 | tf_op jit(solution)/shard_map/ppermute | solution.py:83
  300.9 70.4 %collective-permute-start.29 = (bf16[1024,512]{1,0:T(8,128)(2,1)}, bf16[1024,512]{1,0:T(8,128)(2,1)}, u32[]{:S(2)}, u32[]{:S(2)}) collective-permute-start(bf16[1024,512]{1,0:T(8,128)(2,1)} %collective-permute-done.24.refs_3_), channel_id=1, source_target_pairs={{0,4},{1,5},{2,6},{3,7},{4,0},{5,1},{6,2},{7,3},{8,12},{9,13},{10,... | collective-permute-start | bytes 3145736 | tf_op jit(solution)/shard_map/ppermute | solution.py:83
  403.0 103.4 %collective-permute-start.38 = (bf16[1024,512]{1,0:T(8,128)(2,1)}, bf16[1024,512]{1,0:T(8,128)(2,1)}, u32[]{:S(2)}, u32[]{:S(2)}) collective-permute-start(bf16[1024,512]{1,0:T(8,128)(2,1)} %collective-permute-done.37.refs_2_), channel_id=1, source_target_pairs={{0,2},{1,3},{2,0},{3,1},{4,6},{5,7},{6,4},{7,5},{8,10},{9,11},{10,... | collective-permute-start | bytes 3145736 | tf_op jit(solution)/shard_map/ppermute | solution.py:83
  421.5 85.4 %collective-permute-start.40 = (bf16[1024,512]{1,0:T(8,128)(2,1)}, bf16[1024,512]{1,0:T(8,128)(2,1)}, u32[]{:S(2)}, u32[]{:S(2)}) collective-permute-start(bf16[1024,512]{1,0:T(8,128)(2,1)} %collective-permute-done.39.refs_4_), channel_id=1, source_target_pairs={{0,2},{1,3},{2,0},{3,1},{4,6},{5,7},{6,4},{7,5},{8,10},{9,11},{10,... | collective-permute-start | bytes 3145736 | tf_op jit(solution)/shard_map/ppermute | solution.py:83
  427.5 67.3 %collective-permute-start.35 = (bf16[1024,512]{1,0:T(8,128)(2,1)}, bf16[1024,512]{1,0:T(8,128)(2,1)}, u32[]{:S(2)}, u32[]{:S(2)}) collective-permute-start(bf16[1024,512]{1,0:T(8,128)(2,1)} %collective-permute-done.33.refs_3_), channel_id=1, source_target_pairs={{0,4},{1,5},{2,6},{3,7},{4,0},{5,1},{6,2},{7,3},{8,12},{9,13},{10,... | collective-permute-start | bytes 3145736 | tf_op jit(solution)/shard_map/ppermute | solution.py:83
  455.9 105.1 %collective-permute-start.45 = (bf16[1024,512]{1,0:T(8,128)(2,1)}, bf16[1024,512]{1,0:T(8,128)(2,1)}, u32[]{:S(2)}, u32[]{:S(2)}) collective-permute-start(bf16[1024,512]{1,0:T(8,128)(2,1)} %collective-permute-done.44.refs_2_), channel_id=1, source_target_pairs={{0,2},{1,3},{2,0},{3,1},{4,6},{5,7},{6,4},{7,5},{8,10},{9,11},{10,... | collective-permute-start | bytes 3145736 | tf_op jit(solution)/shard_map/ppermute | solution.py:83
  474.4 86.7 %collective-permute-start.47 = (bf16[1024,512]{1,0:T(8,128)(2,1)}, bf16[1024,512]{1,0:T(8,128)(2,1)}, u32[]{:S(2)}, u32[]{:S(2)}) collective-permute-start(bf16[1024,512]{1,0:T(8,128)(2,1)} %collective-permute-done.46.refs_4_), channel_id=1, source_target_pairs={{0,2},{1,3},{2,0},{3,1},{4,6},{5,7},{6,4},{7,5},{8,10},{9,11},{10,... | collective-permute-start | bytes 3145736 | tf_op jit(solution)/shard_map/ppermute | solution.py:83
  624.4 446.6 %reduce-scatter.2.cloned.1.call-start = ((), (), s32[]{:S(2)}) async-start(), calls=%async_computation.3 | async-start | bytes 7077888 | tf_op jit(solution)/shard_map/reduce_scatter | solution.py:946
  649.5 109.5 %collective-permute-start.58 = (bf16[4,2,1280,512]{3,2,1,0:T(8,128)(2,1)}, bf16[4,2,1280,512]{3,2,1,0:T(8,128)(2,1)}, u32[]{:S(2)}, u32[]{:S(2)}) collective-permute-start(bf16[4,2,1280,512]{3,2,1,0:T(8,128)(2,1)} %get-tuple-element.185), channel_id=1, source_target_pairs={{0,1},{1,0},{2,3},{3,2},{4,5},{5,4},{6,7},{7,6},{8,9},{9,8},{10,11... | collective-permute-start | bytes 31457288 | tf_op jit(solution)/shard_map/ppermute | solution.py:83
  709.9 117.8 %collective-permute-start.64 = (bf16[1024,512]{1,0:T(8,128)(2,1)}, bf16[1024,512]{1,0:T(8,128)(2,1)}, u32[]{:S(2)}, u32[]{:S(2)}) collective-permute-start(bf16[1024,512]{1,0:T(8,128)(2,1)} %fusion.27), channel_id=1, source_target_pairs={{0,16},{1,17},{2,18},{3,19},{4,20},{5,21},{6,22},{7,23},{8,24},{9,... | collective-permute-start | bytes 3145736 | tf_op jit(solution)/shard_map/ppermute | solution.py:83
  716.2 111.5 %collective-permute-start.65 = (bf16[1024,512]{1,0:T(8,128)(2,1)}, bf16[1024,512]{1,0:T(8,128)(2,1)}, u32[]{:S(2)}, u32[]{:S(2)}) collective-permute-start(bf16[1024,512]{1,0:T(8,128)(2,1)} %fusion.25), channel_id=1, source_target_pairs={{0,24},{1,25},{2,26},{3,27},{4,28},{5,29},{6,30},{7,31},{8,16},{9,... | collective-permute-start | bytes 3145736 | tf_op jit(solution)/shard_map/ppermute | solution.py:83
  753.7 119.6 %collective-permute-start.74 = (bf16[4,2,1280,512]{3,2,1,0:T(8,128)(2,1)}, bf16[4,2,1280,512]{3,2,1,0:T(8,128)(2,1)}, u32[]{:S(2)}, u32[]{:S(2)}) collective-permute-start(bf16[4,2,1280,512]{3,2,1,0:T(8,128)(2,1)} %get-tuple-element.221), channel_id=1, source_target_pairs={{0,1},{1,0},{2,3},{3,2},{4,5},{5,4},{6,7},{7,6},{8,9},{9,8},{10,11... | collective-permute-start | bytes 31457288 | tf_op jit(solution)/shard_map/ppermute | solution.py:83
  757.0 70.7 %collective-permute-start.63 = (bf16[1024,512]{1,0:T(8,128)(2,1)}, bf16[1024,512]{1,0:T(8,128)(2,1)}, u32[]{:S(2)}, u32[]{:S(2)}) collective-permute-start(bf16[1024,512]{1,0:T(8,128)(2,1)} %fusion.29), channel_id=1, source_target_pairs={{0,8},{1,9},{2,10},{3,11},{4,12},{5,13},{6,14},{7,15},{8,0},{9,1},... | collective-permute-start | bytes 3145736 | tf_op jit(solution)/shard_map/ppermute | solution.py:83
  928.6 244.6 %all-reduce.3.cloned.1.call-start = ((), (), s32[]{:S(2)}) async-start(), calls=%async_computation.5 | async-start | bytes 4194304 | tf_op jit(solution)/shard_map/psum | solution.py:945
  976.7 390.9 %collective-permute-start.73 = (bf16[2,1024,512]{2,1,0:T(8,128)(2,1)}, bf16[2,1024,512]{2,1,0:T(8,128)(2,1)}, u32[]{:S(2)}, u32[]{:S(2)}) collective-permute-start(bf16[2,1024,512]{2,1,0:T(8,128)(2,1)} %get-tuple-element.219), channel_id=1, source_target_pairs={{0,2},{1,3},{2,0},{3,1},{4,6},{5,7},{6,4},{7,5},{8,10},{9,11},{10,... | collective-permute-start | bytes 6291464 | tf_op jit(solution)/shard_map/ppermute | solution.py:83
  977.2 93.3 %collective-permute-start.75 = (bf16[2,1024,512]{2,1,0:T(8,128)(2,1)}, bf16[2,1024,512]{2,1,0:T(8,128)(2,1)}, u32[]{:S(2)}, u32[]{:S(2)}) collective-permute-start(bf16[2,1024,512]{2,1,0:T(8,128)(2,1)} %get-tuple-element.227), channel_id=1, source_target_pairs={{0,2},{1,3},{2,0},{3,1},{4,6},{5,7},{6,4},{7,5},{8,10},{9,11},{10,... | collective-permute-start | bytes 6291464 | tf_op jit(solution)/shard_map/ppermute | solution.py:83
  978.7 421.8 %all-gather.4.cloned.1.call-start = ((), (), s32[]{:S(2)}) async-start(), calls=%async_computation.4 | async-start | bytes 7077888 | tf_op jit(solution)/shard_map/all_gather | solution.py:955
  987.2 380.4 %collective-permute-start.72 = (bf16[2,1024,512]{2,1,0:T(8,128)(2,1)}, bf16[2,1024,512]{2,1,0:T(8,128)(2,1)}, u32[]{:S(2)}, u32[]{:S(2)}) collective-permute-start(bf16[2,1024,512]{2,1,0:T(8,128)(2,1)} %add_convert_fusion.2), channel_id=1, source_target_pairs={{0,4},{1,5},{2,6},{3,7},{4,0},{5,1},{6,2},{7,3},{8,12},{9,13},{10,... | collective-permute-start | bytes 6291464 | tf_op jit(solution)/shard_map/ppermute | solution.py:83
  990.3 112.1 %collective-permute-start.82 = (bf16[1024,512]{1,0:T(8,128)(2,1)}, bf16[1024,512]{1,0:T(8,128)(2,1)}, u32[]{:S(2)}, u32[]{:S(2)}) collective-permute-start(bf16[1024,512]{1,0:T(8,128)(2,1)} %fusion.46), channel_id=1, source_target_pairs={{0,1},{1,0},{2,3},{3,2},{4,5},{5,4},{6,7},{7,6},{8,9},{9,8},{10,11... | collective-permute-start | bytes 3145736 | tf_op jit(solution)/shard_map/ppermute | solution.py:83
  996.3 106.6 %collective-permute-start.84 = (bf16[1024,512]{1,0:T(8,128)(2,1)}, bf16[1024,512]{1,0:T(8,128)(2,1)}, u32[]{:S(2)}, u32[]{:S(2)}) collective-permute-start(bf16[1024,512]{1,0:T(8,128)(2,1)} %add_convert_fusion.3), channel_id=1, source_target_pairs={{0,2},{1,3},{2,0},{3,1},{4,6},{5,7},{6,4},{7,5},{8,10},{9,11},{10,... | collective-permute-start | bytes 3145736 | tf_op jit(solution)/shard_map/ppermute | solution.py:83
  1070.5 119.8 %collective-permute-start.77 = (bf16[2,1024,512]{2,1,0:T(8,128)(2,1)}, bf16[2,1024,512]{2,1,0:T(8,128)(2,1)}, u32[]{:S(2)}, u32[]{:S(2)}) collective-permute-start(bf16[2,1024,512]{2,1,0:T(8,128)(2,1)} %get-tuple-element.230), channel_id=1, source_target_pairs={{0,2},{1,3},{2,0},{3,1},{4,6},{5,7},{6,4},{7,5},{8,10},{9,11},{10,... | collective-permute-start | bytes 6291464 | tf_op jit(solution)/shard_map/ppermute | solution.py:83
  1102.5 87.7 %collective-permute-start.76 = (bf16[2,1024,512]{2,1,0:T(8,128)(2,1)}, bf16[2,1024,512]{2,1,0:T(8,128)(2,1)}, u32[]{:S(2)}, u32[]{:S(2)}) collective-permute-start(bf16[2,1024,512]{2,1,0:T(8,128)(2,1)} %add_convert_fusion.1), channel_id=1, source_target_pairs={{0,4},{1,5},{2,6},{3,7},{4,0},{5,1},{6,2},{7,3},{8,12},{9,13},{10,... | collective-permute-start | bytes 6291464 | tf_op jit(solution)/shard_map/ppermute | solution.py:83
  1106.8 69.3 %collective-permute-start.85 = (f32[8,128]{1,0:T(8,128)S(1)}, f32[8,128]{1,0:T(8,128)S(1)}, u32[]{:S(2)}, u32[]{:S(2)}) collective-permute-start(f32[8,128]{1,0:T(8,128)S(1)} %bitcast.185), channel_id=1, source_target_pairs={{0,1},{1,0},{2,3},{3,2},{4,5},{5,4},{6,7},{7,6},{8,9},{9,8},{10,11... | collective-permute-start | bytes 12296 | tf_op jit(solution)/shard_map/ppermute | solution.py:83
  1194.1 173.4 %collective-permute-start.78 = (bf16[2,1024,512]{2,1,0:T(8,128)(2,1)S(1)}, bf16[2,1024,512]{2,1,0:T(8,128)(2,1)S(1)}, u32[]{:S(2)}, u32[]{:S(2)}) collective-permute-start(bf16[2,1024,512]{2,1,0:T(8,128)(2,1)S(1)} %add_convert_fusion), channel_id=1, source_target_pairs={{0,16},{1,17},{2,18},{3,19},{4,20},{5,21},{6,22},{7,23},{8,24},{9,... | collective-permute-start | bytes 6291464 | tf_op jit(solution)/shard_map/ppermute | solution.py:83
  1200.0 157.8 %collective-permute-start.89 = (f32[69,512]{1,0:T(8,128)S(1)}, f32[69,512]{1,0:T(8,128)S(1)}, u32[]{:S(2)}, u32[]{:S(2)}) collective-permute-start(f32[69,512]{1,0:T(8,128)S(1)} %pad_maximum_fusion.5), channel_id=1, source_target_pairs={{0,16},{1,17},{2,18},{3,19},{4,20},{5,21},{6,22},{7,23},{8,24},{9,... | collective-permute-start | bytes 423944 | tf_op jit(solution)/shard_map/ppermute | solution.py:83
  (144 other events, 3518.8 us)
Sparse Core Ops, SparseCore 0:
  928.7 131.7 reduce-scatter.1
  1064.1 108.9 all-reduce.2
  1175.3 177.1 all-gather.3

commit v5 on v4

--- a/solution.py
+++ b/solution.py
@@ -22,10 +22,9 @@
 ORDER = (0, 2, 3, 1)
 ODD = (1, 2)
 DUE = {
-    "attended": ("cx0", "cy0"),
-    "normed": ("cz2", "cd0", "cx2"),
-    "row0": ("cz3", "cy2"),
-    "cot2": ("nz2",),
+    "attended": ("cx0", "cy0", "cz2"),
+    "normed": ("cd0",),
+    "row0": ("cx2", "cz3", "cy2"),
     "exp0": ("cx3",),
     "row2": ("sc2", "cy3"),
     "cot3": ("sg0",),
@@ -38,7 +37,8 @@
     "down1": ("ex2", "ey2", "ed3"),
     "pd0": ("ed1", "sd0"),
     "weight": ("ex3", "ey3", "ex1", "ey1"),
-    "weight_down": ("hs", "gd0", "gd1"),
+    "normed_grad": ("gd0",),
+    "weight_down": ("hs", "gd1"),
 }
 
 
@@ -192,6 +192,13 @@
     return [jnp.int32(i) for i in range(lax.axis_size("tensor"))]
 
 
+def order_spots():
+    if not is_cube():
+        return lambda s: s
+    part = lax.axis_index("tensor")
+    return lambda s: (part ^ s) % 2 * 2 + (part ^ s) // 2
+
+
 def tensor_gather(own):
     if not is_cube():
         full = lax.all_gather(own, "tensor")
@@ -218,6 +225,26 @@
         return lax.psum(value, "tensor")
     value = value + core_swap(value)
     return value + send(value, dy=1)
+
+
+def row_blocks():
+    if not is_cube():
+        return [jnp.int32(i) for i in range(8)]
+    owner = lax.axis_index("expert")
+    return [owner ^ (b | first << 1 | second << 2) for b in (0, 1) for first in (0, 1) for second in (0, 1)]
+
+
+def expert_sum(value):
+    half = value.shape[0] // 2
+    if not is_cube():
+        value = lax.psum(value, "expert")
+        return value[:half], value[half:]
+    for step in ({"dx": 1}, {"dz": 1}, {"dz": 2}):
+        half = value.shape[0] // 2
+        value = added(value[:half], send(value[half:], **step)).astype(BF16)
+    for step in ({"dz": 2}, {"dz": 1}):
+        value = jnp.concatenate([value, send(value, **step)], axis=0)
+    return value, send(value, dx=1)
 
 
 def expert_total(sums, tops):
@@ -532,6 +559,48 @@
         cost_estimate=cost(flops=10**10, bytes_accessed=10**6, transcendentals=0),
         name=name,
     )(where, *[a for pair in rows for a in pair], *hiddens)
+
+
+def settle_kernel(where_ref, *refs):
+    halves, (output_ref, value_ref, query_ref, key_ref) = refs[:6], refs[6:]
+
+    def settle(output, value, both):
+        output_ref[...] = output[...].astype(F32).T
+        value_ref[...] = value[...].astype(F32)
+        width = query_ref.shape[1]
+        query_ref[...] = both[:, :width].astype(F32)
+        key_ref[...] = both[:, width:].astype(F32)
+
+    @pl.when(pl.program_id(0) < 4)
+    def _():
+        settle(*halves[0::2])
+
+    @pl.when(pl.program_id(0) >= 4)
+    def _():
+        settle(*halves[1::2])
+
+
+def settle_rows(where, output, value, both):
+    rows = 2 * value[0].shape[0]
+    step = rows // 8
+    width = value[0].shape[1]
+    near = lambda n: pl.BlockSpec((step, n), lambda i, where: (jnp.minimum(i, 3), 0))
+    far = lambda n: pl.BlockSpec((step, n), lambda i, where: (jnp.maximum(i, 4) - 4, 0))
+    placed = pl.BlockSpec((step, width), lambda i, where: (where[i], 0))
+    return pl.pallas_call(
+        settle_kernel,
+        grid_spec=pltpu.PrefetchScalarGridSpec(
+            num_scalar_prefetch=1,
+            grid=(8,),
+            in_specs=[s(n) for n in (width, width, 2 * width) for s in (near, far)],
+            out_specs=[pl.BlockSpec((width, step), lambda i, where: (0, where[i]))] + [placed] * 3,
+        ),
+        out_shape=[jax.ShapeDtypeStruct((width, rows), F32)]
+        + [jax.ShapeDtypeStruct((rows, width), F32)] * 3,
+        compiler_params=pltpu.CompilerParams(vmem_limit_bytes=VMEM),
+        cost_estimate=cost(flops=0, bytes_accessed=24 * rows * width, transcendentals=0),
+        name="settle_rows",
+    )(where, *output, *value, *both)
 
 
 def project_kernel(
@@ -802,6 +871,10 @@
     output_pieces = [lax.dynamic_slice_in_dim(w_output, o * slice_width, slice_width, 1) for o in order]
     normed_a, attn_inv, query_raw, key_raw, queries, keys, values = project(
         inputs, attn_gain, w_query, w_key, w_value, query_gain, key_gain
+    )
+    blocks = row_blocks()
+    normed_rows = jnp.concatenate(
+        [lax.dynamic_slice_in_dim(normed_a, r * (width // 8), width // 8, 1) for r in blocks], axis=1
     )
     pieces = jnp.concatenate([piece_start, piece_length], axis=1).reshape(-1)
     attended, logs, tops = attend(
@@ -934,17 +1007,30 @@
     mixture = scatter_pairs(pairs, seen)
     out = residual + mixture
 
-    grad_output = matmul_tn(attended, grad_branch).astype(BF16)
+    grad_output = matmul_tn(grad_branch, attended).astype(BF16)
+    spots = order_spots()
+    eighth = width // 8
+    wide = slice_width // eighth
+    grad_output = jnp.concatenate(
+        [
+            lax.dynamic_slice_in_dim(
+                grad_output, (spots(r // wide) * wide + r % wide) * eighth, eighth, 0
+            )
+            for r in blocks
+        ],
+        axis=0,
+    )
+    sum_output = expert_sum(grad_output)
     grad_attended = matmul_nt(grad_branch, jnp.concatenate(output_pieces, axis=1)).astype(BF16)
     grad_attended = after(grad_attended, grad_output, last)
     grad_query_raw, grad_key_raw, grad_v, grad_query_gain, grad_key_gain = attend_back(
         pieces, queries, keys, values, grad_attended, logs, query_raw, key_raw, query_gain, key_gain, scale
     )
+    sum_value = expert_sum(matmul_tn(normed_rows, grad_v).astype(BF16))
     grad_raw = jnp.concatenate([grad_query_raw, grad_key_raw, grad_v], axis=1)
-    grad_three = matmul_tn(normed_a, grad_raw).astype(BF16)
-    sum_output = lax.psum(grad_output, "expert").astype(F32)
-    sum_three = lax.psum_scatter(grad_three, "expert", scatter_dimension=0, tiled=True)
-    grad_raw = after(grad_raw, grad_three)
+    grad_both = matmul_tn(normed_rows, grad_raw[:, : 2 * slice_width]).astype(BF16)
+    sum_both = expert_sum(grad_both)
+    grad_raw = after(grad_raw, grad_both, *due("normed_grad", seen))
     weights = jnp.concatenate([w_query, w_key, w_value], axis=1)
     weight_pieces = [lax.dynamic_slice_in_dim(weights, o * slice_width, slice_width, 0) for o in order]
     grad_normed_a = tensor_scatter(partial(matmul_nt, grad_raw), weight_pieces, "h", seen)
@@ -952,8 +1038,6 @@
     (grad_down,) = weight_grads(
         weight_down_kernel, now, cots, scaled, [w_down.shape[1:]], "weight_down_grads"
     )
-    sum_three = lax.all_gather(sum_three, "expert", tiled=True)
-    sum_query, sum_key, sum_value = jnp.split(sum_three.astype(F32), 3, axis=1)
     grad_normed_a = after(grad_normed_a, grad_down)
     attn_hat = own_columns(inputs).astype(F32) * attn_inv
     upstream = grad_normed_a * own_columns(attn_gain)
@@ -982,11 +1066,9 @@
     every = lax.all_gather(small[: E + 1], "tensor")
     sum_router = every[:, :E].transpose(0, 2, 1).reshape(width, E)
     sum_attn_gain = every[:, E].reshape(width)
-    ordered = jnp.zeros_like(sum_output)
-    for i, o in enumerate(order):
-        ordered = lax.dynamic_update_slice_in_dim(
-            ordered, sum_output[:, i * slice_width : (i + 1) * slice_width], o * slice_width, 1
-        )
+    sum_output, sum_value, sum_query, sum_key = settle_rows(
+        jnp.stack(blocks), sum_output, sum_value, sum_both
+    )
     factor = clip_threshold / jnp.maximum(head_top, clip_threshold)
     spread = jnp.repeat(jnp.sqrt(factor), HD)
     query_clipped = (w_query.astype(F32) * spread[None, :]).astype(BF16)
@@ -998,7 +1080,7 @@
         sum_query,
         sum_key,
         sum_value,
-        ordered,
+        sum_output,
         sum_query_gain,
         sum_key_gain,
         sum_moe_gain,

time: 1440 us -> 1400 us (0.972)
  waiting for transfers between devices: 689 us -> 622 us
  starting transfers between devices: 98.9 us -> 130 us
    psum x1 -> x0, waiting for transfers between devices: 66.2 us -> none  [per_device(): sum_output = lax.psum(grad_output, 'expert').astype(F32)]
    ppermute x90 -> x108, starting transfers between devices: 84.6 us -> 116 us  [send(): return lax.ppermute(value, BOTH, flip(dz, dx, dy, dc))]
    ppermute x90 -> x108, waiting for transfers between devices: 623 us -> 622 us  [send(): return lax.ppermute(value, BOTH, flip(dz, dx, dy, dc))]
  transfers between devices with their start and end apart: 95 -> 110, of which waited for: 32 -> 43; matrix products, arithmetic and copies ran while one was open for 9% -> 12% of each run, Pallas kernels for 27% -> 30%
where the time goes in v5:
time: 1400 us; the launch traced here: 1390 us
  waiting for transfers between devices  622 us (44%)
  Pallas kernels  458 us (33%)
  starting transfers between devices  130 us (9%)
  other arithmetic  74.2 us (5%)
  local copies, waits for them, and re-layouts  49.3 us (4%)
  matrix products  47.5 us (3%)
    ppermute x108, waiting for transfers between devices, send(): return lax.ppermute(value, BOTH, flip(dz, dx, dy, dc))  622 us
    ppermute x108, starting transfers between devices, send(): return lax.ppermute(value, BOTH, flip(dz, dx, dy, dc))  116 us
    pallas_call x4, Pallas kernels, expert_slot(): pl.pallas_call(partial(expert_kernel, slices), grid_spec=pltpu.PrefetchSc...  112 us
    pallas_call x6, Pallas kernels, place_rows(): pl.pallas_call(partial(place_kernel, slices, held, slots), grid_spec=pltp...  107 us
    pallas_call x8, Pallas kernels, pick_rows(): pl.pallas_call(partial(pick_kernel, group, slices), grid_spec=pltpu.Prefe...  81.3 us
    pallas_call x2, Pallas kernels, weight_grads(): pl.pallas_call(partial(kernel, slots, slices), grid_spec=pltpu.PrefetchSc...  70.4 us
    pallas_call x2, Pallas kernels, down_slots(): pl.pallas_call(partial(down_kernel, slices, slots), grid_spec=pltpu.Prefe...  31.5 us
  transfers between devices with their start and end apart: 110, of which 43 were waited for; matrix products, arithmetic and copies ran while one was open for 12% of the time, Pallas kernels for 30%

profile of v5, /device:TPU:10, one launch (start us, length us, event | category | flops | bytes accessed | tf_op | source)
XLA Modules:
  0.0 1389.8 jit_solution(9573489836677524193)
XLA Ops:
  10.1 15.6 %project.1 = (bf16[1024,2048]{1,0:T(8,128)(2,1)}, f32[1024,1]{1,0:T(8,128)}, f32[1024,512]{1,0:T(8,128)}, f32[1024,512]{1,0:T(8,128)}, bf16[1024,512]{1,0:T(8,12...) custom-call(bf16[1024,2048]{1,0:T(8,128)(2,1)} %in_ref.1, f32[1,2048]{1,0:T(1,128)} %bitcast.208, ...), custom_call_target="tpu_custom_call" | custom-call | flops 103079215104 | bytes 352321536 | tf_op jit(solution)/shard_map/project/pallas_call | solution.py:638
  33.3 23.5 %collective-permute-done.2 = s32[4,8,1024]{2,1,0:T(8,128)S(1)} collective-permute-done((s32[4,8,1024]{2,1,0:T(8,128)S(1)}, s32[4,8,1024]{2,1,0:T(8,128)S(1)}, u32[]{:S(2)}, u32[]{:S(2)}) %collective-permute-start.2) | collective-permute-done | bytes 131104 | tf_op jit(solution)/shard_map/ppermute | solution.py:83
  77.8 22.2 %collective-permute-done.8 = bf16[1024,512]{1,0:T(8,128)(2,1)S(1)} collective-permute-done((bf16[1024,512]{1,0:T(8,128)(2,1)S(1)}, bf16[1024,512]{1,0:T(8,128)(2,1)S(1)}, u32[]{:S(2)}, u32[]{:S(2)}) %collective-permute-start.8) | collective-permute-done | bytes 1048608 | tf_op jit(solution)/shard_map/ppermute | solution.py:83
  198.5 21.7 %collective-permute-done.17.refs_5_ = bf16[1024,512]{1,0:T(8,128)(2,1)} collective-permute-done((bf16[1024,512]{1,0:T(8,128)(2,1)}, bf16[1024,512]{1,0:T(8,128)(2,1)}, u32[]{:S(2)}, u32[]{:S(2)}) %collective-permute-start.17) | collective-permute-done | bytes 1048608 | tf_op jit(solution)/shard_map/ppermute | solution.py:83
  233.8 28.9 %collective-permute-done.24.refs_2_ = bf16[1024,512]{1,0:T(8,128)(2,1)} collective-permute-done((bf16[1024,512]{1,0:T(8,128)(2,1)}, bf16[1024,512]{1,0:T(8,128)(2,1)}, u32[]{:S(2)}, u32[]{:S(2)}) %collective-permute-start.24) | collective-permute-done | bytes 1048608 | tf_op jit(solution)/shard_map/ppermute | solution.py:83
  291.2 27.8 %expert_slot.4 = (bf16[8,320,256]{2,1,0:T(8,128)(2,1)}, bf16[8,320,256]{2,1,0:T(8,128)(2,1)}, bf16[8,320,256]{2,1,0:T(8,128)(2,1)}, f32[8,2,1024]{2,1,0:T(2,128)...) custom-call(s32[10]{0:T(128)} %stack.118.where_ref, s32[8,8,1024]{2,1,0:T(8,128)} %copy.160.refs_0_.refs_1_, ...), custom_call_target="tpu_custom_call" | custom-call | flops 214748364800 | bytes 905969664 | tf_op jit(solution)/shard_map/expert_slot/pallas_call | solution.py:393
  320.9 14.3 %collective-permute-done.27.refs_5_ = bf16[1024,512]{1,0:T(8,128)(2,1)} collective-permute-done((bf16[1024,512]{1,0:T(8,128)(2,1)}, bf16[1024,512]{1,0:T(8,128)(2,1)}, u32[]{:S(2)}, u32[]{:S(2)}) %collective-permute-start.27) | collective-permute-done | bytes 1048608 | tf_op jit(solution)/shard_map/ppermute | solution.py:83
  356.0 14.4 %place_rows.6 = (bf16[1,1024,512]{2,1,0:T(8,128)(2,1)}, bf16[1,1024,512]{2,1,0:T(8,128)(2,1)}, bf16[1,1024,512]{2,1,0:T(8,128)(2,1)}, bf16[1,1024,512]{2,1,0:T(8,128)(2,1)}) custom-call(s32[2]{0:T(128)} %bitcast.204, s32[8,1024,8]{2,1,0:T(8,128)} %bitcast.151, s32[8,1024,8]{2,1,0:T(8,128)} %bitcast.152, ...), custom_call_target="tpu_custom_call" | custom-call | flops 85899345920 | bytes 234881024 | tf_op jit(solution)/shard_map/place_rows/pallas_call | solution.py:492
  377.6 18.0 %collective-permute-done.42 = bf16[1024,512]{1,0:T(8,128)(2,1)S(1)} collective-permute-done((bf16[1024,512]{1,0:T(8,128)(2,1)}, bf16[1024,512]{1,0:T(8,128)(2,1)S(1)}, u32[]{:S(2)}, u32[]{:S(2)}) %collective-permute-start.42) | collective-permute-done | bytes 1048608 | tf_op jit(solution)/shard_map/ppermute | solution.py:83
  403.3 27.8 %expert_slot.5 = (bf16[8,320,256]{2,1,0:T(8,128)(2,1)}, bf16[8,320,256]{2,1,0:T(8,128)(2,1)}, bf16[8,320,256]{2,1,0:T(8,128)(2,1)}, f32[8,2,1024]{2,1,0:T(2,128)...) custom-call(s32[10]{0:T(128)} %stack.127.where_ref, s32[8,8,1024]{2,1,0:T(8,128)} %copy.160.refs_0_.refs_1_, ...), custom_call_target="tpu_custom_call" | custom-call | flops 214748364800 | bytes 905969664 | tf_op jit(solution)/shard_map/expert_slot/pallas_call | solution.py:393
  431.1 17.6 %collective-permute-done.46.refs_4_ = bf16[1024,512]{1,0:T(8,128)(2,1)} collective-permute-done((bf16[1024,512]{1,0:T(8,128)(2,1)}, bf16[1024,512]{1,0:T(8,128)(2,1)}, u32[]{:S(2)}, u32[]{:S(2)}) %collective-permute-start.46) | collective-permute-done | bytes 1048608 | tf_op jit(solution)/shard_map/ppermute | solution.py:83
  450.7 18.4 %collective-permute-done.35.refs_5_ = bf16[1024,512]{1,0:T(8,128)(2,1)} collective-permute-done((bf16[1024,512]{1,0:T(8,128)(2,1)}, bf16[1024,512]{1,0:T(8,128)(2,1)}, u32[]{:S(2)}, u32[]{:S(2)}) %collective-permute-start.35) | collective-permute-done | bytes 1048608 | tf_op jit(solution)/shard_map/ppermute | solution.py:83
  492.7 14.0 %place_rows.7 = (bf16[1,1024,512]{2,1,0:T(8,128)(2,1)}, bf16[1,1024,512]{2,1,0:T(8,128)(2,1)}, bf16[1,1024,512]{2,1,0:T(8,128)(2,1)}, bf16[1,1024,512]{2,1,0:T(8,128)(2,1)}) custom-call(s32[2]{0:T(128)} %bitcast.206, s32[8,1024,8]{2,1,0:T(8,128)} %bitcast.153, s32[8,1024,8]{2,1,0:T(8,128)} %bitcast.154, ...), custom_call_target="tpu_custom_call" | custom-call | flops 85899345920 | bytes 234881024 | tf_op jit(solution)/shard_map/place_rows/pallas_call | solution.py:492
  508.2 27.8 %expert_slot.6 = (bf16[8,320,256]{2,1,0:T(8,128)(2,1)}, bf16[8,320,256]{2,1,0:T(8,128)(2,1)}, bf16[8,320,256]{2,1,0:T(8,128)(2,1)}, f32[8,2,1024]{2,1,0:T(2,128)...) custom-call(s32[10]{0:T(128)} %stack.124.where_ref, s32[8,8,1024]{2,1,0:T(8,128)} %copy.160.refs_0_.refs_1_, ...), custom_call_target="tpu_custom_call" | custom-call | flops 214748364800 | bytes 905969664 | tf_op jit(solution)/shard_map/expert_slot/pallas_call | solution.py:393
  547.4 13.8 place_rows.8
  561.3 28.2 %expert_slot.7 = (bf16[8,320,256]{2,1,0:T(8,128)(2,1)}, bf16[8,320,256]{2,1,0:T(8,128)(2,1)}, bf16[8,320,256]{2,1,0:T(8,128)(2,1)}, f32[8,2,1024]{2,1,0:T(2,128)...) custom-call(s32[10]{0:T(128)} %stack.121.where_ref, s32[8,8,1024]{2,1,0:T(8,128)} %copy.160.refs_0_.refs_1_, ...), custom_call_target="tpu_custom_call" | custom-call | flops 214748364800 | bytes 905969664 | tf_op jit(solution)/shard_map/expert_slot/pallas_call | solution.py:393
  608.5 15.7 %down_slots.2 = (bf16[4,2,1280,512]{3,2,1,0:T(8,128)(2,1)}, bf16[4,2,1280,512]{3,2,1,0:T(8,128)(2,1)}) custom-call(s32[10]{0:T(128)} %stack.118.where_ref, bf16[8,320,256]{2,1,0:T(8,128)(2,1)} %get-tuple-element.147.refs_0_.refs_8_, bf16[8,320,256]{2,1,0:T(8,128)(2,1)} %get-tuple-element.175.refs_1_.refs_9_, bf16[8,256,2048]{2,1,0:T(8,128)(2,1)} %refs_2_.3), custom_call_target="tpu_custom_call" | custom-call | flops 85899345920 | bytes 469762048 | tf_op jit(solution)/shard_map/down_slots/pallas_call | solution.py:433
  624.5 28.4 %collective-permute-done.56 = bf16[1024,512]{1,0:T(8,128)(2,1)S(1)} collective-permute-done((bf16[1024,512]{1,0:T(8,128)(2,1)}, bf16[1024,512]{1,0:T(8,128)(2,1)S(1)}, u32[]{:S(2)}, u32[]{:S(2)}) %collective-permute-start.56) | collective-permute-done | bytes 1048608 | tf_op jit(solution)/shard_map/ppermute | solution.py:83
  655.3 13.9 %place_rows.9 = (bf16[1,1024,512]{2,1,0:T(8,128)(2,1)}, bf16[1,1024,512]{2,1,0:T(8,128)(2,1)}, bf16[1,1024,512]{2,1,0:T(8,128)(2,1)}, bf16[1,1024,512]{2,1,0:T(8,128)(2,1)}) custom-call(s32[2]{0:T(128)} %bitcast.210, s32[8,1024,8]{2,1,0:T(8,128)} %bitcast.157, s32[8,1024,8]{2,1,0:T(8,128)} %bitcast.158, ...), custom_call_target="tpu_custom_call" | custom-call | flops 85899345920 | bytes 234881024 | tf_op jit(solution)/shard_map/place_rows/pallas_call | solution.py:492
  708.3 15.8 %down_slots.3 = (bf16[4,2,1280,512]{3,2,1,0:T(8,128)(2,1)}, bf16[4,2,1280,512]{3,2,1,0:T(8,128)(2,1)}) custom-call(s32[10]{0:T(128)} %stack.118.where_ref, bf16[8,320,256]{2,1,0:T(8,128)(2,1)} %get-tuple-element.155.refs_0_.refs_10_, bf16[8,320,256]{2,1,0:T(8,128)(2,1)} %get-tuple-element.164.refs_1_.refs_11_, bf16[8,256,2048]{2,1,0:T(8,128)(2,1)} %refs_2_.3), custom_call_target="tpu_custom_call" | custom-call | flops 85899345920 | bytes 469762048 | tf_op jit(solution)/shard_map/down_slots/pallas_call | solution.py:433
  732.9 25.4 %place_rows.10 = (bf16[2,1024,512]{2,1,0:T(8,128)(2,1)}, bf16[2,1024,512]{2,1,0:T(8,128)(2,1)}, bf16[2,1024,512]{2,1,0:T(8,128)(2,1)}, bf16[2,1024,512]{2,1,0:T(8,128)(2,1)}) custom-call(s32[4]{0:T(128)} %pad_add_fusion.3.where_ref, s32[8,1024,8]{2,1,0:T(8,128)} %bitcast.159, s32[8,1024,8]{2,1,0:T(8,128)} %bitcast.160, s32[8,1024,8]{2,1,0:T(8,128)} %bitcast.161, ...), custom_call_target="tpu_custom_call" | custom-call | flops 171798691840 | bytes 469762048 | tf_op jit(solution)/shard_map/place_rows/pallas_call | solution.py:492
  758.4 42.9 %weight_grads.1 = (f32[8,2048,256]{2,1,0:T(8,128)}, f32[8,2048,256]{2,1,0:T(8,128)}) custom-call(s32[10]{0:T(128)} %stack.118.where_ref, bf16[2,2,1280,512]{3,2,1,0:T(8,128)(2,1)} %pick_rows.9.refs_4_.refs_0_, bf16[2,2,1280,512]{3,2,1,0:T(8,128)(2,1)} %collective-permute-done.20.refs_5_.refs_1_, bf16[2,2,1280,512]{3,2,1,0:T(8,128)(2,1)} %pick_rows.15.refs_4_.refs_2_, ...), custom_call_target="tpu_custom_call" | custom-call | flops 160000000000 | bytes 16000000 | tf_op jit(solution)/shard_map/weight_grads/pallas_call | solution.py:549
  814.2 22.7 %collective-permute-done.70 = bf16[1024,512]{1,0:T(8,128)(2,1)S(1)} collective-permute-done((bf16[1024,512]{1,0:T(8,128)(2,1)}, bf16[1024,512]{1,0:T(8,128)(2,1)S(1)}, u32[]{:S(2)}, u32[]{:S(2)}) %collective-permute-start.70) | collective-permute-done | bytes 1048608 | tf_op jit(solution)/shard_map/ppermute | solution.py:83
  927.7 25.2 %place_rows.11 = (bf16[2,1024,512]{2,1,0:T(8,128)(2,1)}, bf16[2,1024,512]{2,1,0:T(8,128)(2,1)}, bf16[2,1024,512]{2,1,0:T(8,128)(2,1)}, bf16[2,1024,512]{2,1,0:T(8,128)(2,1)}) custom-call(s32[4]{0:T(128)} %pad_add_fusion.4.where_ref, s32[8,1024,8]{2,1,0:T(8,128)} %bitcast.163, s32[8,1024,8]{2,1,0:T(8,128)} %bitcast.164, s32[8,1024,8]{2,1,0:T(8,128)} %bitcast.165, ...), custom_call_target="tpu_custom_call" | custom-call | flops 171798691840 | bytes 469762048 | tf_op jit(solution)/shard_map/place_rows/pallas_call | solution.py:492
  952.9 16.3 %attend_back.1 = (bf16[1024,512]{1,0:T(8,128)(2,1)}, bf16[1024,512]{1,0:T(8,128)(2,1)}, bf16[1024,512]{1,0:T(8,128)(2,1)}, f32[1,1,512]{2,1,0:T(1,128)}, f32[1,1,512]{2,1,0:T(1,128)}) custom-call(s32[4]{0:T(128)} %add_bitcast_fusion.pieces_ref, bf16[1024,512]{1,0:T(8,128)(2,1)} %get-tuple-element.138.q_ref, bf16[1024,512]{1,0:T(8,128)(2,1)} %get-tuple-element.139.k_ref, ...), custom_call_target="tpu_custom_call" | custom-call | flops 85899345920 | bytes 184549376 | tf_op jit(solution)/shard_map/attend_back/pallas_call | solution.py:773
  1027.4 16.6 %collective-permute-done.102 = bf16[1024,1024]{1,0:T(8,128)(2,1)S(1)} collective-permute-done((bf16[1024,1024]{1,0:T(8,128)(2,1)S(1)}, bf16[1024,1024]{1,0:T(8,128)(2,1)S(1)}, u32[]{:S(2)}, u32[]{:S(2)}) %collective-permute-start.102) | collective-permute-done | bytes 2097184 | tf_op jit(solution)/shard_map/ppermute | solution.py:83
  1050.0 27.5 %weight_down_grads.1 = f32[8,256,2048]{2,1,0:T(8,128)} custom-call(s32[10]{0:T(128)} %stack.118.where_ref, bf16[2,2,1280,512]{3,2,1,0:T(8,128)(2,1)} %pick_rows.8.refs_6_.refs_0_, bf16[2,2,1280,512]{3,2,1,0:T(8,128)(2,1)} %collective-permute-done.21.refs_7_.refs_1_, bf16[2,2,1280,512]{3,2,1,0:T(8,128)(2,1)} %pick_rows.14.refs_6_.refs_2_, ...), custom_call_target="tpu_custom_call" | custom-call | flops 160000000000 | bytes 16000000 | tf_op jit(solution)/shard_map/weight_down_grads/pallas_call | solution.py:549
  1090.4 43.1 %collective-permute-done.87 = f32[69,512]{1,0:T(8,128)S(1)} collective-permute-done((f32[69,512]{1,0:T(8,128)S(1)}, f32[69,512]{1,0:T(8,128)S(1)}, u32[]{:S(2)}, u32[]{:S(2)}) %collective-permute-start.87) | collective-permute-done | bytes 141344 | tf_op jit(solution)/shard_map/ppermute | solution.py:83
  1170.6 108.1 %collective-permute-done.89 = f32[69,512]{1,0:T(8,128)S(1)} collective-permute-done((f32[69,512]{1,0:T(8,128)S(1)}, f32[69,512]{1,0:T(8,128)S(1)}, u32[]{:S(2)}, u32[]{:S(2)}) %collective-permute-start.89) | collective-permute-done | bytes 141344 | tf_op jit(solution)/shard_map/ppermute | solution.py:83
  1290.5 15.7 %collective-permute-done.106 = bf16[512,1024]{1,0:T(8,128)(2,1)S(1)} collective-permute-done((bf16[512,1024]{1,0:T(8,128)(2,1)S(1)}, bf16[512,1024]{1,0:T(8,128)(2,1)S(1)}, u32[]{:S(2)}, u32[]{:S(2)}) %collective-permute-start.106) | collective-permute-done | bytes 1048608 | tf_op jit(solution)/shard_map/ppermute | solution.py:83
  1325.7 16.0 %collective-permute-done.79 = bf16[1024,512]{1,0:T(8,128)(2,1)S(1)} collective-permute-done((bf16[1024,512]{1,0:T(8,128)(2,1)S(1)}, bf16[1024,512]{1,0:T(8,128)(2,1)S(1)}, u32[]{:S(2)}, u32[]{:S(2)}) %collective-permute-start.79) | collective-permute-done | bytes 1048608 | tf_op jit(solution)/shard_map/ppermute | solution.py:83
  1343.6 33.2 %collective-permute-done.101.refs_3_ = bf16[1024,512]{1,0:T(8,128)(2,1)S(1)} collective-permute-done((bf16[1024,512]{1,0:T(8,128)(2,1)S(1)}, bf16[1024,512]{1,0:T(8,128)(2,1)S(1)}, u32[]{:S(2)}, u32[]{:S(2)}) %collective-permute-start.101) | collective-permute-done | bytes 1048608 | tf_op jit(solution)/shard_map/ppermute | solution.py:83
  (535 shorter events, 586.8 us)
Async XLA Ops:
  4.0 65.3 %collective-permute-start.5 = (bf16[1024,512]{1,0:T(8,128)(2,1)}, bf16[1024,512]{1,0:T(8,128)(2,1)}, u32[]{:S(2)}, u32[]{:S(2)}) collective-permute-start(bf16[1024,512]{1,0:T(8,128)(2,1)} %convert_element_type.331.refs_2_), channel_id=1, source_target_pairs={{0,16},{1,17},{2,18},{3,19},{4,20},{5,21},{6,22},{7,23},{8,24},{9,... | collective-permute-start | bytes 3145736 | tf_op jit(solution)/shard_map/ppermute | solution.py:83
  76.3 94.8 %collective-permute-start.13 = (bf16[1024,512]{1,0:T(8,128)(2,1)}, bf16[1024,512]{1,0:T(8,128)(2,1)}, u32[]{:S(2)}, u32[]{:S(2)}) collective-permute-start(bf16[1024,512]{1,0:T(8,128)(2,1)} %convert_element_type.331.refs_2_), channel_id=1, source_target_pairs={{0,24},{1,25},{2,26},{3,27},{4,28},{5,29},{6,30},{7,31},{8,16},{9,... | collective-permute-start | bytes 3145736 | tf_op jit(solution)/shard_map/ppermute | solution.py:83
  148.9 142.3 %all-to-all-start = ((f32[8,8,1024]{2,1,0:T(8,128)}), f32[8,8,1024]{2,1,0:T(8,128)}, u32[]{:S(2)}, u32[]{:S(2)}) async-start(f32[8,8,1024]{2,1,0:T(8,128)} %fusion.83), calls=%async_computation | async-start | bytes 524288 | tf_op jit(solution)/shard_map/all_to_all | solution.py:911
  180.5 95.0 %collective-permute-start.23 = (bf16[1024,512]{1,0:T(8,128)(2,1)}, bf16[1024,512]{1,0:T(8,128)(2,1)}, u32[]{:S(2)}, u32[]{:S(2)}) collective-permute-start(bf16[1024,512]{1,0:T(8,128)(2,1)} %collective-permute-done.13.refs_2_), channel_id=1, source_target_pairs={{0,2},{1,3},{2,0},{3,1},{4,6},{5,7},{6,4},{7,5},{8,10},{9,11},{10,... | collective-permute-start | bytes 3145736 | tf_op jit(solution)/shard_map/ppermute | solution.py:83
  182.0 93.9 %collective-permute-start.19 = (bf16[1024,512]{1,0:T(8,128)(2,1)}, bf16[1024,512]{1,0:T(8,128)(2,1)}, u32[]{:S(2)}, u32[]{:S(2)}) collective-permute-start(bf16[1024,512]{1,0:T(8,128)(2,1)} %collective-permute-done.13.refs_2_), channel_id=1, source_target_pairs={{0,4},{1,5},{2,6},{3,7},{4,0},{5,1},{6,2},{7,3},{8,12},{9,13},{10,... | collective-permute-start | bytes 3145736 | tf_op jit(solution)/shard_map/ppermute | solution.py:83
  197.0 67.3 %collective-permute-start.18 = (bf16[1024,512]{1,0:T(8,128)(2,1)S(1)}, bf16[1024,512]{1,0:T(8,128)(2,1)S(1)}, u32[]{:S(2)}, u32[]{:S(2)}) collective-permute-start(bf16[1024,512]{1,0:T(8,128)(2,1)S(1)} %collective-permute-done.12.refs_4_), channel_id=1, source_target_pairs={{0,2},{1,3},{2,0},{3,1},{4,6},{5,7},{6,4},{7,5},{8,10},{9,11},{10,... | collective-permute-start | bytes 3145736 | tf_op jit(solution)/shard_map/ppermute | solution.py:83
  275.5 101.6 %collective-permute-start.39 = (bf16[1024,512]{1,0:T(8,128)(2,1)}, bf16[1024,512]{1,0:T(8,128)(2,1)}, u32[]{:S(2)}, u32[]{:S(2)}) collective-permute-start(bf16[1024,512]{1,0:T(8,128)(2,1)} %collective-permute-done.37.refs_2_), channel_id=1, source_target_pairs={{0,4},{1,5},{2,6},{3,7},{4,0},{5,1},{6,2},{7,3},{8,12},{9,13},{10,... | collective-permute-start | bytes 3145736 | tf_op jit(solution)/shard_map/ppermute | solution.py:83
  275.9 69.4 %collective-permute-start.29 = (bf16[1024,512]{1,0:T(8,128)(2,1)}, bf16[1024,512]{1,0:T(8,128)(2,1)}, u32[]{:S(2)}, u32[]{:S(2)}) collective-permute-start(bf16[1024,512]{1,0:T(8,128)(2,1)} %collective-permute-done.23.refs_3_), channel_id=1, source_target_pairs={{0,4},{1,5},{2,6},{3,7},{4,0},{5,1},{6,2},{7,3},{8,12},{9,13},{10,... | collective-permute-start | bytes 3145736 | tf_op jit(solution)/shard_map/ppermute | solution.py:83
  377.1 104.4 %collective-permute-start.38 = (bf16[1024,512]{1,0:T(8,128)(2,1)}, bf16[1024,512]{1,0:T(8,128)(2,1)}, u32[]{:S(2)}, u32[]{:S(2)}) collective-permute-start(bf16[1024,512]{1,0:T(8,128)(2,1)} %collective-permute-done.37.refs_2_), channel_id=1, source_target_pairs={{0,2},{1,3},{2,0},{3,1},{4,6},{5,7},{6,4},{7,5},{8,10},{9,11},{10,... | collective-permute-start | bytes 3145736 | tf_op jit(solution)/shard_map/ppermute | solution.py:83
  395.7 86.3 %collective-permute-start.40 = (bf16[1024,512]{1,0:T(8,128)(2,1)}, bf16[1024,512]{1,0:T(8,128)(2,1)}, u32[]{:S(2)}, u32[]{:S(2)}) collective-permute-start(bf16[1024,512]{1,0:T(8,128)(2,1)} %collective-permute-done.39.refs_4_), channel_id=1, source_target_pairs={{0,2},{1,3},{2,0},{3,1},{4,6},{5,7},{6,4},{7,5},{8,10},{9,11},{10,... | collective-permute-start | bytes 3145736 | tf_op jit(solution)/shard_map/ppermute | solution.py:83
  401.8 67.3 %collective-permute-start.35 = (bf16[1024,512]{1,0:T(8,128)(2,1)}, bf16[1024,512]{1,0:T(8,128)(2,1)}, u32[]{:S(2)}, u32[]{:S(2)}) collective-permute-start(bf16[1024,512]{1,0:T(8,128)(2,1)} %collective-permute-done.33.refs_3_), channel_id=1, source_target_pairs={{0,4},{1,5},{2,6},{3,7},{4,0},{5,1},{6,2},{7,3},{8,12},{9,13},{10,... | collective-permute-start | bytes 3145736 | tf_op jit(solution)/shard_map/ppermute | solution.py:83
  448.6 87.4 %collective-permute-start.45 = (bf16[1024,512]{1,0:T(8,128)(2,1)}, bf16[1024,512]{1,0:T(8,128)(2,1)}, u32[]{:S(2)}, u32[]{:S(2)}) collective-permute-start(bf16[1024,512]{1,0:T(8,128)(2,1)} %collective-permute-done.44.refs_2_), channel_id=1, source_target_pairs={{0,2},{1,3},{2,0},{3,1},{4,6},{5,7},{6,4},{7,5},{8,10},{9,11},{10,... | collective-permute-start | bytes 3145736 | tf_op jit(solution)/shard_map/ppermute | solution.py:83
  449.1 87.0 %collective-permute-start.47 = (bf16[1024,512]{1,0:T(8,128)(2,1)}, bf16[1024,512]{1,0:T(8,128)(2,1)}, u32[]{:S(2)}, u32[]{:S(2)}) collective-permute-start(bf16[1024,512]{1,0:T(8,128)(2,1)} %collective-permute-done.46.refs_4_), channel_id=1, source_target_pairs={{0,2},{1,3},{2,0},{3,1},{4,6},{5,7},{6,4},{7,5},{8,10},{9,11},{10,... | collective-permute-start | bytes 3145736 | tf_op jit(solution)/shard_map/ppermute | solution.py:83
  480.0 66.8 %collective-permute-start.48 = (bf16[1024,512]{1,0:T(8,128)(2,1)}, bf16[1024,512]{1,0:T(8,128)(2,1)}, u32[]{:S(2)}, u32[]{:S(2)}) collective-permute-start(bf16[1024,512]{1,0:T(8,128)(2,1)} %bitcast.28), channel_id=1, source_target_pairs={{0,4},{1,5},{2,6},{3,7},{4,0},{5,1},{6,2},{7,3},{8,12},{9,13},{10,... | collective-permute-start | bytes 3145736 | tf_op jit(solution)/shard_map/ppermute | solution.py:83
  481.5 65.2 %collective-permute-start.49 = (bf16[1024,512]{1,0:T(8,128)(2,1)}, bf16[1024,512]{1,0:T(8,128)(2,1)}, u32[]{:S(2)}, u32[]{:S(2)}) collective-permute-start(bf16[1024,512]{1,0:T(8,128)(2,1)} %fusion.37), channel_id=1, source_target_pairs={{0,2},{1,3},{2,0},{3,1},{4,6},{5,7},{6,4},{7,5},{8,10},{9,11},{10,... | collective-permute-start | bytes 3145736 | tf_op jit(solution)/shard_map/ppermute | solution.py:83
  602.9 66.3 %collective-permute-start.55 = (bf16[1024,512]{1,0:T(8,128)(2,1)}, bf16[1024,512]{1,0:T(8,128)(2,1)}, u32[]{:S(2)}, u32[]{:S(2)}) collective-permute-start(bf16[1024,512]{1,0:T(8,128)(2,1)} %bitcast.32), channel_id=1, source_target_pairs={{0,2},{1,3},{2,0},{3,1},{4,6},{5,7},{6,4},{7,5},{8,10},{9,11},{10,... | collective-permute-start | bytes 3145736 | tf_op jit(solution)/shard_map/ppermute | solution.py:83
  624.2 108.1 %collective-permute-start.58 = (bf16[4,2,1280,512]{3,2,1,0:T(8,128)(2,1)}, bf16[4,2,1280,512]{3,2,1,0:T(8,128)(2,1)}, u32[]{:S(2)}, u32[]{:S(2)}) collective-permute-start(bf16[4,2,1280,512]{3,2,1,0:T(8,128)(2,1)} %get-tuple-element.189), channel_id=1, source_target_pairs={{0,1},{1,0},{2,3},{3,2},{4,5},{5,4},{6,7},{7,6},{8,9},{9,8},{10,11... | collective-permute-start | bytes 31457288 | tf_op jit(solution)/shard_map/ppermute | solution.py:83
  685.5 115.7 %collective-permute-start.64 = (bf16[1024,512]{1,0:T(8,128)(2,1)}, bf16[1024,512]{1,0:T(8,128)(2,1)}, u32[]{:S(2)}, u32[]{:S(2)}) collective-permute-start(bf16[1024,512]{1,0:T(8,128)(2,1)} %fusion.30), channel_id=1, source_target_pairs={{0,16},{1,17},{2,18},{3,19},{4,20},{5,21},{6,22},{7,23},{8,24},{9,... | collective-permute-start | bytes 3145736 | tf_op jit(solution)/shard_map/ppermute | solution.py:83
  691.8 109.4 %collective-permute-start.65 = (bf16[1024,512]{1,0:T(8,128)(2,1)}, bf16[1024,512]{1,0:T(8,128)(2,1)}, u32[]{:S(2)}, u32[]{:S(2)}) collective-permute-start(bf16[1024,512]{1,0:T(8,128)(2,1)} %fusion.28), channel_id=1, source_target_pairs={{0,24},{1,25},{2,26},{3,27},{4,28},{5,29},{6,30},{7,31},{8,16},{9,... | collective-permute-start | bytes 3145736 | tf_op jit(solution)/shard_map/ppermute | solution.py:83
  727.4 200.2 %collective-permute-start.74 = (bf16[4,2,1280,512]{3,2,1,0:T(8,128)(2,1)}, bf16[4,2,1280,512]{3,2,1,0:T(8,128)(2,1)}, u32[]{:S(2)}, u32[]{:S(2)}) collective-permute-start(bf16[4,2,1280,512]{3,2,1,0:T(8,128)(2,1)} %get-tuple-element.225), channel_id=1, source_target_pairs={{0,1},{1,0},{2,3},{3,2},{4,5},{5,4},{6,7},{7,6},{8,9},{9,8},{10,11... | collective-permute-start | bytes 31457288 | tf_op jit(solution)/shard_map/ppermute | solution.py:83
  731.5 69.8 %collective-permute-start.63 = (bf16[1024,512]{1,0:T(8,128)(2,1)}, bf16[1024,512]{1,0:T(8,128)(2,1)}, u32[]{:S(2)}, u32[]{:S(2)}) collective-permute-start(bf16[1024,512]{1,0:T(8,128)(2,1)} %fusion.32), channel_id=1, source_target_pairs={{0,8},{1,9},{2,10},{3,11},{4,12},{5,13},{6,14},{7,15},{8,0},{9,1},... | collective-permute-start | bytes 3145736 | tf_op jit(solution)/shard_map/ppermute | solution.py:83
  920.2 388.0 %collective-permute-start.73 = (bf16[2,1024,512]{2,1,0:T(8,128)(2,1)}, bf16[2,1024,512]{2,1,0:T(8,128)(2,1)}, u32[]{:S(2)}, u32[]{:S(2)}) collective-permute-start(bf16[2,1024,512]{2,1,0:T(8,128)(2,1)} %get-tuple-element.223), channel_id=1, source_target_pairs={{0,2},{1,3},{2,0},{3,1},{4,6},{5,7},{6,4},{7,5},{8,10},{9,11},{10,... | collective-permute-start | bytes 6291464 | tf_op jit(solution)/shard_map/ppermute | solution.py:83
  1012.1 65.4 %collective-permute-start.82 = (bf16[1024,512]{1,0:T(8,128)(2,1)}, bf16[1024,512]{1,0:T(8,128)(2,1)}, u32[]{:S(2)}, u32[]{:S(2)}) collective-permute-start(bf16[1024,512]{1,0:T(8,128)(2,1)} %fusion.49), channel_id=1, source_target_pairs={{0,1},{1,0},{2,3},{3,2},{4,5},{5,4},{6,7},{7,6},{8,9},{9,8},{10,11... | collective-permute-start | bytes 3145736 | tf_op jit(solution)/shard_map/ppermute | solution.py:83
  1049.4 85.5 %collective-permute-start.103 = (bf16[512,1024]{1,0:T(8,128)(2,1)}, bf16[512,1024]{1,0:T(8,128)(2,1)}, u32[]{:S(2)}, u32[]{:S(2)}) collective-permute-start(bf16[512,1024]{1,0:T(8,128)(2,1)} %slice.229), channel_id=1, source_target_pairs={{0,8},{1,9},{2,10},{3,11},{4,12},{5,13},{6,14},{7,15},{8,0},{9,1},... | collective-permute-start | bytes 3145736 | tf_op jit(solution)/shard_map/ppermute | solution.py:83
  1080.3 80.9 %collective-permute-start.77 = (bf16[2,1024,512]{2,1,0:T(8,128)(2,1)}, bf16[2,1024,512]{2,1,0:T(8,128)(2,1)}, u32[]{:S(2)}, u32[]{:S(2)}) collective-permute-start(bf16[2,1024,512]{2,1,0:T(8,128)(2,1)} %get-tuple-element.234), channel_id=1, source_target_pairs={{0,2},{1,3},{2,0},{3,1},{4,6},{5,7},{6,4},{7,5},{8,10},{9,11},{10,... | collective-permute-start | bytes 6291464 | tf_op jit(solution)/shard_map/ppermute | solution.py:83
  1084.3 76.9 %collective-permute-start.76 = (bf16[2,1024,512]{2,1,0:T(8,128)(2,1)}, bf16[2,1024,512]{2,1,0:T(8,128)(2,1)}, u32[]{:S(2)}, u32[]{:S(2)}) collective-permute-start(bf16[2,1024,512]{2,1,0:T(8,128)(2,1)} %add_convert_fusion.2), channel_id=1, source_target_pairs={{0,4},{1,5},{2,6},{3,7},{4,0},{5,1},{6,2},{7,3},{8,12},{9,13},{10,... | collective-permute-start | bytes 6291464 | tf_op jit(solution)/shard_map/ppermute | solution.py:83
  1151.3 157.4 %collective-permute-start.72 = (bf16[2,1024,512]{2,1,0:T(8,128)(2,1)S(1)}, bf16[2,1024,512]{2,1,0:T(8,128)(2,1)S(1)}, u32[]{:S(2)}, u32[]{:S(2)}) collective-permute-start(bf16[2,1024,512]{2,1,0:T(8,128)(2,1)S(1)} %copy-done.18), channel_id=1, source_target_pairs={{0,4},{1,5},{2,6},{3,7},{4,0},{5,1},{6,2},{7,3},{8,12},{9,13},{10,... | collective-permute-start | bytes 6291464 | tf_op jit(solution)/shard_map/ppermute | solution.py:83
  1157.8 122.5 %collective-permute-start.105 = (bf16[256,1024]{1,0:T(8,128)(2,1)S(1)}, bf16[256,1024]{1,0:T(8,128)(2,1)S(1)}, u32[]{:S(2)}, u32[]{:S(2)}) collective-permute-start(bf16[256,1024]{1,0:T(8,128)(2,1)S(1)} %add_convert_fusion.9), channel_id=1, source_target_pairs={{0,16},{1,17},{2,18},{3,19},{4,20},{5,21},{6,22},{7,23},{8,24},{9,... | collective-permute-start | bytes 1572872 | tf_op jit(solution)/shard_map/ppermute | solution.py:83
  1164.4 144.3 %collective-permute-start.78 = (bf16[2,1024,512]{2,1,0:T(8,128)(2,1)S(1)}, bf16[2,1024,512]{2,1,0:T(8,128)(2,1)S(1)}, u32[]{:S(2)}, u32[]{:S(2)}) collective-permute-start(bf16[2,1024,512]{2,1,0:T(8,128)(2,1)S(1)} %add_convert_fusion.1), channel_id=1, source_target_pairs={{0,16},{1,17},{2,18},{3,19},{4,20},{5,21},{6,22},{7,23},{8,24},{9,... | collective-permute-start | bytes 6291464 | tf_op jit(solution)/shard_map/ppermute | solution.py:83
  1164.6 114.1 %collective-permute-start.89 = (f32[69,512]{1,0:T(8,128)S(1)}, f32[69,512]{1,0:T(8,128)S(1)}, u32[]{:S(2)}, u32[]{:S(2)}) collective-permute-start(f32[69,512]{1,0:T(8,128)S(1)} %pad_maximum_fusion.13), channel_id=1, source_target_pairs={{0,16},{1,17},{2,18},{3,19},{4,20},{5,21},{6,22},{7,23},{8,24},{9,... | collective-permute-start | bytes 423944 | tf_op jit(solution)/shard_map/ppermute | solution.py:83
  1278.7 64.8 %collective-permute-start.95 = (bf16[1024,512]{1,0:T(8,128)(2,1)S(1)}, bf16[1024,512]{1,0:T(8,128)(2,1)S(1)}, u32[]{:S(2)}, u32[]{:S(2)}) collective-permute-start(bf16[1024,512]{1,0:T(8,128)(2,1)S(1)} %copy-done.14), channel_id=1, source_target_pairs={{0,4},{1,5},{2,6},{3,7},{4,0},{5,1},{6,2},{7,3},{8,12},{9,13},{10,... | collective-permute-start | bytes 3145736 | tf_op jit(solution)/shard_map/ppermute | solution.py:83
  1308.1 69.6 %collective-permute-start.107 = (bf16[1024,1024]{1,0:T(8,128)(2,1)S(1)}, bf16[1024,1024]{1,0:T(8,128)(2,1)}, u32[]{:S(2)}, u32[]{:S(2)}) collective-permute-start(bf16[1024,1024]{1,0:T(8,128)(2,1)S(1)} %pad_maximum_fusion.2.refs_4_), channel_id=1, source_target_pairs={{0,4},{1,5},{2,6},{3,7},{4,0},{5,1},{6,2},{7,3},{8,12},{9,13},{10,... | collective-permute-start | bytes 6291464 | tf_op jit(solution)/shard_map/ppermute | solution.py:83
  (167 other events, 4063.1 us)

commit v6 on v5

--- a/solution.py
+++ b/solution.py
@@ -22,8 +22,8 @@
 ORDER = (0, 2, 3, 1)
 ODD = (1, 2)
 DUE = {
-    "attended": ("cx0", "cy0", "cz2"),
-    "normed": ("cd0",),
+    "attended": ("cx0", "cy0"),
+    "normed": ("cz2", "cd0"),
     "row0": ("cx2", "cz3", "cy2"),
     "exp0": ("cx3",),
     "row2": ("sc2", "cy3"),
@@ -37,8 +37,9 @@
     "down1": ("ex2", "ey2", "ed3"),
     "pd0": ("ed1", "sd0"),
     "weight": ("ex3", "ey3", "ex1", "ey1"),
-    "normed_grad": ("gd0",),
-    "weight_down": ("hs", "gd1"),
+    "back": ("gd0",),
+    "normed_grad": ("gx0", "gy0", "gd1"),
+    "weight_down": ("gx1", "gy1"),
 }
 
 
@@ -134,12 +135,13 @@
     return full.reshape(owners, parts // 2, *own.shape)
 
 
-def gather_slots(own, tag, seen):
+def gather_slots(own, tag, seen, first=()):
     if not is_cube():
         return [gather_all(own)] * (lax.axis_size("expert") // NB)
     slots = []
+    far_own = after(own, *first) if first else own
     for k in range(4):
-        block = send(own, dz=k) if k else own
+        block = send(far_own, dz=k) if k else own
         over_x = send(block, dx=1)
         over_y = send(block, dy=1)
         far = send(over_x, dy=1) if k in ODD else send(over_y, dx=1)
@@ -153,7 +155,7 @@
     return sum(t.astype(F32) for t in terms)
 
 
-def scatter_plane(parts, odd):
+def scatter_plane(parts, odd, hold=()):
     near, over_y, over_x, far = parts[0][0], parts[0][1], parts[1][0], parts[1][1]
     if odd:
         far = send(far, dy=1)
@@ -161,6 +163,8 @@
     else:
         far = send(far, dx=1)
         over_x, over_y = after(over_x, far), added(over_y, far).astype(BF16)
+    if hold:
+        over_x, over_y = after(over_x, *hold), after(over_y, *hold)
     from_x, from_y = send(over_x, dx=1), send(over_y, dy=1)
     return added(near, from_x, from_y), {"d": far, "x": from_x, "y": from_y}
 
@@ -173,15 +177,24 @@
     return lax.psum_scatter(mine, "expert", scatter_dimension=0).astype(F32)
 
 
-def scatter_pairs(pairs, seen):
+def scatter_planes(pairs, hold, seen):
+    if not is_cube():
+        return pairs
+    planes = []
+    for i, pair in enumerate(pairs):
+        plane, sent = scatter_plane(pair, True, hold)
+        planes.append(plane)
+        seen.update({"g" + link + str(i): value for link, value in sent.items()})
+    return planes
+
+
+def scatter_ends(planes, hold):
     if not is_cube():
         return scatter_all(
-            [[[a[i] for a in b] for b in pair] for pair in pairs for i in range(pair[0][0].shape[0])]
+            [[[a[i] for a in b] for b in pair] for pair in planes for i in range(pair[0][0].shape[0])]
         )
-    (low, low_sent), (high, high_sent) = (scatter_plane(p, True) for p in pairs)
-    seen.update({"g" + link + "0": value for link, value in low_sent.items()})
-    seen.update({"g" + link + "1": value for link, value in high_sent.items()})
-    total = low + send(high.astype(BF16), dz=2).astype(F32)
+    low, high = planes
+    total = low + send(after(high.astype(BF16), hold), dz=2).astype(F32)
     return total[0] + send(total[1].astype(BF16), dz=1).astype(F32)
 
 
@@ -207,7 +220,7 @@
     return [own, over_y, core_swap(own), core_swap(over_y)]
 
 
-def tensor_scatter(product, pieces, tag, seen):
+def tensor_scatter(product, pieces, tag, seen, beside=()):
     if not is_cube():
         full = jnp.concatenate([product(p).astype(BF16) for p in pieces], axis=1)
         return lax.psum_scatter(full, "tensor", scatter_dimension=1, tiled=True).astype(F32)
@@ -215,7 +228,7 @@
     away = product(pieces[2]).astype(BF16)
     from_y, near = core_swap(away_y), core_swap(away)
     away = added(product(pieces[1]), from_y).astype(BF16)
-    over_y = send(away, dy=1)
+    over_y = after(send(away, dy=1), *beside) if beside else send(away, dy=1)
     seen.update({tag + "0": from_y, tag + "1": near, tag + "y": over_y, tag + "s": away})
     return added(product(pieces[0]), near, over_y)
 
@@ -853,7 +866,7 @@
 
     seen = {}
     all_routes = gather_routes(routes.T)
-    cot_slots = gather_slots(cotangent.astype(BF16), "c", seen)
+    cot_slots = gather_slots(cotangent.astype(BF16), "c", seen, [all_routes])
     order = tensor_order()
 
     held_ids = owner * experts_here + jnp.arange(experts_here, dtype=jnp.int32)
@@ -882,7 +895,7 @@
     )
     head_top = jnp.max(tops[:, 0, 0].reshape(sequences, heads_here), axis=0)
     attended = after(attended, *due("attended", seen))
-    branch = tensor_scatter(partial(matmul, attended), output_pieces, "b", seen)
+    branch = tensor_scatter(partial(matmul, attended), output_pieces, "b", seen, [pos, at])
     residual = own_columns(inputs).astype(F32) + branch
     gain_slice = own_columns(moe_gain)
     router_slice = lax.dynamic_slice_in_dim(w_router, column, slice_width, 0)
@@ -996,16 +1009,16 @@
     mean_dot = tensor_sum(jnp.sum(upstream * moe_hat, axis=-1).reshape(8, -1)).reshape(-1, 1) / width
     grad_residual = cotangent + moe_inv * (upstream - moe_hat * mean_dot)
     branch_pieces = tensor_gather(grad_residual.astype(BF16))
-    grad_branch = jnp.concatenate(branch_pieces, axis=1)
 
     for k in range(1, slots // 2):
         now = after(where[2 * k], branch_pieces[0])
         pairs.append(place_rows([now, where[2 * k + 1]], at, *downs[k]))
     last = pairs[-1][0][0]
     if is_cube():
-        pairs = [[[after(a, branch_pieces[1]) for a in b] for b in pair] for pair in pairs]
-    mixture = scatter_pairs(pairs, seen)
-    out = residual + mixture
+        pairs[1] = [[after(a, branch_pieces[1]) for a in b] for b in pairs[1]]
+    planes = scatter_planes(pairs, branch_pieces[1:2], seen)
+    branch_pieces = [after(p, last) for p in branch_pieces]
+    grad_branch = jnp.concatenate(branch_pieces, axis=1)
 
     grad_output = matmul_tn(grad_branch, attended).astype(BF16)
     spots = order_spots()
@@ -1024,7 +1037,17 @@
     grad_attended = matmul_nt(grad_branch, jnp.concatenate(output_pieces, axis=1)).astype(BF16)
     grad_attended = after(grad_attended, grad_output, last)
     grad_query_raw, grad_key_raw, grad_v, grad_query_gain, grad_key_gain = attend_back(
-        pieces, queries, keys, values, grad_attended, logs, query_raw, key_raw, query_gain, key_gain, scale
+        after(pieces, *due("back", seen)),
+        queries,
+        keys,
+        values,
+        grad_attended,
+        logs,
+        query_raw,
+        key_raw,
+        query_gain,
+        key_gain,
+        scale,
     )
     sum_value = expert_sum(matmul_tn(normed_rows, grad_v).astype(BF16))
     grad_raw = jnp.concatenate([grad_query_raw, grad_key_raw, grad_v], axis=1)
@@ -1034,11 +1057,6 @@
     weights = jnp.concatenate([w_query, w_key, w_value], axis=1)
     weight_pieces = [lax.dynamic_slice_in_dim(weights, o * slice_width, slice_width, 0) for o in order]
     grad_normed_a = tensor_scatter(partial(matmul_nt, grad_raw), weight_pieces, "h", seen)
-    now = after(where[0], *due("weight_down", seen))
-    (grad_down,) = weight_grads(
-        weight_down_kernel, now, cots, scaled, [w_down.shape[1:]], "weight_down_grads"
-    )
-    grad_normed_a = after(grad_normed_a, grad_down)
     attn_hat = own_columns(inputs).astype(F32) * attn_inv
     upstream = grad_normed_a * own_columns(attn_gain)
     grad_attn_gain = jnp.sum(grad_normed_a * attn_hat, axis=0)
@@ -1062,6 +1080,18 @@
     top_row = jnp.pad(head_top, (0, slice_width - heads_here), constant_values=-3e38)
     small, top_row = expert_total(small, top_row[None])
     head_top = top_row[0, :heads_here]
+    if is_cube():
+        seen["small"] = small
+    (grad_down,) = weight_grads(
+        weight_down_kernel,
+        after(where[0], small, *due("weight_down", seen)),
+        cots,
+        scaled,
+        [w_down.shape[1:]],
+        "weight_down_grads",
+    )
+    mixture = scatter_ends(planes, small)
+    out = residual + mixture
     sum_moe_gain, sum_query_gain, sum_key_gain = small[E + 1], small[E + 2], small[E + 3]
     every = lax.all_gather(small[: E + 1], "tensor")
     sum_router = every[:, :E].transpose(0, 2, 1).reshape(width, E)

time: 1400 us -> 1330 us (0.950)
  waiting for transfers between devices: 622 us -> 526 us
    ppermute x108, waiting for transfers between devices: 622 us -> 526 us  [send(): return lax.ppermute(value, BOTH, flip(dz, dx, dy, dc))]
  transfers between devices with their start and end apart: 110 -> 110, of which waited for: 43 -> 40; matrix products, arithmetic and copies ran while one was open for 12% -> 13% of each run, Pallas kernels for 30% -> 33%
where the time goes in v6:
time: 1330 us; the launch traced here: 1320 us
  waiting for transfers between devices  526 us (40%)
  Pallas kernels  458 us (34%)
  starting transfers between devices  130 us (10%)
  other arithmetic  83.9 us (6%)
  local copies, waits for them, and re-layouts  61.8 us (5%)
  matrix products  50.8 us (4%)
    ppermute x108, waiting for transfers between devices, send(): return lax.ppermute(value, BOTH, flip(dz, dx, dy, dc))  526 us
    ppermute x108, starting transfers between devices, send(): return lax.ppermute(value, BOTH, flip(dz, dx, dy, dc))  115 us
    pallas_call x4, Pallas kernels, expert_slot(): pl.pallas_call(partial(expert_kernel, slices), grid_spec=pltpu.PrefetchSc...  112 us
    pallas_call x6, Pallas kernels, place_rows(): pl.pallas_call(partial(place_kernel, slices, held, slots), grid_spec=pltp...  107 us
    pallas_call x8, Pallas kernels, pick_rows(): pl.pallas_call(partial(pick_kernel, group, slices), grid_spec=pltpu.Prefe...  81.4 us
    pallas_call x2, Pallas kernels, weight_grads(): pl.pallas_call(partial(kernel, slots, slices), grid_spec=pltpu.PrefetchSc...  70.5 us
    pallas_call x2, Pallas kernels, down_slots(): pl.pallas_call(partial(down_kernel, slices, slots), grid_spec=pltpu.Prefe...  31.4 us
  transfers between devices with their start and end apart: 110, of which 40 were waited for; matrix products, arithmetic and copies ran while one was open for 13% of the time, Pallas kernels for 33%

profile of v6, /device:TPU:10, one launch (start us, length us, event | category | flops | bytes accessed | tf_op | source)
XLA Modules:
  0.0 1320.0 jit_solution(13112580276905610248)
XLA Ops:
  7.5 15.7 %project.1 = (bf16[1024,2048]{1,0:T(8,128)(2,1)}, f32[1024,1]{1,0:T(8,128)}, f32[1024,512]{1,0:T(8,128)}, f32[1024,512]{1,0:T(8,128)}, bf16[1024,512]{1,0:T(8,12...) custom-call(bf16[1024,2048]{1,0:T(8,128)(2,1)} %in_ref.1, f32[1,2048]{1,0:T(1,128)} %bitcast.208, ...), custom_call_target="tpu_custom_call" | custom-call | flops 103079215104 | bytes 352321536 | tf_op jit(solution)/shard_map/project/pallas_call | solution.py:651
  95.1 34.1 %collective-permute-done.10.refs_2_ = bf16[1024,512]{1,0:T(8,128)(2,1)S(1)} collective-permute-done((bf16[1024,512]{1,0:T(8,128)(2,1)}, bf16[1024,512]{1,0:T(8,128)(2,1)S(1)}, u32[]{:S(2)}, u32[]{:S(2)}) %collective-permute-start.10) | collective-permute-done | bytes 1048608 | tf_op jit(solution)/shard_map/ppermute | solution.py:84
  166.2 17.2 %collective-permute-done.13.refs_2_ = bf16[1024,512]{1,0:T(8,128)(2,1)} collective-permute-done((bf16[1024,512]{1,0:T(8,128)(2,1)}, bf16[1024,512]{1,0:T(8,128)(2,1)}, u32[]{:S(2)}, u32[]{:S(2)}) %collective-permute-start.13) | collective-permute-done | bytes 1048608 | tf_op jit(solution)/shard_map/ppermute | solution.py:84
  189.1 22.7 %collective-permute-done.17.refs_5_ = bf16[1024,512]{1,0:T(8,128)(2,1)} collective-permute-done((bf16[1024,512]{1,0:T(8,128)(2,1)S(1)}, bf16[1024,512]{1,0:T(8,128)(2,1)}, u32[]{:S(2)}, u32[]{:S(2)}) %collective-permute-start.17) | collective-permute-done | bytes 1048608 | tf_op jit(solution)/shard_map/ppermute | solution.py:84
  226.1 30.8 %collective-permute-done.24.refs_2_ = bf16[1024,512]{1,0:T(8,128)(2,1)} collective-permute-done((bf16[1024,512]{1,0:T(8,128)(2,1)}, bf16[1024,512]{1,0:T(8,128)(2,1)}, u32[]{:S(2)}, u32[]{:S(2)}) %collective-permute-start.24) | collective-permute-done | bytes 1048608 | tf_op jit(solution)/shard_map/ppermute | solution.py:84
  285.4 27.8 %expert_slot.4 = (bf16[8,320,256]{2,1,0:T(8,128)(2,1)}, bf16[8,320,256]{2,1,0:T(8,128)(2,1)}, bf16[8,320,256]{2,1,0:T(8,128)(2,1)}, f32[8,2,1024]{2,1,0:T(2,128)...) custom-call(s32[10]{0:T(128)} %stack.118.where_ref, s32[8,8,1024]{2,1,0:T(8,128)} %copy.159.refs_0_.refs_1_, ...), custom_call_target="tpu_custom_call" | custom-call | flops 214748364800 | bytes 905969664 | tf_op jit(solution)/shard_map/expert_slot/pallas_call | solution.py:406
  314.4 15.0 %collective-permute-done.27.refs_5_ = bf16[1024,512]{1,0:T(8,128)(2,1)} collective-permute-done((bf16[1024,512]{1,0:T(8,128)(2,1)}, bf16[1024,512]{1,0:T(8,128)(2,1)}, u32[]{:S(2)}, u32[]{:S(2)}) %collective-permute-start.27) | collective-permute-done | bytes 1048608 | tf_op jit(solution)/shard_map/ppermute | solution.py:84
  350.2 14.3 %place_rows.6 = (bf16[1,1024,512]{2,1,0:T(8,128)(2,1)}, bf16[1,1024,512]{2,1,0:T(8,128)(2,1)}, bf16[1,1024,512]{2,1,0:T(8,128)(2,1)}, bf16[1,1024,512]{2,1,0:T(8,128)(2,1)}) custom-call(s32[2]{0:T(128)} %bitcast.204, s32[8,1024,8]{2,1,0:T(8,128)} %bitcast.153, s32[8,1024,8]{2,1,0:T(8,128)} %bitcast.154, ...), custom_call_target="tpu_custom_call" | custom-call | flops 85899345920 | bytes 234881024 | tf_op jit(solution)/shard_map/place_rows/pallas_call | solution.py:505
  372.1 17.8 %collective-permute-done.42 = bf16[1024,512]{1,0:T(8,128)(2,1)S(1)} collective-permute-done((bf16[1024,512]{1,0:T(8,128)(2,1)}, bf16[1024,512]{1,0:T(8,128)(2,1)S(1)}, u32[]{:S(2)}, u32[]{:S(2)}) %collective-permute-start.42) | collective-permute-done | bytes 1048608 | tf_op jit(solution)/shard_map/ppermute | solution.py:84
  396.6 27.8 %expert_slot.5 = (bf16[8,320,256]{2,1,0:T(8,128)(2,1)}, bf16[8,320,256]{2,1,0:T(8,128)(2,1)}, bf16[8,320,256]{2,1,0:T(8,128)(2,1)}, f32[8,2,1024]{2,1,0:T(2,128)...) custom-call(s32[10]{0:T(128)} %stack.127.where_ref, s32[8,8,1024]{2,1,0:T(8,128)} %copy.159.refs_0_.refs_1_, ...), custom_call_target="tpu_custom_call" | custom-call | flops 214748364800 | bytes 905969664 | tf_op jit(solution)/shard_map/expert_slot/pallas_call | solution.py:406
  424.4 17.4 %collective-permute-done.46.refs_4_ = bf16[1024,512]{1,0:T(8,128)(2,1)} collective-permute-done((bf16[1024,512]{1,0:T(8,128)(2,1)}, bf16[1024,512]{1,0:T(8,128)(2,1)}, u32[]{:S(2)}, u32[]{:S(2)}) %collective-permute-start.46) | collective-permute-done | bytes 1048608 | tf_op jit(solution)/shard_map/ppermute | solution.py:84
  443.8 18.4 %collective-permute-done.35.refs_5_ = bf16[1024,512]{1,0:T(8,128)(2,1)} collective-permute-done((bf16[1024,512]{1,0:T(8,128)(2,1)}, bf16[1024,512]{1,0:T(8,128)(2,1)}, u32[]{:S(2)}, u32[]{:S(2)}) %collective-permute-start.35) | collective-permute-done | bytes 1048608 | tf_op jit(solution)/shard_map/ppermute | solution.py:84
  485.9 14.0 %place_rows.7 = (bf16[1,1024,512]{2,1,0:T(8,128)(2,1)}, bf16[1,1024,512]{2,1,0:T(8,128)(2,1)}, bf16[1,1024,512]{2,1,0:T(8,128)(2,1)}, bf16[1,1024,512]{2,1,0:T(8,128)(2,1)}) custom-call(s32[2]{0:T(128)} %bitcast.206, s32[8,1024,8]{2,1,0:T(8,128)} %bitcast.155, s32[8,1024,8]{2,1,0:T(8,128)} %bitcast.156, ...), custom_call_target="tpu_custom_call" | custom-call | flops 85899345920 | bytes 234881024 | tf_op jit(solution)/shard_map/place_rows/pallas_call | solution.py:505
  500.4 27.8 %expert_slot.6 = (bf16[8,320,256]{2,1,0:T(8,128)(2,1)}, bf16[8,320,256]{2,1,0:T(8,128)(2,1)}, bf16[8,320,256]{2,1,0:T(8,128)(2,1)}, f32[8,2,1024]{2,1,0:T(2,128)...) custom-call(s32[10]{0:T(128)} %stack.124.where_ref, s32[8,8,1024]{2,1,0:T(8,128)} %copy.159.refs_0_.refs_1_, ...), custom_call_target="tpu_custom_call" | custom-call | flops 214748364800 | bytes 905969664 | tf_op jit(solution)/shard_map/expert_slot/pallas_call | solution.py:406
  539.6 13.9 %place_rows.8 = (bf16[1,1024,512]{2,1,0:T(8,128)(2,1)}, bf16[1,1024,512]{2,1,0:T(8,128)(2,1)}, bf16[1,1024,512]{2,1,0:T(8,128)(2,1)}, bf16[1,1024,512]{2,1,0:T(8,128)(2,1)}) custom-call(s32[2]{0:T(128)} %bitcast.209, s32[8,1024,8]{2,1,0:T(8,128)} %bitcast.157, s32[8,1024,8]{2,1,0:T(8,128)} %bitcast.158, ...), custom_call_target="tpu_custom_call" | custom-call | flops 85899345920 | bytes 234881024 | tf_op jit(solution)/shard_map/place_rows/pallas_call | solution.py:505
  553.6 28.2 %expert_slot.7 = (bf16[8,320,256]{2,1,0:T(8,128)(2,1)}, bf16[8,320,256]{2,1,0:T(8,128)(2,1)}, bf16[8,320,256]{2,1,0:T(8,128)(2,1)}, f32[8,2,1024]{2,1,0:T(2,128)...) custom-call(s32[10]{0:T(128)} %stack.121.where_ref, s32[8,8,1024]{2,1,0:T(8,128)} %copy.159.refs_0_.refs_1_, ...), custom_call_target="tpu_custom_call" | custom-call | flops 214748364800 | bytes 905969664 | tf_op jit(solution)/shard_map/expert_slot/pallas_call | solution.py:406
  602.1 15.7 %down_slots.2 = (bf16[4,2,1280,512]{3,2,1,0:T(8,128)(2,1)}, bf16[4,2,1280,512]{3,2,1,0:T(8,128)(2,1)}) custom-call(s32[10]{0:T(128)} %stack.118.where_ref, bf16[8,320,256]{2,1,0:T(8,128)(2,1)} %get-tuple-element.156.refs_0_.refs_8_, bf16[8,320,256]{2,1,0:T(8,128)(2,1)} %get-tuple-element.184.refs_1_.refs_9_, bf16[8,256,2048]{2,1,0:T(8,128)(2,1)} %refs_2_.3), custom_call_target="tpu_custom_call" | custom-call | flops 85899345920 | bytes 469762048 | tf_op jit(solution)/shard_map/down_slots/pallas_call | solution.py:446
  618.0 28.7 %collective-permute-done.56 = bf16[1024,512]{1,0:T(8,128)(2,1)S(1)} collective-permute-done((bf16[1024,512]{1,0:T(8,128)(2,1)}, bf16[1024,512]{1,0:T(8,128)(2,1)S(1)}, u32[]{:S(2)}, u32[]{:S(2)}) %collective-permute-start.56) | collective-permute-done | bytes 1048608 | tf_op jit(solution)/shard_map/ppermute | solution.py:84
  648.2 13.9 %place_rows.9 = (bf16[1,1024,512]{2,1,0:T(8,128)(2,1)}, bf16[1,1024,512]{2,1,0:T(8,128)(2,1)}, bf16[1,1024,512]{2,1,0:T(8,128)(2,1)}, bf16[1,1024,512]{2,1,0:T(8,128)(2,1)}) custom-call(s32[2]{0:T(128)} %bitcast.210, s32[8,1024,8]{2,1,0:T(8,128)} %bitcast.159, s32[8,1024,8]{2,1,0:T(8,128)} %bitcast.160, ...), custom_call_target="tpu_custom_call" | custom-call | flops 85899345920 | bytes 234881024 | tf_op jit(solution)/shard_map/place_rows/pallas_call | solution.py:505
  685.7 13.4 %collective-permute-done.57 = bf16[1024,512]{1,0:T(8,128)(2,1)S(1)} collective-permute-done((bf16[1024,512]{1,0:T(8,128)(2,1)}, bf16[1024,512]{1,0:T(8,128)(2,1)S(1)}, u32[]{:S(2)}, u32[]{:S(2)}) %collective-permute-start.57) | collective-permute-done | bytes 1048608 | tf_op jit(solution)/shard_map/ppermute | solution.py:84
  701.5 15.7 %down_slots.3 = (bf16[4,2,1280,512]{3,2,1,0:T(8,128)(2,1)}, bf16[4,2,1280,512]{3,2,1,0:T(8,128)(2,1)}) custom-call(s32[10]{0:T(128)} %stack.118.where_ref, bf16[8,320,256]{2,1,0:T(8,128)(2,1)} %get-tuple-element.164.refs_0_.refs_10_, bf16[8,320,256]{2,1,0:T(8,128)(2,1)} %get-tuple-element.173.refs_1_.refs_11_, bf16[8,256,2048]{2,1,0:T(8,128)(2,1)} %refs_2_.3), custom_call_target="tpu_custom_call" | custom-call | flops 85899345920 | bytes 469762048 | tf_op jit(solution)/shard_map/down_slots/pallas_call | solution.py:446
  727.5 25.4 %place_rows.10 = (bf16[2,1024,512]{2,1,0:T(8,128)(2,1)}, bf16[2,1024,512]{2,1,0:T(8,128)(2,1)}, bf16[2,1024,512]{2,1,0:T(8,128)(2,1)}, bf16[2,1024,512]{2,1,0:T(8,128)(2,1)}) custom-call(s32[4]{0:T(128)} %pad_add_fusion.3.where_ref, s32[8,1024,8]{2,1,0:T(8,128)} %bitcast.161, s32[8,1024,8]{2,1,0:T(8,128)} %bitcast.162, s32[8,1024,8]{2,1,0:T(8,128)} %bitcast.163, ...), custom_call_target="tpu_custom_call" | custom-call | flops 171798691840 | bytes 469762048 | tf_op jit(solution)/shard_map/place_rows/pallas_call | solution.py:505
  753.0 42.8 %weight_grads.1 = (f32[8,2048,256]{2,1,0:T(8,128)}, f32[8,2048,256]{2,1,0:T(8,128)}) custom-call(s32[10]{0:T(128)} %stack.118.where_ref, bf16[2,2,1280,512]{3,2,1,0:T(8,128)(2,1)} %pick_rows.9.refs_4_.refs_0_, bf16[2,2,1280,512]{3,2,1,0:T(8,128)(2,1)} %collective-permute-done.20.refs_5_.refs_1_, bf16[2,2,1280,512]{3,2,1,0:T(8,128)(2,1)} %pick_rows.15.refs_4_.refs_2_, ...), custom_call_target="tpu_custom_call" | custom-call | flops 160000000000 | bytes 16000000 | tf_op jit(solution)/shard_map/weight_grads/pallas_call | solution.py:562
  804.6 38.0 %collective-permute-done.70 = f32[8,128]{1,0:T(8,128)S(1)} collective-permute-done((f32[8,128]{1,0:T(8,128)S(1)}, f32[8,128]{1,0:T(8,128)S(1)}, u32[]{:S(2)}, u32[]{:S(2)}) %collective-permute-start.70) | collective-permute-done | bytes 4128 | tf_op jit(solution)/shard_map/ppermute | solution.py:84
  871.1 25.3 %place_rows.11 = (bf16[2,1024,512]{2,1,0:T(8,128)(2,1)}, bf16[2,1024,512]{2,1,0:T(8,128)(2,1)}, bf16[2,1024,512]{2,1,0:T(8,128)(2,1)}, bf16[2,1024,512]{2,1,0:T(8,128)(2,1)}) custom-call(s32[4]{0:T(128)} %pad_add_fusion.4.where_ref, s32[8,1024,8]{2,1,0:T(8,128)} %bitcast.165, s32[8,1024,8]{2,1,0:T(8,128)} %bitcast.166, s32[8,1024,8]{2,1,0:T(8,128)} %bitcast.167, ...), custom_call_target="tpu_custom_call" | custom-call | flops 171798691840 | bytes 469762048 | tf_op jit(solution)/shard_map/place_rows/pallas_call | solution.py:505
  910.7 16.3 %attend_back.1 = (bf16[1024,512]{1,0:T(8,128)(2,1)}, bf16[1024,512]{1,0:T(8,128)(2,1)}, bf16[1024,512]{1,0:T(8,128)(2,1)}, f32[1,1,512]{2,1,0:T(1,128)}, f32[1,1,512]{2,1,0:T(1,128)}) custom-call(s32[4]{0:T(128)} %add_bitcast_fusion.pieces_ref, bf16[1024,512]{1,0:T(8,128)(2,1)} %get-tuple-element.145.q_ref, bf16[1024,512]{1,0:T(8,128)(2,1)} %get-tuple-element.146.k_ref, ...), custom_call_target="tpu_custom_call" | custom-call | flops 85899345920 | bytes 184549376 | tf_op jit(solution)/shard_map/attend_back/pallas_call | solution.py:786
  1062.3 13.3 %collective-permute-done.103 = bf16[512,1024]{1,0:T(8,128)(2,1)S(1)} collective-permute-done((bf16[512,1024]{1,0:T(8,128)(2,1)S(1)}, bf16[512,1024]{1,0:T(8,128)(2,1)S(1)}, u32[]{:S(2)}, u32[]{:S(2)}) %collective-permute-start.103) | collective-permute-done | bytes 1048608 | tf_op jit(solution)/shard_map/ppermute | solution.py:84
  1082.0 17.4 %collective-permute-done.104 = bf16[256,1024]{1,0:T(8,128)(2,1)S(1)} collective-permute-done((bf16[256,1024]{1,0:T(8,128)(2,1)S(1)}, bf16[256,1024]{1,0:T(8,128)(2,1)S(1)}, u32[]{:S(2)}, u32[]{:S(2)}) %collective-permute-start.104) | collective-permute-done | bytes 524320 | tf_op jit(solution)/shard_map/ppermute | solution.py:84
  1101.8 25.0 %collective-permute-done.82 = bf16[1024,512]{1,0:T(8,128)(2,1)S(1)} collective-permute-done((bf16[1024,512]{1,0:T(8,128)(2,1)S(1)}, bf16[1024,512]{1,0:T(8,128)(2,1)S(1)}, u32[]{:S(2)}, u32[]{:S(2)}) %collective-permute-start.82) | collective-permute-done | bytes 1048608 | tf_op jit(solution)/shard_map/ppermute | solution.py:84
  1165.8 16.1 %collective-permute-done.84 = f32[69,512]{1,0:T(8,128)S(1)} collective-permute-done((f32[69,512]{1,0:T(8,128)S(1)}, f32[69,512]{1,0:T(8,128)S(1)}, u32[]{:S(2)}, u32[]{:S(2)}) %collective-permute-start.84) | collective-permute-done | bytes 141344 | tf_op jit(solution)/shard_map/ppermute | solution.py:84
  1195.0 27.7 %weight_down_grads.1 = f32[8,256,2048]{2,1,0:T(8,128)} custom-call(s32[10]{0:T(128)} %stack.118.where_ref, bf16[2,2,1280,512]{3,2,1,0:T(8,128)(2,1)} %pick_rows.8.refs_6_.refs_0_, bf16[2,2,1280,512]{3,2,1,0:T(8,128)(2,1)} %collective-permute-done.21.refs_7_.refs_1_, bf16[2,2,1280,512]{3,2,1,0:T(8,128)(2,1)} %pick_rows.14.refs_6_.refs_2_, ...), custom_call_target="tpu_custom_call" | custom-call | flops 160000000000 | bytes 16000000 | tf_op jit(solution)/shard_map/weight_down_grads/pallas_call | solution.py:562
  1236.7 47.1 %collective-permute-done.86 = bf16[2,1024,512]{2,1,0:T(8,128)(2,1)} collective-permute-done((bf16[2,1024,512]{2,1,0:T(8,128)(2,1)}, bf16[2,1024,512]{2,1,0:T(8,128)(2,1)}, u32[]{:S(2)}, u32[]{:S(2)}) %collective-permute-start.86) | collective-permute-done | bytes 2097184 | tf_op jit(solution)/shard_map/ppermute | solution.py:84
  (528 shorter events, 593.0 us)
Async XLA Ops:
  141.8 143.6 %all-to-all-start = ((f32[8,8,1024]{2,1,0:T(8,128)}), f32[8,8,1024]{2,1,0:T(8,128)}, u32[]{:S(2)}, u32[]{:S(2)}) async-start(f32[8,8,1024]{2,1,0:T(8,128)} %fusion.82), calls=%async_computation | async-start | bytes 524288 | tf_op jit(solution)/shard_map/all_to_all | solution.py:924
  183.4 85.3 %collective-permute-start.23 = (bf16[1024,512]{1,0:T(8,128)(2,1)}, bf16[1024,512]{1,0:T(8,128)(2,1)}, u32[]{:S(2)}, u32[]{:S(2)}) collective-permute-start(bf16[1024,512]{1,0:T(8,128)(2,1)} %collective-permute-done.13.refs_2_), channel_id=1, source_target_pairs={{0,2},{1,3},{2,0},{3,1},{4,6},{5,7},{6,4},{7,5},{8,10},{9,11},{10,... | collective-permute-start | bytes 3145736 | tf_op jit(solution)/shard_map/ppermute | solution.py:84
  184.9 85.2 %collective-permute-start.19 = (bf16[1024,512]{1,0:T(8,128)(2,1)}, bf16[1024,512]{1,0:T(8,128)(2,1)}, u32[]{:S(2)}, u32[]{:S(2)}) collective-permute-start(bf16[1024,512]{1,0:T(8,128)(2,1)} %collective-permute-done.13.refs_2_), channel_id=1, source_target_pairs={{0,4},{1,5},{2,6},{3,7},{4,0},{5,1},{6,2},{7,3},{8,12},{9,13},{10,... | collective-permute-start | bytes 3145736 | tf_op jit(solution)/shard_map/ppermute | solution.py:84
  188.6 68.9 %collective-permute-start.18 = (bf16[1024,512]{1,0:T(8,128)(2,1)}, bf16[1024,512]{1,0:T(8,128)(2,1)S(1)}, u32[]{:S(2)}, u32[]{:S(2)}) collective-permute-start(bf16[1024,512]{1,0:T(8,128)(2,1)} %collective-permute-done.12.refs_4_), channel_id=1, source_target_pairs={{0,2},{1,3},{2,0},{3,1},{4,6},{5,7},{6,4},{7,5},{8,10},{9,11},{10,... | collective-permute-start | bytes 3145736 | tf_op jit(solution)/shard_map/ppermute | solution.py:84
  268.7 101.9 %collective-permute-start.39 = (bf16[1024,512]{1,0:T(8,128)(2,1)}, bf16[1024,512]{1,0:T(8,128)(2,1)}, u32[]{:S(2)}, u32[]{:S(2)}) collective-permute-start(bf16[1024,512]{1,0:T(8,128)(2,1)} %collective-permute-done.37.refs_2_), channel_id=1, source_target_pairs={{0,4},{1,5},{2,6},{3,7},{4,0},{5,1},{6,2},{7,3},{8,12},{9,13},{10,... | collective-permute-start | bytes 3145736 | tf_op jit(solution)/shard_map/ppermute | solution.py:84
  270.2 69.4 %collective-permute-start.29 = (bf16[1024,512]{1,0:T(8,128)(2,1)}, bf16[1024,512]{1,0:T(8,128)(2,1)}, u32[]{:S(2)}, u32[]{:S(2)}) collective-permute-start(bf16[1024,512]{1,0:T(8,128)(2,1)} %collective-permute-done.23.refs_3_), channel_id=1, source_target_pairs={{0,4},{1,5},{2,6},{3,7},{4,0},{5,1},{6,2},{7,3},{8,12},{9,13},{10,... | collective-permute-start | bytes 3145736 | tf_op jit(solution)/shard_map/ppermute | solution.py:84
  370.6 103.1 %collective-permute-start.38 = (bf16[1024,512]{1,0:T(8,128)(2,1)}, bf16[1024,512]{1,0:T(8,128)(2,1)}, u32[]{:S(2)}, u32[]{:S(2)}) collective-permute-start(bf16[1024,512]{1,0:T(8,128)(2,1)} %collective-permute-done.37.refs_2_), channel_id=1, source_target_pairs={{0,2},{1,3},{2,0},{3,1},{4,6},{5,7},{6,4},{7,5},{8,10},{9,11},{10,... | collective-permute-start | bytes 3145736 | tf_op jit(solution)/shard_map/ppermute | solution.py:84
  389.9 85.3 %collective-permute-start.40 = (bf16[1024,512]{1,0:T(8,128)(2,1)}, bf16[1024,512]{1,0:T(8,128)(2,1)}, u32[]{:S(2)}, u32[]{:S(2)}) collective-permute-start(bf16[1024,512]{1,0:T(8,128)(2,1)} %collective-permute-done.39.refs_4_), channel_id=1, source_target_pairs={{0,2},{1,3},{2,0},{3,1},{4,6},{5,7},{6,4},{7,5},{8,10},{9,11},{10,... | collective-permute-start | bytes 3145736 | tf_op jit(solution)/shard_map/ppermute | solution.py:84
  396.0 66.2 %collective-permute-start.35 = (bf16[1024,512]{1,0:T(8,128)(2,1)}, bf16[1024,512]{1,0:T(8,128)(2,1)}, u32[]{:S(2)}, u32[]{:S(2)}) collective-permute-start(bf16[1024,512]{1,0:T(8,128)(2,1)} %collective-permute-done.33.refs_3_), channel_id=1, source_target_pairs={{0,4},{1,5},{2,6},{3,7},{4,0},{5,1},{6,2},{7,3},{8,12},{9,13},{10,... | collective-permute-start | bytes 3145736 | tf_op jit(solution)/shard_map/ppermute | solution.py:84
  441.8 86.4 %collective-permute-start.45 = (bf16[1024,512]{1,0:T(8,128)(2,1)}, bf16[1024,512]{1,0:T(8,128)(2,1)}, u32[]{:S(2)}, u32[]{:S(2)}) collective-permute-start(bf16[1024,512]{1,0:T(8,128)(2,1)} %collective-permute-done.44.refs_2_), channel_id=1, source_target_pairs={{0,2},{1,3},{2,0},{3,1},{4,6},{5,7},{6,4},{7,5},{8,10},{9,11},{10,... | collective-permute-start | bytes 3145736 | tf_op jit(solution)/shard_map/ppermute | solution.py:84
  443.3 85.0 %collective-permute-start.47 = (bf16[1024,512]{1,0:T(8,128)(2,1)}, bf16[1024,512]{1,0:T(8,128)(2,1)}, u32[]{:S(2)}, u32[]{:S(2)}) collective-permute-start(bf16[1024,512]{1,0:T(8,128)(2,1)} %collective-permute-done.46.refs_4_), channel_id=1, source_target_pairs={{0,2},{1,3},{2,0},{3,1},{4,6},{5,7},{6,4},{7,5},{8,10},{9,11},{10,... | collective-permute-start | bytes 3145736 | tf_op jit(solution)/shard_map/ppermute | solution.py:84
  473.2 65.8 %collective-permute-start.48 = (bf16[1024,512]{1,0:T(8,128)(2,1)}, bf16[1024,512]{1,0:T(8,128)(2,1)}, u32[]{:S(2)}, u32[]{:S(2)}) collective-permute-start(bf16[1024,512]{1,0:T(8,128)(2,1)} %bitcast.28), channel_id=1, source_target_pairs={{0,4},{1,5},{2,6},{3,7},{4,0},{5,1},{6,2},{7,3},{8,12},{9,13},{10,... | collective-permute-start | bytes 3145736 | tf_op jit(solution)/shard_map/ppermute | solution.py:84
  473.7 65.3 %collective-permute-start.49 = (bf16[1024,512]{1,0:T(8,128)(2,1)}, bf16[1024,512]{1,0:T(8,128)(2,1)}, u32[]{:S(2)}, u32[]{:S(2)}) collective-permute-start(bf16[1024,512]{1,0:T(8,128)(2,1)} %fusion.37), channel_id=1, source_target_pairs={{0,2},{1,3},{2,0},{3,1},{4,6},{5,7},{6,4},{7,5},{8,10},{9,11},{10,... | collective-permute-start | bytes 3145736 | tf_op jit(solution)/shard_map/ppermute | solution.py:84
  595.5 66.6 %collective-permute-start.55 = (bf16[1024,512]{1,0:T(8,128)(2,1)}, bf16[1024,512]{1,0:T(8,128)(2,1)}, u32[]{:S(2)}, u32[]{:S(2)}) collective-permute-start(bf16[1024,512]{1,0:T(8,128)(2,1)} %bitcast.32), channel_id=1, source_target_pairs={{0,2},{1,3},{2,0},{3,1},{4,6},{5,7},{6,4},{7,5},{8,10},{9,11},{10,... | collective-permute-start | bytes 3145736 | tf_op jit(solution)/shard_map/ppermute | solution.py:84
  599.5 64.1 %collective-permute-start.54 = (bf16[1024,512]{1,0:T(8,128)(2,1)}, bf16[1024,512]{1,0:T(8,128)(2,1)}, u32[]{:S(2)}, u32[]{:S(2)}) collective-permute-start(bf16[1024,512]{1,0:T(8,128)(2,1)} %fusion.36), channel_id=1, source_target_pairs={{0,4},{1,5},{2,6},{3,7},{4,0},{5,1},{6,2},{7,3},{8,12},{9,13},{10,... | collective-permute-start | bytes 3145736 | tf_op jit(solution)/shard_map/ppermute | solution.py:84
  617.8 109.1 %collective-permute-start.58 = (bf16[4,2,1280,512]{3,2,1,0:T(8,128)(2,1)}, bf16[4,2,1280,512]{3,2,1,0:T(8,128)(2,1)}, u32[]{:S(2)}, u32[]{:S(2)}) collective-permute-start(bf16[4,2,1280,512]{3,2,1,0:T(8,128)(2,1)} %get-tuple-element.198), channel_id=1, source_target_pairs={{0,1},{1,0},{2,3},{3,2},{4,5},{5,4},{6,7},{7,6},{8,9},{9,8},{10,11... | collective-permute-start | bytes 31457288 | tf_op jit(solution)/shard_map/ppermute | solution.py:84
  679.4 116.5 %collective-permute-start.65 = (bf16[1024,512]{1,0:T(8,128)(2,1)}, bf16[1024,512]{1,0:T(8,128)(2,1)}, u32[]{:S(2)}, u32[]{:S(2)}) collective-permute-start(bf16[1024,512]{1,0:T(8,128)(2,1)} %fusion.30), channel_id=1, source_target_pairs={{0,16},{1,17},{2,18},{3,19},{4,20},{5,21},{6,22},{7,23},{8,24},{9,... | collective-permute-start | bytes 3145736 | tf_op jit(solution)/shard_map/ppermute | solution.py:84
  685.7 110.2 %collective-permute-start.66 = (bf16[1024,512]{1,0:T(8,128)(2,1)}, bf16[1024,512]{1,0:T(8,128)(2,1)}, u32[]{:S(2)}, u32[]{:S(2)}) collective-permute-start(bf16[1024,512]{1,0:T(8,128)(2,1)} %fusion.28), channel_id=1, source_target_pairs={{0,24},{1,25},{2,26},{3,27},{4,28},{5,29},{6,30},{7,31},{8,16},{9,... | collective-permute-start | bytes 3145736 | tf_op jit(solution)/shard_map/ppermute | solution.py:84
  721.8 149.2 %collective-permute-start.74 = (bf16[4,2,1280,512]{3,2,1,0:T(8,128)(2,1)}, bf16[4,2,1280,512]{3,2,1,0:T(8,128)(2,1)}, u32[]{:S(2)}, u32[]{:S(2)}) collective-permute-start(bf16[4,2,1280,512]{3,2,1,0:T(8,128)(2,1)} %get-tuple-element.232), channel_id=1, source_target_pairs={{0,1},{1,0},{2,3},{3,2},{4,5},{5,4},{6,7},{7,6},{8,9},{9,8},{10,11... | collective-permute-start | bytes 31457288 | tf_op jit(solution)/shard_map/ppermute | solution.py:84
  724.9 70.9 %collective-permute-start.64 = (bf16[1024,512]{1,0:T(8,128)(2,1)}, bf16[1024,512]{1,0:T(8,128)(2,1)}, u32[]{:S(2)}, u32[]{:S(2)}) collective-permute-start(bf16[1024,512]{1,0:T(8,128)(2,1)} %fusion.32), channel_id=1, source_target_pairs={{0,8},{1,9},{2,10},{3,11},{4,12},{5,13},{6,14},{7,15},{8,0},{9,1},... | collective-permute-start | bytes 3145736 | tf_op jit(solution)/shard_map/ppermute | solution.py:84
  795.9 75.2 %collective-permute-start.59 = (bf16[2,1024,512]{2,1,0:T(8,128)(2,1)}, bf16[2,1024,512]{2,1,0:T(8,128)(2,1)}, u32[]{:S(2)}, u32[]{:S(2)}) collective-permute-start(bf16[2,1024,512]{2,1,0:T(8,128)(2,1)} %get-tuple-element.202), channel_id=1, source_target_pairs={{0,2},{1,3},{2,0},{3,1},{4,6},{5,7},{6,4},{7,5},{8,10},{9,11},{10,... | collective-permute-start | bytes 6291464 | tf_op jit(solution)/shard_map/ppermute | solution.py:84
  940.8 87.3 %collective-permute-start.73 = (bf16[2,1024,512]{2,1,0:T(8,128)(2,1)}, bf16[2,1024,512]{2,1,0:T(8,128)(2,1)}, u32[]{:S(2)}, u32[]{:S(2)}) collective-permute-start(bf16[2,1024,512]{2,1,0:T(8,128)(2,1)} %get-tuple-element.230), channel_id=1, source_target_pairs={{0,2},{1,3},{2,0},{3,1},{4,6},{5,7},{6,4},{7,5},{8,10},{9,11},{10,... | collective-permute-start | bytes 6291464 | tf_op jit(solution)/shard_map/ppermute | solution.py:84
  942.4 85.9 %collective-permute-start.72 = (bf16[2,1024,512]{2,1,0:T(8,128)(2,1)}, bf16[2,1024,512]{2,1,0:T(8,128)(2,1)}, u32[]{:S(2)}, u32[]{:S(2)}) collective-permute-start(bf16[2,1024,512]{2,1,0:T(8,128)(2,1)} %add_convert_fusion.3), channel_id=1, source_target_pairs={{0,4},{1,5},{2,6},{3,7},{4,0},{5,1},{6,2},{7,3},{8,12},{9,13},{10,... | collective-permute-start | bytes 6291464 | tf_op jit(solution)/shard_map/ppermute | solution.py:84
  943.8 89.9 %collective-permute-start.75 = (bf16[2,1024,512]{2,1,0:T(8,128)(2,1)}, bf16[2,1024,512]{2,1,0:T(8,128)(2,1)S(1)}, u32[]{:S(2)}, u32[]{:S(2)}) collective-permute-start(bf16[2,1024,512]{2,1,0:T(8,128)(2,1)} %get-tuple-element.238), channel_id=1, source_target_pairs={{0,2},{1,3},{2,0},{3,1},{4,6},{5,7},{6,4},{7,5},{8,10},{9,11},{10,... | collective-permute-start | bytes 6291464 | tf_op jit(solution)/shard_map/ppermute | solution.py:84
  967.1 81.1 %collective-permute-start.102 = (bf16[1024,1024]{1,0:T(8,128)(2,1)}, bf16[1024,1024]{1,0:T(8,128)(2,1)}, u32[]{:S(2)}, u32[]{:S(2)}) collective-permute-start(bf16[1024,1024]{1,0:T(8,128)(2,1)} %slice.227), channel_id=1, source_target_pairs={{0,4},{1,5},{2,6},{3,7},{4,0},{5,1},{6,2},{7,3},{8,12},{9,13},{10,... | collective-permute-start | bytes 6291464 | tf_op jit(solution)/shard_map/ppermute | solution.py:84
  1057.3 94.0 %collective-permute-start.77 = (bf16[2,1024,512]{2,1,0:T(8,128)(2,1)}, bf16[2,1024,512]{2,1,0:T(8,128)(2,1)S(1)}, u32[]{:S(2)}, u32[]{:S(2)}) collective-permute-start(bf16[2,1024,512]{2,1,0:T(8,128)(2,1)} %get-tuple-element.243), channel_id=1, source_target_pairs={{0,2},{1,3},{2,0},{3,1},{4,6},{5,7},{6,4},{7,5},{8,10},{9,11},{10,... | collective-permute-start | bytes 6291464 | tf_op jit(solution)/shard_map/ppermute | solution.py:84
  1057.9 95.1 %collective-permute-start.76 = (bf16[2,1024,512]{2,1,0:T(8,128)(2,1)}, bf16[2,1024,512]{2,1,0:T(8,128)(2,1)}, u32[]{:S(2)}, u32[]{:S(2)}) collective-permute-start(bf16[2,1024,512]{2,1,0:T(8,128)(2,1)} %add_convert_fusion.2), channel_id=1, source_target_pairs={{0,4},{1,5},{2,6},{3,7},{4,0},{5,1},{6,2},{7,3},{8,12},{9,13},{10,... | collective-permute-start | bytes 6291464 | tf_op jit(solution)/shard_map/ppermute | solution.py:84
  1099.4 196.9 %collective-permute-start.95 = (bf16[1024,512]{1,0:T(8,128)(2,1)}, bf16[1024,512]{1,0:T(8,128)(2,1)}, u32[]{:S(2)}, u32[]{:S(2)}) collective-permute-start(bf16[1024,512]{1,0:T(8,128)(2,1)} %pad_maximum_fusion.3.refs_0_), channel_id=1, source_target_pairs={{0,4},{1,5},{2,6},{3,7},{4,0},{5,1},{6,2},{7,3},{8,12},{9,13},{10,... | collective-permute-start | bytes 3145736 | tf_op jit(solution)/shard_map/ppermute | solution.py:84
  1101.6 194.8 %collective-permute-start.101 = (bf16[1024,512]{1,0:T(8,128)(2,1)}, bf16[1024,512]{1,0:T(8,128)(2,1)}, u32[]{:S(2)}, u32[]{:S(2)}) collective-permute-start(bf16[1024,512]{1,0:T(8,128)(2,1)} %pad_maximum_fusion.4.refs_2_), channel_id=1, source_target_pairs={{0,4},{1,5},{2,6},{3,7},{4,0},{5,1},{6,2},{7,3},{8,12},{9,13},{10,... | collective-permute-start | bytes 3145736 | tf_op jit(solution)/shard_map/ppermute | solution.py:84
  1153.0 79.0 %collective-permute-start.106 = (bf16[512,1024]{1,0:T(8,128)(2,1)}, bf16[512,1024]{1,0:T(8,128)(2,1)}, u32[]{:S(2)}, u32[]{:S(2)}) collective-permute-start(bf16[512,1024]{1,0:T(8,128)(2,1)} %pad_maximum_fusion.5), channel_id=1, source_target_pairs={{0,8},{1,9},{2,10},{3,11},{4,12},{5,13},{6,14},{7,15},{8,0},{9,1},... | collective-permute-start | bytes 3145736 | tf_op jit(solution)/shard_map/ppermute | solution.py:84
  1191.6 92.3 %collective-permute-start.86 = (bf16[2,1024,512]{2,1,0:T(8,128)(2,1)}, bf16[2,1024,512]{2,1,0:T(8,128)(2,1)}, u32[]{:S(2)}, u32[]{:S(2)}) collective-permute-start(bf16[2,1024,512]{2,1,0:T(8,128)(2,1)} %add_convert_fusion.1), channel_id=1, source_target_pairs={{0,16},{1,17},{2,18},{3,19},{4,20},{5,21},{6,22},{7,23},{8,24},{9,... | collective-permute-start | bytes 6291464 | tf_op jit(solution)/shard_map/ppermute | solution.py:84
  1233.6 62.7 %collective-permute-start.107 = (bf16[1024,1024]{1,0:T(8,128)(2,1)S(1)}, bf16[1024,1024]{1,0:T(8,128)(2,1)}, u32[]{:S(2)}, u32[]{:S(2)}) collective-permute-start(bf16[1024,1024]{1,0:T(8,128)(2,1)S(1)} %pad_maximum_fusion.1.refs_4_), channel_id=1, source_target_pairs={{0,4},{1,5},{2,6},{3,7},{4,0},{5,1},{6,2},{7,3},{8,12},{9,13},{10,... | collective-permute-start | bytes 6291464 | tf_op jit(solution)/shard_map/ppermute | solution.py:84
  (163 other events, 3777.6 us)

commit v7 on v6

--- a/solution.py
+++ b/solution.py
@@ -23,10 +23,10 @@
 ODD = (1, 2)
 DUE = {
     "attended": ("cx0", "cy0"),
-    "normed": ("cz2", "cd0"),
-    "row0": ("cx2", "cz3", "cy2"),
-    "exp0": ("cx3",),
-    "row2": ("sc2", "cy3"),
+    "normed": ("cd0",),
+    "row0": ("cx2", "cy2", "nz2"),
+    "cot2": ("cz3",),
+    "row2": ("sc2",),
     "cot3": ("sg0",),
     "place0": ("sr2",),
     "exp2": ("sc3",),
@@ -34,12 +34,15 @@
     "place2": ("sr3", "ed0"),
     "exp3": ("sc1",),
     "place3": ("ex0", "ey0", "ed2"),
-    "down1": ("ex2", "ey2", "ed3"),
-    "pd0": ("ed1", "sd0"),
-    "weight": ("ex3", "ey3", "ex1", "ey1"),
-    "back": ("gd0",),
-    "normed_grad": ("gx0", "gy0", "gd1"),
-    "weight_down": ("gx1", "gy1"),
+    "down1": ("sg1",),
+    "place1": ("ed3", "ex2", "ey2"),
+    "pd0": ("sd0",),
+    "pd1": ("sd1", "ed1", "ex3", "ey3"),
+    "weight": ("ex1", "ey1"),
+    "residual_grad": ("gd0",),
+    "back": ("gd1",),
+    "normed_grad": ("gx0", "gy0"),
+    "weight_down": ("hs",),
 }
 
 
@@ -155,13 +158,15 @@
     return sum(t.astype(F32) for t in terms)
 
 
-def scatter_plane(parts, odd, hold=()):
-    near, over_y, over_x, far = parts[0][0], parts[0][1], parts[1][0], parts[1][1]
+def scatter_corner(parts, odd):
+    return send(parts[1][1], dy=1) if odd else send(parts[1][1], dx=1)
+
+
+def scatter_plane(parts, far, odd, hold=()):
+    near, over_y, over_x = parts[0][0], parts[0][1], parts[1][0]
     if odd:
-        far = send(far, dy=1)
         over_x, over_y = added(over_x, far).astype(BF16), after(over_y, far)
     else:
-        far = send(far, dx=1)
         over_x, over_y = after(over_x, far), added(over_y, far).astype(BF16)
     if hold:
         over_x, over_y = after(over_x, *hold), after(over_y, *hold)
@@ -177,12 +182,20 @@
     return lax.psum_scatter(mine, "expert", scatter_dimension=0).astype(F32)
 
 
-def scatter_planes(pairs, hold, seen):
+def scatter_corners(pairs, seen):
+    if not is_cube():
+        return []
+    far = [scatter_corner(pair, False) for pair in pairs]
+    seen.update({"gd" + str(i): value for i, value in enumerate(far)})
+    return far
+
+
+def scatter_planes(pairs, far, hold, seen):
     if not is_cube():
         return pairs
     planes = []
     for i, pair in enumerate(pairs):
-        plane, sent = scatter_plane(pair, True, hold)
+        plane, sent = scatter_plane(pair, far[i], False, hold)
         planes.append(plane)
         seen.update({"g" + link + str(i): value for link, value in sent.items()})
     return planes
@@ -815,7 +828,7 @@
         if i + 1 < slots:
             steps.append(("row", order[i + 1]))
         else:
-            steps.append(("down", 0))
+            steps += [("down", j) for j in range(slots // 2)]
         if i + 2 < slots:
             steps.append(("cot", order[i + 2]))
         steps.append(("place", k))
@@ -967,14 +980,16 @@
             last = placed[0][0]
             back[k] = [[a[0] for a in b] for b in placed]
             if is_cube():
-                sums[k], sent = scatter_plane(back[k], k in ODD)
+                odd = k in ODD
+                sums[k], sent = scatter_plane(back[k], scatter_corner(back[k], odd), odd)
                 if k:
                     sums[k] = sent["z"] = send(sums[k].astype(BF16), dz=k)
                 seen.update({"e" + link + str(k): value for link, value in sent.items()})
-    for k in range(1, slots // 2):
-        last = lower(k)
-    pairs = [place_rows([turn("pd0", 0), where[1]], at, *downs[0])]
-    last = pairs[0][0][0]
+    pairs = []
+    for k in range(slots // 2):
+        pairs.append(place_rows([turn("pd" + str(k), 2 * k), where[2 * k + 1]], at, *downs[k]))
+        last = pairs[k][0][0]
+    far = scatter_corners(pairs, seen)
     grad_gate, grad_up = weight_grads(
         weight_kernel,
         turn("weight", 0),
@@ -1008,16 +1023,9 @@
     upstream = grad_normed * gain_slice
     mean_dot = tensor_sum(jnp.sum(upstream * moe_hat, axis=-1).reshape(8, -1)).reshape(-1, 1) / width
     grad_residual = cotangent + moe_inv * (upstream - moe_hat * mean_dot)
-    branch_pieces = tensor_gather(grad_residual.astype(BF16))
-
-    for k in range(1, slots // 2):
-        now = after(where[2 * k], branch_pieces[0])
-        pairs.append(place_rows([now, where[2 * k + 1]], at, *downs[k]))
-    last = pairs[-1][0][0]
-    if is_cube():
-        pairs[1] = [[after(a, branch_pieces[1]) for a in b] for b in pairs[1]]
-    planes = scatter_planes(pairs, branch_pieces[1:2], seen)
-    branch_pieces = [after(p, last) for p in branch_pieces]
+    branch_pieces = tensor_gather(after(grad_residual.astype(BF16), *due("residual_grad", seen)))
+
+    planes = scatter_planes(pairs, far, branch_pieces[1:2], seen)
     grad_branch = jnp.concatenate(branch_pieces, axis=1)
 
     grad_output = matmul_tn(grad_branch, attended).astype(BF16)
@@ -1035,7 +1043,7 @@
     )
     sum_output = expert_sum(grad_output)
     grad_attended = matmul_nt(grad_branch, jnp.concatenate(output_pieces, axis=1)).astype(BF16)
-    grad_attended = after(grad_attended, grad_output, last)
+    grad_attended = after(grad_attended, grad_output)
     grad_query_raw, grad_key_raw, grad_v, grad_query_gain, grad_key_gain = attend_back(
         after(pieces, *due("back", seen)),
         queries,
@@ -1057,6 +1065,14 @@
     weights = jnp.concatenate([w_query, w_key, w_value], axis=1)
     weight_pieces = [lax.dynamic_slice_in_dim(weights, o * slice_width, slice_width, 0) for o in order]
     grad_normed_a = tensor_scatter(partial(matmul_nt, grad_raw), weight_pieces, "h", seen)
+    (grad_down,) = weight_grads(
+        weight_down_kernel,
+        after(where[0], *due("weight_down", seen)),
+        cots,
+        scaled,
+        [w_down.shape[1:]],
+        "weight_down_grads",
+    )
     attn_hat = own_columns(inputs).astype(F32) * attn_inv
     upstream = grad_normed_a * own_columns(attn_gain)
     grad_attn_gain = jnp.sum(grad_normed_a * attn_hat, axis=0)
@@ -1080,16 +1096,6 @@
     top_row = jnp.pad(head_top, (0, slice_width - heads_here), constant_values=-3e38)
     small, top_row = expert_total(small, top_row[None])
     head_top = top_row[0, :heads_here]
-    if is_cube():
-        seen["small"] = small
-    (grad_down,) = weight_grads(
-        weight_down_kernel,
-        after(where[0], small, *due("weight_down", seen)),
-        cots,
-        scaled,
-        [w_down.shape[1:]],
-        "weight_down_grads",
-    )
     mixture = scatter_ends(planes, small)
     out = residual + mixture
     sum_moe_gain, sum_query_gain, sum_key_gain = small[E + 1], small[E + 2], small[E + 3]

time: 1330 us -> 1440 us (1.083)
  waiting for transfers between devices: 526 us -> 658 us
    ppermute x108, waiting for transfers between devices: 526 us -> 658 us  [send(): return lax.ppermute(value, BOTH, flip(dz, dx, dy, dc))]
    unnamed x184 -> x232, local copies, waits for them, and re-layouts: 23.8 us -> 30.8 us
  transfers between devices with their start and end apart: 110 -> 110, of which waited for: 40 -> 40; matrix products, arithmetic and copies ran while one was open for 13% -> 12% of each run, Pallas kernels for 33% -> 31%
where the time goes in v7:
time: 1440 us; the launch traced here: 1430 us
  waiting for transfers between devices  658 us (46%)
  Pallas kernels  457 us (32%)
  starting transfers between devices  117 us (8%)
  other arithmetic  73.8 us (5%)
  local copies, waits for them, and re-layouts  63.2 us (4%)
  matrix products  48.8 us (3%)
    ppermute x108, waiting for transfers between devices, send(): return lax.ppermute(value, BOTH, flip(dz, dx, dy, dc))  658 us
    pallas_call x4, Pallas kernels, expert_slot(): pl.pallas_call(partial(expert_kernel, slices), grid_spec=pltpu.PrefetchSc...  111 us
    ppermute x108, starting transfers between devices, send(): return lax.ppermute(value, BOTH, flip(dz, dx, dy, dc))  107 us
    pallas_call x6, Pallas kernels, place_rows(): pl.pallas_call(partial(place_kernel, slices, held, slots), grid_spec=pltp...  107 us
    pallas_call x8, Pallas kernels, pick_rows(): pl.pallas_call(partial(pick_kernel, group, slices), grid_spec=pltpu.Prefe...  81.3 us
    pallas_call x2, Pallas kernels, weight_grads(): pl.pallas_call(partial(kernel, slots, slices), grid_spec=pltpu.PrefetchSc...  70.8 us
    pallas_call x2, Pallas kernels, down_slots(): pl.pallas_call(partial(down_kernel, slices, slots), grid_spec=pltpu.Prefe...  31.5 us
    unnamed x232, local copies, waits for them, and re-layouts  30.8 us
  transfers between devices with their start and end apart: 110, of which 40 were waited for; matrix products, arithmetic and copies ran while one was open for 12% of the time, Pallas kernels for 31%

profile of v7, /device:TPU:10, one launch (start us, length us, event | category | flops | bytes accessed | tf_op | source)
XLA Modules:
  0.0 1427.5 jit_solution(15573622080114390302)
XLA Ops:
  7.5 15.7 %project.1 = (bf16[1024,2048]{1,0:T(8,128)(2,1)}, f32[1024,1]{1,0:T(8,128)}, f32[1024,512]{1,0:T(8,128)}, f32[1024,512]{1,0:T(8,128)}, bf16[1024,512]{1,0:T(8,12...) custom-call(bf16[1024,2048]{1,0:T(8,128)(2,1)} %in_ref.1, f32[1,2048]{1,0:T(1,128)} %bitcast.209, ...), custom_call_target="tpu_custom_call" | custom-call | flops 103079215104 | bytes 352321536 | tf_op jit(solution)/shard_map/project/pallas_call | solution.py:664
  119.4 34.0 %collective-permute-done.11.refs_2_ = bf16[1024,512]{1,0:T(8,128)(2,1)S(1)} collective-permute-done((bf16[1024,512]{1,0:T(8,128)(2,1)}, bf16[1024,512]{1,0:T(8,128)(2,1)S(1)}, u32[]{:S(2)}, u32[]{:S(2)}) %collective-permute-start.11) | collective-permute-done | bytes 1048608 | tf_op jit(solution)/shard_map/ppermute | solution.py:87
  165.4 37.2 %collective-permute-done.18.refs_2_ = bf16[1024,512]{1,0:T(8,128)(2,1)} collective-permute-done((bf16[1024,512]{1,0:T(8,128)(2,1)}, bf16[1024,512]{1,0:T(8,128)(2,1)}, u32[]{:S(2)}, u32[]{:S(2)}) %collective-permute-start.18) | collective-permute-done | bytes 1048608 | tf_op jit(solution)/shard_map/ppermute | solution.py:87
  229.7 21.4 %collective-permute-done.17.refs_5_ = bf16[1024,512]{1,0:T(8,128)(2,1)} collective-permute-done((bf16[1024,512]{1,0:T(8,128)(2,1)S(1)}, bf16[1024,512]{1,0:T(8,128)(2,1)}, u32[]{:S(2)}, u32[]{:S(2)}) %collective-permute-start.17) | collective-permute-done | bytes 1048608 | tf_op jit(solution)/shard_map/ppermute | solution.py:87
  277.7 27.8 %expert_slot.4 = (bf16[8,320,256]{2,1,0:T(8,128)(2,1)}, bf16[8,320,256]{2,1,0:T(8,128)(2,1)}, bf16[8,320,256]{2,1,0:T(8,128)(2,1)}, f32[8,2,1024]{2,1,0:T(2,128)...) custom-call(s32[10]{0:T(128)} %stack.118.where_ref, s32[8,8,1024]{2,1,0:T(8,128)} %copy.159.refs_0_.refs_1_, ...), custom_call_target="tpu_custom_call" | custom-call | flops 214748364800 | bytes 905969664 | tf_op jit(solution)/shard_map/expert_slot/pallas_call | solution.py:419
  331.7 22.6 %collective-permute-done.39.refs_4_ = bf16[1024,512]{1,0:T(8,128)(2,1)} collective-permute-done((bf16[1024,512]{1,0:T(8,128)(2,1)}, bf16[1024,512]{1,0:T(8,128)(2,1)}, u32[]{:S(2)}, u32[]{:S(2)}) %collective-permute-start.39) | collective-permute-done | bytes 1048608 | tf_op jit(solution)/shard_map/ppermute | solution.py:87
  358.0 18.0 %collective-permute-done.29.refs_5_ = bf16[1024,512]{1,0:T(8,128)(2,1)S(1)} collective-permute-done((bf16[1024,512]{1,0:T(8,128)(2,1)}, bf16[1024,512]{1,0:T(8,128)(2,1)S(1)}, u32[]{:S(2)}, u32[]{:S(2)}) %collective-permute-start.29) | collective-permute-done | bytes 1048608 | tf_op jit(solution)/shard_map/ppermute | solution.py:87
  387.1 14.0 place_rows.6
  401.6 21.6 %collective-permute-done.33.refs_3_ = bf16[1024,512]{1,0:T(8,128)(2,1)} collective-permute-done((bf16[1024,512]{1,0:T(8,128)(2,1)}, bf16[1024,512]{1,0:T(8,128)(2,1)}, u32[]{:S(2)}, u32[]{:S(2)}) %collective-permute-start.33) | collective-permute-done | bytes 1048608 | tf_op jit(solution)/shard_map/ppermute | solution.py:87
  425.3 27.8 %expert_slot.5 = (bf16[8,320,256]{2,1,0:T(8,128)(2,1)}, bf16[8,320,256]{2,1,0:T(8,128)(2,1)}, bf16[8,320,256]{2,1,0:T(8,128)(2,1)}, f32[8,2,1024]{2,1,0:T(2,128)...) custom-call(s32[10]{0:T(128)} %stack.127.where_ref, s32[8,8,1024]{2,1,0:T(8,128)} %copy.159.refs_0_.refs_1_, ...), custom_call_target="tpu_custom_call" | custom-call | flops 214748364800 | bytes 905969664 | tf_op jit(solution)/shard_map/expert_slot/pallas_call | solution.py:419
  453.7 18.6 %collective-permute-done.35.refs_5_ = bf16[1024,512]{1,0:T(8,128)(2,1)} collective-permute-done((bf16[1024,512]{1,0:T(8,128)(2,1)}, bf16[1024,512]{1,0:T(8,128)(2,1)}, u32[]{:S(2)}, u32[]{:S(2)}) %collective-permute-start.35) | collective-permute-done | bytes 1048608 | tf_op jit(solution)/shard_map/ppermute | solution.py:87
  494.4 14.2 place_rows.7
  518.5 16.3 %collective-permute-done.50 = bf16[1024,512]{1,0:T(8,128)(2,1)S(1)} collective-permute-done((bf16[1024,512]{1,0:T(8,128)(2,1)}, bf16[1024,512]{1,0:T(8,128)(2,1)S(1)}, u32[]{:S(2)}, u32[]{:S(2)}) %collective-permute-start.50) | collective-permute-done | bytes 1048608 | tf_op jit(solution)/shard_map/ppermute | solution.py:87
  538.2 27.8 %expert_slot.6 = (bf16[8,320,256]{2,1,0:T(8,128)(2,1)}, bf16[8,320,256]{2,1,0:T(8,128)(2,1)}, bf16[8,320,256]{2,1,0:T(8,128)(2,1)}, f32[8,2,1024]{2,1,0:T(2,128)...) custom-call(s32[10]{0:T(128)} %stack.124.where_ref, s32[8,8,1024]{2,1,0:T(8,128)} %copy.159.refs_0_.refs_1_, ...), custom_call_target="tpu_custom_call" | custom-call | flops 214748364800 | bytes 905969664 | tf_op jit(solution)/shard_map/expert_slot/pallas_call | solution.py:419
  603.0 14.1 place_rows.8
  617.1 27.8 %expert_slot.7 = (bf16[8,320,256]{2,1,0:T(8,128)(2,1)}, bf16[8,320,256]{2,1,0:T(8,128)(2,1)}, bf16[8,320,256]{2,1,0:T(8,128)(2,1)}, f32[8,2,1024]{2,1,0:T(2,128)...) custom-call(s32[10]{0:T(128)} %stack.121.where_ref, s32[8,8,1024]{2,1,0:T(8,128)} %copy.159.refs_0_.refs_1_, ...), custom_call_target="tpu_custom_call" | custom-call | flops 214748364800 | bytes 905969664 | tf_op jit(solution)/shard_map/expert_slot/pallas_call | solution.py:419
  646.1 15.8 %down_slots.2 = (bf16[4,2,1280,512]{3,2,1,0:T(8,128)(2,1)}, bf16[4,2,1280,512]{3,2,1,0:T(8,128)(2,1)}) custom-call(s32[10]{0:T(128)} %stack.118.where_ref, bf16[8,320,256]{2,1,0:T(8,128)(2,1)} %get-tuple-element.148.refs_0_.refs_8_, bf16[8,320,256]{2,1,0:T(8,128)(2,1)} %get-tuple-element.176.refs_1_.refs_9_, bf16[8,256,2048]{2,1,0:T(8,128)(2,1)} %refs_2_.3), custom_call_target="tpu_custom_call" | custom-call | flops 85899345920 | bytes 469762048 | tf_op jit(solution)/shard_map/down_slots/pallas_call | solution.py:459
  669.1 15.7 %down_slots.3 = (bf16[4,2,1280,512]{3,2,1,0:T(8,128)(2,1)}, bf16[4,2,1280,512]{3,2,1,0:T(8,128)(2,1)}) custom-call(s32[10]{0:T(128)} %stack.118.where_ref, bf16[8,320,256]{2,1,0:T(8,128)(2,1)} %get-tuple-element.156.refs_0_.refs_10_, bf16[8,320,256]{2,1,0:T(8,128)(2,1)} %get-tuple-element.165.refs_1_.refs_11_, bf16[8,256,2048]{2,1,0:T(8,128)(2,1)} %refs_2_.3), custom_call_target="tpu_custom_call" | custom-call | flops 85899345920 | bytes 469762048 | tf_op jit(solution)/shard_map/down_slots/pallas_call | solution.py:459
  735.2 17.9 %collective-permute-done.62 = bf16[1024,512]{1,0:T(8,128)(2,1)S(1)} collective-permute-done((bf16[1024,512]{1,0:T(8,128)(2,1)S(1)}, bf16[1024,512]{1,0:T(8,128)(2,1)S(1)}, u32[]{:S(2)}, u32[]{:S(2)}) %collective-permute-start.62) | collective-permute-done | bytes 1048608 | tf_op jit(solution)/shard_map/ppermute | solution.py:87
  756.8 17.7 %collective-permute-done.64 = bf16[1024,512]{1,0:T(8,128)(2,1)S(1)} collective-permute-done((bf16[1024,512]{1,0:T(8,128)(2,1)S(1)}, bf16[1024,512]{1,0:T(8,128)(2,1)S(1)}, u32[]{:S(2)}, u32[]{:S(2)}) %collective-permute-start.64) | collective-permute-done | bytes 1048608 | tf_op jit(solution)/shard_map/ppermute | solution.py:87
  777.1 25.2 %place_rows.10 = (bf16[2,1024,512]{2,1,0:T(8,128)(2,1)}, bf16[2,1024,512]{2,1,0:T(8,128)(2,1)}, bf16[2,1024,512]{2,1,0:T(8,128)(2,1)}, bf16[2,1024,512]{2,1,0:T(8,128)(2,1)}) custom-call(s32[4]{0:T(128)} %pad_add_fusion.3.where_ref, s32[8,1024,8]{2,1,0:T(8,128)} %bitcast.161, s32[8,1024,8]{2,1,0:T(8,128)} %bitcast.162, s32[8,1024,8]{2,1,0:T(8,128)} %bitcast.163, ...), custom_call_target="tpu_custom_call" | custom-call | flops 171798691840 | bytes 469762048 | tf_op jit(solution)/shard_map/place_rows/pallas_call | solution.py:518
  803.8 25.3 %place_rows.11 = (bf16[2,1024,512]{2,1,0:T(8,128)(2,1)}, bf16[2,1024,512]{2,1,0:T(8,128)(2,1)}, bf16[2,1024,512]{2,1,0:T(8,128)(2,1)}, bf16[2,1024,512]{2,1,0:T(8,128)(2,1)}) custom-call(s32[4]{0:T(128)} %pad_add_fusion.4.where_ref, s32[8,1024,8]{2,1,0:T(8,128)} %bitcast.165, s32[8,1024,8]{2,1,0:T(8,128)} %bitcast.166, s32[8,1024,8]{2,1,0:T(8,128)} %bitcast.167, ...), custom_call_target="tpu_custom_call" | custom-call | flops 171798691840 | bytes 469762048 | tf_op jit(solution)/shard_map/place_rows/pallas_call | solution.py:518
  829.2 43.1 %weight_grads.1 = (f32[8,2048,256]{2,1,0:T(8,128)}, f32[8,2048,256]{2,1,0:T(8,128)}) custom-call(s32[10]{0:T(128)} %stack.118.where_ref, bf16[2,2,1280,512]{3,2,1,0:T(8,128)(2,1)} %pick_rows.9.refs_4_.refs_0_, bf16[2,2,1280,512]{3,2,1,0:T(8,128)(2,1)} %collective-permute-done.20.refs_5_.refs_1_, bf16[2,2,1280,512]{3,2,1,0:T(8,128)(2,1)} %pick_rows.15.refs_4_.refs_2_, ...), custom_call_target="tpu_custom_call" | custom-call | flops 160000000000 | bytes 16000000 | tf_op jit(solution)/shard_map/weight_grads/pallas_call | solution.py:575
  901.1 13.9 collective-permute-done.72
  941.4 16.1 %attend_back.1 = (bf16[1024,512]{1,0:T(8,128)(2,1)}, bf16[1024,512]{1,0:T(8,128)(2,1)}, bf16[1024,512]{1,0:T(8,128)(2,1)}, f32[1,1,512]{2,1,0:T(1,128)}, f32[1,1,512]{2,1,0:T(1,128)}) custom-call(s32[4]{0:T(128)} %add_bitcast_fusion.pieces_ref, bf16[1024,512]{1,0:T(8,128)(2,1)} %get-tuple-element.137.q_ref, bf16[1024,512]{1,0:T(8,128)(2,1)} %get-tuple-element.138.k_ref, ...), custom_call_target="tpu_custom_call" | custom-call | flops 85899345920 | bytes 184549376 | tf_op jit(solution)/shard_map/attend_back/pallas_call | solution.py:799
  979.3 66.4 %collective-permute-done.96 = bf16[1024,512]{1,0:T(8,128)(2,1)S(1)} collective-permute-done((bf16[1024,512]{1,0:T(8,128)(2,1)S(1)}, bf16[1024,512]{1,0:T(8,128)(2,1)S(1)}, u32[]{:S(2)}, u32[]{:S(2)}) %collective-permute-start.96) | collective-permute-done | bytes 1048608 | tf_op jit(solution)/shard_map/ppermute | solution.py:87
  1049.7 18.5 %collective-permute-done.90 = bf16[1024,512]{1,0:T(8,128)(2,1)S(1)} collective-permute-done((bf16[1024,512]{1,0:T(8,128)(2,1)S(1)}, bf16[1024,512]{1,0:T(8,128)(2,1)S(1)}, u32[]{:S(2)}, u32[]{:S(2)}) %collective-permute-start.90) | collective-permute-done | bytes 1048608 | tf_op jit(solution)/shard_map/ppermute | solution.py:87
  1164.4 28.7 %collective-permute-done.84 = f32[69,512]{1,0:T(8,128)S(1)} collective-permute-done((f32[69,512]{1,0:T(8,128)S(1)}, f32[69,512]{1,0:T(8,128)S(1)}, u32[]{:S(2)}, u32[]{:S(2)}) %collective-permute-start.84) | collective-permute-done | bytes 141344 | tf_op jit(solution)/shard_map/ppermute | solution.py:87
  1196.7 27.7 %weight_down_grads.1 = f32[8,256,2048]{2,1,0:T(8,128)} custom-call(s32[10]{0:T(128)} %stack.118.where_ref, bf16[2,2,1280,512]{3,2,1,0:T(8,128)(2,1)} %pick_rows.8.refs_6_.refs_0_, bf16[2,2,1280,512]{3,2,1,0:T(8,128)(2,1)} %collective-permute-done.21.refs_7_.refs_1_, bf16[2,2,1280,512]{3,2,1,0:T(8,128)(2,1)} %pick_rows.14.refs_6_.refs_2_, ...), custom_call_target="tpu_custom_call" | custom-call | flops 160000000000 | bytes 16000000 | tf_op jit(solution)/shard_map/weight_down_grads/pallas_call | solution.py:575
  1236.1 105.3 %collective-permute-done.105 = bf16[256,1024]{1,0:T(8,128)(2,1)S(1)} collective-permute-done((bf16[256,1024]{1,0:T(8,128)(2,1)S(1)}, bf16[256,1024]{1,0:T(8,128)(2,1)S(1)}, u32[]{:S(2)}, u32[]{:S(2)}) %collective-permute-start.105) | collective-permute-done | bytes 524320 | tf_op jit(solution)/shard_map/ppermute | solution.py:87
  1378.1 18.8 %collective-permute-done.87 = bf16[1024,512]{1,0:T(8,128)(2,1)S(1)} collective-permute-done((bf16[1024,512]{1,0:T(8,128)(2,1)S(1)}, bf16[1024,512]{1,0:T(8,128)(2,1)S(1)}, u32[]{:S(2)}, u32[]{:S(2)}) %collective-permute-start.87) | collective-permute-done | bytes 1048608 | tf_op jit(solution)/shard_map/ppermute | solution.py:87
  1400.9 14.4 %collective-permute-done.107.refs_5_ = bf16[1024,1024]{1,0:T(8,128)(2,1)} collective-permute-done((bf16[1024,1024]{1,0:T(8,128)(2,1)S(1)}, bf16[1024,1024]{1,0:T(8,128)(2,1)}, u32[]{:S(2)}, u32[]{:S(2)}) %collective-permute-start.107) | collective-permute-done | bytes 2097184 | tf_op jit(solution)/shard_map/ppermute | solution.py:87
  (577 shorter events, 595.4 us)
Async XLA Ops:
  83.0 70.3 %collective-permute-start.11 = (bf16[1024,512]{1,0:T(8,128)(2,1)}, bf16[1024,512]{1,0:T(8,128)(2,1)S(1)}, u32[]{:S(2)}, u32[]{:S(2)}) collective-permute-start(bf16[1024,512]{1,0:T(8,128)(2,1)} %convert_element_type.331.refs_2_), channel_id=1, source_target_pairs={{0,16},{1,17},{2,18},{3,19},{4,20},{5,21},{6,22},{7,23},{8,24},{9,... | collective-permute-start | bytes 3145736 | tf_op jit(solution)/shard_map/ppermute | solution.py:87
  86.4 116.3 %collective-permute-start.18 = (bf16[1024,512]{1,0:T(8,128)(2,1)}, bf16[1024,512]{1,0:T(8,128)(2,1)}, u32[]{:S(2)}, u32[]{:S(2)}) collective-permute-start(bf16[1024,512]{1,0:T(8,128)(2,1)} %convert_element_type.331.refs_2_), channel_id=1, source_target_pairs={{0,24},{1,25},{2,26},{3,27},{4,28},{5,29},{6,30},{7,31},{8,16},{9,... | collective-permute-start | bytes 3145736 | tf_op jit(solution)/shard_map/ppermute | solution.py:87
  106.7 96.5 %collective-permute-start.15 = (bf16[1024,512]{1,0:T(8,128)(2,1)}, bf16[1024,512]{1,0:T(8,128)(2,1)S(1)}, u32[]{:S(2)}, u32[]{:S(2)}) collective-permute-start(bf16[1024,512]{1,0:T(8,128)(2,1)} %multiply_convert_fusion.2.refs_2_), channel_id=1, source_target_pairs={{0,2},{1,3},{2,0},{3,1},{4,6},{5,7},{6,4},{7,5},{8,10},{9,11},{10,... | collective-permute-start | bytes 3145736 | tf_op jit(solution)/shard_map/ppermute | solution.py:87
  155.4 68.2 %collective-permute-start.14 = (bf16[1024,512]{1,0:T(8,128)(2,1)}, bf16[1024,512]{1,0:T(8,128)(2,1)}, u32[]{:S(2)}, u32[]{:S(2)}) collective-permute-start(bf16[1024,512]{1,0:T(8,128)(2,1)} %multiply_convert_fusion.2.refs_2_), channel_id=1, source_target_pairs={{0,16},{1,17},{2,18},{3,19},{4,20},{5,21},{6,22},{7,23},{8,24},{9,... | collective-permute-start | bytes 3145736 | tf_op jit(solution)/shard_map/ppermute | solution.py:87
  160.7 117.0 %all-to-all-start = ((f32[8,8,1024]{2,1,0:T(8,128)}), f32[8,8,1024]{2,1,0:T(8,128)}, u32[]{:S(2)}, u32[]{:S(2)}) async-start(f32[8,8,1024]{2,1,0:T(8,128)} %fusion.82), calls=%async_computation | async-start | bytes 524288 | tf_op jit(solution)/shard_map/all_to_all | solution.py:937
  214.8 90.7 %collective-permute-start.37 = (bf16[1024,512]{1,0:T(8,128)(2,1)}, bf16[1024,512]{1,0:T(8,128)(2,1)}, u32[]{:S(2)}, u32[]{:S(2)}) collective-permute-start(bf16[1024,512]{1,0:T(8,128)(2,1)} %convert_element_type.331.refs_2_), channel_id=1, source_target_pairs={{0,8},{1,9},{2,10},{3,11},{4,12},{5,13},{6,14},{7,15},{8,0},{9,1},... | collective-permute-start | bytes 3145736 | tf_op jit(solution)/shard_map/ppermute | solution.py:87
  214.9 91.2 %collective-permute-start.27 = (bf16[1024,512]{1,0:T(8,128)(2,1)}, bf16[1024,512]{1,0:T(8,128)(2,1)}, u32[]{:S(2)}, u32[]{:S(2)}) collective-permute-start(bf16[1024,512]{1,0:T(8,128)(2,1)} %collective-permute-done.18.refs_2_), channel_id=1, source_target_pairs={{0,2},{1,3},{2,0},{3,1},{4,6},{5,7},{6,4},{7,5},{8,10},{9,11},{10,... | collective-permute-start | bytes 3145736 | tf_op jit(solution)/shard_map/ppermute | solution.py:87
  307.6 68.4 %collective-permute-start.29 = (bf16[1024,512]{1,0:T(8,128)(2,1)}, bf16[1024,512]{1,0:T(8,128)(2,1)S(1)}, u32[]{:S(2)}, u32[]{:S(2)}) collective-permute-start(bf16[1024,512]{1,0:T(8,128)(2,1)} %collective-permute-done.27.refs_3_), channel_id=1, source_target_pairs={{0,4},{1,5},{2,6},{3,7},{4,0},{5,1},{6,2},{7,3},{8,12},{9,13},{10,... | collective-permute-start | bytes 3145736 | tf_op jit(solution)/shard_map/ppermute | solution.py:87
  354.4 128.6 %collective-permute-start.38 = (bf16[1024,512]{1,0:T(8,128)(2,1)}, bf16[1024,512]{1,0:T(8,128)(2,1)}, u32[]{:S(2)}, u32[]{:S(2)}) collective-permute-start(bf16[1024,512]{1,0:T(8,128)(2,1)} %collective-permute-done.37.refs_2_), channel_id=1, source_target_pairs={{0,2},{1,3},{2,0},{3,1},{4,6},{5,7},{6,4},{7,5},{8,10},{9,11},{10,... | collective-permute-start | bytes 3145736 | tf_op jit(solution)/shard_map/ppermute | solution.py:87
  355.9 127.1 %collective-permute-start.40 = (bf16[1024,512]{1,0:T(8,128)(2,1)}, bf16[1024,512]{1,0:T(8,128)(2,1)}, u32[]{:S(2)}, u32[]{:S(2)}) collective-permute-start(bf16[1024,512]{1,0:T(8,128)(2,1)} %collective-permute-done.39.refs_4_), channel_id=1, source_target_pairs={{0,2},{1,3},{2,0},{3,1},{4,6},{5,7},{6,4},{7,5},{8,10},{9,11},{10,... | collective-permute-start | bytes 3145736 | tf_op jit(solution)/shard_map/ppermute | solution.py:87
  423.3 89.4 %collective-permute-start.46 = (bf16[1024,512]{1,0:T(8,128)(2,1)}, bf16[1024,512]{1,0:T(8,128)(2,1)}, u32[]{:S(2)}, u32[]{:S(2)}) collective-permute-start(bf16[1024,512]{1,0:T(8,128)(2,1)} %collective-permute-done.44.refs_2_), channel_id=1, source_target_pairs={{0,4},{1,5},{2,6},{3,7},{4,0},{5,1},{6,2},{7,3},{8,12},{9,13},{10,... | collective-permute-start | bytes 3145736 | tf_op jit(solution)/shard_map/ppermute | solution.py:87
  512.7 67.2 %collective-permute-start.47 = (bf16[1024,512]{1,0:T(8,128)(2,1)}, bf16[1024,512]{1,0:T(8,128)(2,1)}, u32[]{:S(2)}, u32[]{:S(2)}) collective-permute-start(bf16[1024,512]{1,0:T(8,128)(2,1)} %collective-permute-done.46.refs_4_), channel_id=1, source_target_pairs={{0,2},{1,3},{2,0},{3,1},{4,6},{5,7},{6,4},{7,5},{8,10},{9,11},{10,... | collective-permute-start | bytes 3145736 | tf_op jit(solution)/shard_map/ppermute | solution.py:87
  517.3 85.0 %collective-permute-start.49 = (bf16[1024,512]{1,0:T(8,128)(2,1)}, bf16[1024,512]{1,0:T(8,128)(2,1)}, u32[]{:S(2)}, u32[]{:S(2)}) collective-permute-start(bf16[1024,512]{1,0:T(8,128)(2,1)} %fusion.37), channel_id=1, source_target_pairs={{0,2},{1,3},{2,0},{3,1},{4,6},{5,7},{6,4},{7,5},{8,10},{9,11},{10,... | collective-permute-start | bytes 3145736 | tf_op jit(solution)/shard_map/ppermute | solution.py:87
  534.8 67.5 %collective-permute-start.48 = (bf16[1024,512]{1,0:T(8,128)(2,1)}, bf16[1024,512]{1,0:T(8,128)(2,1)}, u32[]{:S(2)}, u32[]{:S(2)}) collective-permute-start(bf16[1024,512]{1,0:T(8,128)(2,1)} %bitcast.28), channel_id=1, source_target_pairs={{0,4},{1,5},{2,6},{3,7},{4,0},{5,1},{6,2},{7,3},{8,12},{9,13},{10,... | collective-permute-start | bytes 3145736 | tf_op jit(solution)/shard_map/ppermute | solution.py:87
  536.7 148.2 %collective-permute-start.56 = (bf16[1024,512]{1,0:T(8,128)(2,1)}, bf16[1024,512]{1,0:T(8,128)(2,1)}, u32[]{:S(2)}, u32[]{:S(2)}) collective-permute-start(bf16[1024,512]{1,0:T(8,128)(2,1)} %bitcast.33), channel_id=1, source_target_pairs={{0,2},{1,3},{2,0},{3,1},{4,6},{5,7},{6,4},{7,5},{8,10},{9,11},{10,... | collective-permute-start | bytes 3145736 | tf_op jit(solution)/shard_map/ppermute | solution.py:87
  566.0 118.8 %collective-permute-start.55 = (bf16[1024,512]{1,0:T(8,128)(2,1)}, bf16[1024,512]{1,0:T(8,128)(2,1)}, u32[]{:S(2)}, u32[]{:S(2)}) collective-permute-start(bf16[1024,512]{1,0:T(8,128)(2,1)} %fusion.36), channel_id=1, source_target_pairs={{0,4},{1,5},{2,6},{3,7},{4,0},{5,1},{6,2},{7,3},{8,12},{9,13},{10,... | collective-permute-start | bytes 3145736 | tf_op jit(solution)/shard_map/ppermute | solution.py:87
  661.9 114.6 %collective-permute-start.57 = (bf16[4,2,1280,512]{3,2,1,0:T(8,128)(2,1)}, bf16[4,2,1280,512]{3,2,1,0:T(8,128)(2,1)}, u32[]{:S(2)}, u32[]{:S(2)}) collective-permute-start(bf16[4,2,1280,512]{3,2,1,0:T(8,128)(2,1)} %get-tuple-element.189), channel_id=1, source_target_pairs={{0,1},{1,0},{2,3},{3,2},{4,5},{5,4},{6,7},{7,6},{8,9},{9,8},{10,11... | collective-permute-start | bytes 31457288 | tf_op jit(solution)/shard_map/ppermute | solution.py:87
  753.1 119.2 %collective-permute-start.66 = (bf16[1024,512]{1,0:T(8,128)(2,1)}, bf16[1024,512]{1,0:T(8,128)(2,1)}, u32[]{:S(2)}, u32[]{:S(2)}) collective-permute-start(bf16[1024,512]{1,0:T(8,128)(2,1)} %fusion.30), channel_id=1, source_target_pairs={{0,16},{1,17},{2,18},{3,19},{4,20},{5,21},{6,22},{7,23},{8,24},{9,... | collective-permute-start | bytes 3145736 | tf_op jit(solution)/shard_map/ppermute | solution.py:87
  756.8 115.4 %collective-permute-start.67 = (bf16[1024,512]{1,0:T(8,128)(2,1)}, bf16[1024,512]{1,0:T(8,128)(2,1)}, u32[]{:S(2)}, u32[]{:S(2)}) collective-permute-start(bf16[1024,512]{1,0:T(8,128)(2,1)} %fusion.28), channel_id=1, source_target_pairs={{0,24},{1,25},{2,26},{3,27},{4,28},{5,29},{6,30},{7,31},{8,16},{9,... | collective-permute-start | bytes 3145736 | tf_op jit(solution)/shard_map/ppermute | solution.py:87
  775.9 96.3 %collective-permute-start.65 = (bf16[1024,512]{1,0:T(8,128)(2,1)}, bf16[1024,512]{1,0:T(8,128)(2,1)}, u32[]{:S(2)}, u32[]{:S(2)}) collective-permute-start(bf16[1024,512]{1,0:T(8,128)(2,1)} %fusion.32), channel_id=1, source_target_pairs={{0,8},{1,9},{2,10},{3,11},{4,12},{5,13},{6,14},{7,15},{8,0},{9,1},... | collective-permute-start | bytes 3145736 | tf_op jit(solution)/shard_map/ppermute | solution.py:87
  802.4 87.5 %collective-permute-start.58 = (bf16[2,1024,512]{2,1,0:T(8,128)(2,1)}, bf16[2,1024,512]{2,1,0:T(8,128)(2,1)}, u32[]{:S(2)}, u32[]{:S(2)}) collective-permute-start(bf16[2,1024,512]{2,1,0:T(8,128)(2,1)} %get-tuple-element.193), channel_id=1, source_target_pairs={{0,4},{1,5},{2,6},{3,7},{4,0},{5,1},{6,2},{7,3},{8,12},{9,13},{10,... | collective-permute-start | bytes 6291464 | tf_op jit(solution)/shard_map/ppermute | solution.py:87
  933.4 177.8 %collective-permute-start.76 = (bf16[2,1024,512]{2,1,0:T(8,128)(2,1)}, bf16[2,1024,512]{2,1,0:T(8,128)(2,1)}, u32[]{:S(2)}, u32[]{:S(2)}) collective-permute-start(bf16[2,1024,512]{2,1,0:T(8,128)(2,1)} %get-tuple-element.230), channel_id=1, source_target_pairs={{0,4},{1,5},{2,6},{3,7},{4,0},{5,1},{6,2},{7,3},{8,12},{9,13},{10,... | collective-permute-start | bytes 6291464 | tf_op jit(solution)/shard_map/ppermute | solution.py:87
  970.9 74.8 %collective-permute-start.96 = (bf16[1024,512]{1,0:T(8,128)(2,1)S(1)}, bf16[1024,512]{1,0:T(8,128)(2,1)S(1)}, u32[]{:S(2)}, u32[]{:S(2)}) collective-permute-start(bf16[1024,512]{1,0:T(8,128)(2,1)S(1)} %slice.221), channel_id=1, source_target_pairs={{0,4},{1,5},{2,6},{3,7},{4,0},{5,1},{6,2},{7,3},{8,12},{9,13},{10,... | collective-permute-start | bytes 3145736 | tf_op jit(solution)/shard_map/ppermute | solution.py:87
  974.8 93.3 %collective-permute-start.90 = (bf16[1024,512]{1,0:T(8,128)(2,1)S(1)}, bf16[1024,512]{1,0:T(8,128)(2,1)S(1)}, u32[]{:S(2)}, u32[]{:S(2)}) collective-permute-start(bf16[1024,512]{1,0:T(8,128)(2,1)S(1)} %pad_maximum_fusion.2), channel_id=1, source_target_pairs={{0,4},{1,5},{2,6},{3,7},{4,0},{5,1},{6,2},{7,3},{8,12},{9,13},{10,... | collective-permute-start | bytes 3145736 | tf_op jit(solution)/shard_map/ppermute | solution.py:87
  976.7 137.9 %collective-permute-start.77 = (bf16[2,1024,512]{2,1,0:T(8,128)(2,1)S(1)}, bf16[2,1024,512]{2,1,0:T(8,128)(2,1)S(1)}, u32[]{:S(2)}, u32[]{:S(2)}) collective-permute-start(bf16[2,1024,512]{2,1,0:T(8,128)(2,1)S(1)} %add_convert_fusion.2), channel_id=1, source_target_pairs={{0,2},{1,3},{2,0},{3,1},{4,6},{5,7},{6,4},{7,5},{8,10},{9,11},{10,... | collective-permute-start | bytes 6291464 | tf_op jit(solution)/shard_map/ppermute | solution.py:87
  978.4 140.2 %collective-permute-start.102 = (bf16[1024,1024]{1,0:T(8,128)(2,1)S(1)}, bf16[1024,1024]{1,0:T(8,128)(2,1)S(1)}, u32[]{:S(2)}, u32[]{:S(2)}) collective-permute-start(bf16[1024,1024]{1,0:T(8,128)(2,1)S(1)} %slice.227), channel_id=1, source_target_pairs={{0,4},{1,5},{2,6},{3,7},{4,0},{5,1},{6,2},{7,3},{8,12},{9,13},{10,... | collective-permute-start | bytes 6291464 | tf_op jit(solution)/shard_map/ppermute | solution.py:87
  1145.3 79.2 %collective-permute-start.100 = (bf16[512,512]{1,0:T(8,128)(2,1)}, bf16[512,512]{1,0:T(8,128)(2,1)}, u32[]{:S(2)}, u32[]{:S(2)}) collective-permute-start(bf16[512,512]{1,0:T(8,128)(2,1)} %pad_maximum_fusion.7), channel_id=1, source_target_pairs={{0,8},{1,9},{2,10},{3,11},{4,12},{5,13},{6,14},{7,15},{8,0},{9,1},... | collective-permute-start | bytes 1572872 | tf_op jit(solution)/shard_map/ppermute | solution.py:87
  1149.6 84.1 %collective-permute-start.94 = (bf16[512,512]{1,0:T(8,128)(2,1)}, bf16[512,512]{1,0:T(8,128)(2,1)}, u32[]{:S(2)}, u32[]{:S(2)}) collective-permute-start(bf16[512,512]{1,0:T(8,128)(2,1)} %pad_maximum_fusion.6), channel_id=1, source_target_pairs={{0,8},{1,9},{2,10},{3,11},{4,12},{5,13},{6,14},{7,15},{8,0},{9,1},... | collective-permute-start | bytes 1572872 | tf_op jit(solution)/shard_map/ppermute | solution.py:87
  1225.8 173.1 %collective-permute-start.101 = (bf16[1024,512]{1,0:T(8,128)(2,1)S(1)}, bf16[1024,512]{1,0:T(8,128)(2,1)S(1)}, u32[]{:S(2)}, u32[]{:S(2)}) collective-permute-start(bf16[1024,512]{1,0:T(8,128)(2,1)S(1)} %pad_maximum_fusion.4.refs_2_), channel_id=1, source_target_pairs={{0,4},{1,5},{2,6},{3,7},{4,0},{5,1},{6,2},{7,3},{8,12},{9,13},{10,... | collective-permute-start | bytes 3145736 | tf_op jit(solution)/shard_map/ppermute | solution.py:87
  1227.7 141.4 %collective-permute-start.86 = (bf16[2,1024,512]{2,1,0:T(8,128)(2,1)}, bf16[2,1024,512]{2,1,0:T(8,128)(2,1)S(1)}, u32[]{:S(2)}, u32[]{:S(2)}) collective-permute-start(bf16[2,1024,512]{2,1,0:T(8,128)(2,1)} %add_convert_fusion.1), channel_id=1, source_target_pairs={{0,16},{1,17},{2,18},{3,19},{4,20},{5,21},{6,22},{7,23},{8,24},{9,... | collective-permute-start | bytes 6291464 | tf_op jit(solution)/shard_map/ppermute | solution.py:87
  1229.5 111.8 %collective-permute-start.105 = (bf16[256,1024]{1,0:T(8,128)(2,1)S(1)}, bf16[256,1024]{1,0:T(8,128)(2,1)S(1)}, u32[]{:S(2)}, u32[]{:S(2)}) collective-permute-start(bf16[256,1024]{1,0:T(8,128)(2,1)S(1)} %add_convert_fusion.9), channel_id=1, source_target_pairs={{0,16},{1,17},{2,18},{3,19},{4,20},{5,21},{6,22},{7,23},{8,24},{9,... | collective-permute-start | bytes 1572872 | tf_op jit(solution)/shard_map/ppermute | solution.py:87
  1234.8 164.1 %collective-permute-start.95 = (bf16[1024,512]{1,0:T(8,128)(2,1)S(1)}, bf16[1024,512]{1,0:T(8,128)(2,1)S(1)}, u32[]{:S(2)}, u32[]{:S(2)}) collective-permute-start(bf16[1024,512]{1,0:T(8,128)(2,1)S(1)} %pad_maximum_fusion.3.refs_0_), channel_id=1, source_target_pairs={{0,4},{1,5},{2,6},{3,7},{4,0},{5,1},{6,2},{7,3},{8,12},{9,13},{10,... | collective-permute-start | bytes 3145736 | tf_op jit(solution)/shard_map/ppermute | solution.py:87
  (187 other events, 5245.6 us)

commit v8 on v7

--- a/solution.py
+++ b/solution.py
@@ -23,10 +23,10 @@
 ODD = (1, 2)
 DUE = {
     "attended": ("cx0", "cy0"),
-    "normed": ("cd0",),
-    "row0": ("cx2", "cy2", "nz2"),
-    "cot2": ("cz3",),
-    "row2": ("sc2",),
+    "normed": ("cz2", "cd0"),
+    "row0": ("cx2", "cz3", "cy2"),
+    "exp0": ("cx3",),
+    "row2": ("sc2", "cy3"),
     "cot3": ("sg0",),
     "place0": ("sr2",),
     "exp2": ("sc3",),
@@ -34,15 +34,13 @@
     "place2": ("sr3", "ed0"),
     "exp3": ("sc1",),
     "place3": ("ex0", "ey0", "ed2"),
-    "down1": ("sg1",),
-    "place1": ("ed3", "ex2", "ey2"),
-    "pd0": ("sd0",),
-    "pd1": ("sd1", "ed1", "ex3", "ey3"),
-    "weight": ("ex1", "ey1"),
-    "residual_grad": ("gd0",),
-    "back": ("gd1",),
-    "normed_grad": ("gx0", "gy0"),
-    "weight_down": ("hs",),
+    "down1": ("ex2", "ey2", "ed3"),
+    "pd0": ("ed1", "sd0"),
+    "weight": ("ex3", "ey3", "ex1", "ey1"),
+    "residual_grad": ("gd0", "gd1"),
+    "back": ("gx0",),
+    "normed_grad": ("gx1", "gy0"),
+    "ends": ("qk2",),
 }
 
 
@@ -169,7 +167,7 @@
     else:
         over_x, over_y = after(over_x, far), added(over_y, far).astype(BF16)
     if hold:
-        over_x, over_y = after(over_x, *hold), after(over_y, *hold)
+        over_y = after(over_y, *hold)
     from_x, from_y = send(over_x, dx=1), send(over_y, dy=1)
     return added(near, from_x, from_y), {"d": far, "x": from_x, "y": from_y}
 
@@ -185,7 +183,7 @@
 def scatter_corners(pairs, seen):
     if not is_cube():
         return []
-    far = [scatter_corner(pair, False) for pair in pairs]
+    far = [scatter_corner(pair, i == 0) for i, pair in enumerate(pairs)]
     seen.update({"gd" + str(i): value for i, value in enumerate(far)})
     return far
 
@@ -195,7 +193,7 @@
         return pairs
     planes = []
     for i, pair in enumerate(pairs):
-        plane, sent = scatter_plane(pair, far[i], False, hold)
+        plane, sent = scatter_plane(pair, far[i], i == 0, hold)
         planes.append(plane)
         seen.update({"g" + link + str(i): value for link, value in sent.items()})
     return planes
@@ -207,7 +205,7 @@
             [[[a[i] for a in b] for b in pair] for pair in planes for i in range(pair[0][0].shape[0])]
         )
     low, high = planes
-    total = low + send(after(high.astype(BF16), hold), dz=2).astype(F32)
+    total = low + send(after(high.astype(BF16), *hold), dz=2).astype(F32)
     return total[0] + send(total[1].astype(BF16), dz=1).astype(F32)
 
 
@@ -225,11 +223,11 @@
     return lambda s: (part ^ s) % 2 * 2 + (part ^ s) // 2
 
 
-def tensor_gather(own):
+def tensor_gather(own, beside=()):
     if not is_cube():
         full = lax.all_gather(own, "tensor")
         return [full[i] for i in range(full.shape[0])]
-    over_y = send(own, dy=1)
+    over_y = after(send(own, dy=1), *beside)
     return [own, over_y, core_swap(own), core_swap(over_y)]
 
 
@@ -260,7 +258,7 @@
     return [owner ^ (b | first << 1 | second << 2) for b in (0, 1) for first in (0, 1) for second in (0, 1)]
 
 
-def expert_sum(value):
+def expert_sum(value, tag, seen):
     half = value.shape[0] // 2
     if not is_cube():
         value = lax.psum(value, "expert")
@@ -269,7 +267,9 @@
         half = value.shape[0] // 2
         value = added(value[:half], send(value[half:], **step)).astype(BF16)
     for step in ({"dz": 2}, {"dz": 1}):
-        value = jnp.concatenate([value, send(value, **step)], axis=0)
+        seen[tag] = send(value, **step)
+        value = jnp.concatenate([value, seen[tag]], axis=0)
+        seen[tag + str(step["dz"])] = seen[tag]
     return value, send(value, dx=1)
 
 
@@ -828,7 +828,7 @@
         if i + 1 < slots:
             steps.append(("row", order[i + 1]))
         else:
-            steps += [("down", j) for j in range(slots // 2)]
+            steps.append(("down", 0))
         if i + 2 < slots:
             steps.append(("cot", order[i + 2]))
         steps.append(("place", k))
@@ -985,6 +985,8 @@
                 if k:
                     sums[k] = sent["z"] = send(sums[k].astype(BF16), dz=k)
                 seen.update({"e" + link + str(k): value for link, value in sent.items()})
+    for k in range(1, slots // 2):
+        last = lower(k)
     pairs = []
     for k in range(slots // 2):
         pairs.append(place_rows([turn("pd" + str(k), 2 * k), where[2 * k + 1]], at, *downs[k]))
@@ -1023,7 +1025,16 @@
     upstream = grad_normed * gain_slice
     mean_dot = tensor_sum(jnp.sum(upstream * moe_hat, axis=-1).reshape(8, -1)).reshape(-1, 1) / width
     grad_residual = cotangent + moe_inv * (upstream - moe_hat * mean_dot)
-    branch_pieces = tensor_gather(after(grad_residual.astype(BF16), *due("residual_grad", seen)))
+    grad_branch = after(grad_residual.astype(BF16), *due("residual_grad", seen))
+    (grad_down,) = weight_grads(
+        weight_down_kernel,
+        after(where[0], grad_branch),
+        cots,
+        scaled,
+        [w_down.shape[1:]],
+        "weight_down_grads",
+    )
+    branch_pieces = tensor_gather(grad_branch, [grad_down])
 
     planes = scatter_planes(pairs, far, branch_pieces[1:2], seen)
     grad_branch = jnp.concatenate(branch_pieces, axis=1)
@@ -1041,7 +1052,7 @@
         ],
         axis=0,
     )
-    sum_output = expert_sum(grad_output)
+    sum_output = expert_sum(grad_output, "o", seen)
     grad_attended = matmul_nt(grad_branch, jnp.concatenate(output_pieces, axis=1)).astype(BF16)
     grad_attended = after(grad_attended, grad_output)
     grad_query_raw, grad_key_raw, grad_v, grad_query_gain, grad_key_gain = attend_back(
@@ -1057,22 +1068,14 @@
         key_gain,
         scale,
     )
-    sum_value = expert_sum(matmul_tn(normed_rows, grad_v).astype(BF16))
+    sum_value = expert_sum(matmul_tn(normed_rows, grad_v).astype(BF16), "v", seen)
     grad_raw = jnp.concatenate([grad_query_raw, grad_key_raw, grad_v], axis=1)
     grad_both = matmul_tn(normed_rows, grad_raw[:, : 2 * slice_width]).astype(BF16)
-    sum_both = expert_sum(grad_both)
+    sum_both = expert_sum(grad_both, "qk", seen)
     grad_raw = after(grad_raw, grad_both, *due("normed_grad", seen))
     weights = jnp.concatenate([w_query, w_key, w_value], axis=1)
     weight_pieces = [lax.dynamic_slice_in_dim(weights, o * slice_width, slice_width, 0) for o in order]
     grad_normed_a = tensor_scatter(partial(matmul_nt, grad_raw), weight_pieces, "h", seen)
-    (grad_down,) = weight_grads(
-        weight_down_kernel,
-        after(where[0], *due("weight_down", seen)),
-        cots,
-        scaled,
-        [w_down.shape[1:]],
-        "weight_down_grads",
-    )
     attn_hat = own_columns(inputs).astype(F32) * attn_inv
     upstream = grad_normed_a * own_columns(attn_gain)
     grad_attn_gain = jnp.sum(grad_normed_a * attn_hat, axis=0)
@@ -1096,7 +1099,7 @@
     top_row = jnp.pad(head_top, (0, slice_width - heads_here), constant_values=-3e38)
     small, top_row = expert_total(small, top_row[None])
     head_top = top_row[0, :heads_here]
-    mixture = scatter_ends(planes, small)
+    mixture = scatter_ends(planes, [small, *due("ends", seen)])
     out = residual + mixture
     sum_moe_gain, sum_query_gain, sum_key_gain = small[E + 1], small[E + 2], small[E + 3]
     every = lax.all_gather(small[: E + 1], "tensor")

time: 1440 us -> 1270 us (0.88)
  waiting for transfers between devices: 658 us -> 483 us
    ppermute x108, waiting for transfers between devices: 658 us -> 483 us  [send(): return lax.ppermute(value, BOTH, flip(dz, dx, dy, dc))]
    unnamed x232 -> x200, local copies, waits for them, and re-layouts: 30.8 us -> 21.6 us
  transfers between devices with their start and end apart: 110 -> 110, of which waited for: 40 -> 34; matrix products, arithmetic and copies ran while one was open for 12% -> 12% of each run, Pallas kernels for 31% -> 33%
where the time goes in v8:
time: 1270 us; the launch traced here: 1250 us
  waiting for transfers between devices  483 us (38%)
  Pallas kernels  458 us (36%)
  starting transfers between devices  128 us (10%)
  other arithmetic  71.9 us (6%)
  local copies, waits for them, and re-layouts  53.6 us (4%)
  matrix products  46 us (4%)
    ppermute x108, waiting for transfers between devices, send(): return lax.ppermute(value, BOTH, flip(dz, dx, dy, dc))  483 us
    ppermute x108, starting transfers between devices, send(): return lax.ppermute(value, BOTH, flip(dz, dx, dy, dc))  114 us
    pallas_call x4, Pallas kernels, expert_slot(): pl.pallas_call(partial(expert_kernel, slices), grid_spec=pltpu.PrefetchSc...  112 us
    pallas_call x6, Pallas kernels, place_rows(): pl.pallas_call(partial(place_kernel, slices, held, slots), grid_spec=pltp...  107 us
    pallas_call x8, Pallas kernels, pick_rows(): pl.pallas_call(partial(pick_kernel, group, slices), grid_spec=pltpu.Prefe...  81.4 us
    pallas_call x2, Pallas kernels, weight_grads(): pl.pallas_call(partial(kernel, slots, slices), grid_spec=pltpu.PrefetchSc...  70.4 us
    pallas_call x2, Pallas kernels, down_slots(): pl.pallas_call(partial(down_kernel, slices, slots), grid_spec=pltpu.Prefe...  31.5 us
  transfers between devices with their start and end apart: 110, of which 34 were waited for; matrix products, arithmetic and copies ran while one was open for 12% of the time, Pallas kernels for 33%

profile of v8, /device:TPU:10, one launch (start us, length us, event | category | flops | bytes accessed | tf_op | source)
XLA Modules:
  0.0 1250.3 jit_solution(17162694715500455161)
XLA Ops:
  7.5 15.7 %project.1 = (bf16[1024,2048]{1,0:T(8,128)(2,1)}, f32[1024,1]{1,0:T(8,128)}, f32[1024,512]{1,0:T(8,128)}, f32[1024,512]{1,0:T(8,128)}, bf16[1024,512]{1,0:T(8,12...) custom-call(bf16[1024,2048]{1,0:T(8,128)(2,1)} %in_ref.1, f32[1,2048]{1,0:T(1,128)} %bitcast.210, ...), custom_call_target="tpu_custom_call" | custom-call | flops 103079215104 | bytes 352321536 | tf_op jit(solution)/shard_map/project/pallas_call | solution.py:664
  102.0 31.0 %collective-permute-done.10.refs_2_ = bf16[1024,512]{1,0:T(8,128)(2,1)} collective-permute-done((bf16[1024,512]{1,0:T(8,128)(2,1)}, bf16[1024,512]{1,0:T(8,128)(2,1)}, u32[]{:S(2)}, u32[]{:S(2)}) %collective-permute-start.10) | collective-permute-done | bytes 1048608 | tf_op jit(solution)/shard_map/ppermute | solution.py:85
  169.9 19.3 %collective-permute-done.13.refs_2_ = bf16[1024,512]{1,0:T(8,128)(2,1)} collective-permute-done((bf16[1024,512]{1,0:T(8,128)(2,1)}, bf16[1024,512]{1,0:T(8,128)(2,1)}, u32[]{:S(2)}, u32[]{:S(2)}) %collective-permute-start.13) | collective-permute-done | bytes 1048608 | tf_op jit(solution)/shard_map/ppermute | solution.py:85
  195.2 22.6 %collective-permute-done.17.refs_5_ = bf16[1024,512]{1,0:T(8,128)(2,1)S(1)} collective-permute-done((bf16[1024,512]{1,0:T(8,128)(2,1)S(1)}, bf16[1024,512]{1,0:T(8,128)(2,1)S(1)}, u32[]{:S(2)}, u32[]{:S(2)}) %collective-permute-start.17) | collective-permute-done | bytes 1048608 | tf_op jit(solution)/shard_map/ppermute | solution.py:85
  232.3 30.8 %collective-permute-done.24.refs_2_ = bf16[1024,512]{1,0:T(8,128)(2,1)} collective-permute-done((bf16[1024,512]{1,0:T(8,128)(2,1)}, bf16[1024,512]{1,0:T(8,128)(2,1)}, u32[]{:S(2)}, u32[]{:S(2)}) %collective-permute-start.24) | collective-permute-done | bytes 1048608 | tf_op jit(solution)/shard_map/ppermute | solution.py:85
  291.5 27.8 %expert_slot.4 = (bf16[8,320,256]{2,1,0:T(8,128)(2,1)}, bf16[8,320,256]{2,1,0:T(8,128)(2,1)}, bf16[8,320,256]{2,1,0:T(8,128)(2,1)}, f32[8,2,1024]{2,1,0:T(2,128)...) custom-call(s32[10]{0:T(128)} %stack.118.where_ref, s32[8,8,1024]{2,1,0:T(8,128)} %copy.159.refs_0_.refs_1_, ...), custom_call_target="tpu_custom_call" | custom-call | flops 214748364800 | bytes 905969664 | tf_op jit(solution)/shard_map/expert_slot/pallas_call | solution.py:419
  320.6 15.0 %collective-permute-done.27.refs_5_ = bf16[1024,512]{1,0:T(8,128)(2,1)} collective-permute-done((bf16[1024,512]{1,0:T(8,128)(2,1)}, bf16[1024,512]{1,0:T(8,128)(2,1)}, u32[]{:S(2)}, u32[]{:S(2)}) %collective-permute-start.27) | collective-permute-done | bytes 1048608 | tf_op jit(solution)/shard_map/ppermute | solution.py:85
  356.3 14.4 %place_rows.6 = (bf16[1,1024,512]{2,1,0:T(8,128)(2,1)}, bf16[1,1024,512]{2,1,0:T(8,128)(2,1)}, bf16[1,1024,512]{2,1,0:T(8,128)(2,1)}, bf16[1,1024,512]{2,1,0:T(8,128)(2,1)}) custom-call(s32[2]{0:T(128)} %bitcast.206, s32[8,1024,8]{2,1,0:T(8,128)} %bitcast.153, s32[8,1024,8]{2,1,0:T(8,128)} %bitcast.154, ...), custom_call_target="tpu_custom_call" | custom-call | flops 85899345920 | bytes 234881024 | tf_op jit(solution)/shard_map/place_rows/pallas_call | solution.py:518
  378.2 17.8 %collective-permute-done.42 = bf16[1024,512]{1,0:T(8,128)(2,1)S(1)} collective-permute-done((bf16[1024,512]{1,0:T(8,128)(2,1)}, bf16[1024,512]{1,0:T(8,128)(2,1)S(1)}, u32[]{:S(2)}, u32[]{:S(2)}) %collective-permute-start.42) | collective-permute-done | bytes 1048608 | tf_op jit(solution)/shard_map/ppermute | solution.py:85
  402.9 27.8 %expert_slot.5 = (bf16[8,320,256]{2,1,0:T(8,128)(2,1)}, bf16[8,320,256]{2,1,0:T(8,128)(2,1)}, bf16[8,320,256]{2,1,0:T(8,128)(2,1)}, f32[8,2,1024]{2,1,0:T(2,128)...) custom-call(s32[10]{0:T(128)} %stack.127.where_ref, s32[8,8,1024]{2,1,0:T(8,128)} %copy.159.refs_0_.refs_1_, ...), custom_call_target="tpu_custom_call" | custom-call | flops 214748364800 | bytes 905969664 | tf_op jit(solution)/shard_map/expert_slot/pallas_call | solution.py:419
  430.7 16.0 %collective-permute-done.46.refs_4_ = bf16[1024,512]{1,0:T(8,128)(2,1)} collective-permute-done((bf16[1024,512]{1,0:T(8,128)(2,1)}, bf16[1024,512]{1,0:T(8,128)(2,1)}, u32[]{:S(2)}, u32[]{:S(2)}) %collective-permute-start.46) | collective-permute-done | bytes 1048608 | tf_op jit(solution)/shard_map/ppermute | solution.py:85
  448.8 18.6 %collective-permute-done.35.refs_5_ = bf16[1024,512]{1,0:T(8,128)(2,1)} collective-permute-done((bf16[1024,512]{1,0:T(8,128)(2,1)}, bf16[1024,512]{1,0:T(8,128)(2,1)}, u32[]{:S(2)}, u32[]{:S(2)}) %collective-permute-start.35) | collective-permute-done | bytes 1048608 | tf_op jit(solution)/shard_map/ppermute | solution.py:85
  506.5 27.8 %expert_slot.6 = (bf16[8,320,256]{2,1,0:T(8,128)(2,1)}, bf16[8,320,256]{2,1,0:T(8,128)(2,1)}, bf16[8,320,256]{2,1,0:T(8,128)(2,1)}, f32[8,2,1024]{2,1,0:T(2,128)...) custom-call(s32[10]{0:T(128)} %stack.124.where_ref, s32[8,8,1024]{2,1,0:T(8,128)} %copy.159.refs_0_.refs_1_, ...), custom_call_target="tpu_custom_call" | custom-call | flops 214748364800 | bytes 905969664 | tf_op jit(solution)/shard_map/expert_slot/pallas_call | solution.py:419
  559.7 28.2 %expert_slot.7 = (bf16[8,320,256]{2,1,0:T(8,128)(2,1)}, bf16[8,320,256]{2,1,0:T(8,128)(2,1)}, bf16[8,320,256]{2,1,0:T(8,128)(2,1)}, f32[8,2,1024]{2,1,0:T(2,128)...) custom-call(s32[10]{0:T(128)} %stack.121.where_ref, s32[8,8,1024]{2,1,0:T(8,128)} %copy.159.refs_0_.refs_1_, ...), custom_call_target="tpu_custom_call" | custom-call | flops 214748364800 | bytes 905969664 | tf_op jit(solution)/shard_map/expert_slot/pallas_call | solution.py:419
  606.9 15.8 %down_slots.2 = (bf16[4,2,1280,512]{3,2,1,0:T(8,128)(2,1)}, bf16[4,2,1280,512]{3,2,1,0:T(8,128)(2,1)}) custom-call(s32[10]{0:T(128)} %stack.118.where_ref, bf16[8,320,256]{2,1,0:T(8,128)(2,1)} %get-tuple-element.147.refs_0_.refs_8_, bf16[8,320,256]{2,1,0:T(8,128)(2,1)} %get-tuple-element.175.refs_1_.refs_9_, bf16[8,256,2048]{2,1,0:T(8,128)(2,1)} %refs_2_.3), custom_call_target="tpu_custom_call" | custom-call | flops 85899345920 | bytes 469762048 | tf_op jit(solution)/shard_map/down_slots/pallas_call | solution.py:459
  622.9 28.7 %collective-permute-done.56 = bf16[1024,512]{1,0:T(8,128)(2,1)S(1)} collective-permute-done((bf16[1024,512]{1,0:T(8,128)(2,1)}, bf16[1024,512]{1,0:T(8,128)(2,1)S(1)}, u32[]{:S(2)}, u32[]{:S(2)}) %collective-permute-start.56) | collective-permute-done | bytes 1048608 | tf_op jit(solution)/shard_map/ppermute | solution.py:85
  653.0 14.0 %place_rows.9 = (bf16[1,1024,512]{2,1,0:T(8,128)(2,1)}, bf16[1,1024,512]{2,1,0:T(8,128)(2,1)}, bf16[1,1024,512]{2,1,0:T(8,128)(2,1)}, bf16[1,1024,512]{2,1,0:T(8,128)(2,1)}) custom-call(s32[2]{0:T(128)} %bitcast.211, s32[8,1024,8]{2,1,0:T(8,128)} %bitcast.159, s32[8,1024,8]{2,1,0:T(8,128)} %bitcast.160, ...), custom_call_target="tpu_custom_call" | custom-call | flops 85899345920 | bytes 234881024 | tf_op jit(solution)/shard_map/place_rows/pallas_call | solution.py:518
  706.3 15.7 %down_slots.3 = (bf16[4,2,1280,512]{3,2,1,0:T(8,128)(2,1)}, bf16[4,2,1280,512]{3,2,1,0:T(8,128)(2,1)}) custom-call(s32[10]{0:T(128)} %stack.118.where_ref, bf16[8,320,256]{2,1,0:T(8,128)(2,1)} %get-tuple-element.155.refs_0_.refs_10_, bf16[8,320,256]{2,1,0:T(8,128)(2,1)} %get-tuple-element.164.refs_1_.refs_11_, bf16[8,256,2048]{2,1,0:T(8,128)(2,1)} %refs_2_.3), custom_call_target="tpu_custom_call" | custom-call | flops 85899345920 | bytes 469762048 | tf_op jit(solution)/shard_map/down_slots/pallas_call | solution.py:459
  732.4 25.5 %place_rows.10 = (bf16[2,1024,512]{2,1,0:T(8,128)(2,1)}, bf16[2,1024,512]{2,1,0:T(8,128)(2,1)}, bf16[2,1024,512]{2,1,0:T(8,128)(2,1)}, bf16[2,1024,512]{2,1,0:T(8,128)(2,1)}) custom-call(s32[4]{0:T(128)} %pad_add_fusion.3.where_ref, s32[8,1024,8]{2,1,0:T(8,128)} %bitcast.161, s32[8,1024,8]{2,1,0:T(8,128)} %bitcast.162, s32[8,1024,8]{2,1,0:T(8,128)} %bitcast.163, ...), custom_call_target="tpu_custom_call" | custom-call | flops 171798691840 | bytes 469762048 | tf_op jit(solution)/shard_map/place_rows/pallas_call | solution.py:518
  758.9 25.3 %place_rows.11 = (bf16[2,1024,512]{2,1,0:T(8,128)(2,1)}, bf16[2,1024,512]{2,1,0:T(8,128)(2,1)}, bf16[2,1024,512]{2,1,0:T(8,128)(2,1)}, bf16[2,1024,512]{2,1,0:T(8,128)(2,1)}) custom-call(s32[4]{0:T(128)} %pad_add_fusion.4.where_ref, s32[8,1024,8]{2,1,0:T(8,128)} %bitcast.165, s32[8,1024,8]{2,1,0:T(8,128)} %bitcast.166, s32[8,1024,8]{2,1,0:T(8,128)} %bitcast.167, ...), custom_call_target="tpu_custom_call" | custom-call | flops 171798691840 | bytes 469762048 | tf_op jit(solution)/shard_map/place_rows/pallas_call | solution.py:518
  785.1 42.9 %weight_grads.1 = (f32[8,2048,256]{2,1,0:T(8,128)}, f32[8,2048,256]{2,1,0:T(8,128)}) custom-call(s32[10]{0:T(128)} %stack.118.where_ref, bf16[2,2,1280,512]{3,2,1,0:T(8,128)(2,1)} %pick_rows.9.refs_4_.refs_0_, bf16[2,2,1280,512]{3,2,1,0:T(8,128)(2,1)} %collective-permute-done.20.refs_5_.refs_1_, bf16[2,2,1280,512]{3,2,1,0:T(8,128)(2,1)} %pick_rows.15.refs_4_.refs_2_, ...), custom_call_target="tpu_custom_call" | custom-call | flops 160000000000 | bytes 16000000 | tf_op jit(solution)/shard_map/weight_grads/pallas_call | solution.py:575
  843.0 27.5 %weight_down_grads.1 = f32[8,256,2048]{2,1,0:T(8,128)} custom-call(s32[10]{0:T(128)} %stack.118.where_ref, bf16[2,2,1280,512]{3,2,1,0:T(8,128)(2,1)} %pick_rows.8.refs_6_.refs_0_, bf16[2,2,1280,512]{3,2,1,0:T(8,128)(2,1)} %collective-permute-done.21.refs_7_.refs_1_, bf16[2,2,1280,512]{3,2,1,0:T(8,128)(2,1)} %pick_rows.14.refs_6_.refs_2_, ...), custom_call_target="tpu_custom_call" | custom-call | flops 160000000000 | bytes 16000000 | tf_op jit(solution)/shard_map/weight_down_grads/pallas_call | solution.py:575
  872.5 14.1 %collective-permute-done.60 = bf16[2,1024,512]{2,1,0:T(8,128)(2,1)} collective-permute-done((bf16[2,1024,512]{2,1,0:T(8,128)(2,1)}, bf16[2,1024,512]{2,1,0:T(8,128)(2,1)}, u32[]{:S(2)}, u32[]{:S(2)}) %collective-permute-start.60) | collective-permute-done | bytes 2097184 | tf_op jit(solution)/shard_map/ppermute | solution.py:85
  905.1 16.3 %attend_back.1 = (bf16[1024,512]{1,0:T(8,128)(2,1)}, bf16[1024,512]{1,0:T(8,128)(2,1)}, bf16[1024,512]{1,0:T(8,128)(2,1)}, f32[1,1,512]{2,1,0:T(1,128)}, f32[1,1,512]{2,1,0:T(1,128)}) custom-call(s32[4]{0:T(128)} %add_bitcast_fusion.pieces_ref, bf16[1024,512]{1,0:T(8,128)(2,1)} %get-tuple-element.136.q_ref, bf16[1024,512]{1,0:T(8,128)(2,1)} %get-tuple-element.137.k_ref, ...), custom_call_target="tpu_custom_call" | custom-call | flops 85899345920 | bytes 184549376 | tf_op jit(solution)/shard_map/attend_back/pallas_call | solution.py:799
  935.1 22.7 %collective-permute-done.94 = bf16[1024,512]{1,0:T(8,128)(2,1)} collective-permute-done((bf16[1024,512]{1,0:T(8,128)(2,1)}, bf16[1024,512]{1,0:T(8,128)(2,1)}, u32[]{:S(2)}, u32[]{:S(2)}) %collective-permute-start.94) | collective-permute-done | bytes 1048608 | tf_op jit(solution)/shard_map/ppermute | solution.py:85
  963.2 17.0 %collective-permute-done.100 = bf16[1024,512]{1,0:T(8,128)(2,1)S(1)} collective-permute-done((bf16[1024,512]{1,0:T(8,128)(2,1)S(1)}, bf16[1024,512]{1,0:T(8,128)(2,1)S(1)}, u32[]{:S(2)}, u32[]{:S(2)}) %collective-permute-start.100) | collective-permute-done | bytes 1048608 | tf_op jit(solution)/shard_map/ppermute | solution.py:85
  995.0 16.5 %collective-permute-done.96 = bf16[256,512]{1,0:T(8,128)(2,1)S(1)} collective-permute-done((bf16[256,512]{1,0:T(8,128)(2,1)S(1)}, bf16[256,512]{1,0:T(8,128)(2,1)S(1)}, u32[]{:S(2)}, u32[]{:S(2)}) %collective-permute-start.96) | collective-permute-done | bytes 262176 | tf_op jit(solution)/shard_map/ppermute | solution.py:85
  1062.6 20.4 %collective-permute-done.88 = bf16[256,1024]{1,0:T(8,128)(2,1)S(1)} collective-permute-done((bf16[256,1024]{1,0:T(8,128)(2,1)S(1)}, bf16[256,1024]{1,0:T(8,128)(2,1)S(1)}, u32[]{:S(2)}, u32[]{:S(2)}) %collective-permute-start.88) | collective-permute-done | bytes 524320 | tf_op jit(solution)/shard_map/ppermute | solution.py:85
  1091.0 21.0 %collective-permute-done.85 = f32[69,512]{1,0:T(8,128)S(1)} collective-permute-done((f32[69,512]{1,0:T(8,128)S(1)}, f32[69,512]{1,0:T(8,128)S(1)}, u32[]{:S(2)}, u32[]{:S(2)}) %collective-permute-start.85) | collective-permute-done | bytes 141344 | tf_op jit(solution)/shard_map/ppermute | solution.py:85
  1132.6 49.2 %collective-permute-done.106 = bf16[512,1024]{1,0:T(8,128)(2,1)S(1)} collective-permute-done((bf16[512,1024]{1,0:T(8,128)(2,1)S(1)}, bf16[512,1024]{1,0:T(8,128)(2,1)S(1)}, u32[]{:S(2)}, u32[]{:S(2)}) %collective-permute-start.106) | collective-permute-done | bytes 1048608 | tf_op jit(solution)/shard_map/ppermute | solution.py:85
  1186.9 16.3 %collective-permute-done.90 = bf16[2,1024,512]{2,1,0:T(8,128)(2,1)S(1)} collective-permute-done((bf16[2,1024,512]{2,1,0:T(8,128)(2,1)S(1)}, bf16[2,1024,512]{2,1,0:T(8,128)(2,1)S(1)}, u32[]{:S(2)}, u32[]{:S(2)}) %collective-permute-start.90) | collective-permute-done | bytes 2097184 | tf_op jit(solution)/shard_map/ppermute | solution.py:85
  1214.1 18.8 %collective-permute-done.91 = bf16[1024,512]{1,0:T(8,128)(2,1)S(1)} collective-permute-done((bf16[1024,512]{1,0:T(8,128)(2,1)S(1)}, bf16[1024,512]{1,0:T(8,128)(2,1)S(1)}, u32[]{:S(2)}, u32[]{:S(2)}) %collective-permute-start.91) | collective-permute-done | bytes 1048608 | tf_op jit(solution)/shard_map/ppermute | solution.py:85
  (545 shorter events, 527.6 us)
Async XLA Ops:
  147.7 143.9 %all-to-all-start = ((f32[8,8,1024]{2,1,0:T(8,128)}), f32[8,8,1024]{2,1,0:T(8,128)}, u32[]{:S(2)}, u32[]{:S(2)}) async-start(f32[8,8,1024]{2,1,0:T(8,128)} %fusion.82), calls=%async_computation | async-start | bytes 524288 | tf_op jit(solution)/shard_map/all_to_all | solution.py:937
  159.2 58.5 %collective-permute-start.17 = (bf16[1024,512]{1,0:T(8,128)(2,1)S(1)}, bf16[1024,512]{1,0:T(8,128)(2,1)S(1)}, u32[]{:S(2)}, u32[]{:S(2)}) collective-permute-start(bf16[1024,512]{1,0:T(8,128)(2,1)S(1)} %collective-permute-done.15.refs_3_), channel_id=1, source_target_pairs={{0,4},{1,5},{2,6},{3,7},{4,0},{5,1},{6,2},{7,3},{8,12},{9,13},{10,... | collective-permute-start | bytes 3145736 | tf_op jit(solution)/shard_map/ppermute | solution.py:85
  189.3 84.6 %collective-permute-start.23 = (bf16[1024,512]{1,0:T(8,128)(2,1)}, bf16[1024,512]{1,0:T(8,128)(2,1)}, u32[]{:S(2)}, u32[]{:S(2)}) collective-permute-start(bf16[1024,512]{1,0:T(8,128)(2,1)} %collective-permute-done.13.refs_2_), channel_id=1, source_target_pairs={{0,2},{1,3},{2,0},{3,1},{4,6},{5,7},{6,4},{7,5},{8,10},{9,11},{10,... | collective-permute-start | bytes 3145736 | tf_op jit(solution)/shard_map/ppermute | solution.py:85
  190.8 84.5 %collective-permute-start.19 = (bf16[1024,512]{1,0:T(8,128)(2,1)}, bf16[1024,512]{1,0:T(8,128)(2,1)}, u32[]{:S(2)}, u32[]{:S(2)}) collective-permute-start(bf16[1024,512]{1,0:T(8,128)(2,1)} %collective-permute-done.13.refs_2_), channel_id=1, source_target_pairs={{0,4},{1,5},{2,6},{3,7},{4,0},{5,1},{6,2},{7,3},{8,12},{9,13},{10,... | collective-permute-start | bytes 3145736 | tf_op jit(solution)/shard_map/ppermute | solution.py:85
  194.7 69.0 %collective-permute-start.18 = (bf16[1024,512]{1,0:T(8,128)(2,1)}, bf16[1024,512]{1,0:T(8,128)(2,1)}, u32[]{:S(2)}, u32[]{:S(2)}) collective-permute-start(bf16[1024,512]{1,0:T(8,128)(2,1)} %collective-permute-done.12.refs_4_), channel_id=1, source_target_pairs={{0,2},{1,3},{2,0},{3,1},{4,6},{5,7},{6,4},{7,5},{8,10},{9,11},{10,... | collective-permute-start | bytes 3145736 | tf_op jit(solution)/shard_map/ppermute | solution.py:85
  232.2 57.8 %collective-permute-start.21 = (bf16[2,2,1280,512]{3,2,1,0:T(8,128)(2,1)}, bf16[2,2,1280,512]{3,2,1,0:T(8,128)(2,1)}, u32[]{:S(2)}, u32[]{:S(2)}) collective-permute-start(bf16[2,2,1280,512]{3,2,1,0:T(8,128)(2,1)} %pick_rows.8.refs_6_.refs_0_), channel_id=1, source_target_pairs={{0,1},{1,0},{2,3},{3,2},{4,5},{5,4},{6,7},{7,6},{8,9},{9,8},{10,11... | collective-permute-start | bytes 15728648 | tf_op jit(solution)/shard_map/ppermute | solution.py:85
  273.8 102.8 %collective-permute-start.39 = (bf16[1024,512]{1,0:T(8,128)(2,1)}, bf16[1024,512]{1,0:T(8,128)(2,1)}, u32[]{:S(2)}, u32[]{:S(2)}) collective-permute-start(bf16[1024,512]{1,0:T(8,128)(2,1)} %collective-permute-done.37.refs_2_), channel_id=1, source_target_pairs={{0,4},{1,5},{2,6},{3,7},{4,0},{5,1},{6,2},{7,3},{8,12},{9,13},{10,... | collective-permute-start | bytes 3145736 | tf_op jit(solution)/shard_map/ppermute | solution.py:85
  275.3 70.3 %collective-permute-start.29 = (bf16[1024,512]{1,0:T(8,128)(2,1)}, bf16[1024,512]{1,0:T(8,128)(2,1)}, u32[]{:S(2)}, u32[]{:S(2)}) collective-permute-start(bf16[1024,512]{1,0:T(8,128)(2,1)} %collective-permute-done.23.refs_3_), channel_id=1, source_target_pairs={{0,4},{1,5},{2,6},{3,7},{4,0},{5,1},{6,2},{7,3},{8,12},{9,13},{10,... | collective-permute-start | bytes 3145736 | tf_op jit(solution)/shard_map/ppermute | solution.py:85
  319.4 55.1 %collective-permute-start.32 = (bf16[1024,512]{1,0:T(8,128)(2,1)}, bf16[1024,512]{1,0:T(8,128)(2,1)}, u32[]{:S(2)}, u32[]{:S(2)}) collective-permute-start(bf16[1024,512]{1,0:T(8,128)(2,1)} %multiply_convert_fusion.2.refs_2_), channel_id=1, source_target_pairs={{0,24},{1,25},{2,26},{3,27},{4,28},{5,29},{6,30},{7,31},{8,16},{9,... | collective-permute-start | bytes 3145736 | tf_op jit(solution)/shard_map/ppermute | solution.py:85
  376.6 103.2 %collective-permute-start.38 = (bf16[1024,512]{1,0:T(8,128)(2,1)}, bf16[1024,512]{1,0:T(8,128)(2,1)}, u32[]{:S(2)}, u32[]{:S(2)}) collective-permute-start(bf16[1024,512]{1,0:T(8,128)(2,1)} %collective-permute-done.37.refs_2_), channel_id=1, source_target_pairs={{0,2},{1,3},{2,0},{3,1},{4,6},{5,7},{6,4},{7,5},{8,10},{9,11},{10,... | collective-permute-start | bytes 3145736 | tf_op jit(solution)/shard_map/ppermute | solution.py:85
  396.0 84.4 %collective-permute-start.40 = (bf16[1024,512]{1,0:T(8,128)(2,1)}, bf16[1024,512]{1,0:T(8,128)(2,1)}, u32[]{:S(2)}, u32[]{:S(2)}) collective-permute-start(bf16[1024,512]{1,0:T(8,128)(2,1)} %collective-permute-done.39.refs_4_), channel_id=1, source_target_pairs={{0,2},{1,3},{2,0},{3,1},{4,6},{5,7},{6,4},{7,5},{8,10},{9,11},{10,... | collective-permute-start | bytes 3145736 | tf_op jit(solution)/shard_map/ppermute | solution.py:85
  402.4 65.0 %collective-permute-start.35 = (bf16[1024,512]{1,0:T(8,128)(2,1)}, bf16[1024,512]{1,0:T(8,128)(2,1)}, u32[]{:S(2)}, u32[]{:S(2)}) collective-permute-start(bf16[1024,512]{1,0:T(8,128)(2,1)} %collective-permute-done.33.refs_3_), channel_id=1, source_target_pairs={{0,4},{1,5},{2,6},{3,7},{4,0},{5,1},{6,2},{7,3},{8,12},{9,13},{10,... | collective-permute-start | bytes 3145736 | tf_op jit(solution)/shard_map/ppermute | solution.py:85
  446.8 87.6 %collective-permute-start.45 = (bf16[1024,512]{1,0:T(8,128)(2,1)}, bf16[1024,512]{1,0:T(8,128)(2,1)}, u32[]{:S(2)}, u32[]{:S(2)}) collective-permute-start(bf16[1024,512]{1,0:T(8,128)(2,1)} %collective-permute-done.44.refs_2_), channel_id=1, source_target_pairs={{0,2},{1,3},{2,0},{3,1},{4,6},{5,7},{6,4},{7,5},{8,10},{9,11},{10,... | collective-permute-start | bytes 3145736 | tf_op jit(solution)/shard_map/ppermute | solution.py:85
  448.2 86.3 %collective-permute-start.47 = (bf16[1024,512]{1,0:T(8,128)(2,1)}, bf16[1024,512]{1,0:T(8,128)(2,1)}, u32[]{:S(2)}, u32[]{:S(2)}) collective-permute-start(bf16[1024,512]{1,0:T(8,128)(2,1)} %collective-permute-done.46.refs_4_), channel_id=1, source_target_pairs={{0,2},{1,3},{2,0},{3,1},{4,6},{5,7},{6,4},{7,5},{8,10},{9,11},{10,... | collective-permute-start | bytes 3145736 | tf_op jit(solution)/shard_map/ppermute | solution.py:85
  478.3 66.8 %collective-permute-start.48 = (bf16[1024,512]{1,0:T(8,128)(2,1)}, bf16[1024,512]{1,0:T(8,128)(2,1)}, u32[]{:S(2)}, u32[]{:S(2)}) collective-permute-start(bf16[1024,512]{1,0:T(8,128)(2,1)} %bitcast.28), channel_id=1, source_target_pairs={{0,4},{1,5},{2,6},{3,7},{4,0},{5,1},{6,2},{7,3},{8,12},{9,13},{10,... | collective-permute-start | bytes 3145736 | tf_op jit(solution)/shard_map/ppermute | solution.py:85
  479.8 65.3 %collective-permute-start.49 = (bf16[1024,512]{1,0:T(8,128)(2,1)}, bf16[1024,512]{1,0:T(8,128)(2,1)}, u32[]{:S(2)}, u32[]{:S(2)}) collective-permute-start(bf16[1024,512]{1,0:T(8,128)(2,1)} %fusion.37), channel_id=1, source_target_pairs={{0,2},{1,3},{2,0},{3,1},{4,6},{5,7},{6,4},{7,5},{8,10},{9,11},{10,... | collective-permute-start | bytes 3145736 | tf_op jit(solution)/shard_map/ppermute | solution.py:85
  600.3 66.7 %collective-permute-start.55 = (bf16[1024,512]{1,0:T(8,128)(2,1)}, bf16[1024,512]{1,0:T(8,128)(2,1)}, u32[]{:S(2)}, u32[]{:S(2)}) collective-permute-start(bf16[1024,512]{1,0:T(8,128)(2,1)} %bitcast.32), channel_id=1, source_target_pairs={{0,2},{1,3},{2,0},{3,1},{4,6},{5,7},{6,4},{7,5},{8,10},{9,11},{10,... | collective-permute-start | bytes 3145736 | tf_op jit(solution)/shard_map/ppermute | solution.py:85
  604.3 64.2 %collective-permute-start.54 = (bf16[1024,512]{1,0:T(8,128)(2,1)}, bf16[1024,512]{1,0:T(8,128)(2,1)}, u32[]{:S(2)}, u32[]{:S(2)}) collective-permute-start(bf16[1024,512]{1,0:T(8,128)(2,1)} %fusion.36), channel_id=1, source_target_pairs={{0,4},{1,5},{2,6},{3,7},{4,0},{5,1},{6,2},{7,3},{8,12},{9,13},{10,... | collective-permute-start | bytes 3145736 | tf_op jit(solution)/shard_map/ppermute | solution.py:85
  622.6 109.2 %collective-permute-start.58 = (bf16[4,2,1280,512]{3,2,1,0:T(8,128)(2,1)}, bf16[4,2,1280,512]{3,2,1,0:T(8,128)(2,1)}, u32[]{:S(2)}, u32[]{:S(2)}) collective-permute-start(bf16[4,2,1280,512]{3,2,1,0:T(8,128)(2,1)} %get-tuple-element.189), channel_id=1, source_target_pairs={{0,1},{1,0},{2,3},{3,2},{4,5},{5,4},{6,7},{7,6},{8,9},{9,8},{10,11... | collective-permute-start | bytes 31457288 | tf_op jit(solution)/shard_map/ppermute | solution.py:85
  684.2 143.9 %collective-permute-start.67 = (bf16[1024,512]{1,0:T(8,128)(2,1)}, bf16[1024,512]{1,0:T(8,128)(2,1)}, u32[]{:S(2)}, u32[]{:S(2)}) collective-permute-start(bf16[1024,512]{1,0:T(8,128)(2,1)} %fusion.30), channel_id=1, source_target_pairs={{0,16},{1,17},{2,18},{3,19},{4,20},{5,21},{6,22},{7,23},{8,24},{9,... | collective-permute-start | bytes 3145736 | tf_op jit(solution)/shard_map/ppermute | solution.py:85
  690.5 137.6 %collective-permute-start.68 = (bf16[1024,512]{1,0:T(8,128)(2,1)}, bf16[1024,512]{1,0:T(8,128)(2,1)}, u32[]{:S(2)}, u32[]{:S(2)}) collective-permute-start(bf16[1024,512]{1,0:T(8,128)(2,1)} %fusion.28), channel_id=1, source_target_pairs={{0,24},{1,25},{2,26},{3,27},{4,28},{5,29},{6,30},{7,31},{8,16},{9,... | collective-permute-start | bytes 3145736 | tf_op jit(solution)/shard_map/ppermute | solution.py:85
  729.8 98.3 %collective-permute-start.66 = (bf16[1024,512]{1,0:T(8,128)(2,1)}, bf16[1024,512]{1,0:T(8,128)(2,1)}, u32[]{:S(2)}, u32[]{:S(2)}) collective-permute-start(bf16[1024,512]{1,0:T(8,128)(2,1)} %fusion.32), channel_id=1, source_target_pairs={{0,8},{1,9},{2,10},{3,11},{4,12},{5,13},{6,14},{7,15},{8,0},{9,1},... | collective-permute-start | bytes 3145736 | tf_op jit(solution)/shard_map/ppermute | solution.py:85
  757.9 76.9 %collective-permute-start.59 = (bf16[2,1024,512]{2,1,0:T(8,128)(2,1)}, bf16[2,1024,512]{2,1,0:T(8,128)(2,1)}, u32[]{:S(2)}, u32[]{:S(2)}) collective-permute-start(bf16[2,1024,512]{2,1,0:T(8,128)(2,1)} %get-tuple-element.193), channel_id=1, source_target_pairs={{0,2},{1,3},{2,0},{3,1},{4,6},{5,7},{6,4},{7,5},{8,10},{9,11},{10,... | collective-permute-start | bytes 6291464 | tf_op jit(solution)/shard_map/ppermute | solution.py:85
  784.1 58.4 %collective-permute-start.73 = (bf16[2,1024,512]{2,1,0:T(8,128)(2,1)}, bf16[2,1024,512]{2,1,0:T(8,128)(2,1)}, u32[]{:S(2)}, u32[]{:S(2)}) collective-permute-start(bf16[2,1024,512]{2,1,0:T(8,128)(2,1)} %get-tuple-element.223), channel_id=1, source_target_pairs={{0,4},{1,5},{2,6},{3,7},{4,0},{5,1},{6,2},{7,3},{8,12},{9,13},{10,... | collective-permute-start | bytes 6291464 | tf_op jit(solution)/shard_map/ppermute | solution.py:85
  886.5 74.7 %collective-permute-start.76 = (bf16[2,1024,512]{2,1,0:T(8,128)(2,1)}, bf16[2,1024,512]{2,1,0:T(8,128)(2,1)}, u32[]{:S(2)}, u32[]{:S(2)}) collective-permute-start(bf16[2,1024,512]{2,1,0:T(8,128)(2,1)} %get-tuple-element.229), channel_id=1, source_target_pairs={{0,4},{1,5},{2,6},{3,7},{4,0},{5,1},{6,2},{7,3},{8,12},{9,13},{10,... | collective-permute-start | bytes 6291464 | tf_op jit(solution)/shard_map/ppermute | solution.py:85
  891.8 69.5 %collective-permute-start.75 = (bf16[2,1024,512]{2,1,0:T(8,128)(2,1)}, bf16[2,1024,512]{2,1,0:T(8,128)(2,1)}, u32[]{:S(2)}, u32[]{:S(2)}) collective-permute-start(bf16[2,1024,512]{2,1,0:T(8,128)(2,1)} %get-tuple-element.227), channel_id=1, source_target_pairs={{0,2},{1,3},{2,0},{3,1},{4,6},{5,7},{6,4},{7,5},{8,10},{9,11},{10,... | collective-permute-start | bytes 6291464 | tf_op jit(solution)/shard_map/ppermute | solution.py:85
  892.3 91.5 %collective-permute-start.77 = (bf16[2,1024,512]{2,1,0:T(8,128)(2,1)S(1)}, bf16[2,1024,512]{2,1,0:T(8,128)(2,1)}, u32[]{:S(2)}, u32[]{:S(2)}) collective-permute-start(bf16[2,1024,512]{2,1,0:T(8,128)(2,1)S(1)} %add_convert_fusion.2), channel_id=1, source_target_pairs={{0,2},{1,3},{2,0},{3,1},{4,6},{5,7},{6,4},{7,5},{8,10},{9,11},{10,... | collective-permute-start | bytes 6291464 | tf_op jit(solution)/shard_map/ppermute | solution.py:85
  957.9 65.7 %collective-permute-start.86 = (bf16[1024,1024]{1,0:T(8,128)(2,1)S(1)}, bf16[1024,1024]{1,0:T(8,128)(2,1)S(1)}, u32[]{:S(2)}, u32[]{:S(2)}) collective-permute-start(bf16[1024,1024]{1,0:T(8,128)(2,1)S(1)} %slice.213), channel_id=1, source_target_pairs={{0,4},{1,5},{2,6},{3,7},{4,0},{5,1},{6,2},{7,3},{8,12},{9,13},{10,... | collective-permute-start | bytes 6291464 | tf_op jit(solution)/shard_map/ppermute | solution.py:85
  1089.3 145.7 %collective-permute-start.99 = (bf16[1024,512]{1,0:T(8,128)(2,1)S(1)}, bf16[1024,512]{1,0:T(8,128)(2,1)S(1)}, u32[]{:S(2)}, u32[]{:S(2)}) collective-permute-start(bf16[1024,512]{1,0:T(8,128)(2,1)S(1)} %pad_maximum_fusion.3.refs_0_), channel_id=1, source_target_pairs={{0,4},{1,5},{2,6},{3,7},{4,0},{5,1},{6,2},{7,3},{8,12},{9,13},{10,... | collective-permute-start | bytes 3145736 | tf_op jit(solution)/shard_map/ppermute | solution.py:85
  1112.0 91.1 %collective-permute-start.90 = (bf16[2,1024,512]{2,1,0:T(8,128)(2,1)S(1)}, bf16[2,1024,512]{2,1,0:T(8,128)(2,1)S(1)}, u32[]{:S(2)}, u32[]{:S(2)}) collective-permute-start(bf16[2,1024,512]{2,1,0:T(8,128)(2,1)S(1)} %copy-done.22), channel_id=1, source_target_pairs={{0,16},{1,17},{2,18},{3,19},{4,20},{5,21},{6,22},{7,23},{8,24},{9,... | collective-permute-start | bytes 6291464 | tf_op jit(solution)/shard_map/ppermute | solution.py:85
  1116.8 118.1 %collective-permute-start.105 = (bf16[1024,512]{1,0:T(8,128)(2,1)S(1)}, bf16[1024,512]{1,0:T(8,128)(2,1)S(1)}, u32[]{:S(2)}, u32[]{:S(2)}) collective-permute-start(bf16[1024,512]{1,0:T(8,128)(2,1)S(1)} %pad_maximum_fusion.4.refs_2_), channel_id=1, source_target_pairs={{0,4},{1,5},{2,6},{3,7},{4,0},{5,1},{6,2},{7,3},{8,12},{9,13},{10,... | collective-permute-start | bytes 3145736 | tf_op jit(solution)/shard_map/ppermute | solution.py:85
  1119.3 62.4 %collective-permute-start.106 = (bf16[512,1024]{1,0:T(8,128)(2,1)S(1)}, bf16[512,1024]{1,0:T(8,128)(2,1)S(1)}, u32[]{:S(2)}, u32[]{:S(2)}) collective-permute-start(bf16[512,1024]{1,0:T(8,128)(2,1)S(1)} %pad_maximum_fusion.5), channel_id=1, source_target_pairs={{0,8},{1,9},{2,10},{3,11},{4,12},{5,13},{6,14},{7,15},{8,0},{9,1},... | collective-permute-start | bytes 3145736 | tf_op jit(solution)/shard_map/ppermute | solution.py:85
  (171 other events, 3979.4 us)

commit v9 on v8

--- a/solution.py
+++ b/solution.py
@@ -23,7 +23,8 @@
 ODD = (1, 2)
 DUE = {
     "attended": ("cx0", "cy0"),
-    "normed": ("cz2", "cd0"),
+    "branch": ("cz2",),
+    "normed": ("cd0",),
     "row0": ("cx2", "cz3", "cy2"),
     "exp0": ("cx3",),
     "row2": ("sc2", "cy3"),
@@ -34,12 +35,13 @@
     "place2": ("sr3", "ed0"),
     "exp3": ("sc1",),
     "place3": ("ex0", "ey0", "ed2"),
-    "down1": ("ex2", "ey2", "ed3"),
+    "down0": ("ex2", "ey2"),
+    "place1": ("ed3",),
     "pd0": ("ed1", "sd0"),
-    "weight": ("ex3", "ey3", "ex1", "ey1"),
-    "residual_grad": ("gd0", "gd1"),
-    "back": ("gx0",),
-    "normed_grad": ("gx1", "gy0"),
+    "pd1": ("ex3", "ey3", "ex1", "ey1"),
+    "residual_grad": ("gd0",),
+    "back": ("gd1",),
+    "normed_grad": ("gx0", "gx1", "gy0"),
     "ends": ("qk2",),
 }
 
@@ -909,6 +911,7 @@
     head_top = jnp.max(tops[:, 0, 0].reshape(sequences, heads_here), axis=0)
     attended = after(attended, *due("attended", seen))
     branch = tensor_scatter(partial(matmul, attended), output_pieces, "b", seen, [pos, at])
+    branch = after(branch, *due("branch", seen))
     residual = own_columns(inputs).astype(F32) + branch
     gain_slice = own_columns(moe_gain)
     router_slice = lax.dynamic_slice_in_dim(w_router, column, slice_width, 0)
@@ -992,16 +995,8 @@
         pairs.append(place_rows([turn("pd" + str(k), 2 * k), where[2 * k + 1]], at, *downs[k]))
         last = pairs[k][0][0]
     far = scatter_corners(pairs, seen)
-    grad_gate, grad_up = weight_grads(
-        weight_kernel,
-        turn("weight", 0),
-        rows,
-        gate_grads + up_grads,
-        [w_gate.shape[1:]] * 2,
-        "weight_grads",
-    )
     if is_cube():
-        expert_path = added(*[after(s, grad_gate) for s in sums])
+        expert_path = added(*[after(s, last) for s in sums])
     else:
         expert_path = scatter_all(back)
 
@@ -1099,6 +1094,14 @@
     top_row = jnp.pad(head_top, (0, slice_width - heads_here), constant_values=-3e38)
     small, top_row = expert_total(small, top_row[None])
     head_top = top_row[0, :heads_here]
+    grad_gate, grad_up = weight_grads(
+        weight_kernel,
+        after(where[0], small, *due("ends", seen)),
+        rows,
+        gate_grads + up_grads,
+        [w_gate.shape[1:]] * 2,
+        "weight_grads",
+    )
     mixture = scatter_ends(planes, [small, *due("ends", seen)])
     out = residual + mixture
     sum_moe_gain, sum_query_gain, sum_key_gain = small[E + 1], small[E + 2], small[E + 3]

time: 1270 us -> 1340 us (1.055)
  blocking collectives: 7.5 us -> 48.1 us
  waiting for transfers between devices: 483 us -> 509 us
    all_gather x1, blocking collectives: 7.5 us -> 48.1 us  [per_device(): every = lax.all_gather(small[:E + 1], 'tensor')]
    ppermute x108, waiting for transfers between devices: 483 us -> 509 us  [send(): return lax.ppermute(value, BOTH, flip(dz, dx, dy, dc))]
  transfers between devices with their start and end apart: 110 -> 110, of which waited for: 34 -> 42; matrix products, arithmetic and copies ran while one was open for 12% -> 13% of each run, Pallas kernels for 33% -> 35%
where the time goes in v9:
time: 1340 us; the launch traced here: 1330 us
  waiting for transfers between devices  509 us (38%)
  Pallas kernels  458 us (34%)
  starting transfers between devices  120 us (9%)
  other arithmetic  74.9 us (6%)
  local copies, waits for them, and re-layouts  61.5 us (5%)
  matrix products  53 us (4%)
  blocking collectives  48.1 us (4%)
    ppermute x108, waiting for transfers between devices, send(): return lax.ppermute(value, BOTH, flip(dz, dx, dy, dc))  509 us
    pallas_call x4, Pallas kernels, expert_slot(): pl.pallas_call(partial(expert_kernel, slices), grid_spec=pltpu.PrefetchSc...  111 us
    ppermute x108, starting transfers between devices, send(): return lax.ppermute(value, BOTH, flip(dz, dx, dy, dc))  108 us
    pallas_call x6, Pallas kernels, place_rows(): pl.pallas_call(partial(place_kernel, slices, held, slots), grid_spec=pltp...  107 us
    pallas_call x8, Pallas kernels, pick_rows(): pl.pallas_call(partial(pick_kernel, group, slices), grid_spec=pltpu.Prefe...  81.4 us
    pallas_call x2, Pallas kernels, weight_grads(): pl.pallas_call(partial(kernel, slots, slices), grid_spec=pltpu.PrefetchSc...  70.7 us
    all_gather x1, blocking collectives, per_device(): every = lax.all_gather(small[:E + 1], 'tensor')  48.1 us
    pallas_call x2, Pallas kernels, down_slots(): pl.pallas_call(partial(down_kernel, slices, slots), grid_spec=pltpu.Prefe...  31.6 us
  transfers between devices with their start and end apart: 110, of which 42 were waited for; matrix products, arithmetic and copies ran while one was open for 13% of the time, Pallas kernels for 35%

profile of v9, /device:TPU:10, one launch (start us, length us, event | category | flops | bytes accessed | tf_op | source)
XLA Modules:
  0.0 1327.0 jit_solution(10742753571233322440)
XLA Ops:
  7.5 15.7 %project.1 = (bf16[1024,2048]{1,0:T(8,128)(2,1)}, f32[1024,1]{1,0:T(8,128)}, f32[1024,512]{1,0:T(8,128)}, f32[1024,512]{1,0:T(8,128)}, bf16[1024,512]{1,0:T(8,12...) custom-call(bf16[1024,2048]{1,0:T(8,128)(2,1)} %in_ref.1, f32[1,2048]{1,0:T(1,128)} %bitcast.208, ...), custom_call_target="tpu_custom_call" | custom-call | flops 103079215104 | bytes 352321536 | tf_op jit(solution)/shard_map/project/pallas_call | solution.py:666
  85.3 26.4 %collective-permute-done.8.refs_2_ = bf16[1024,512]{1,0:T(8,128)(2,1)} collective-permute-done((bf16[1024,512]{1,0:T(8,128)(2,1)}, bf16[1024,512]{1,0:T(8,128)(2,1)}, u32[]{:S(2)}, u32[]{:S(2)}) %collective-permute-start.8) | collective-permute-done | bytes 1048608 | tf_op jit(solution)/shard_map/ppermute | solution.py:87
  128.8 14.7 %collective-permute-done.11.refs_5_ = bf16[1024,512]{1,0:T(8,128)(2,1)} collective-permute-done((bf16[1024,512]{1,0:T(8,128)(2,1)}, bf16[1024,512]{1,0:T(8,128)(2,1)}, u32[]{:S(2)}, u32[]{:S(2)}) %collective-permute-start.11) | collective-permute-done | bytes 1048608 | tf_op jit(solution)/shard_map/ppermute | solution.py:87
  166.0 32.4 %collective-permute-done.13.refs_2_ = bf16[1024,512]{1,0:T(8,128)(2,1)} collective-permute-done((bf16[1024,512]{1,0:T(8,128)(2,1)}, bf16[1024,512]{1,0:T(8,128)(2,1)}, u32[]{:S(2)}, u32[]{:S(2)}) %collective-permute-start.13) | collective-permute-done | bytes 1048608 | tf_op jit(solution)/shard_map/ppermute | solution.py:87
  225.4 22.6 %collective-permute-done.17.refs_5_ = bf16[1024,512]{1,0:T(8,128)(2,1)} collective-permute-done((bf16[1024,512]{1,0:T(8,128)(2,1)S(1)}, bf16[1024,512]{1,0:T(8,128)(2,1)}, u32[]{:S(2)}, u32[]{:S(2)}) %collective-permute-start.17) | collective-permute-done | bytes 1048608 | tf_op jit(solution)/shard_map/ppermute | solution.py:87
  272.0 21.0 %collective-permute-done.26.refs_4_ = bf16[1024,512]{1,0:T(8,128)(2,1)} collective-permute-done((bf16[1024,512]{1,0:T(8,128)(2,1)}, bf16[1024,512]{1,0:T(8,128)(2,1)}, u32[]{:S(2)}, u32[]{:S(2)}) %collective-permute-start.26) | collective-permute-done | bytes 1048608 | tf_op jit(solution)/shard_map/ppermute | solution.py:87
  295.0 27.8 %expert_slot.4 = (bf16[8,320,256]{2,1,0:T(8,128)(2,1)}, bf16[8,320,256]{2,1,0:T(8,128)(2,1)}, bf16[8,320,256]{2,1,0:T(8,128)(2,1)}, f32[8,2,1024]{2,1,0:T(2,128)...) custom-call(s32[10]{0:T(128)} %stack.118.where_ref, s32[8,8,1024]{2,1,0:T(8,128)} %copy.154.refs_0_.refs_1_, ...), custom_call_target="tpu_custom_call" | custom-call | flops 214748364800 | bytes 905969664 | tf_op jit(solution)/shard_map/expert_slot/pallas_call | solution.py:421
  327.6 14.2 %collective-permute-done.27.refs_5_ = bf16[1024,512]{1,0:T(8,128)(2,1)} collective-permute-done((bf16[1024,512]{1,0:T(8,128)(2,1)}, bf16[1024,512]{1,0:T(8,128)(2,1)}, u32[]{:S(2)}, u32[]{:S(2)}) %collective-permute-start.27) | collective-permute-done | bytes 1048608 | tf_op jit(solution)/shard_map/ppermute | solution.py:87
  371.3 14.2 %place_rows.6 = (bf16[1,1024,512]{2,1,0:T(8,128)(2,1)}, bf16[1,1024,512]{2,1,0:T(8,128)(2,1)}, bf16[1,1024,512]{2,1,0:T(8,128)(2,1)}, bf16[1,1024,512]{2,1,0:T(8,128)(2,1)}) custom-call(s32[2]{0:T(128)} %bitcast.204, s32[8,1024,8]{2,1,0:T(8,128)} %bitcast.153, s32[8,1024,8]{2,1,0:T(8,128)} %bitcast.154, ...), custom_call_target="tpu_custom_call" | custom-call | flops 85899345920 | bytes 234881024 | tf_op jit(solution)/shard_map/place_rows/pallas_call | solution.py:520
  387.0 21.0 %collective-permute-done.33.refs_3_ = bf16[1024,512]{1,0:T(8,128)(2,1)} collective-permute-done((bf16[1024,512]{1,0:T(8,128)(2,1)}, bf16[1024,512]{1,0:T(8,128)(2,1)}, u32[]{:S(2)}, u32[]{:S(2)}) %collective-permute-start.33) | collective-permute-done | bytes 1048608 | tf_op jit(solution)/shard_map/ppermute | solution.py:87
  410.1 27.8 %expert_slot.5 = (bf16[8,320,256]{2,1,0:T(8,128)(2,1)}, bf16[8,320,256]{2,1,0:T(8,128)(2,1)}, bf16[8,320,256]{2,1,0:T(8,128)(2,1)}, f32[8,2,1024]{2,1,0:T(2,128)...) custom-call(s32[10]{0:T(128)} %stack.127.where_ref, s32[8,8,1024]{2,1,0:T(8,128)} %copy.154.refs_0_.refs_1_, ...), custom_call_target="tpu_custom_call" | custom-call | flops 214748364800 | bytes 905969664 | tf_op jit(solution)/shard_map/expert_slot/pallas_call | solution.py:421
  438.5 18.4 %collective-permute-done.35.refs_5_ = bf16[1024,512]{1,0:T(8,128)(2,1)} collective-permute-done((bf16[1024,512]{1,0:T(8,128)(2,1)}, bf16[1024,512]{1,0:T(8,128)(2,1)}, u32[]{:S(2)}, u32[]{:S(2)}) %collective-permute-start.35) | collective-permute-done | bytes 1048608 | tf_op jit(solution)/shard_map/ppermute | solution.py:87
  478.9 14.1 %place_rows.7 = (bf16[1,1024,512]{2,1,0:T(8,128)(2,1)}, bf16[1,1024,512]{2,1,0:T(8,128)(2,1)}, bf16[1,1024,512]{2,1,0:T(8,128)(2,1)}, bf16[1,1024,512]{2,1,0:T(8,128)(2,1)}) custom-call(s32[2]{0:T(128)} %bitcast.206, s32[8,1024,8]{2,1,0:T(8,128)} %bitcast.155, s32[8,1024,8]{2,1,0:T(8,128)} %bitcast.156, ...), custom_call_target="tpu_custom_call" | custom-call | flops 85899345920 | bytes 234881024 | tf_op jit(solution)/shard_map/place_rows/pallas_call | solution.py:520
  506.1 13.2 collective-permute-done.50
  522.7 27.8 %expert_slot.6 = (bf16[8,320,256]{2,1,0:T(8,128)(2,1)}, bf16[8,320,256]{2,1,0:T(8,128)(2,1)}, bf16[8,320,256]{2,1,0:T(8,128)(2,1)}, f32[8,2,1024]{2,1,0:T(2,128)...) custom-call(s32[10]{0:T(128)} %stack.124.where_ref, s32[8,8,1024]{2,1,0:T(8,128)} %copy.154.refs_0_.refs_1_, ...), custom_call_target="tpu_custom_call" | custom-call | flops 214748364800 | bytes 905969664 | tf_op jit(solution)/shard_map/expert_slot/pallas_call | solution.py:421
  552.0 12.3 collective-permute-done.47.refs_5_
  587.5 14.1 %place_rows.8 = (bf16[1,1024,512]{2,1,0:T(8,128)(2,1)}, bf16[1,1024,512]{2,1,0:T(8,128)(2,1)}, bf16[1,1024,512]{2,1,0:T(8,128)(2,1)}, bf16[1,1024,512]{2,1,0:T(8,128)(2,1)}) custom-call(s32[2]{0:T(128)} %bitcast.210, s32[8,1024,8]{2,1,0:T(8,128)} %bitcast.157, s32[8,1024,8]{2,1,0:T(8,128)} %bitcast.158, ...), custom_call_target="tpu_custom_call" | custom-call | flops 85899345920 | bytes 234881024 | tf_op jit(solution)/shard_map/place_rows/pallas_call | solution.py:520
  601.6 27.9 %expert_slot.7 = (bf16[8,320,256]{2,1,0:T(8,128)(2,1)}, bf16[8,320,256]{2,1,0:T(8,128)(2,1)}, bf16[8,320,256]{2,1,0:T(8,128)(2,1)}, f32[8,2,1024]{2,1,0:T(2,128)...) custom-call(s32[10]{0:T(128)} %stack.121.where_ref, s32[8,8,1024]{2,1,0:T(8,128)} %copy.154.refs_0_.refs_1_, ...), custom_call_target="tpu_custom_call" | custom-call | flops 214748364800 | bytes 905969664 | tf_op jit(solution)/shard_map/expert_slot/pallas_call | solution.py:421
  645.3 15.9 %down_slots.2 = (bf16[4,2,1280,512]{3,2,1,0:T(8,128)(2,1)}, bf16[4,2,1280,512]{3,2,1,0:T(8,128)(2,1)}) custom-call(s32[10]{0:T(128)} %stack.118.where_ref, bf16[8,320,256]{2,1,0:T(8,128)(2,1)} %get-tuple-element.149.refs_0_.refs_8_, bf16[8,320,256]{2,1,0:T(8,128)(2,1)} %get-tuple-element.177.refs_1_.refs_9_, bf16[8,256,2048]{2,1,0:T(8,128)(2,1)} %refs_2_.3), custom_call_target="tpu_custom_call" | custom-call | flops 85899345920 | bytes 469762048 | tf_op jit(solution)/shard_map/down_slots/pallas_call | solution.py:461
  669.0 14.0 %place_rows.9 = (bf16[1,1024,512]{2,1,0:T(8,128)(2,1)}, bf16[1,1024,512]{2,1,0:T(8,128)(2,1)}, bf16[1,1024,512]{2,1,0:T(8,128)(2,1)}, bf16[1,1024,512]{2,1,0:T(8,128)(2,1)}) custom-call(s32[2]{0:T(128)} %bitcast.209, s32[8,1024,8]{2,1,0:T(8,128)} %bitcast.159, s32[8,1024,8]{2,1,0:T(8,128)} %bitcast.160, ...), custom_call_target="tpu_custom_call" | custom-call | flops 85899345920 | bytes 234881024 | tf_op jit(solution)/shard_map/place_rows/pallas_call | solution.py:520
  699.1 15.9 %collective-permute-done.57 = bf16[1024,512]{1,0:T(8,128)(2,1)S(1)} collective-permute-done((bf16[1024,512]{1,0:T(8,128)(2,1)}, bf16[1024,512]{1,0:T(8,128)(2,1)S(1)}, u32[]{:S(2)}, u32[]{:S(2)}) %collective-permute-start.57) | collective-permute-done | bytes 1048608 | tf_op jit(solution)/shard_map/ppermute | solution.py:87
  717.2 15.7 %down_slots.3 = (bf16[4,2,1280,512]{3,2,1,0:T(8,128)(2,1)}, bf16[4,2,1280,512]{3,2,1,0:T(8,128)(2,1)}) custom-call(s32[10]{0:T(128)} %stack.118.where_ref, bf16[8,320,256]{2,1,0:T(8,128)(2,1)} %get-tuple-element.157.refs_0_.refs_10_, bf16[8,320,256]{2,1,0:T(8,128)(2,1)} %get-tuple-element.166.refs_1_.refs_11_, bf16[8,256,2048]{2,1,0:T(8,128)(2,1)} %refs_2_.3), custom_call_target="tpu_custom_call" | custom-call | flops 85899345920 | bytes 469762048 | tf_op jit(solution)/shard_map/down_slots/pallas_call | solution.py:461
  743.6 25.6 %place_rows.10 = (bf16[2,1024,512]{2,1,0:T(8,128)(2,1)}, bf16[2,1024,512]{2,1,0:T(8,128)(2,1)}, bf16[2,1024,512]{2,1,0:T(8,128)(2,1)}, bf16[2,1024,512]{2,1,0:T(8,128)(2,1)}) custom-call(s32[4]{0:T(128)} %pad_add_fusion.3.where_ref, s32[8,1024,8]{2,1,0:T(8,128)} %bitcast.161, s32[8,1024,8]{2,1,0:T(8,128)} %bitcast.162, s32[8,1024,8]{2,1,0:T(8,128)} %bitcast.163, ...), custom_call_target="tpu_custom_call" | custom-call | flops 171798691840 | bytes 469762048 | tf_op jit(solution)/shard_map/place_rows/pallas_call | solution.py:520
  771.3 25.4 %place_rows.11 = (bf16[2,1024,512]{2,1,0:T(8,128)(2,1)}, bf16[2,1024,512]{2,1,0:T(8,128)(2,1)}, bf16[2,1024,512]{2,1,0:T(8,128)(2,1)}, bf16[2,1024,512]{2,1,0:T(8,128)(2,1)}) custom-call(s32[4]{0:T(128)} %pad_add_fusion.4.where_ref, s32[8,1024,8]{2,1,0:T(8,128)} %bitcast.165, s32[8,1024,8]{2,1,0:T(8,128)} %bitcast.166, s32[8,1024,8]{2,1,0:T(8,128)} %bitcast.167, ...), custom_call_target="tpu_custom_call" | custom-call | flops 171798691840 | bytes 469762048 | tf_op jit(solution)/shard_map/place_rows/pallas_call | solution.py:520
  821.4 27.9 %weight_down_grads.1 = f32[8,256,2048]{2,1,0:T(8,128)} custom-call(s32[10]{0:T(128)} %stack.118.where_ref, bf16[2,2,1280,512]{3,2,1,0:T(8,128)(2,1)} %pick_rows.8.refs_6_.refs_0_, bf16[2,2,1280,512]{3,2,1,0:T(8,128)(2,1)} %collective-permute-done.21.refs_7_.refs_1_, bf16[2,2,1280,512]{3,2,1,0:T(8,128)(2,1)} %pick_rows.14.refs_6_.refs_2_, ...), custom_call_target="tpu_custom_call" | custom-call | flops 160000000000 | bytes 16000000 | tf_op jit(solution)/shard_map/weight_down_grads/pallas_call | solution.py:577
  878.9 15.9 %attend_back.1 = (bf16[1024,512]{1,0:T(8,128)(2,1)}, bf16[1024,512]{1,0:T(8,128)(2,1)}, bf16[1024,512]{1,0:T(8,128)(2,1)}, f32[1,1,512]{2,1,0:T(1,128)}, f32[1,1,512]{2,1,0:T(1,128)}) custom-call(s32[4]{0:T(128)} %add_bitcast_fusion.pieces_ref, bf16[1024,512]{1,0:T(8,128)(2,1)} %get-tuple-element.137.q_ref, bf16[1024,512]{1,0:T(8,128)(2,1)} %get-tuple-element.138.k_ref, ...), custom_call_target="tpu_custom_call" | custom-call | flops 85899345920 | bytes 184549376 | tf_op jit(solution)/shard_map/attend_back/pallas_call | solution.py:801
  900.7 77.0 %collective-permute-done.94 = bf16[1024,512]{1,0:T(8,128)(2,1)S(1)} collective-permute-done((bf16[1024,512]{1,0:T(8,128)(2,1)}, bf16[1024,512]{1,0:T(8,128)(2,1)S(1)}, u32[]{:S(2)}, u32[]{:S(2)}) %collective-permute-start.94) | collective-permute-done | bytes 1048608 | tf_op jit(solution)/shard_map/ppermute | solution.py:87
  1056.9 19.8 %collective-permute-done.87 = bf16[512,1024]{1,0:T(8,128)(2,1)S(1)} collective-permute-done((bf16[512,1024]{1,0:T(8,128)(2,1)S(1)}, bf16[512,1024]{1,0:T(8,128)(2,1)S(1)}, u32[]{:S(2)}, u32[]{:S(2)}) %collective-permute-start.87) | collective-permute-done | bytes 1048608 | tf_op jit(solution)/shard_map/ppermute | solution.py:87
  1128.8 14.0 %collective-permute-done.83 = f32[69,512]{1,0:T(8,128)S(1)} collective-permute-done((f32[69,512]{1,0:T(8,128)}, f32[69,512]{1,0:T(8,128)S(1)}, u32[]{:S(2)}, u32[]{:S(2)}) %collective-permute-start.83) | collective-permute-done | bytes 141344 | tf_op jit(solution)/shard_map/ppermute | solution.py:87
  1168.6 42.9 %weight_grads.1 = (f32[8,2048,256]{2,1,0:T(8,128)}, f32[8,2048,256]{2,1,0:T(8,128)}) custom-call(s32[10]{0:T(128)} %stack.118.where_ref, bf16[2,2,1280,512]{3,2,1,0:T(8,128)(2,1)} %pick_rows.9.refs_4_.refs_0_, bf16[2,2,1280,512]{3,2,1,0:T(8,128)(2,1)} %collective-permute-done.20.refs_5_.refs_1_, bf16[2,2,1280,512]{3,2,1,0:T(8,128)(2,1)} %pick_rows.15.refs_4_.refs_2_, ...), custom_call_target="tpu_custom_call" | custom-call | flops 160000000000 | bytes 16000000 | tf_op jit(solution)/shard_map/weight_grads/pallas_call | solution.py:577
  1211.5 48.1 %all-gather.1 = f32[4,65,512]{2,1,0:T(8,128)S(1)} all-gather(f32[1,65,512]{2,1,0:T(8,128)S(1)} %slice_bitcast_fusion.2), channel_id=2, replica_groups=mesh['expert'=8,'tensor'=4] {'tensor'}, dimensions={0}, use_global_device_ids=true | all-gather | bytes 665600 | tf_op jit(solution)/shard_map/all_gather | solution.py:1108
  1274.9 36.5 %collective-permute-done.107.refs_5_ = bf16[1024,1024]{1,0:T(8,128)(2,1)} collective-permute-done((bf16[1024,1024]{1,0:T(8,128)(2,1)S(1)}, bf16[1024,1024]{1,0:T(8,128)(2,1)}, u32[]{:S(2)}, u32[]{:S(2)}) %collective-permute-start.107) | collective-permute-done | bytes 2097184 | tf_op jit(solution)/shard_map/ppermute | solution.py:87
  (529 shorter events, 564.3 us)
Async XLA Ops:
  124.3 74.1 %collective-permute-start.13 = (bf16[1024,512]{1,0:T(8,128)(2,1)}, bf16[1024,512]{1,0:T(8,128)(2,1)}, u32[]{:S(2)}, u32[]{:S(2)}) collective-permute-start(bf16[1024,512]{1,0:T(8,128)(2,1)} %convert_element_type.331.refs_2_), channel_id=1, source_target_pairs={{0,24},{1,25},{2,26},{3,27},{4,28},{5,29},{6,30},{7,31},{8,16},{9,... | collective-permute-start | bytes 3145736 | tf_op jit(solution)/shard_map/ppermute | solution.py:87
  143.5 56.4 %collective-permute-start.15 = (bf16[1024,512]{1,0:T(8,128)(2,1)}, bf16[1024,512]{1,0:T(8,128)(2,1)S(1)}, u32[]{:S(2)}, u32[]{:S(2)}) collective-permute-start(bf16[1024,512]{1,0:T(8,128)(2,1)} %multiply_convert_fusion.2.refs_2_), channel_id=1, source_target_pairs={{0,2},{1,3},{2,0},{3,1},{4,6},{5,7},{6,4},{7,5},{8,10},{9,11},{10,... | collective-permute-start | bytes 3145736 | tf_op jit(solution)/shard_map/ppermute | solution.py:87
  155.9 54.7 %collective-permute-start.14 = (bf16[1024,512]{1,0:T(8,128)(2,1)}, bf16[1024,512]{1,0:T(8,128)(2,1)}, u32[]{:S(2)}, u32[]{:S(2)}) collective-permute-start(bf16[1024,512]{1,0:T(8,128)(2,1)} %collective-permute-done.8.refs_2_), channel_id=1, source_target_pairs={{0,2},{1,3},{2,0},{3,1},{4,6},{5,7},{6,4},{7,5},{8,10},{9,11},{10,... | collective-permute-start | bytes 3145736 | tf_op jit(solution)/shard_map/ppermute | solution.py:87
  156.4 54.3 %collective-permute-start.12 = (bf16[1024,512]{1,0:T(8,128)(2,1)}, bf16[1024,512]{1,0:T(8,128)(2,1)}, u32[]{:S(2)}, u32[]{:S(2)}) collective-permute-start(bf16[1024,512]{1,0:T(8,128)(2,1)} %collective-permute-done.8.refs_2_), channel_id=1, source_target_pairs={{0,4},{1,5},{2,6},{3,7},{4,0},{5,1},{6,2},{7,3},{8,12},{9,13},{10,... | collective-permute-start | bytes 3145736 | tf_op jit(solution)/shard_map/ppermute | solution.py:87
  156.9 62.7 %collective-permute-start.24 = (bf16[1024,512]{1,0:T(8,128)(2,1)}, bf16[1024,512]{1,0:T(8,128)(2,1)}, u32[]{:S(2)}, u32[]{:S(2)}) collective-permute-start(bf16[1024,512]{1,0:T(8,128)(2,1)} %multiply_convert_fusion.2.refs_2_), channel_id=1, source_target_pairs={{0,16},{1,17},{2,18},{3,19},{4,20},{5,21},{6,22},{7,23},{8,24},{9,... | collective-permute-start | bytes 3145736 | tf_op jit(solution)/shard_map/ppermute | solution.py:87
  161.2 133.8 %all-to-all-start = ((f32[8,8,1024]{2,1,0:T(8,128)}), f32[8,8,1024]{2,1,0:T(8,128)}, u32[]{:S(2)}, u32[]{:S(2)}) async-start(f32[8,8,1024]{2,1,0:T(8,128)} %fusion.82), calls=%async_computation | async-start | bytes 524288 | tf_op jit(solution)/shard_map/all_to_all | solution.py:940
  210.6 59.2 %collective-permute-start.37 = (bf16[1024,512]{1,0:T(8,128)(2,1)}, bf16[1024,512]{1,0:T(8,128)(2,1)}, u32[]{:S(2)}, u32[]{:S(2)}) collective-permute-start(bf16[1024,512]{1,0:T(8,128)(2,1)} %convert_element_type.331.refs_2_), channel_id=1, source_target_pairs={{0,8},{1,9},{2,10},{3,11},{4,12},{5,13},{6,14},{7,15},{8,0},{9,1},... | collective-permute-start | bytes 3145736 | tf_op jit(solution)/shard_map/ppermute | solution.py:87
  210.7 59.8 %collective-permute-start.19 = (bf16[1024,512]{1,0:T(8,128)(2,1)}, bf16[1024,512]{1,0:T(8,128)(2,1)}, u32[]{:S(2)}, u32[]{:S(2)}) collective-permute-start(bf16[1024,512]{1,0:T(8,128)(2,1)} %collective-permute-done.13.refs_2_), channel_id=1, source_target_pairs={{0,4},{1,5},{2,6},{3,7},{4,0},{5,1},{6,2},{7,3},{8,12},{9,13},{10,... | collective-permute-start | bytes 3145736 | tf_op jit(solution)/shard_map/ppermute | solution.py:87
  225.4 68.0 %collective-permute-start.21 = (bf16[2,2,1280,512]{3,2,1,0:T(8,128)(2,1)}, bf16[2,2,1280,512]{3,2,1,0:T(8,128)(2,1)}, u32[]{:S(2)}, u32[]{:S(2)}) collective-permute-start(bf16[2,2,1280,512]{3,2,1,0:T(8,128)(2,1)} %pick_rows.8.refs_6_.refs_0_), channel_id=1, source_target_pairs={{0,1},{1,0},{2,3},{3,2},{4,5},{5,4},{6,7},{7,6},{8,9},{9,8},{10,11... | collective-permute-start | bytes 15728648 | tf_op jit(solution)/shard_map/ppermute | solution.py:87
  322.9 144.8 %collective-permute-start.38 = (bf16[1024,512]{1,0:T(8,128)(2,1)}, bf16[1024,512]{1,0:T(8,128)(2,1)}, u32[]{:S(2)}, u32[]{:S(2)}) collective-permute-start(bf16[1024,512]{1,0:T(8,128)(2,1)} %collective-permute-done.37.refs_2_), channel_id=1, source_target_pairs={{0,2},{1,3},{2,0},{3,1},{4,6},{5,7},{6,4},{7,5},{8,10},{9,11},{10,... | collective-permute-start | bytes 3145736 | tf_op jit(solution)/shard_map/ppermute | solution.py:87
  323.4 144.2 %collective-permute-start.40 = (bf16[1024,512]{1,0:T(8,128)(2,1)}, bf16[1024,512]{1,0:T(8,128)(2,1)}, u32[]{:S(2)}, u32[]{:S(2)}) collective-permute-start(bf16[1024,512]{1,0:T(8,128)(2,1)} %collective-permute-done.39.refs_4_), channel_id=1, source_target_pairs={{0,2},{1,3},{2,0},{3,1},{4,6},{5,7},{6,4},{7,5},{8,10},{9,11},{10,... | collective-permute-start | bytes 3145736 | tf_op jit(solution)/shard_map/ppermute | solution.py:87
  408.0 92.2 %collective-permute-start.46 = (bf16[1024,512]{1,0:T(8,128)(2,1)}, bf16[1024,512]{1,0:T(8,128)(2,1)}, u32[]{:S(2)}, u32[]{:S(2)}) collective-permute-start(bf16[1024,512]{1,0:T(8,128)(2,1)} %collective-permute-done.44.refs_2_), channel_id=1, source_target_pairs={{0,4},{1,5},{2,6},{3,7},{4,0},{5,1},{6,2},{7,3},{8,12},{9,13},{10,... | collective-permute-start | bytes 3145736 | tf_op jit(solution)/shard_map/ppermute | solution.py:87
  500.3 64.1 %collective-permute-start.47 = (bf16[1024,512]{1,0:T(8,128)(2,1)}, bf16[1024,512]{1,0:T(8,128)(2,1)}, u32[]{:S(2)}, u32[]{:S(2)}) collective-permute-start(bf16[1024,512]{1,0:T(8,128)(2,1)} %collective-permute-done.46.refs_4_), channel_id=1, source_target_pairs={{0,2},{1,3},{2,0},{3,1},{4,6},{5,7},{6,4},{7,5},{8,10},{9,11},{10,... | collective-permute-start | bytes 3145736 | tf_op jit(solution)/shard_map/ppermute | solution.py:87
  501.4 73.2 %collective-permute-start.48 = (bf16[1024,512]{1,0:T(8,128)(2,1)}, bf16[1024,512]{1,0:T(8,128)(2,1)}, u32[]{:S(2)}, u32[]{:S(2)}) collective-permute-start(bf16[1024,512]{1,0:T(8,128)(2,1)} %bitcast.28), channel_id=1, source_target_pairs={{0,4},{1,5},{2,6},{3,7},{4,0},{5,1},{6,2},{7,3},{8,12},{9,13},{10,... | collective-permute-start | bytes 3145736 | tf_op jit(solution)/shard_map/ppermute | solution.py:87
  519.3 67.5 %collective-permute-start.49 = (bf16[1024,512]{1,0:T(8,128)(2,1)}, bf16[1024,512]{1,0:T(8,128)(2,1)}, u32[]{:S(2)}, u32[]{:S(2)}) collective-permute-start(bf16[1024,512]{1,0:T(8,128)(2,1)} %fusion.37), channel_id=1, source_target_pairs={{0,2},{1,3},{2,0},{3,1},{4,6},{5,7},{6,4},{7,5},{8,10},{9,11},{10,... | collective-permute-start | bytes 3145736 | tf_op jit(solution)/shard_map/ppermute | solution.py:87
  521.1 123.7 %collective-permute-start.54 = (bf16[1024,512]{1,0:T(8,128)(2,1)}, bf16[1024,512]{1,0:T(8,128)(2,1)}, u32[]{:S(2)}, u32[]{:S(2)}) collective-permute-start(bf16[1024,512]{1,0:T(8,128)(2,1)} %bitcast.32), channel_id=1, source_target_pairs={{0,2},{1,3},{2,0},{3,1},{4,6},{5,7},{6,4},{7,5},{8,10},{9,11},{10,... | collective-permute-start | bytes 3145736 | tf_op jit(solution)/shard_map/ppermute | solution.py:87
  550.5 94.3 %collective-permute-start.53 = (bf16[1024,512]{1,0:T(8,128)(2,1)}, bf16[1024,512]{1,0:T(8,128)(2,1)}, u32[]{:S(2)}, u32[]{:S(2)}) collective-permute-start(bf16[1024,512]{1,0:T(8,128)(2,1)} %fusion.36), channel_id=1, source_target_pairs={{0,4},{1,5},{2,6},{3,7},{4,0},{5,1},{6,2},{7,3},{8,12},{9,13},{10,... | collective-permute-start | bytes 3145736 | tf_op jit(solution)/shard_map/ppermute | solution.py:87
  661.3 81.8 %collective-permute-start.58 = (bf16[4,2,1280,512]{3,2,1,0:T(8,128)(2,1)}, bf16[4,2,1280,512]{3,2,1,0:T(8,128)(2,1)}, u32[]{:S(2)}, u32[]{:S(2)}) collective-permute-start(bf16[4,2,1280,512]{3,2,1,0:T(8,128)(2,1)} %get-tuple-element.191), channel_id=1, source_target_pairs={{0,1},{1,0},{2,3},{3,2},{4,5},{5,4},{6,7},{7,6},{8,9},{9,8},{10,11... | collective-permute-start | bytes 31457288 | tf_op jit(solution)/shard_map/ppermute | solution.py:87
  687.6 109.1 %collective-permute-start.67 = (bf16[1024,512]{1,0:T(8,128)(2,1)}, bf16[1024,512]{1,0:T(8,128)(2,1)}, u32[]{:S(2)}, u32[]{:S(2)}) collective-permute-start(bf16[1024,512]{1,0:T(8,128)(2,1)} %fusion.30), channel_id=1, source_target_pairs={{0,16},{1,17},{2,18},{3,19},{4,20},{5,21},{6,22},{7,23},{8,24},{9,... | collective-permute-start | bytes 3145736 | tf_op jit(solution)/shard_map/ppermute | solution.py:87
  697.6 99.1 %collective-permute-start.68 = (bf16[1024,512]{1,0:T(8,128)(2,1)}, bf16[1024,512]{1,0:T(8,128)(2,1)}, u32[]{:S(2)}, u32[]{:S(2)}) collective-permute-start(bf16[1024,512]{1,0:T(8,128)(2,1)} %fusion.28), channel_id=1, source_target_pairs={{0,24},{1,25},{2,26},{3,27},{4,28},{5,29},{6,30},{7,31},{8,16},{9,... | collective-permute-start | bytes 3145736 | tf_op jit(solution)/shard_map/ppermute | solution.py:87
  741.6 55.1 %collective-permute-start.66 = (bf16[1024,512]{1,0:T(8,128)(2,1)}, bf16[1024,512]{1,0:T(8,128)(2,1)}, u32[]{:S(2)}, u32[]{:S(2)}) collective-permute-start(bf16[1024,512]{1,0:T(8,128)(2,1)} %fusion.32), channel_id=1, source_target_pairs={{0,8},{1,9},{2,10},{3,11},{4,12},{5,13},{6,14},{7,15},{8,0},{9,1},... | collective-permute-start | bytes 3145736 | tf_op jit(solution)/shard_map/ppermute | solution.py:87
  853.1 167.9 %collective-permute-start.60 = (bf16[2,1024,512]{2,1,0:T(8,128)(2,1)}, bf16[2,1024,512]{2,1,0:T(8,128)(2,1)}, u32[]{:S(2)}, u32[]{:S(2)}) collective-permute-start(bf16[2,1024,512]{2,1,0:T(8,128)(2,1)} %add_convert_fusion.3), channel_id=1, source_target_pairs={{0,4},{1,5},{2,6},{3,7},{4,0},{5,1},{6,2},{7,3},{8,12},{9,13},{10,... | collective-permute-start | bytes 6291464 | tf_op jit(solution)/shard_map/ppermute | solution.py:87
  854.5 169.9 %collective-permute-start.74 = (bf16[2,1024,512]{2,1,0:T(8,128)(2,1)}, bf16[2,1024,512]{2,1,0:T(8,128)(2,1)}, u32[]{:S(2)}, u32[]{:S(2)}) collective-permute-start(bf16[2,1024,512]{2,1,0:T(8,128)(2,1)} %get-tuple-element.218), channel_id=1, source_target_pairs={{0,2},{1,3},{2,0},{3,1},{4,6},{5,7},{6,4},{7,5},{8,10},{9,11},{10,... | collective-permute-start | bytes 6291464 | tf_op jit(solution)/shard_map/ppermute | solution.py:87
  867.7 156.8 %collective-permute-start.76 = (bf16[2,1024,512]{2,1,0:T(8,128)(2,1)}, bf16[2,1024,512]{2,1,0:T(8,128)(2,1)}, u32[]{:S(2)}, u32[]{:S(2)}) collective-permute-start(bf16[2,1024,512]{2,1,0:T(8,128)(2,1)} %get-tuple-element.221), channel_id=1, source_target_pairs={{0,4},{1,5},{2,6},{3,7},{4,0},{5,1},{6,2},{7,3},{8,12},{9,13},{10,... | collective-permute-start | bytes 6291464 | tf_op jit(solution)/shard_map/ppermute | solution.py:87
  877.7 100.0 %collective-permute-start.94 = (bf16[1024,512]{1,0:T(8,128)(2,1)}, bf16[1024,512]{1,0:T(8,128)(2,1)S(1)}, u32[]{:S(2)}, u32[]{:S(2)}) collective-permute-start(bf16[1024,512]{1,0:T(8,128)(2,1)} %pad_maximum_fusion.2), channel_id=1, source_target_pairs={{0,4},{1,5},{2,6},{3,7},{4,0},{5,1},{6,2},{7,3},{8,12},{9,13},{10,... | collective-permute-start | bytes 3145736 | tf_op jit(solution)/shard_map/ppermute | solution.py:87
  899.8 98.4 %collective-permute-start.100 = (bf16[1024,512]{1,0:T(8,128)(2,1)S(1)}, bf16[1024,512]{1,0:T(8,128)(2,1)S(1)}, u32[]{:S(2)}, u32[]{:S(2)}) collective-permute-start(bf16[1024,512]{1,0:T(8,128)(2,1)S(1)} %slice.227), channel_id=1, source_target_pairs={{0,4},{1,5},{2,6},{3,7},{4,0},{5,1},{6,2},{7,3},{8,12},{9,13},{10,... | collective-permute-start | bytes 3145736 | tf_op jit(solution)/shard_map/ppermute | solution.py:87
  1020.8 57.0 %collective-permute-start.77 = (bf16[2,1024,512]{2,1,0:T(8,128)(2,1)S(1)}, bf16[2,1024,512]{2,1,0:T(8,128)(2,1)S(1)}, u32[]{:S(2)}, u32[]{:S(2)}) collective-permute-start(bf16[2,1024,512]{2,1,0:T(8,128)(2,1)S(1)} %add_convert_fusion.2), channel_id=1, source_target_pairs={{0,2},{1,3},{2,0},{3,1},{4,6},{5,7},{6,4},{7,5},{8,10},{9,11},{10,... | collective-permute-start | bytes 6291464 | tf_op jit(solution)/shard_map/ppermute | solution.py:87
  1051.3 54.7 %collective-permute-start.80 = (bf16[1024,512]{1,0:T(8,128)(2,1)S(1)}, bf16[1024,512]{1,0:T(8,128)(2,1)S(1)}, u32[]{:S(2)}, u32[]{:S(2)}) collective-permute-start(bf16[1024,512]{1,0:T(8,128)(2,1)S(1)} %fusion.49), channel_id=1, source_target_pairs={{0,1},{1,0},{2,3},{3,2},{4,5},{5,4},{6,7},{7,6},{8,9},{9,8},{10,11... | collective-permute-start | bytes 3145736 | tf_op jit(solution)/shard_map/ppermute | solution.py:87
  1092.5 182.4 %collective-permute-start.99 = (bf16[1024,512]{1,0:T(8,128)(2,1)}, bf16[1024,512]{1,0:T(8,128)(2,1)}, u32[]{:S(2)}, u32[]{:S(2)}) collective-permute-start(bf16[1024,512]{1,0:T(8,128)(2,1)} %pad_maximum_fusion.3.refs_0_), channel_id=1, source_target_pairs={{0,4},{1,5},{2,6},{3,7},{4,0},{5,1},{6,2},{7,3},{8,12},{9,13},{10,... | collective-permute-start | bytes 3145736 | tf_op jit(solution)/shard_map/ppermute | solution.py:87
  1113.9 161.0 %collective-permute-start.105 = (bf16[1024,512]{1,0:T(8,128)(2,1)}, bf16[1024,512]{1,0:T(8,128)(2,1)}, u32[]{:S(2)}, u32[]{:S(2)}) collective-permute-start(bf16[1024,512]{1,0:T(8,128)(2,1)} %pad_maximum_fusion.4.refs_2_), channel_id=1, source_target_pairs={{0,4},{1,5},{2,6},{3,7},{4,0},{5,1},{6,2},{7,3},{8,12},{9,13},{10,... | collective-permute-start | bytes 3145736 | tf_op jit(solution)/shard_map/ppermute | solution.py:87
  1127.4 134.4 %collective-permute-start.106 = (bf16[512,1024]{1,0:T(8,128)(2,1)}, bf16[512,1024]{1,0:T(8,128)(2,1)}, u32[]{:S(2)}, u32[]{:S(2)}) collective-permute-start(bf16[512,1024]{1,0:T(8,128)(2,1)} %pad_maximum_fusion.5), channel_id=1, source_target_pairs={{0,8},{1,9},{2,10},{3,11},{4,12},{5,13},{6,14},{7,15},{8,0},{9,1},... | collective-permute-start | bytes 3145736 | tf_op jit(solution)/shard_map/ppermute | solution.py:87
  1165.2 99.5 %collective-permute-start.90 = (bf16[2,1024,512]{2,1,0:T(8,128)(2,1)}, bf16[2,1024,512]{2,1,0:T(8,128)(2,1)}, u32[]{:S(2)}, u32[]{:S(2)}) collective-permute-start(bf16[2,1024,512]{2,1,0:T(8,128)(2,1)} %add_convert_fusion.1), channel_id=1, source_target_pairs={{0,16},{1,17},{2,18},{3,19},{4,20},{5,21},{6,22},{7,23},{8,24},{9,... | collective-permute-start | bytes 6291464 | tf_op jit(solution)/shard_map/ppermute | solution.py:87
  (163 other events, 4055.7 us)

commit v10 on v8

--- a/solution.py
+++ b/solution.py
@@ -39,7 +39,7 @@
     "weight": ("ex3", "ey3", "ex1", "ey1"),
     "residual_grad": ("gd0", "gd1"),
     "back": ("gx0",),
-    "normed_grad": ("gx1", "gy0"),
+    "normed_grad": ("gy0",),
     "ends": ("qk2",),
 }
 
@@ -160,7 +160,7 @@
     return send(parts[1][1], dy=1) if odd else send(parts[1][1], dx=1)
 
 
-def scatter_plane(parts, far, odd, hold=()):
+def scatter_plane(parts, far, odd, hold=(), hold_x=()):
     near, over_y, over_x = parts[0][0], parts[0][1], parts[1][0]
     if odd:
         over_x, over_y = added(over_x, far).astype(BF16), after(over_y, far)
@@ -168,6 +168,8 @@
         over_x, over_y = after(over_x, far), added(over_y, far).astype(BF16)
     if hold:
         over_y = after(over_y, *hold)
+    if hold_x:
+        over_x = after(over_x, *hold_x)
     from_x, from_y = send(over_x, dx=1), send(over_y, dy=1)
     return added(near, from_x, from_y), {"d": far, "x": from_x, "y": from_y}
 
@@ -186,17 +188,6 @@
     far = [scatter_corner(pair, i == 0) for i, pair in enumerate(pairs)]
     seen.update({"gd" + str(i): value for i, value in enumerate(far)})
     return far
-
-
-def scatter_planes(pairs, far, hold, seen):
-    if not is_cube():
-        return pairs
-    planes = []
-    for i, pair in enumerate(pairs):
-        plane, sent = scatter_plane(pair, far[i], i == 0, hold)
-        planes.append(plane)
-        seen.update({"g" + link + str(i): value for link, value in sent.items()})
-    return planes
 
 
 def scatter_ends(planes, hold):
@@ -265,7 +256,9 @@
         return value[:half], value[half:]
     for step in ({"dx": 1}, {"dz": 1}, {"dz": 2}):
         half = value.shape[0] // 2
-        value = added(value[:half], send(value[half:], **step)).astype(BF16)
+        other = send(value[half:], **step)
+        seen.setdefault(tag + "x", other)
+        value = added(value[:half], other).astype(BF16)
     for step in ({"dz": 2}, {"dz": 1}):
         seen[tag] = send(value, **step)
         value = jnp.concatenate([value, seen[tag]], axis=0)
@@ -273,13 +266,14 @@
     return value, send(value, dx=1)
 
 
-def expert_total(sums, tops):
+def expert_total(sums, tops, seen):
     if not is_cube():
         return lax.psum(sums, "expert"), lax.pmax(tops, "expert")
     count = sums.shape[0]
     both = jnp.concatenate([sums, tops], axis=0)
     for step in ({"dx": 1}, {"dz": 1}, {"dz": 2}):
         other = send(both, **step)
+        seen.setdefault("t1", other)
         both = jnp.concatenate([both[:count] + other[:count], jnp.maximum(both[count:], other[count:])])
     return both[:count], both[count:]
 
@@ -1036,7 +1030,11 @@
     )
     branch_pieces = tensor_gather(grad_branch, [grad_down])
 
-    planes = scatter_planes(pairs, far, branch_pieces[1:2], seen)
+    planes = pairs
+    if is_cube():
+        plane, sent = scatter_plane(pairs[0], far[0], True, branch_pieces[1:2])
+        planes = [plane]
+        seen.update({"g" + link + "0": value for link, value in sent.items()})
     grad_branch = jnp.concatenate(branch_pieces, axis=1)
 
     grad_output = matmul_tn(grad_branch, attended).astype(BF16)
@@ -1097,8 +1095,11 @@
         axis=0,
     )
     top_row = jnp.pad(head_top, (0, slice_width - heads_here), constant_values=-3e38)
-    small, top_row = expert_total(small, top_row[None])
+    small, top_row = expert_total(small, top_row[None], seen)
     head_top = top_row[0, :heads_here]
+    if is_cube():
+        free = [seen["qkx"], seen["t1"]]
+        planes.append(scatter_plane(pairs[1], far[1], False, branch_pieces[1:2], free)[0])
     mixture = scatter_ends(planes, [small, *due("ends", seen)])
     out = residual + mixture
     sum_moe_gain, sum_query_gain, sum_key_gain = small[E + 1], small[E + 2], small[E + 3]

time: 1270 us -> 1310 us (1.031)
  starting transfers between devices: 128 us -> 167 us
    ppermute x108, starting transfers between devices: 114 us -> 154 us  [send(): return lax.ppermute(value, BOTH, flip(dz, dx, dy, dc))]
  transfers between devices with their start and end apart: 110 -> 110, of which waited for: 34 -> 35; matrix products, arithmetic and copies ran while one was open for 12% -> 12% of each run, Pallas kernels for 33% -> 33%
where the time goes in v10:
time: 1310 us; the launch traced here: 1290 us
  waiting for transfers between devices  479 us (37%)
  Pallas kernels  458 us (35%)
  starting transfers between devices  167 us (13%)
  other arithmetic  72.5 us (6%)
  local copies, waits for them, and re-layouts  58.3 us (4%)
  matrix products  46.4 us (4%)
    ppermute x108, waiting for transfers between devices, send(): return lax.ppermute(value, BOTH, flip(dz, dx, dy, dc))  479 us
    ppermute x108, starting transfers between devices, send(): return lax.ppermute(value, BOTH, flip(dz, dx, dy, dc))  154 us
    pallas_call x4, Pallas kernels, expert_slot(): pl.pallas_call(partial(expert_kernel, slices), grid_spec=pltpu.PrefetchSc...  112 us
    pallas_call x6, Pallas kernels, place_rows(): pl.pallas_call(partial(place_kernel, slices, held, slots), grid_spec=pltp...  106 us
    pallas_call x8, Pallas kernels, pick_rows(): pl.pallas_call(partial(pick_kernel, group, slices), grid_spec=pltpu.Prefe...  81.5 us
    pallas_call x2, Pallas kernels, weight_grads(): pl.pallas_call(partial(kernel, slots, slices), grid_spec=pltpu.PrefetchSc...  70.4 us
    pallas_call x2, Pallas kernels, down_slots(): pl.pallas_call(partial(down_kernel, slices, slots), grid_spec=pltpu.Prefe...  31.5 us
  transfers between devices with their start and end apart: 110, of which 35 were waited for; matrix products, arithmetic and copies ran while one was open for 12% of the time, Pallas kernels for 33%

profile of v10, /device:TPU:10, one launch (start us, length us, event | category | flops | bytes accessed | tf_op | source)
XLA Modules:
  0.0 1291.6 jit_solution(4235358041937648639)
XLA Ops:
  7.5 15.7 %project.1 = (bf16[1024,2048]{1,0:T(8,128)(2,1)}, f32[1024,1]{1,0:T(8,128)}, f32[1024,512]{1,0:T(8,128)}, f32[1024,512]{1,0:T(8,128)}, bf16[1024,512]{1,0:T(8,12...) custom-call(bf16[1024,2048]{1,0:T(8,128)(2,1)} %in_ref.1, f32[1,2048]{1,0:T(1,128)} %bitcast.210, ...), custom_call_target="tpu_custom_call" | custom-call | flops 103079215104 | bytes 352321536 | tf_op jit(solution)/shard_map/project/pallas_call | solution.py:658
  95.1 34.2 %collective-permute-done.10.refs_2_ = bf16[1024,512]{1,0:T(8,128)(2,1)} collective-permute-done((bf16[1024,512]{1,0:T(8,128)(2,1)}, bf16[1024,512]{1,0:T(8,128)(2,1)}, u32[]{:S(2)}, u32[]{:S(2)}) %collective-permute-start.10) | collective-permute-done | bytes 1048608 | tf_op jit(solution)/shard_map/ppermute | solution.py:85
  168.7 23.9 %collective-permute-done.13.refs_2_ = bf16[1024,512]{1,0:T(8,128)(2,1)} collective-permute-done((bf16[1024,512]{1,0:T(8,128)(2,1)}, bf16[1024,512]{1,0:T(8,128)(2,1)}, u32[]{:S(2)}, u32[]{:S(2)}) %collective-permute-start.13) | collective-permute-done | bytes 1048608 | tf_op jit(solution)/shard_map/ppermute | solution.py:85
  198.6 22.6 %collective-permute-done.17.refs_5_ = bf16[1024,512]{1,0:T(8,128)(2,1)S(1)} collective-permute-done((bf16[1024,512]{1,0:T(8,128)(2,1)S(1)}, bf16[1024,512]{1,0:T(8,128)(2,1)S(1)}, u32[]{:S(2)}, u32[]{:S(2)}) %collective-permute-start.17) | collective-permute-done | bytes 1048608 | tf_op jit(solution)/shard_map/ppermute | solution.py:85
  235.6 30.9 %collective-permute-done.24.refs_2_ = bf16[1024,512]{1,0:T(8,128)(2,1)} collective-permute-done((bf16[1024,512]{1,0:T(8,128)(2,1)}, bf16[1024,512]{1,0:T(8,128)(2,1)}, u32[]{:S(2)}, u32[]{:S(2)}) %collective-permute-start.24) | collective-permute-done | bytes 1048608 | tf_op jit(solution)/shard_map/ppermute | solution.py:85
  279.4 13.5 %collective-permute-done.26.refs_4_ = bf16[1024,512]{1,0:T(8,128)(2,1)} collective-permute-done((bf16[1024,512]{1,0:T(8,128)(2,1)}, bf16[1024,512]{1,0:T(8,128)(2,1)}, u32[]{:S(2)}, u32[]{:S(2)}) %collective-permute-start.26) | collective-permute-done | bytes 1048608 | tf_op jit(solution)/shard_map/ppermute | solution.py:85
  295.0 27.8 %expert_slot.4 = (bf16[8,320,256]{2,1,0:T(8,128)(2,1)}, bf16[8,320,256]{2,1,0:T(8,128)(2,1)}, bf16[8,320,256]{2,1,0:T(8,128)(2,1)}, f32[8,2,1024]{2,1,0:T(2,128)...) custom-call(s32[10]{0:T(128)} %stack.118.where_ref, s32[8,8,1024]{2,1,0:T(8,128)} %copy.159.refs_0_.refs_1_, ...), custom_call_target="tpu_custom_call" | custom-call | flops 214748364800 | bytes 905969664 | tf_op jit(solution)/shard_map/expert_slot/pallas_call | solution.py:413
  324.0 15.0 %collective-permute-done.27.refs_5_ = bf16[1024,512]{1,0:T(8,128)(2,1)} collective-permute-done((bf16[1024,512]{1,0:T(8,128)(2,1)}, bf16[1024,512]{1,0:T(8,128)(2,1)}, u32[]{:S(2)}, u32[]{:S(2)}) %collective-permute-start.27) | collective-permute-done | bytes 1048608 | tf_op jit(solution)/shard_map/ppermute | solution.py:85
  359.8 14.0 %place_rows.6 = (bf16[1,1024,512]{2,1,0:T(8,128)(2,1)}, bf16[1,1024,512]{2,1,0:T(8,128)(2,1)}, bf16[1,1024,512]{2,1,0:T(8,128)(2,1)}, bf16[1,1024,512]{2,1,0:T(8,128)(2,1)}) custom-call(s32[2]{0:T(128)} %bitcast.206, s32[8,1024,8]{2,1,0:T(8,128)} %bitcast.153, s32[8,1024,8]{2,1,0:T(8,128)} %bitcast.154, ...), custom_call_target="tpu_custom_call" | custom-call | flops 85899345920 | bytes 234881024 | tf_op jit(solution)/shard_map/place_rows/pallas_call | solution.py:512
  409.6 27.8 %expert_slot.5 = (bf16[8,320,256]{2,1,0:T(8,128)(2,1)}, bf16[8,320,256]{2,1,0:T(8,128)(2,1)}, bf16[8,320,256]{2,1,0:T(8,128)(2,1)}, f32[8,2,1024]{2,1,0:T(2,128)...) custom-call(s32[10]{0:T(128)} %stack.127.where_ref, s32[8,8,1024]{2,1,0:T(8,128)} %copy.159.refs_0_.refs_1_, ...), custom_call_target="tpu_custom_call" | custom-call | flops 214748364800 | bytes 905969664 | tf_op jit(solution)/shard_map/expert_slot/pallas_call | solution.py:413
  437.4 16.3 %collective-permute-done.46.refs_4_ = bf16[1024,512]{1,0:T(8,128)(2,1)} collective-permute-done((bf16[1024,512]{1,0:T(8,128)(2,1)}, bf16[1024,512]{1,0:T(8,128)(2,1)}, u32[]{:S(2)}, u32[]{:S(2)}) %collective-permute-start.46) | collective-permute-done | bytes 1048608 | tf_op jit(solution)/shard_map/ppermute | solution.py:85
  455.7 18.9 %collective-permute-done.35.refs_5_ = bf16[1024,512]{1,0:T(8,128)(2,1)} collective-permute-done((bf16[1024,512]{1,0:T(8,128)(2,1)}, bf16[1024,512]{1,0:T(8,128)(2,1)}, u32[]{:S(2)}, u32[]{:S(2)}) %collective-permute-start.35) | collective-permute-done | bytes 1048608 | tf_op jit(solution)/shard_map/ppermute | solution.py:85
  497.6 14.0 %place_rows.7 = (bf16[1,1024,512]{2,1,0:T(8,128)(2,1)}, bf16[1,1024,512]{2,1,0:T(8,128)(2,1)}, bf16[1,1024,512]{2,1,0:T(8,128)(2,1)}, bf16[1,1024,512]{2,1,0:T(8,128)(2,1)}) custom-call(s32[2]{0:T(128)} %bitcast.208, s32[8,1024,8]{2,1,0:T(8,128)} %bitcast.155, s32[8,1024,8]{2,1,0:T(8,128)} %bitcast.156, ...), custom_call_target="tpu_custom_call" | custom-call | flops 85899345920 | bytes 234881024 | tf_op jit(solution)/shard_map/place_rows/pallas_call | solution.py:512
  513.2 27.8 %expert_slot.6 = (bf16[8,320,256]{2,1,0:T(8,128)(2,1)}, bf16[8,320,256]{2,1,0:T(8,128)(2,1)}, bf16[8,320,256]{2,1,0:T(8,128)(2,1)}, f32[8,2,1024]{2,1,0:T(2,128)...) custom-call(s32[10]{0:T(128)} %stack.124.where_ref, s32[8,8,1024]{2,1,0:T(8,128)} %copy.159.refs_0_.refs_1_, ...), custom_call_target="tpu_custom_call" | custom-call | flops 214748364800 | bytes 905969664 | tf_op jit(solution)/shard_map/expert_slot/pallas_call | solution.py:413
  552.5 13.8 %place_rows.8 = (bf16[1,1024,512]{2,1,0:T(8,128)(2,1)}, bf16[1,1024,512]{2,1,0:T(8,128)(2,1)}, bf16[1,1024,512]{2,1,0:T(8,128)(2,1)}, bf16[1,1024,512]{2,1,0:T(8,128)(2,1)}) custom-call(s32[2]{0:T(128)} %bitcast.211, s32[8,1024,8]{2,1,0:T(8,128)} %bitcast.157, s32[8,1024,8]{2,1,0:T(8,128)} %bitcast.158, ...), custom_call_target="tpu_custom_call" | custom-call | flops 85899345920 | bytes 234881024 | tf_op jit(solution)/shard_map/place_rows/pallas_call | solution.py:512
  566.4 28.3 %expert_slot.7 = (bf16[8,320,256]{2,1,0:T(8,128)(2,1)}, bf16[8,320,256]{2,1,0:T(8,128)(2,1)}, bf16[8,320,256]{2,1,0:T(8,128)(2,1)}, f32[8,2,1024]{2,1,0:T(2,128)...) custom-call(s32[10]{0:T(128)} %stack.121.where_ref, s32[8,8,1024]{2,1,0:T(8,128)} %copy.159.refs_0_.refs_1_, ...), custom_call_target="tpu_custom_call" | custom-call | flops 214748364800 | bytes 905969664 | tf_op jit(solution)/shard_map/expert_slot/pallas_call | solution.py:413
  612.1 15.7 %down_slots.2 = (bf16[4,2,1280,512]{3,2,1,0:T(8,128)(2,1)}, bf16[4,2,1280,512]{3,2,1,0:T(8,128)(2,1)}) custom-call(s32[10]{0:T(128)} %stack.118.where_ref, bf16[8,320,256]{2,1,0:T(8,128)(2,1)} %get-tuple-element.148.refs_0_.refs_8_, bf16[8,320,256]{2,1,0:T(8,128)(2,1)} %get-tuple-element.176.refs_1_.refs_9_, bf16[8,256,2048]{2,1,0:T(8,128)(2,1)} %refs_2_.3), custom_call_target="tpu_custom_call" | custom-call | flops 85899345920 | bytes 469762048 | tf_op jit(solution)/shard_map/down_slots/pallas_call | solution.py:453
  628.1 28.7 %collective-permute-done.56 = bf16[1024,512]{1,0:T(8,128)(2,1)S(1)} collective-permute-done((bf16[1024,512]{1,0:T(8,128)(2,1)}, bf16[1024,512]{1,0:T(8,128)(2,1)S(1)}, u32[]{:S(2)}, u32[]{:S(2)}) %collective-permute-start.56) | collective-permute-done | bytes 1048608 | tf_op jit(solution)/shard_map/ppermute | solution.py:85
  659.2 14.0 %place_rows.9 = (bf16[1,1024,512]{2,1,0:T(8,128)(2,1)}, bf16[1,1024,512]{2,1,0:T(8,128)(2,1)}, bf16[1,1024,512]{2,1,0:T(8,128)(2,1)}, bf16[1,1024,512]{2,1,0:T(8,128)(2,1)}) custom-call(s32[2]{0:T(128)} %bitcast.212, s32[8,1024,8]{2,1,0:T(8,128)} %bitcast.159, s32[8,1024,8]{2,1,0:T(8,128)} %bitcast.160, ...), custom_call_target="tpu_custom_call" | custom-call | flops 85899345920 | bytes 234881024 | tf_op jit(solution)/shard_map/place_rows/pallas_call | solution.py:512
  695.7 13.4 %collective-permute-done.57 = bf16[1024,512]{1,0:T(8,128)(2,1)S(1)} collective-permute-done((bf16[1024,512]{1,0:T(8,128)(2,1)}, bf16[1024,512]{1,0:T(8,128)(2,1)S(1)}, u32[]{:S(2)}, u32[]{:S(2)}) %collective-permute-start.57) | collective-permute-done | bytes 1048608 | tf_op jit(solution)/shard_map/ppermute | solution.py:85
  712.4 15.7 %down_slots.3 = (bf16[4,2,1280,512]{3,2,1,0:T(8,128)(2,1)}, bf16[4,2,1280,512]{3,2,1,0:T(8,128)(2,1)}) custom-call(s32[10]{0:T(128)} %stack.118.where_ref, bf16[8,320,256]{2,1,0:T(8,128)(2,1)} %get-tuple-element.156.refs_0_.refs_10_, bf16[8,320,256]{2,1,0:T(8,128)(2,1)} %get-tuple-element.165.refs_1_.refs_11_, bf16[8,256,2048]{2,1,0:T(8,128)(2,1)} %refs_2_.3), custom_call_target="tpu_custom_call" | custom-call | flops 85899345920 | bytes 469762048 | tf_op jit(solution)/shard_map/down_slots/pallas_call | solution.py:453
  737.5 25.3 %place_rows.10 = (bf16[2,1024,512]{2,1,0:T(8,128)(2,1)}, bf16[2,1024,512]{2,1,0:T(8,128)(2,1)}, bf16[2,1024,512]{2,1,0:T(8,128)(2,1)}, bf16[2,1024,512]{2,1,0:T(8,128)(2,1)}) custom-call(s32[4]{0:T(128)} %pad_add_fusion.3.where_ref, s32[8,1024,8]{2,1,0:T(8,128)} %bitcast.161, s32[8,1024,8]{2,1,0:T(8,128)} %bitcast.162, s32[8,1024,8]{2,1,0:T(8,128)} %bitcast.163, ...), custom_call_target="tpu_custom_call" | custom-call | flops 171798691840 | bytes 469762048 | tf_op jit(solution)/shard_map/place_rows/pallas_call | solution.py:512
  765.0 25.3 %place_rows.11 = (bf16[2,1024,512]{2,1,0:T(8,128)(2,1)}, bf16[2,1024,512]{2,1,0:T(8,128)(2,1)}, bf16[2,1024,512]{2,1,0:T(8,128)(2,1)}, bf16[2,1024,512]{2,1,0:T(8,128)(2,1)}) custom-call(s32[4]{0:T(128)} %pad_add_fusion.4.where_ref, s32[8,1024,8]{2,1,0:T(8,128)} %bitcast.165, s32[8,1024,8]{2,1,0:T(8,128)} %bitcast.166, s32[8,1024,8]{2,1,0:T(8,128)} %bitcast.167, ...), custom_call_target="tpu_custom_call" | custom-call | flops 171798691840 | bytes 469762048 | tf_op jit(solution)/shard_map/place_rows/pallas_call | solution.py:512
  790.6 42.9 %weight_grads.1 = (f32[8,2048,256]{2,1,0:T(8,128)}, f32[8,2048,256]{2,1,0:T(8,128)}) custom-call(s32[10]{0:T(128)} %stack.118.where_ref, bf16[2,2,1280,512]{3,2,1,0:T(8,128)(2,1)} %pick_rows.9.refs_4_.refs_0_, bf16[2,2,1280,512]{3,2,1,0:T(8,128)(2,1)} %collective-permute-done.20.refs_5_.refs_1_, bf16[2,2,1280,512]{3,2,1,0:T(8,128)(2,1)} %pick_rows.15.refs_4_.refs_2_, ...), custom_call_target="tpu_custom_call" | custom-call | flops 160000000000 | bytes 16000000 | tf_op jit(solution)/shard_map/weight_grads/pallas_call | solution.py:569
  852.4 27.5 %weight_down_grads.1 = f32[8,256,2048]{2,1,0:T(8,128)} custom-call(s32[10]{0:T(128)} %stack.118.where_ref, bf16[2,2,1280,512]{3,2,1,0:T(8,128)(2,1)} %pick_rows.8.refs_6_.refs_0_, bf16[2,2,1280,512]{3,2,1,0:T(8,128)(2,1)} %collective-permute-done.21.refs_7_.refs_1_, bf16[2,2,1280,512]{3,2,1,0:T(8,128)(2,1)} %pick_rows.14.refs_6_.refs_2_, ...), custom_call_target="tpu_custom_call" | custom-call | flops 160000000000 | bytes 16000000 | tf_op jit(solution)/shard_map/weight_down_grads/pallas_call | solution.py:569
  910.4 16.4 %attend_back.1 = (bf16[1024,512]{1,0:T(8,128)(2,1)}, bf16[1024,512]{1,0:T(8,128)(2,1)}, bf16[1024,512]{1,0:T(8,128)(2,1)}, f32[1,1,512]{2,1,0:T(1,128)}, f32[1,1,512]{2,1,0:T(1,128)}) custom-call(s32[4]{0:T(128)} %add_bitcast_fusion.pieces_ref, bf16[1024,512]{1,0:T(8,128)(2,1)} %get-tuple-element.137.q_ref, bf16[1024,512]{1,0:T(8,128)(2,1)} %get-tuple-element.138.k_ref, ...), custom_call_target="tpu_custom_call" | custom-call | flops 85899345920 | bytes 184549376 | tf_op jit(solution)/shard_map/attend_back/pallas_call | solution.py:793
  945.8 12.3 collective-permute-done.100
  1060.2 22.1 %collective-permute-done.88 = bf16[256,1024]{1,0:T(8,128)(2,1)S(1)} collective-permute-done((bf16[256,1024]{1,0:T(8,128)(2,1)S(1)}, bf16[256,1024]{1,0:T(8,128)(2,1)S(1)}, u32[]{:S(2)}, u32[]{:S(2)}) %collective-permute-start.88) | collective-permute-done | bytes 524320 | tf_op jit(solution)/shard_map/ppermute | solution.py:85
  1098.0 18.6 %collective-permute-done.89 = bf16[256,1024]{1,0:T(8,128)(2,1)S(1)} collective-permute-done((bf16[256,1024]{1,0:T(8,128)(2,1)S(1)}, bf16[256,1024]{1,0:T(8,128)(2,1)S(1)}, u32[]{:S(2)}, u32[]{:S(2)}) %collective-permute-start.89) | collective-permute-done | bytes 524320 | tf_op jit(solution)/shard_map/ppermute | solution.py:85
  1120.0 40.8 %collective-permute-start.93 = (f32[8,128]{1,0:T(8,128)S(1)}, f32[8,128]{1,0:T(8,128)S(1)}, u32[]{:S(2)}, u32[]{:S(2)}) collective-permute-start(f32[8,128]{1,0:T(8,128)S(1)} %bitcast_add_fusion), channel_id=1, source_target_pairs={{0,2},{1,3},{2,0},{3,1},{4,6},{5,7},{6,4},{7,5},{8,10},{9,11},{10,... | collective-permute-start | bytes 12296 | tf_op jit(solution)/shard_map/ppermute | solution.py:85
  1175.8 53.6 %collective-permute-done.106 = bf16[512,1024]{1,0:T(8,128)(2,1)S(1)} collective-permute-done((bf16[512,1024]{1,0:T(8,128)(2,1)S(1)}, bf16[512,1024]{1,0:T(8,128)(2,1)S(1)}, u32[]{:S(2)}, u32[]{:S(2)}) %collective-permute-start.106) | collective-permute-done | bytes 1048608 | tf_op jit(solution)/shard_map/ppermute | solution.py:85
  1243.0 32.9 %collective-permute-done.107.refs_5_ = bf16[1024,1024]{1,0:T(8,128)(2,1)} collective-permute-done((bf16[1024,1024]{1,0:T(8,128)(2,1)S(1)}, bf16[1024,1024]{1,0:T(8,128)(2,1)}, u32[]{:S(2)}, u32[]{:S(2)}) %collective-permute-start.107) | collective-permute-done | bytes 2097184 | tf_op jit(solution)/shard_map/ppermute | solution.py:85
  (559 shorter events, 539.4 us)
Async XLA Ops:
  150.0 145.0 %all-to-all-start = ((f32[8,8,1024]{2,1,0:T(8,128)}), f32[8,8,1024]{2,1,0:T(8,128)}, u32[]{:S(2)}, u32[]{:S(2)}) async-start(f32[8,8,1024]{2,1,0:T(8,128)} %fusion.82), calls=%async_computation | async-start | bytes 524288 | tf_op jit(solution)/shard_map/all_to_all | solution.py:931
  157.9 63.2 %collective-permute-start.17 = (bf16[1024,512]{1,0:T(8,128)(2,1)S(1)}, bf16[1024,512]{1,0:T(8,128)(2,1)S(1)}, u32[]{:S(2)}, u32[]{:S(2)}) collective-permute-start(bf16[1024,512]{1,0:T(8,128)(2,1)S(1)} %collective-permute-done.15.refs_3_), channel_id=1, source_target_pairs={{0,4},{1,5},{2,6},{3,7},{4,0},{5,1},{6,2},{7,3},{8,12},{9,13},{10,... | collective-permute-start | bytes 3145736 | tf_op jit(solution)/shard_map/ppermute | solution.py:85
  192.7 84.7 %collective-permute-start.23 = (bf16[1024,512]{1,0:T(8,128)(2,1)}, bf16[1024,512]{1,0:T(8,128)(2,1)}, u32[]{:S(2)}, u32[]{:S(2)}) collective-permute-start(bf16[1024,512]{1,0:T(8,128)(2,1)} %collective-permute-done.13.refs_2_), channel_id=1, source_target_pairs={{0,2},{1,3},{2,0},{3,1},{4,6},{5,7},{6,4},{7,5},{8,10},{9,11},{10,... | collective-permute-start | bytes 3145736 | tf_op jit(solution)/shard_map/ppermute | solution.py:85
  194.2 84.7 %collective-permute-start.19 = (bf16[1024,512]{1,0:T(8,128)(2,1)}, bf16[1024,512]{1,0:T(8,128)(2,1)}, u32[]{:S(2)}, u32[]{:S(2)}) collective-permute-start(bf16[1024,512]{1,0:T(8,128)(2,1)} %collective-permute-done.13.refs_2_), channel_id=1, source_target_pairs={{0,4},{1,5},{2,6},{3,7},{4,0},{5,1},{6,2},{7,3},{8,12},{9,13},{10,... | collective-permute-start | bytes 3145736 | tf_op jit(solution)/shard_map/ppermute | solution.py:85
  198.1 69.0 %collective-permute-start.18 = (bf16[1024,512]{1,0:T(8,128)(2,1)}, bf16[1024,512]{1,0:T(8,128)(2,1)}, u32[]{:S(2)}, u32[]{:S(2)}) collective-permute-start(bf16[1024,512]{1,0:T(8,128)(2,1)} %collective-permute-done.12.refs_4_), channel_id=1, source_target_pairs={{0,2},{1,3},{2,0},{3,1},{4,6},{5,7},{6,4},{7,5},{8,10},{9,11},{10,... | collective-permute-start | bytes 3145736 | tf_op jit(solution)/shard_map/ppermute | solution.py:85
  235.6 57.8 %collective-permute-start.21 = (bf16[2,2,1280,512]{3,2,1,0:T(8,128)(2,1)}, bf16[2,2,1280,512]{3,2,1,0:T(8,128)(2,1)}, u32[]{:S(2)}, u32[]{:S(2)}) collective-permute-start(bf16[2,2,1280,512]{3,2,1,0:T(8,128)(2,1)} %pick_rows.8.refs_6_.refs_0_), channel_id=1, source_target_pairs={{0,1},{1,0},{2,3},{3,2},{4,5},{5,4},{6,7},{7,6},{8,9},{9,8},{10,11... | collective-permute-start | bytes 15728648 | tf_op jit(solution)/shard_map/ppermute | solution.py:85
  277.4 109.6 %collective-permute-start.39 = (bf16[1024,512]{1,0:T(8,128)(2,1)}, bf16[1024,512]{1,0:T(8,128)(2,1)}, u32[]{:S(2)}, u32[]{:S(2)}) collective-permute-start(bf16[1024,512]{1,0:T(8,128)(2,1)} %collective-permute-done.37.refs_2_), channel_id=1, source_target_pairs={{0,4},{1,5},{2,6},{3,7},{4,0},{5,1},{6,2},{7,3},{8,12},{9,13},{10,... | collective-permute-start | bytes 3145736 | tf_op jit(solution)/shard_map/ppermute | solution.py:85
  278.9 70.3 %collective-permute-start.29 = (bf16[1024,512]{1,0:T(8,128)(2,1)}, bf16[1024,512]{1,0:T(8,128)(2,1)}, u32[]{:S(2)}, u32[]{:S(2)}) collective-permute-start(bf16[1024,512]{1,0:T(8,128)(2,1)} %collective-permute-done.23.refs_3_), channel_id=1, source_target_pairs={{0,4},{1,5},{2,6},{3,7},{4,0},{5,1},{6,2},{7,3},{8,12},{9,13},{10,... | collective-permute-start | bytes 3145736 | tf_op jit(solution)/shard_map/ppermute | solution.py:85
  322.8 58.4 %collective-permute-start.32 = (bf16[1024,512]{1,0:T(8,128)(2,1)}, bf16[1024,512]{1,0:T(8,128)(2,1)}, u32[]{:S(2)}, u32[]{:S(2)}) collective-permute-start(bf16[1024,512]{1,0:T(8,128)(2,1)} %multiply_convert_fusion.2.refs_2_), channel_id=1, source_target_pairs={{0,24},{1,25},{2,26},{3,27},{4,28},{5,29},{6,30},{7,31},{8,16},{9,... | collective-permute-start | bytes 3145736 | tf_op jit(solution)/shard_map/ppermute | solution.py:85
  386.9 99.5 %collective-permute-start.38 = (bf16[1024,512]{1,0:T(8,128)(2,1)}, bf16[1024,512]{1,0:T(8,128)(2,1)}, u32[]{:S(2)}, u32[]{:S(2)}) collective-permute-start(bf16[1024,512]{1,0:T(8,128)(2,1)} %collective-permute-done.37.refs_2_), channel_id=1, source_target_pairs={{0,2},{1,3},{2,0},{3,1},{4,6},{5,7},{6,4},{7,5},{8,10},{9,11},{10,... | collective-permute-start | bytes 3145736 | tf_op jit(solution)/shard_map/ppermute | solution.py:85
  399.1 87.9 %collective-permute-start.40 = (bf16[1024,512]{1,0:T(8,128)(2,1)}, bf16[1024,512]{1,0:T(8,128)(2,1)}, u32[]{:S(2)}, u32[]{:S(2)}) collective-permute-start(bf16[1024,512]{1,0:T(8,128)(2,1)} %collective-permute-done.39.refs_4_), channel_id=1, source_target_pairs={{0,2},{1,3},{2,0},{3,1},{4,6},{5,7},{6,4},{7,5},{8,10},{9,11},{10,... | collective-permute-start | bytes 3145736 | tf_op jit(solution)/shard_map/ppermute | solution.py:85
  409.0 65.6 %collective-permute-start.35 = (bf16[1024,512]{1,0:T(8,128)(2,1)}, bf16[1024,512]{1,0:T(8,128)(2,1)}, u32[]{:S(2)}, u32[]{:S(2)}) collective-permute-start(bf16[1024,512]{1,0:T(8,128)(2,1)} %collective-permute-done.33.refs_3_), channel_id=1, source_target_pairs={{0,4},{1,5},{2,6},{3,7},{4,0},{5,1},{6,2},{7,3},{8,12},{9,13},{10,... | collective-permute-start | bytes 3145736 | tf_op jit(solution)/shard_map/ppermute | solution.py:85
  453.7 87.3 %collective-permute-start.45 = (bf16[1024,512]{1,0:T(8,128)(2,1)}, bf16[1024,512]{1,0:T(8,128)(2,1)}, u32[]{:S(2)}, u32[]{:S(2)}) collective-permute-start(bf16[1024,512]{1,0:T(8,128)(2,1)} %collective-permute-done.44.refs_2_), channel_id=1, source_target_pairs={{0,2},{1,3},{2,0},{3,1},{4,6},{5,7},{6,4},{7,5},{8,10},{9,11},{10,... | collective-permute-start | bytes 3145736 | tf_op jit(solution)/shard_map/ppermute | solution.py:85
  454.2 86.9 %collective-permute-start.47 = (bf16[1024,512]{1,0:T(8,128)(2,1)}, bf16[1024,512]{1,0:T(8,128)(2,1)}, u32[]{:S(2)}, u32[]{:S(2)}) collective-permute-start(bf16[1024,512]{1,0:T(8,128)(2,1)} %collective-permute-done.46.refs_4_), channel_id=1, source_target_pairs={{0,2},{1,3},{2,0},{3,1},{4,6},{5,7},{6,4},{7,5},{8,10},{9,11},{10,... | collective-permute-start | bytes 3145736 | tf_op jit(solution)/shard_map/ppermute | solution.py:85
  485.6 66.2 %collective-permute-start.48 = (bf16[1024,512]{1,0:T(8,128)(2,1)}, bf16[1024,512]{1,0:T(8,128)(2,1)}, u32[]{:S(2)}, u32[]{:S(2)}) collective-permute-start(bf16[1024,512]{1,0:T(8,128)(2,1)} %bitcast.28), channel_id=1, source_target_pairs={{0,4},{1,5},{2,6},{3,7},{4,0},{5,1},{6,2},{7,3},{8,12},{9,13},{10,... | collective-permute-start | bytes 3145736 | tf_op jit(solution)/shard_map/ppermute | solution.py:85
  486.4 65.4 %collective-permute-start.49 = (bf16[1024,512]{1,0:T(8,128)(2,1)}, bf16[1024,512]{1,0:T(8,128)(2,1)}, u32[]{:S(2)}, u32[]{:S(2)}) collective-permute-start(bf16[1024,512]{1,0:T(8,128)(2,1)} %fusion.37), channel_id=1, source_target_pairs={{0,2},{1,3},{2,0},{3,1},{4,6},{5,7},{6,4},{7,5},{8,10},{9,11},{10,... | collective-permute-start | bytes 3145736 | tf_op jit(solution)/shard_map/ppermute | solution.py:85
  606.6 66.6 %collective-permute-start.55 = (bf16[1024,512]{1,0:T(8,128)(2,1)}, bf16[1024,512]{1,0:T(8,128)(2,1)}, u32[]{:S(2)}, u32[]{:S(2)}) collective-permute-start(bf16[1024,512]{1,0:T(8,128)(2,1)} %bitcast.32), channel_id=1, source_target_pairs={{0,2},{1,3},{2,0},{3,1},{4,6},{5,7},{6,4},{7,5},{8,10},{9,11},{10,... | collective-permute-start | bytes 3145736 | tf_op jit(solution)/shard_map/ppermute | solution.py:85
  609.6 64.2 %collective-permute-start.54 = (bf16[1024,512]{1,0:T(8,128)(2,1)}, bf16[1024,512]{1,0:T(8,128)(2,1)}, u32[]{:S(2)}, u32[]{:S(2)}) collective-permute-start(bf16[1024,512]{1,0:T(8,128)(2,1)} %fusion.36), channel_id=1, source_target_pairs={{0,4},{1,5},{2,6},{3,7},{4,0},{5,1},{6,2},{7,3},{8,12},{9,13},{10,... | collective-permute-start | bytes 3145736 | tf_op jit(solution)/shard_map/ppermute | solution.py:85
  627.9 109.1 %collective-permute-start.58 = (bf16[4,2,1280,512]{3,2,1,0:T(8,128)(2,1)}, bf16[4,2,1280,512]{3,2,1,0:T(8,128)(2,1)}, u32[]{:S(2)}, u32[]{:S(2)}) collective-permute-start(bf16[4,2,1280,512]{3,2,1,0:T(8,128)(2,1)} %get-tuple-element.190), channel_id=1, source_target_pairs={{0,1},{1,0},{2,3},{3,2},{4,5},{5,4},{6,7},{7,6},{8,9},{9,8},{10,11... | collective-permute-start | bytes 31457288 | tf_op jit(solution)/shard_map/ppermute | solution.py:85
  689.4 144.1 %collective-permute-start.67 = (bf16[1024,512]{1,0:T(8,128)(2,1)}, bf16[1024,512]{1,0:T(8,128)(2,1)}, u32[]{:S(2)}, u32[]{:S(2)}) collective-permute-start(bf16[1024,512]{1,0:T(8,128)(2,1)} %fusion.30), channel_id=1, source_target_pairs={{0,16},{1,17},{2,18},{3,19},{4,20},{5,21},{6,22},{7,23},{8,24},{9,... | collective-permute-start | bytes 3145736 | tf_op jit(solution)/shard_map/ppermute | solution.py:85
  695.7 137.8 %collective-permute-start.68 = (bf16[1024,512]{1,0:T(8,128)(2,1)}, bf16[1024,512]{1,0:T(8,128)(2,1)}, u32[]{:S(2)}, u32[]{:S(2)}) collective-permute-start(bf16[1024,512]{1,0:T(8,128)(2,1)} %fusion.28), channel_id=1, source_target_pairs={{0,24},{1,25},{2,26},{3,27},{4,28},{5,29},{6,30},{7,31},{8,16},{9,... | collective-permute-start | bytes 3145736 | tf_op jit(solution)/shard_map/ppermute | solution.py:85
  735.9 97.6 %collective-permute-start.66 = (bf16[1024,512]{1,0:T(8,128)(2,1)}, bf16[1024,512]{1,0:T(8,128)(2,1)}, u32[]{:S(2)}, u32[]{:S(2)}) collective-permute-start(bf16[1024,512]{1,0:T(8,128)(2,1)} %fusion.32), channel_id=1, source_target_pairs={{0,8},{1,9},{2,10},{3,11},{4,12},{5,13},{6,14},{7,15},{8,0},{9,1},... | collective-permute-start | bytes 3145736 | tf_op jit(solution)/shard_map/ppermute | solution.py:85
  762.8 80.1 %collective-permute-start.59 = (bf16[2,1024,512]{2,1,0:T(8,128)(2,1)}, bf16[2,1024,512]{2,1,0:T(8,128)(2,1)}, u32[]{:S(2)}, u32[]{:S(2)}) collective-permute-start(bf16[2,1024,512]{2,1,0:T(8,128)(2,1)} %get-tuple-element.194), channel_id=1, source_target_pairs={{0,2},{1,3},{2,0},{3,1},{4,6},{5,7},{6,4},{7,5},{8,10},{9,11},{10,... | collective-permute-start | bytes 6291464 | tf_op jit(solution)/shard_map/ppermute | solution.py:85
  790.3 60.6 %collective-permute-start.73 = (bf16[2,1024,512]{2,1,0:T(8,128)(2,1)}, bf16[2,1024,512]{2,1,0:T(8,128)(2,1)}, u32[]{:S(2)}, u32[]{:S(2)}) collective-permute-start(bf16[2,1024,512]{2,1,0:T(8,128)(2,1)} %get-tuple-element.224), channel_id=1, source_target_pairs={{0,4},{1,5},{2,6},{3,7},{4,0},{5,1},{6,2},{7,3},{8,12},{9,13},{10,... | collective-permute-start | bytes 6291464 | tf_op jit(solution)/shard_map/ppermute | solution.py:85
  938.7 68.6 %collective-permute-start.78 = (bf16[1024,1024]{1,0:T(8,128)(2,1)S(1)}, bf16[1024,1024]{1,0:T(8,128)(2,1)S(1)}, u32[]{:S(2)}, u32[]{:S(2)}) collective-permute-start(bf16[1024,1024]{1,0:T(8,128)(2,1)S(1)} %slice.207), channel_id=1, source_target_pairs={{0,4},{1,5},{2,6},{3,7},{4,0},{5,1},{6,2},{7,3},{8,12},{9,13},{10,... | collective-permute-start | bytes 6291464 | tf_op jit(solution)/shard_map/ppermute | solution.py:85
  1020.4 74.2 %collective-permute-start.84 = (bf16[2,1024,512]{2,1,0:T(8,128)(2,1)}, bf16[2,1024,512]{2,1,0:T(8,128)(2,1)}, u32[]{:S(2)}, u32[]{:S(2)}) collective-permute-start(bf16[2,1024,512]{2,1,0:T(8,128)(2,1)} %add_convert_fusion.2), channel_id=1, source_target_pairs={{0,2},{1,3},{2,0},{3,1},{4,6},{5,7},{6,4},{7,5},{8,10},{9,11},{10,... | collective-permute-start | bytes 6291464 | tf_op jit(solution)/shard_map/ppermute | solution.py:85
  1021.6 73.1 %collective-permute-start.83 = (bf16[2,1024,512]{2,1,0:T(8,128)(2,1)}, bf16[2,1024,512]{2,1,0:T(8,128)(2,1)}, u32[]{:S(2)}, u32[]{:S(2)}) collective-permute-start(bf16[2,1024,512]{2,1,0:T(8,128)(2,1)} %get-tuple-element.244), channel_id=1, source_target_pairs={{0,4},{1,5},{2,6},{3,7},{4,0},{5,1},{6,2},{7,3},{8,12},{9,13},{10,... | collective-permute-start | bytes 6291464 | tf_op jit(solution)/shard_map/ppermute | solution.py:85
  1023.1 137.7 %collective-permute-start.104 = (bf16[512,512]{1,0:T(8,128)(2,1)}, bf16[512,512]{1,0:T(8,128)(2,1)}, u32[]{:S(2)}, u32[]{:S(2)}) collective-permute-start(bf16[512,512]{1,0:T(8,128)(2,1)} %pad_maximum_fusion.7), channel_id=1, source_target_pairs={{0,8},{1,9},{2,10},{3,11},{4,12},{5,13},{6,14},{7,15},{8,0},{9,1},... | collective-permute-start | bytes 1572872 | tf_op jit(solution)/shard_map/ppermute | solution.py:85
  1026.1 215.8 %collective-permute-start.99 = (bf16[1024,512]{1,0:T(8,128)(2,1)S(1)}, bf16[1024,512]{1,0:T(8,128)(2,1)}, u32[]{:S(2)}, u32[]{:S(2)}) collective-permute-start(bf16[1024,512]{1,0:T(8,128)(2,1)S(1)} %pad_maximum_fusion.3.refs_0_), channel_id=1, source_target_pairs={{0,4},{1,5},{2,6},{3,7},{4,0},{5,1},{6,2},{7,3},{8,12},{9,13},{10,... | collective-permute-start | bytes 3145736 | tf_op jit(solution)/shard_map/ppermute | solution.py:85
  1116.6 115.2 %collective-permute-start.90 = (bf16[2,1024,512]{2,1,0:T(8,128)(2,1)S(1)}, bf16[2,1024,512]{2,1,0:T(8,128)(2,1)S(1)}, u32[]{:S(2)}, u32[]{:S(2)}) collective-permute-start(bf16[2,1024,512]{2,1,0:T(8,128)(2,1)S(1)} %add_convert_fusion.1), channel_id=1, source_target_pairs={{0,16},{1,17},{2,18},{3,19},{4,20},{5,21},{6,22},{7,23},{8,24},{9,... | collective-permute-start | bytes 6291464 | tf_op jit(solution)/shard_map/ppermute | solution.py:85
  1161.9 80.0 %collective-permute-start.105 = (bf16[1024,512]{1,0:T(8,128)(2,1)S(1)}, bf16[1024,512]{1,0:T(8,128)(2,1)S(1)}, u32[]{:S(2)}, u32[]{:S(2)}) collective-permute-start(bf16[1024,512]{1,0:T(8,128)(2,1)S(1)} %pad_maximum_fusion.4.refs_2_), channel_id=1, source_target_pairs={{0,4},{1,5},{2,6},{3,7},{4,0},{5,1},{6,2},{7,3},{8,12},{9,13},{10,... | collective-permute-start | bytes 3145736 | tf_op jit(solution)/shard_map/ppermute | solution.py:85
  1162.5 66.9 %collective-permute-start.106 = (bf16[512,1024]{1,0:T(8,128)(2,1)S(1)}, bf16[512,1024]{1,0:T(8,128)(2,1)S(1)}, u32[]{:S(2)}, u32[]{:S(2)}) collective-permute-start(bf16[512,1024]{1,0:T(8,128)(2,1)S(1)} %pad_maximum_fusion.5), channel_id=1, source_target_pairs={{0,8},{1,9},{2,10},{3,11},{4,12},{5,13},{6,14},{7,15},{8,0},{9,1},... | collective-permute-start | bytes 3145736 | tf_op jit(solution)/shard_map/ppermute | solution.py:85
  (178 other events, 4221.3 us)

commit v11 on v10

--- a/solution.py
+++ b/solution.py
@@ -188,16 +188,6 @@
     far = [scatter_corner(pair, i == 0) for i, pair in enumerate(pairs)]
     seen.update({"gd" + str(i): value for i, value in enumerate(far)})
     return far
-
-
-def scatter_ends(planes, hold):
-    if not is_cube():
-        return scatter_all(
-            [[[a[i] for a in b] for b in pair] for pair in planes for i in range(pair[0][0].shape[0])]
-        )
-    low, high = planes
-    total = low + send(after(high.astype(BF16), *hold), dz=2).astype(F32)
-    return total[0] + send(total[1].astype(BF16), dz=1).astype(F32)
 
 
 def tensor_order():
@@ -945,7 +935,10 @@
         return after(where[k], last, *due(name, seen))
 
     def lower(k):
-        keep, give = down_slots(turn("down" + str(k), 0), scaled[2 * k : 2 * k + 2], w_down, slices)
+        first = slots - 2 - 2 * k
+        keep, give = down_slots(
+            turn("down" + str(k), 0), scaled[first : first + 2], w_down, slices
+        )
         downs[k] = (keep, core_swap(give))
         seen["sd" + str(k)] = downs[k][1]
         return keep
@@ -983,7 +976,8 @@
         last = lower(k)
     pairs = []
     for k in range(slots // 2):
-        pairs.append(place_rows([turn("pd" + str(k), 2 * k), where[2 * k + 1]], at, *downs[k]))
+        first = slots - 2 - 2 * k
+        pairs.append(place_rows([turn("pd" + str(k), first), where[first + 1]], at, *downs[k]))
         last = pairs[k][0][0]
     far = scatter_corners(pairs, seen)
     grad_gate, grad_up = weight_grads(
@@ -1030,10 +1024,9 @@
     )
     branch_pieces = tensor_gather(grad_branch, [grad_down])
 
-    planes = pairs
     if is_cube():
-        plane, sent = scatter_plane(pairs[0], far[0], True, branch_pieces[1:2])
-        planes = [plane]
+        high, sent = scatter_plane(pairs[0], far[0], True, branch_pieces[1:2])
+        high = seen["gz"] = send(high.astype(BF16), dz=2)
         seen.update({"g" + link + "0": value for link, value in sent.items()})
     grad_branch = jnp.concatenate(branch_pieces, axis=1)
 
@@ -1098,9 +1091,13 @@
     small, top_row = expert_total(small, top_row[None], seen)
     head_top = top_row[0, :heads_here]
     if is_cube():
-        free = [seen["qkx"], seen["t1"]]
-        planes.append(scatter_plane(pairs[1], far[1], False, branch_pieces[1:2], free)[0])
-    mixture = scatter_ends(planes, [small, *due("ends", seen)])
+        free = [seen["qkx"], seen["t1"], high]
+        total = added(scatter_plane(pairs[1], far[1], False, branch_pieces[1:2], free)[0], high)
+        mixture = total[0] + send(total[1].astype(BF16), dz=1).astype(F32)
+    else:
+        mixture = scatter_all(
+            [[[a[i] for a in b] for b in pair] for pair in pairs[::-1] for i in range(2)]
+        )
     out = residual + mixture
     sum_moe_gain, sum_query_gain, sum_key_gain = small[E + 1], small[E + 2], small[E + 3]
     every = lax.all_gather(small[: E + 1], "tensor")

time: 1310 us -> 1270 us (0.969)
  starting transfers between devices: 167 us -> 124 us
    ppermute x108, starting transfers between devices: 154 us -> 110 us  [send(): return lax.ppermute(value, BOTH, flip(dz, dx, dy, dc))]
  transfers between devices with their start and end apart: 110 -> 110, of which waited for: 35 -> 37; matrix products, arithmetic and copies ran while one was open for 12% -> 12% of each run, Pallas kernels for 33% -> 33%
where the time goes in v11:
time: 1270 us; the launch traced here: 1250 us
  waiting for transfers between devices  491 us (39%)
  Pallas kernels  458 us (36%)
  starting transfers between devices  124 us (10%)
  other arithmetic  69.8 us (5%)
  local copies, waits for them, and re-layouts  54.3 us (4%)
  matrix products  45.7 us (4%)
    ppermute x108, waiting for transfers between devices, send(): return lax.ppermute(value, BOTH, flip(dz, dx, dy, dc))  491 us
    pallas_call x4, Pallas kernels, expert_slot(): pl.pallas_call(partial(expert_kernel, slices), grid_spec=pltpu.PrefetchSc...  112 us
    ppermute x108, starting transfers between devices, send(): return lax.ppermute(value, BOTH, flip(dz, dx, dy, dc))  110 us
    pallas_call x6, Pallas kernels, place_rows(): pl.pallas_call(partial(place_kernel, slices, held, slots), grid_spec=pltp...  107 us
    pallas_call x8, Pallas kernels, pick_rows(): pl.pallas_call(partial(pick_kernel, group, slices), grid_spec=pltpu.Prefe...  81.4 us
    pallas_call x2, Pallas kernels, weight_grads(): pl.pallas_call(partial(kernel, slots, slices), grid_spec=pltpu.PrefetchSc...  70.4 us
    pallas_call x2, Pallas kernels, down_slots(): pl.pallas_call(partial(down_kernel, slices, slots), grid_spec=pltpu.Prefe...  31.5 us
  transfers between devices with their start and end apart: 110, of which 37 were waited for; matrix products, arithmetic and copies ran while one was open for 12% of the time, Pallas kernels for 33%

profile of v11, /device:TPU:10, one launch (start us, length us, event | category | flops | bytes accessed | tf_op | source)
XLA Modules:
  0.0 1252.5 jit_solution(768713060535297870)
XLA Ops:
  7.5 15.7 %project.1 = (bf16[1024,2048]{1,0:T(8,128)(2,1)}, f32[1024,1]{1,0:T(8,128)}, f32[1024,512]{1,0:T(8,128)}, f32[1024,512]{1,0:T(8,128)}, bf16[1024,512]{1,0:T(8,12...) custom-call(bf16[1024,2048]{1,0:T(8,128)(2,1)} %in_ref.1, f32[1,2048]{1,0:T(1,128)} %bitcast.210, ...), custom_call_target="tpu_custom_call" | custom-call | flops 103079215104 | bytes 352321536 | tf_op jit(solution)/shard_map/project/pallas_call | solution.py:648
  101.8 31.1 %collective-permute-done.10.refs_2_ = bf16[1024,512]{1,0:T(8,128)(2,1)} collective-permute-done((bf16[1024,512]{1,0:T(8,128)(2,1)}, bf16[1024,512]{1,0:T(8,128)(2,1)}, u32[]{:S(2)}, u32[]{:S(2)}) %collective-permute-start.10) | collective-permute-done | bytes 1048608 | tf_op jit(solution)/shard_map/ppermute | solution.py:85
  169.9 19.3 %collective-permute-done.13.refs_2_ = bf16[1024,512]{1,0:T(8,128)(2,1)} collective-permute-done((bf16[1024,512]{1,0:T(8,128)(2,1)}, bf16[1024,512]{1,0:T(8,128)(2,1)}, u32[]{:S(2)}, u32[]{:S(2)}) %collective-permute-start.13) | collective-permute-done | bytes 1048608 | tf_op jit(solution)/shard_map/ppermute | solution.py:85
  195.2 22.6 %collective-permute-done.17.refs_5_ = bf16[1024,512]{1,0:T(8,128)(2,1)S(1)} collective-permute-done((bf16[1024,512]{1,0:T(8,128)(2,1)S(1)}, bf16[1024,512]{1,0:T(8,128)(2,1)S(1)}, u32[]{:S(2)}, u32[]{:S(2)}) %collective-permute-start.17) | collective-permute-done | bytes 1048608 | tf_op jit(solution)/shard_map/ppermute | solution.py:85
  232.3 30.8 %collective-permute-done.24.refs_2_ = bf16[1024,512]{1,0:T(8,128)(2,1)} collective-permute-done((bf16[1024,512]{1,0:T(8,128)(2,1)}, bf16[1024,512]{1,0:T(8,128)(2,1)}, u32[]{:S(2)}, u32[]{:S(2)}) %collective-permute-start.24) | collective-permute-done | bytes 1048608 | tf_op jit(solution)/shard_map/ppermute | solution.py:85
  291.5 27.8 %expert_slot.4 = (bf16[8,320,256]{2,1,0:T(8,128)(2,1)}, bf16[8,320,256]{2,1,0:T(8,128)(2,1)}, bf16[8,320,256]{2,1,0:T(8,128)(2,1)}, f32[8,2,1024]{2,1,0:T(2,128)...) custom-call(s32[10]{0:T(128)} %stack.118.where_ref, s32[8,8,1024]{2,1,0:T(8,128)} %copy.159.refs_0_.refs_1_, ...), custom_call_target="tpu_custom_call" | custom-call | flops 214748364800 | bytes 905969664 | tf_op jit(solution)/shard_map/expert_slot/pallas_call | solution.py:403
  320.5 15.0 %collective-permute-done.27.refs_5_ = bf16[1024,512]{1,0:T(8,128)(2,1)} collective-permute-done((bf16[1024,512]{1,0:T(8,128)(2,1)}, bf16[1024,512]{1,0:T(8,128)(2,1)}, u32[]{:S(2)}, u32[]{:S(2)}) %collective-permute-start.27) | collective-permute-done | bytes 1048608 | tf_op jit(solution)/shard_map/ppermute | solution.py:85
  356.3 14.4 %place_rows.6 = (bf16[1,1024,512]{2,1,0:T(8,128)(2,1)}, bf16[1,1024,512]{2,1,0:T(8,128)(2,1)}, bf16[1,1024,512]{2,1,0:T(8,128)(2,1)}, bf16[1,1024,512]{2,1,0:T(8,128)(2,1)}) custom-call(s32[2]{0:T(128)} %bitcast.206, s32[8,1024,8]{2,1,0:T(8,128)} %bitcast.153, s32[8,1024,8]{2,1,0:T(8,128)} %bitcast.154, ...), custom_call_target="tpu_custom_call" | custom-call | flops 85899345920 | bytes 234881024 | tf_op jit(solution)/shard_map/place_rows/pallas_call | solution.py:502
  378.1 17.8 %collective-permute-done.42 = bf16[1024,512]{1,0:T(8,128)(2,1)S(1)} collective-permute-done((bf16[1024,512]{1,0:T(8,128)(2,1)}, bf16[1024,512]{1,0:T(8,128)(2,1)S(1)}, u32[]{:S(2)}, u32[]{:S(2)}) %collective-permute-start.42) | collective-permute-done | bytes 1048608 | tf_op jit(solution)/shard_map/ppermute | solution.py:85
  402.9 27.8 %expert_slot.5 = (bf16[8,320,256]{2,1,0:T(8,128)(2,1)}, bf16[8,320,256]{2,1,0:T(8,128)(2,1)}, bf16[8,320,256]{2,1,0:T(8,128)(2,1)}, f32[8,2,1024]{2,1,0:T(2,128)...) custom-call(s32[10]{0:T(128)} %stack.121.where_ref, s32[8,8,1024]{2,1,0:T(8,128)} %copy.159.refs_0_.refs_1_, ...), custom_call_target="tpu_custom_call" | custom-call | flops 214748364800 | bytes 905969664 | tf_op jit(solution)/shard_map/expert_slot/pallas_call | solution.py:403
  430.7 16.0 %collective-permute-done.46.refs_4_ = bf16[1024,512]{1,0:T(8,128)(2,1)} collective-permute-done((bf16[1024,512]{1,0:T(8,128)(2,1)}, bf16[1024,512]{1,0:T(8,128)(2,1)}, u32[]{:S(2)}, u32[]{:S(2)}) %collective-permute-start.46) | collective-permute-done | bytes 1048608 | tf_op jit(solution)/shard_map/ppermute | solution.py:85
  448.8 18.6 %collective-permute-done.35.refs_5_ = bf16[1024,512]{1,0:T(8,128)(2,1)} collective-permute-done((bf16[1024,512]{1,0:T(8,128)(2,1)}, bf16[1024,512]{1,0:T(8,128)(2,1)}, u32[]{:S(2)}, u32[]{:S(2)}) %collective-permute-start.35) | collective-permute-done | bytes 1048608 | tf_op jit(solution)/shard_map/ppermute | solution.py:85
  491.0 14.0 %place_rows.7 = (bf16[1,1024,512]{2,1,0:T(8,128)(2,1)}, bf16[1,1024,512]{2,1,0:T(8,128)(2,1)}, bf16[1,1024,512]{2,1,0:T(8,128)(2,1)}, bf16[1,1024,512]{2,1,0:T(8,128)(2,1)}) custom-call(s32[2]{0:T(128)} %bitcast.208, s32[8,1024,8]{2,1,0:T(8,128)} %bitcast.155, s32[8,1024,8]{2,1,0:T(8,128)} %bitcast.156, ...), custom_call_target="tpu_custom_call" | custom-call | flops 85899345920 | bytes 234881024 | tf_op jit(solution)/shard_map/place_rows/pallas_call | solution.py:502
  506.5 27.8 %expert_slot.6 = (bf16[8,320,256]{2,1,0:T(8,128)(2,1)}, bf16[8,320,256]{2,1,0:T(8,128)(2,1)}, bf16[8,320,256]{2,1,0:T(8,128)(2,1)}, f32[8,2,1024]{2,1,0:T(2,128)...) custom-call(s32[10]{0:T(128)} %stack.127.where_ref, s32[8,8,1024]{2,1,0:T(8,128)} %copy.159.refs_0_.refs_1_, ...), custom_call_target="tpu_custom_call" | custom-call | flops 214748364800 | bytes 905969664 | tf_op jit(solution)/shard_map/expert_slot/pallas_call | solution.py:403
  559.7 28.2 %expert_slot.7 = (bf16[8,320,256]{2,1,0:T(8,128)(2,1)}, bf16[8,320,256]{2,1,0:T(8,128)(2,1)}, bf16[8,320,256]{2,1,0:T(8,128)(2,1)}, f32[8,2,1024]{2,1,0:T(2,128)...) custom-call(s32[10]{0:T(128)} %stack.124.where_ref, s32[8,8,1024]{2,1,0:T(8,128)} %copy.159.refs_0_.refs_1_, ...), custom_call_target="tpu_custom_call" | custom-call | flops 214748364800 | bytes 905969664 | tf_op jit(solution)/shard_map/expert_slot/pallas_call | solution.py:403
  607.0 15.7 %down_slots.2 = (bf16[4,2,1280,512]{3,2,1,0:T(8,128)(2,1)}, bf16[4,2,1280,512]{3,2,1,0:T(8,128)(2,1)}) custom-call(s32[10]{0:T(128)} %stack.118.where_ref, bf16[8,320,256]{2,1,0:T(8,128)(2,1)} %get-tuple-element.155.refs_0_.refs_10_, bf16[8,320,256]{2,1,0:T(8,128)(2,1)} %get-tuple-element.164.refs_1_.refs_11_, bf16[8,256,2048]{2,1,0:T(8,128)(2,1)} %refs_2_.3), custom_call_target="tpu_custom_call" | custom-call | flops 85899345920 | bytes 469762048 | tf_op jit(solution)/shard_map/down_slots/pallas_call | solution.py:443
  623.0 28.7 %collective-permute-done.56 = bf16[1024,512]{1,0:T(8,128)(2,1)S(1)} collective-permute-done((bf16[1024,512]{1,0:T(8,128)(2,1)}, bf16[1024,512]{1,0:T(8,128)(2,1)S(1)}, u32[]{:S(2)}, u32[]{:S(2)}) %collective-permute-start.56) | collective-permute-done | bytes 1048608 | tf_op jit(solution)/shard_map/ppermute | solution.py:85
  706.4 15.7 %down_slots.3 = (bf16[4,2,1280,512]{3,2,1,0:T(8,128)(2,1)}, bf16[4,2,1280,512]{3,2,1,0:T(8,128)(2,1)}) custom-call(s32[10]{0:T(128)} %stack.118.where_ref, bf16[8,320,256]{2,1,0:T(8,128)(2,1)} %get-tuple-element.147.refs_0_.refs_8_, bf16[8,320,256]{2,1,0:T(8,128)(2,1)} %get-tuple-element.175.refs_1_.refs_9_, bf16[8,256,2048]{2,1,0:T(8,128)(2,1)} %refs_2_.3), custom_call_target="tpu_custom_call" | custom-call | flops 85899345920 | bytes 469762048 | tf_op jit(solution)/shard_map/down_slots/pallas_call | solution.py:443
  732.5 25.6 %place_rows.10 = (bf16[2,1024,512]{2,1,0:T(8,128)(2,1)}, bf16[2,1024,512]{2,1,0:T(8,128)(2,1)}, bf16[2,1024,512]{2,1,0:T(8,128)(2,1)}, bf16[2,1024,512]{2,1,0:T(8,128)(2,1)}) custom-call(s32[4]{0:T(128)} %pad_add_fusion.3.where_ref, s32[8,1024,8]{2,1,0:T(8,128)} %bitcast.161, s32[8,1024,8]{2,1,0:T(8,128)} %bitcast.162, s32[8,1024,8]{2,1,0:T(8,128)} %bitcast.163, ...), custom_call_target="tpu_custom_call" | custom-call | flops 171798691840 | bytes 469762048 | tf_op jit(solution)/shard_map/place_rows/pallas_call | solution.py:502
  759.2 25.2 %place_rows.11 = (bf16[2,1024,512]{2,1,0:T(8,128)(2,1)}, bf16[2,1024,512]{2,1,0:T(8,128)(2,1)}, bf16[2,1024,512]{2,1,0:T(8,128)(2,1)}, bf16[2,1024,512]{2,1,0:T(8,128)(2,1)}) custom-call(s32[4]{0:T(128)} %pad_add_fusion.4.where_ref, s32[8,1024,8]{2,1,0:T(8,128)} %bitcast.165, s32[8,1024,8]{2,1,0:T(8,128)} %bitcast.166, s32[8,1024,8]{2,1,0:T(8,128)} %bitcast.167, ...), custom_call_target="tpu_custom_call" | custom-call | flops 171798691840 | bytes 469762048 | tf_op jit(solution)/shard_map/place_rows/pallas_call | solution.py:502
  785.4 42.9 %weight_grads.1 = (f32[8,2048,256]{2,1,0:T(8,128)}, f32[8,2048,256]{2,1,0:T(8,128)}) custom-call(s32[10]{0:T(128)} %stack.118.where_ref, bf16[2,2,1280,512]{3,2,1,0:T(8,128)(2,1)} %pick_rows.9.refs_4_.refs_0_, bf16[2,2,1280,512]{3,2,1,0:T(8,128)(2,1)} %collective-permute-done.20.refs_5_.refs_1_, bf16[2,2,1280,512]{3,2,1,0:T(8,128)(2,1)} %pick_rows.15.refs_4_.refs_2_, ...), custom_call_target="tpu_custom_call" | custom-call | flops 160000000000 | bytes 16000000 | tf_op jit(solution)/shard_map/weight_grads/pallas_call | solution.py:559
  843.1 27.5 %weight_down_grads.1 = f32[8,256,2048]{2,1,0:T(8,128)} custom-call(s32[10]{0:T(128)} %stack.118.where_ref, bf16[2,2,1280,512]{3,2,1,0:T(8,128)(2,1)} %pick_rows.8.refs_6_.refs_0_, bf16[2,2,1280,512]{3,2,1,0:T(8,128)(2,1)} %collective-permute-done.21.refs_7_.refs_1_, bf16[2,2,1280,512]{3,2,1,0:T(8,128)(2,1)} %pick_rows.14.refs_6_.refs_2_, ...), custom_call_target="tpu_custom_call" | custom-call | flops 160000000000 | bytes 16000000 | tf_op jit(solution)/shard_map/weight_down_grads/pallas_call | solution.py:559
  872.6 14.2 %collective-permute-done.62 = bf16[2,1024,512]{2,1,0:T(8,128)(2,1)} collective-permute-done((bf16[2,1024,512]{2,1,0:T(8,128)(2,1)}, bf16[2,1024,512]{2,1,0:T(8,128)(2,1)}, u32[]{:S(2)}, u32[]{:S(2)}) %collective-permute-start.62) | collective-permute-done | bytes 2097184 | tf_op jit(solution)/shard_map/ppermute | solution.py:85
  904.9 16.4 %attend_back.1 = (bf16[1024,512]{1,0:T(8,128)(2,1)}, bf16[1024,512]{1,0:T(8,128)(2,1)}, bf16[1024,512]{1,0:T(8,128)(2,1)}, f32[1,1,512]{2,1,0:T(1,128)}, f32[1,1,512]{2,1,0:T(1,128)}) custom-call(s32[4]{0:T(128)} %add_bitcast_fusion.pieces_ref, bf16[1024,512]{1,0:T(8,128)(2,1)} %get-tuple-element.136.q_ref, bf16[1024,512]{1,0:T(8,128)(2,1)} %get-tuple-element.137.k_ref, ...), custom_call_target="tpu_custom_call" | custom-call | flops 85899345920 | bytes 184549376 | tf_op jit(solution)/shard_map/attend_back/pallas_call | solution.py:783
  936.1 16.4 %collective-permute-done.97 = bf16[1024,512]{1,0:T(8,128)(2,1)S(1)} collective-permute-done((bf16[1024,512]{1,0:T(8,128)(2,1)S(1)}, bf16[1024,512]{1,0:T(8,128)(2,1)S(1)}, u32[]{:S(2)}, u32[]{:S(2)}) %collective-permute-start.97) | collective-permute-done | bytes 1048608 | tf_op jit(solution)/shard_map/ppermute | solution.py:85
  1017.8 35.5 %collective-permute-done.101 = bf16[512,512]{1,0:T(8,128)(2,1)S(1)} collective-permute-done((bf16[512,512]{1,0:T(8,128)(2,1)S(1)}, bf16[512,512]{1,0:T(8,128)(2,1)S(1)}, u32[]{:S(2)}, u32[]{:S(2)}) %collective-permute-start.101) | collective-permute-done | bytes 524320 | tf_op jit(solution)/shard_map/ppermute | solution.py:85
  1084.4 16.7 %collective-permute-done.88 = f32[8,128]{1,0:T(8,128)S(1)} collective-permute-done((f32[8,128]{1,0:T(8,128)S(1)}, f32[8,128]{1,0:T(8,128)S(1)}, u32[]{:S(2)}, u32[]{:S(2)}) %collective-permute-start.88) | collective-permute-done | bytes 4128 | tf_op jit(solution)/shard_map/ppermute | solution.py:85
  1104.4 15.9 %collective-permute-done.83 = bf16[2,1024,512]{2,1,0:T(8,128)(2,1)} collective-permute-done((bf16[2,1024,512]{2,1,0:T(8,128)(2,1)}, bf16[2,1024,512]{2,1,0:T(8,128)(2,1)}, u32[]{:S(2)}, u32[]{:S(2)}) %collective-permute-start.83) | collective-permute-done | bytes 2097184 | tf_op jit(solution)/shard_map/ppermute | solution.py:85
  1141.2 21.5 %collective-permute-done.105 = bf16[256,1024]{1,0:T(8,128)(2,1)S(1)} collective-permute-done((bf16[256,1024]{1,0:T(8,128)(2,1)S(1)}, bf16[256,1024]{1,0:T(8,128)(2,1)S(1)}, u32[]{:S(2)}, u32[]{:S(2)}) %collective-permute-start.105) | collective-permute-done | bytes 524320 | tf_op jit(solution)/shard_map/ppermute | solution.py:85
  1177.8 14.0 %collective-permute-done.106 = bf16[512,1024]{1,0:T(8,128)(2,1)S(1)} collective-permute-done((bf16[512,1024]{1,0:T(8,128)(2,1)S(1)}, bf16[512,1024]{1,0:T(8,128)(2,1)S(1)}, u32[]{:S(2)}, u32[]{:S(2)}) %collective-permute-start.106) | collective-permute-done | bytes 1048608 | tf_op jit(solution)/shard_map/ppermute | solution.py:85
  1201.7 19.3 %collective-permute-done.86 = bf16[1024,512]{1,0:T(8,128)(2,1)S(1)} collective-permute-done((bf16[1024,512]{1,0:T(8,128)(2,1)S(1)}, bf16[1024,512]{1,0:T(8,128)(2,1)S(1)}, u32[]{:S(2)}, u32[]{:S(2)}) %collective-permute-start.86) | collective-permute-done | bytes 1048608 | tf_op jit(solution)/shard_map/ppermute | solution.py:85
  1223.9 15.2 %collective-permute-done.107.refs_5_ = bf16[1024,1024]{1,0:T(8,128)(2,1)S(1)} collective-permute-done((bf16[1024,1024]{1,0:T(8,128)(2,1)S(1)}, bf16[1024,1024]{1,0:T(8,128)(2,1)S(1)}, u32[]{:S(2)}, u32[]{:S(2)}) %collective-permute-start.107) | collective-permute-done | bytes 2097184 | tf_op jit(solution)/shard_map/ppermute | solution.py:85
  (547 shorter events, 556.9 us)
Async XLA Ops:
  147.7 143.9 %all-to-all-start = ((f32[8,8,1024]{2,1,0:T(8,128)}), f32[8,8,1024]{2,1,0:T(8,128)}, u32[]{:S(2)}, u32[]{:S(2)}) async-start(f32[8,8,1024]{2,1,0:T(8,128)} %fusion.82), calls=%async_computation | async-start | bytes 524288 | tf_op jit(solution)/shard_map/all_to_all | solution.py:921
  159.2 58.5 %collective-permute-start.17 = (bf16[1024,512]{1,0:T(8,128)(2,1)S(1)}, bf16[1024,512]{1,0:T(8,128)(2,1)S(1)}, u32[]{:S(2)}, u32[]{:S(2)}) collective-permute-start(bf16[1024,512]{1,0:T(8,128)(2,1)S(1)} %collective-permute-done.15.refs_3_), channel_id=1, source_target_pairs={{0,4},{1,5},{2,6},{3,7},{4,0},{5,1},{6,2},{7,3},{8,12},{9,13},{10,... | collective-permute-start | bytes 3145736 | tf_op jit(solution)/shard_map/ppermute | solution.py:85
  189.2 84.6 %collective-permute-start.23 = (bf16[1024,512]{1,0:T(8,128)(2,1)}, bf16[1024,512]{1,0:T(8,128)(2,1)}, u32[]{:S(2)}, u32[]{:S(2)}) collective-permute-start(bf16[1024,512]{1,0:T(8,128)(2,1)} %collective-permute-done.13.refs_2_), channel_id=1, source_target_pairs={{0,2},{1,3},{2,0},{3,1},{4,6},{5,7},{6,4},{7,5},{8,10},{9,11},{10,... | collective-permute-start | bytes 3145736 | tf_op jit(solution)/shard_map/ppermute | solution.py:85
  190.8 84.5 %collective-permute-start.19 = (bf16[1024,512]{1,0:T(8,128)(2,1)}, bf16[1024,512]{1,0:T(8,128)(2,1)}, u32[]{:S(2)}, u32[]{:S(2)}) collective-permute-start(bf16[1024,512]{1,0:T(8,128)(2,1)} %collective-permute-done.13.refs_2_), channel_id=1, source_target_pairs={{0,4},{1,5},{2,6},{3,7},{4,0},{5,1},{6,2},{7,3},{8,12},{9,13},{10,... | collective-permute-start | bytes 3145736 | tf_op jit(solution)/shard_map/ppermute | solution.py:85
  194.7 69.0 %collective-permute-start.18 = (bf16[1024,512]{1,0:T(8,128)(2,1)}, bf16[1024,512]{1,0:T(8,128)(2,1)}, u32[]{:S(2)}, u32[]{:S(2)}) collective-permute-start(bf16[1024,512]{1,0:T(8,128)(2,1)} %collective-permute-done.12.refs_4_), channel_id=1, source_target_pairs={{0,2},{1,3},{2,0},{3,1},{4,6},{5,7},{6,4},{7,5},{8,10},{9,11},{10,... | collective-permute-start | bytes 3145736 | tf_op jit(solution)/shard_map/ppermute | solution.py:85
  232.2 57.7 %collective-permute-start.21 = (bf16[2,2,1280,512]{3,2,1,0:T(8,128)(2,1)}, bf16[2,2,1280,512]{3,2,1,0:T(8,128)(2,1)}, u32[]{:S(2)}, u32[]{:S(2)}) collective-permute-start(bf16[2,2,1280,512]{3,2,1,0:T(8,128)(2,1)} %pick_rows.8.refs_6_.refs_0_), channel_id=1, source_target_pairs={{0,1},{1,0},{2,3},{3,2},{4,5},{5,4},{6,7},{7,6},{8,9},{9,8},{10,11... | collective-permute-start | bytes 15728648 | tf_op jit(solution)/shard_map/ppermute | solution.py:85
  273.9 102.7 %collective-permute-start.39 = (bf16[1024,512]{1,0:T(8,128)(2,1)}, bf16[1024,512]{1,0:T(8,128)(2,1)}, u32[]{:S(2)}, u32[]{:S(2)}) collective-permute-start(bf16[1024,512]{1,0:T(8,128)(2,1)} %collective-permute-done.37.refs_2_), channel_id=1, source_target_pairs={{0,4},{1,5},{2,6},{3,7},{4,0},{5,1},{6,2},{7,3},{8,12},{9,13},{10,... | collective-permute-start | bytes 3145736 | tf_op jit(solution)/shard_map/ppermute | solution.py:85
  275.3 70.3 %collective-permute-start.29 = (bf16[1024,512]{1,0:T(8,128)(2,1)}, bf16[1024,512]{1,0:T(8,128)(2,1)}, u32[]{:S(2)}, u32[]{:S(2)}) collective-permute-start(bf16[1024,512]{1,0:T(8,128)(2,1)} %collective-permute-done.23.refs_3_), channel_id=1, source_target_pairs={{0,4},{1,5},{2,6},{3,7},{4,0},{5,1},{6,2},{7,3},{8,12},{9,13},{10,... | collective-permute-start | bytes 3145736 | tf_op jit(solution)/shard_map/ppermute | solution.py:85
  376.6 103.2 %collective-permute-start.38 = (bf16[1024,512]{1,0:T(8,128)(2,1)}, bf16[1024,512]{1,0:T(8,128)(2,1)}, u32[]{:S(2)}, u32[]{:S(2)}) collective-permute-start(bf16[1024,512]{1,0:T(8,128)(2,1)} %collective-permute-done.37.refs_2_), channel_id=1, source_target_pairs={{0,2},{1,3},{2,0},{3,1},{4,6},{5,7},{6,4},{7,5},{8,10},{9,11},{10,... | collective-permute-start | bytes 3145736 | tf_op jit(solution)/shard_map/ppermute | solution.py:85
  395.9 84.4 %collective-permute-start.40 = (bf16[1024,512]{1,0:T(8,128)(2,1)}, bf16[1024,512]{1,0:T(8,128)(2,1)}, u32[]{:S(2)}, u32[]{:S(2)}) collective-permute-start(bf16[1024,512]{1,0:T(8,128)(2,1)} %collective-permute-done.39.refs_4_), channel_id=1, source_target_pairs={{0,2},{1,3},{2,0},{3,1},{4,6},{5,7},{6,4},{7,5},{8,10},{9,11},{10,... | collective-permute-start | bytes 3145736 | tf_op jit(solution)/shard_map/ppermute | solution.py:85
  402.3 65.0 %collective-permute-start.35 = (bf16[1024,512]{1,0:T(8,128)(2,1)}, bf16[1024,512]{1,0:T(8,128)(2,1)}, u32[]{:S(2)}, u32[]{:S(2)}) collective-permute-start(bf16[1024,512]{1,0:T(8,128)(2,1)} %collective-permute-done.33.refs_3_), channel_id=1, source_target_pairs={{0,4},{1,5},{2,6},{3,7},{4,0},{5,1},{6,2},{7,3},{8,12},{9,13},{10,... | collective-permute-start | bytes 3145736 | tf_op jit(solution)/shard_map/ppermute | solution.py:85
  446.7 87.6 %collective-permute-start.45 = (bf16[1024,512]{1,0:T(8,128)(2,1)}, bf16[1024,512]{1,0:T(8,128)(2,1)}, u32[]{:S(2)}, u32[]{:S(2)}) collective-permute-start(bf16[1024,512]{1,0:T(8,128)(2,1)} %collective-permute-done.44.refs_2_), channel_id=1, source_target_pairs={{0,2},{1,3},{2,0},{3,1},{4,6},{5,7},{6,4},{7,5},{8,10},{9,11},{10,... | collective-permute-start | bytes 3145736 | tf_op jit(solution)/shard_map/ppermute | solution.py:85
  448.1 86.3 %collective-permute-start.47 = (bf16[1024,512]{1,0:T(8,128)(2,1)}, bf16[1024,512]{1,0:T(8,128)(2,1)}, u32[]{:S(2)}, u32[]{:S(2)}) collective-permute-start(bf16[1024,512]{1,0:T(8,128)(2,1)} %collective-permute-done.46.refs_4_), channel_id=1, source_target_pairs={{0,2},{1,3},{2,0},{3,1},{4,6},{5,7},{6,4},{7,5},{8,10},{9,11},{10,... | collective-permute-start | bytes 3145736 | tf_op jit(solution)/shard_map/ppermute | solution.py:85
  478.3 66.8 %collective-permute-start.48 = (bf16[1024,512]{1,0:T(8,128)(2,1)}, bf16[1024,512]{1,0:T(8,128)(2,1)}, u32[]{:S(2)}, u32[]{:S(2)}) collective-permute-start(bf16[1024,512]{1,0:T(8,128)(2,1)} %bitcast.28), channel_id=1, source_target_pairs={{0,4},{1,5},{2,6},{3,7},{4,0},{5,1},{6,2},{7,3},{8,12},{9,13},{10,... | collective-permute-start | bytes 3145736 | tf_op jit(solution)/shard_map/ppermute | solution.py:85
  479.8 65.3 %collective-permute-start.49 = (bf16[1024,512]{1,0:T(8,128)(2,1)}, bf16[1024,512]{1,0:T(8,128)(2,1)}, u32[]{:S(2)}, u32[]{:S(2)}) collective-permute-start(bf16[1024,512]{1,0:T(8,128)(2,1)} %fusion.37), channel_id=1, source_target_pairs={{0,2},{1,3},{2,0},{3,1},{4,6},{5,7},{6,4},{7,5},{8,10},{9,11},{10,... | collective-permute-start | bytes 3145736 | tf_op jit(solution)/shard_map/ppermute | solution.py:85
  600.4 66.7 %collective-permute-start.55 = (bf16[1024,512]{1,0:T(8,128)(2,1)}, bf16[1024,512]{1,0:T(8,128)(2,1)}, u32[]{:S(2)}, u32[]{:S(2)}) collective-permute-start(bf16[1024,512]{1,0:T(8,128)(2,1)} %bitcast.32), channel_id=1, source_target_pairs={{0,2},{1,3},{2,0},{3,1},{4,6},{5,7},{6,4},{7,5},{8,10},{9,11},{10,... | collective-permute-start | bytes 3145736 | tf_op jit(solution)/shard_map/ppermute | solution.py:85
  604.4 64.2 %collective-permute-start.54 = (bf16[1024,512]{1,0:T(8,128)(2,1)}, bf16[1024,512]{1,0:T(8,128)(2,1)}, u32[]{:S(2)}, u32[]{:S(2)}) collective-permute-start(bf16[1024,512]{1,0:T(8,128)(2,1)} %fusion.36), channel_id=1, source_target_pairs={{0,4},{1,5},{2,6},{3,7},{4,0},{5,1},{6,2},{7,3},{8,12},{9,13},{10,... | collective-permute-start | bytes 3145736 | tf_op jit(solution)/shard_map/ppermute | solution.py:85
  622.7 109.2 %collective-permute-start.58 = (bf16[4,2,1280,512]{3,2,1,0:T(8,128)(2,1)}, bf16[4,2,1280,512]{3,2,1,0:T(8,128)(2,1)}, u32[]{:S(2)}, u32[]{:S(2)}) collective-permute-start(bf16[4,2,1280,512]{3,2,1,0:T(8,128)(2,1)} %get-tuple-element.189), channel_id=1, source_target_pairs={{0,1},{1,0},{2,3},{3,2},{4,5},{5,4},{6,7},{7,6},{8,9},{9,8},{10,11... | collective-permute-start | bytes 31457288 | tf_op jit(solution)/shard_map/ppermute | solution.py:85
  684.3 144.0 %collective-permute-start.68 = (bf16[1024,512]{1,0:T(8,128)(2,1)}, bf16[1024,512]{1,0:T(8,128)(2,1)}, u32[]{:S(2)}, u32[]{:S(2)}) collective-permute-start(bf16[1024,512]{1,0:T(8,128)(2,1)} %fusion.30), channel_id=1, source_target_pairs={{0,16},{1,17},{2,18},{3,19},{4,20},{5,21},{6,22},{7,23},{8,24},{9,... | collective-permute-start | bytes 3145736 | tf_op jit(solution)/shard_map/ppermute | solution.py:85
  690.6 137.7 %collective-permute-start.69 = (bf16[1024,512]{1,0:T(8,128)(2,1)}, bf16[1024,512]{1,0:T(8,128)(2,1)}, u32[]{:S(2)}, u32[]{:S(2)}) collective-permute-start(bf16[1024,512]{1,0:T(8,128)(2,1)} %fusion.28), channel_id=1, source_target_pairs={{0,24},{1,25},{2,26},{3,27},{4,28},{5,29},{6,30},{7,31},{8,16},{9,... | collective-permute-start | bytes 3145736 | tf_op jit(solution)/shard_map/ppermute | solution.py:85
  729.9 98.4 %collective-permute-start.67 = (bf16[1024,512]{1,0:T(8,128)(2,1)}, bf16[1024,512]{1,0:T(8,128)(2,1)}, u32[]{:S(2)}, u32[]{:S(2)}) collective-permute-start(bf16[1024,512]{1,0:T(8,128)(2,1)} %fusion.32), channel_id=1, source_target_pairs={{0,8},{1,9},{2,10},{3,11},{4,12},{5,13},{6,14},{7,15},{8,0},{9,1},... | collective-permute-start | bytes 3145736 | tf_op jit(solution)/shard_map/ppermute | solution.py:85
  758.1 76.9 %collective-permute-start.61 = (bf16[2,1024,512]{2,1,0:T(8,128)(2,1)}, bf16[2,1024,512]{2,1,0:T(8,128)(2,1)}, u32[]{:S(2)}, u32[]{:S(2)}) collective-permute-start(bf16[2,1024,512]{2,1,0:T(8,128)(2,1)} %get-tuple-element.200), channel_id=1, source_target_pairs={{0,2},{1,3},{2,0},{3,1},{4,6},{5,7},{6,4},{7,5},{8,10},{9,11},{10,... | collective-permute-start | bytes 6291464 | tf_op jit(solution)/shard_map/ppermute | solution.py:85
  784.4 58.2 %collective-permute-start.60 = (bf16[2,1024,512]{2,1,0:T(8,128)(2,1)}, bf16[2,1024,512]{2,1,0:T(8,128)(2,1)}, u32[]{:S(2)}, u32[]{:S(2)}) collective-permute-start(bf16[2,1024,512]{2,1,0:T(8,128)(2,1)} %get-tuple-element.196), channel_id=1, source_target_pairs={{0,4},{1,5},{2,6},{3,7},{4,0},{5,1},{6,2},{7,3},{8,12},{9,13},{10,... | collective-permute-start | bytes 6291464 | tf_op jit(solution)/shard_map/ppermute | solution.py:85
  891.6 62.9 %collective-permute-start.78 = (bf16[2,1024,512]{2,1,0:T(8,128)(2,1)}, bf16[2,1024,512]{2,1,0:T(8,128)(2,1)S(1)}, u32[]{:S(2)}, u32[]{:S(2)}) collective-permute-start(bf16[2,1024,512]{2,1,0:T(8,128)(2,1)} %get-tuple-element.237), channel_id=1, source_target_pairs={{0,2},{1,3},{2,0},{3,1},{4,6},{5,7},{6,4},{7,5},{8,10},{9,11},{10,... | collective-permute-start | bytes 6291464 | tf_op jit(solution)/shard_map/ppermute | solution.py:85
  933.1 75.9 %collective-permute-start.77 = (bf16[1024,1024]{1,0:T(8,128)(2,1)S(1)}, bf16[1024,1024]{1,0:T(8,128)(2,1)S(1)}, u32[]{:S(2)}, u32[]{:S(2)}) collective-permute-start(bf16[1024,1024]{1,0:T(8,128)(2,1)S(1)} %slice.207), channel_id=1, source_target_pairs={{0,4},{1,5},{2,6},{3,7},{4,0},{5,1},{6,2},{7,3},{8,12},{9,13},{10,... | collective-permute-start | bytes 6291464 | tf_op jit(solution)/shard_map/ppermute | solution.py:85
  991.6 63.3 %collective-permute-start.79 = (bf16[1024,512]{1,0:T(8,128)(2,1)S(1)}, bf16[1024,512]{1,0:T(8,128)(2,1)S(1)}, u32[]{:S(2)}, u32[]{:S(2)}) collective-permute-start(bf16[1024,512]{1,0:T(8,128)(2,1)S(1)} %fusion.49), channel_id=1, source_target_pairs={{0,1},{1,0},{2,3},{3,2},{4,5},{5,4},{6,7},{7,6},{8,9},{9,8},{10,11... | collective-permute-start | bytes 3145736 | tf_op jit(solution)/shard_map/ppermute | solution.py:85
  1011.0 64.8 %collective-permute-start.103 = (bf16[512,1024]{1,0:T(8,128)(2,1)}, bf16[512,1024]{1,0:T(8,128)(2,1)}, u32[]{:S(2)}, u32[]{:S(2)}) collective-permute-start(bf16[512,1024]{1,0:T(8,128)(2,1)} %slice.229), channel_id=1, source_target_pairs={{0,8},{1,9},{2,10},{3,11},{4,12},{5,13},{6,14},{7,15},{8,0},{9,1},... | collective-permute-start | bytes 3145736 | tf_op jit(solution)/shard_map/ppermute | solution.py:85
  1015.9 104.4 %collective-permute-start.83 = (bf16[2,1024,512]{2,1,0:T(8,128)(2,1)}, bf16[2,1024,512]{2,1,0:T(8,128)(2,1)}, u32[]{:S(2)}, u32[]{:S(2)}) collective-permute-start(bf16[2,1024,512]{2,1,0:T(8,128)(2,1)} %add_convert_fusion.2), channel_id=1, source_target_pairs={{0,16},{1,17},{2,18},{3,19},{4,20},{5,21},{6,22},{7,23},{8,24},{9,... | collective-permute-start | bytes 6291464 | tf_op jit(solution)/shard_map/ppermute | solution.py:85
  1053.4 138.7 %collective-permute-start.85 = (bf16[2,1024,512]{2,1,0:T(8,128)(2,1)}, bf16[2,1024,512]{2,1,0:T(8,128)(2,1)}, u32[]{:S(2)}, u32[]{:S(2)}) collective-permute-start(bf16[2,1024,512]{2,1,0:T(8,128)(2,1)} %add_convert_fusion.1), channel_id=1, source_target_pairs={{0,2},{1,3},{2,0},{3,1},{4,6},{5,7},{6,4},{7,5},{8,10},{9,11},{10,... | collective-permute-start | bytes 6291464 | tf_op jit(solution)/shard_map/ppermute | solution.py:85
  1054.9 168.0 %collective-permute-start.96 = (bf16[1024,512]{1,0:T(8,128)(2,1)S(1)}, bf16[1024,512]{1,0:T(8,128)(2,1)}, u32[]{:S(2)}, u32[]{:S(2)}) collective-permute-start(bf16[1024,512]{1,0:T(8,128)(2,1)S(1)} %pad_maximum_fusion.3.refs_0_), channel_id=1, source_target_pairs={{0,4},{1,5},{2,6},{3,7},{4,0},{5,1},{6,2},{7,3},{8,12},{9,13},{10,... | collective-permute-start | bytes 3145736 | tf_op jit(solution)/shard_map/ppermute | solution.py:85
  1120.3 71.8 %collective-permute-start.84 = (bf16[2,1024,512]{2,1,0:T(8,128)(2,1)}, bf16[2,1024,512]{2,1,0:T(8,128)(2,1)S(1)}, u32[]{:S(2)}, u32[]{:S(2)}) collective-permute-start(bf16[2,1024,512]{2,1,0:T(8,128)(2,1)} %get-tuple-element.243), channel_id=1, source_target_pairs={{0,4},{1,5},{2,6},{3,7},{4,0},{5,1},{6,2},{7,3},{8,12},{9,13},{10,... | collective-permute-start | bytes 6291464 | tf_op jit(solution)/shard_map/ppermute | solution.py:85
  1162.7 60.2 %collective-permute-start.102 = (bf16[1024,512]{1,0:T(8,128)(2,1)S(1)}, bf16[1024,512]{1,0:T(8,128)(2,1)S(1)}, u32[]{:S(2)}, u32[]{:S(2)}) collective-permute-start(bf16[1024,512]{1,0:T(8,128)(2,1)S(1)} %copy-done.14), channel_id=1, source_target_pairs={{0,4},{1,5},{2,6},{3,7},{4,0},{5,1},{6,2},{7,3},{8,12},{9,13},{10,... | collective-permute-start | bytes 3145736 | tf_op jit(solution)/shard_map/ppermute | solution.py:85
  (172 other events, 4118.6 us)
